TPU v7x, 32 devices: a whole 2x2x4 slice. The times are simulated.
32 devices in a mesh: groups: 2 (over y), pool: 4 (over z), heads: 2 (over x), rep: 2 (over core).
Axes of the slice: x: 2, y: 2, z: 4, core: 2. Of those that a mesh axis runs over, the one named last changes fastest.
Arguments:
- queries: bfloat16 [4, 4, 8192], P(('groups', 'rep'), 'pool', 'heads'), parts along dimension 0, may hold values from -64 to 64
- latents: bfloat16 [4, 4, 4096, 1024], P(('groups', 'rep'), None, 'pool', 'heads'), parts along dimension 0, may hold values from -6 to 6
- key_latent_maps: bfloat16 [512, 1024], P(None, 'heads'), may hold values from -0.25 to 0.25
- value_latent_maps: bfloat16 [512, 1024], P(None, 'heads'), may hold values from -0.25 to 0.25
- out_weight: bfloat16 [8192, 8192], P('heads', ('pool', 'rep')), may hold values from -2 to 2
- lengths: int32 [4, 4], P(('groups', 'rep')), parts along dimension 0, may hold values from 2048 to 4096, as said below
- selected: int32 [4, 4, 4], P(('groups', 'rep')), parts along dimension 0, may hold values from 0 to 31, as said below
Outputs:
- mixed: bfloat16 [4, 4, 8192], P(('groups', 'rep'), 'heads', 'pool'), parts along dimension 0
There are 2 independent parts, one for each index of `groups`. A program takes and returns all parts, laid end to end along the dimension named above; an argument that names none is the same for every part. Nothing has to cross between parts.
Inputs may be any that keep to these rules, and one draw needn't show every extreme that they name: `lengths`: in every draw one sequence has exactly 2048 cached tokens and another exactly 4096. Each sequence's 4 block indices are distinct and ascending, and every selected block holds at least one token below the sequence's length. Of the blocks 8 k to 8 k + 8 - 1 (any k) at most 2 are selected for one sequence, and in every draw some sequence has exactly 2 selected there.
All inputs are finite; a program needn't handle non-finite values.
Results may differ from a plain program's by a relative error of at most 0.0095.
The roundings to bfloat16 on the way count: a program that leaves them out, or rounds other values in their place, can miss the bound.
Values may be sent and summed in bfloat16 or wider, within the bound.
No kernel may reach another device: no remote copies, remote signals or barrier semaphores. Data moves between devices by JAX's collectives and lax.ppermute only.
A program may use at most 128 MiB of HBM per device.

v0:
```python
import jax
import jax.numpy as jnp
from jax import lax
from jax.sharding import PartitionSpec as P

HEAD_SIZE = 128
LANE = 64
BLOCK = 128
CAP = 2
QUERY_PER_GROUP = 8


ROPE_BASE = 500000.0
MASKED = -1e30


def rope_angles(positions, head_width):
    half_width = head_width // 2
    exponents = jnp.arange(half_width, dtype=jnp.float32) * (2.0 / head_width)
    frequency = jnp.power(jnp.float32(ROPE_BASE), -exponents)
    angles = positions.astype(jnp.float32)[..., None] * frequency
    return (jnp.cos(angles), jnp.sin(angles))


def rotate(values, cosine_part, sine_part):
    half_width = values.shape[-1] // 2
    front_half = values[..., :half_width]
    back_half = values[..., half_width:]
    return jnp.concatenate(
        [
            front_half * cosine_part - back_half * sine_part,
            back_half * cosine_part + front_half * sine_part,
        ],
        axis=-1,
    )


def split_latents(latent_rows):
    leading = latent_rows.shape[0]
    row_total = latent_rows.shape[1] * latent_rows.shape[2]
    latent_width = latent_rows.shape[3] // 2
    paired = latent_rows.reshape(leading, row_total, latent_width // LANE, 2, LANE)
    key_latent_rows = paired[:, :, :, 0, :].reshape(leading, row_total, latent_width)
    value_lat = paired[:, :, :, 1, :].reshape(leading, row_total, latent_width)
    return (key_latent_rows, value_lat)


def token_positions(picked):
    offsets = jnp.arange(BLOCK, dtype=jnp.int32)
    return (picked[:, :, None] * BLOCK + offsets[None, None, :]).reshape(picked.shape[0], -1)


def rotated_keys(key_latent_rows, map_table, positions):
    rebuilt_key_rows = jnp.einsum(
        "jsr,rc->jsc", key_latent_rows, map_table, preferred_element_type=jnp.float32
    )
    group_total = map_table.shape[1] // HEAD_SIZE
    rebuilt_key_rows = rebuilt_key_rows.reshape(
        key_latent_rows.shape[0], key_latent_rows.shape[1], group_total, HEAD_SIZE
    )
    cosine_part, sine_part = rope_angles(positions, HEAD_SIZE)
    return rotate(rebuilt_key_rows, cosine_part[:, :, None, :], sine_part[:, :, None, :]).astype(
        jnp.bfloat16
    )


def rotated_queries(query_rows, seq_lengths, group_total):
    query_head_rows = query_rows.astype(jnp.float32).reshape(
        query_rows.shape[0], group_total, QUERY_PER_GROUP, HEAD_SIZE
    )
    cosine_part, sine_part = rope_angles(seq_lengths, HEAD_SIZE)
    return rotate(
        query_head_rows, cosine_part[:, None, None, :], sine_part[:, None, None, :]
    ).astype(jnp.bfloat16)


def masked_scores(query_rot, rebuilt_key_rows, positions, seq_lengths):
    scores = jnp.einsum(
        "jgqd,jsgd->jgqs", query_rot, rebuilt_key_rows, preferred_element_type=jnp.float32
    ) * HEAD_SIZE ** (-0.5)
    return jnp.where(positions[:, None, None, :] < seq_lengths[:, None, None, None], scores, MASKED)


def compact_slots(received, slot_of):
    return jnp.take_along_axis(received, slot_of[:, :, None, None], axis=1)


def per_device(queries, latents, key_latent_maps, value_latent_maps, out_weight, lengths, selected):
    pool_count = lax.axis_size("pool")
    head_count = lax.axis_size("heads")
    pool_index = lax.axis_index("pool")
    half_seqs = lengths.shape[1]
    seq_count = half_seqs // pool_count
    shard_blocks = latents.shape[2] // BLOCK
    columns = latents.shape[3]
    picks_all = selected[0]
    sel_count = picks_all.shape[1]
    picks_grid = picks_all.reshape(pool_count, seq_count, sel_count).transpose(1, 0, 2)
    in_shard = picks_grid // shard_blocks == pool_index
    shard_rank = jnp.cumsum(in_shard.astype(jnp.int32), axis=2) - 1
    local_block = picks_grid - pool_index * shard_blocks
    slot_ids = jnp.arange(CAP, dtype=jnp.int32)
    slot_match = in_shard[:, :, :, None] & (
        shard_rank[:, :, :, None] == slot_ids[None, None, None, :]
    )
    source_block = jnp.sum(jnp.where(slot_match, local_block[:, :, :, None], 0), axis=2)
    block_view = latents[0].reshape(pool_count, seq_count, shard_blocks, BLOCK, columns)
    dest_ids = jnp.arange(pool_count, dtype=jnp.int32)[None, :, None]
    seq_ids = jnp.arange(seq_count, dtype=jnp.int32)[:, None, None]
    outgoing = block_view[dest_ids, seq_ids, source_block]
    my_picks = lax.dynamic_slice_in_dim(picks_all, pool_index * seq_count, seq_count, 0)
    my_lengths = lax.dynamic_slice_in_dim(lengths[0], pool_index * seq_count, seq_count, 0)
    owner_shard = my_picks // shard_blocks
    before = jnp.sum((owner_shard[:, None, :] < owner_shard[:, :, None]).astype(jnp.int32), axis=2)
    slot_of = owner_shard * CAP + (jnp.arange(sel_count, dtype=jnp.int32)[None, :] - before)
    own_width = value_latent_maps.shape[1]
    own_groups = own_width // HEAD_SIZE
    copies = jnp.broadcast_to(
        outgoing[:, :, None], (seq_count, pool_count, head_count, CAP, BLOCK, columns)
    )
    copies = copies.reshape(seq_count, pool_count * head_count, CAP, BLOCK, columns)
    received = lax.all_to_all(copies, ("pool", "heads"), split_axis=1, concat_axis=1, tiled=True)
    received = received.reshape(seq_count, pool_count, head_count, CAP, BLOCK, columns)
    received = received.transpose(0, 1, 3, 4, 2, 5).reshape(
        seq_count, pool_count * CAP, BLOCK, head_count * columns
    )
    full_rows = compact_slots(received, slot_of)
    key_latent_rows, value_lat = split_latents(full_rows)
    positions = token_positions(my_picks)
    rebuilt_key_rows = rotated_keys(key_latent_rows, key_latent_maps, positions)
    query_rot = rotated_queries(queries[0], my_lengths, own_groups)
    scores = masked_scores(query_rot, rebuilt_key_rows, positions, my_lengths)
    row_max = jnp.max(scores, axis=3, keepdims=True)
    weights = jnp.exp(scores - row_max)
    row_total = jnp.sum(weights, axis=3, keepdims=True)
    attention = (weights / row_total).astype(jnp.bfloat16)
    context = jnp.einsum(
        "jgqs,jsr->jgqr", attention, value_lat, preferred_element_type=jnp.float32
    ).astype(jnp.bfloat16)
    value_latent_table = value_latent_maps.reshape(
        value_latent_maps.shape[0], own_groups, HEAD_SIZE
    )
    heads_out = jnp.einsum(
        "jgqr,rgd->jgqd", context, value_latent_table, preferred_element_type=jnp.float32
    ).astype(jnp.bfloat16)
    heads_out = heads_out.reshape(seq_count, own_groups * QUERY_PER_GROUP * HEAD_SIZE)
    gathered = lax.all_gather(heads_out, "pool", axis=0, tiled=True)
    full_weight = lax.all_gather(out_weight, "rep", axis=1, tiled=True)
    mixed_out = lax.psum_scatter(
        jnp.dot(gathered, full_weight, preferred_element_type=jnp.float32),
        "heads",
        scatter_dimension=0,
        tiled=True,
    )
    return mixed_out.astype(jnp.bfloat16)[None]


def solution(mesh):
    return jax.shard_map(
        per_device,
        mesh=mesh,
        in_specs=(
            P(("groups", "rep"), "pool", "heads"),
            P(("groups", "rep"), None, "pool", "heads"),
            P(None, "heads"),
            P(None, "heads"),
            P("heads", ("pool", "rep")),
            P(("groups", "rep"), None),
            P(("groups", "rep"), None, None),
        ),
        out_specs=P(("groups", "rep"), "heads", "pool"),
        check_vma=False,
    )
```

profile of v0, /device:TPU:0, one launch (start us, length us, event | category | flops | bytes accessed | tf_op | source)
XLA Modules:
  0.0 112.3 jit_solution(3738507465660836744)
XLA Ops:
  6.5 0.7 all-gather.3.cloned.1.call-update
  7.3 0.2 reduce_window_sum.14
  7.5 0.1 select_reduce_fusion
  7.7 0.1 copy.36
  7.8 0.1 reshape.837
  7.9 2.8 %gather_fusion = bf16[8,128,512]{2,1,0:T(8,128)(2,1)S(1)} fusion(bf16[4,1,8,128,512]{4,3,2,0,1:T(8,128)(2,1)} %bitcast.114, s32[8]{0:T(128)S(1)} %reshape.837), kind=kCustom, calls=%fused_computation | custom fusion | bytes 2097248 | tf_op jit(solution)/shard_map/gather | solution.py:110
  10.7 1.6 %broadcast_in_dim.91 = bf16[4,2,2,128,512]{4,3,2,1,0:T(8,128)(2,1)} broadcast(bf16[4,2,128,512]{3,2,1,0:T(8,128)(2,1)S(1)} %bitcast.109), dimensions={0,2,3,4} | broadcast | bytes 3145728 | tf_op jit(solution)/shard_map/broadcast_in_dim | solution.py:118
  12.3 7.3 %all-to-all-start = ((bf16[1,8,2,128,512]{4,3,2,0,1:T(8,128)(2,1)}), bf16[1,8,2,128,512]{4,3,2,0,1:T(8,128)(2,1)S(1)}, u32[]{:S(2)}, u32[]{:S(2)}) async-start(bf16[1,8,2,128,512]{4,3,2,0,1:T(8,128)(2,1)} %bitcast.107), calls=%async_computation | async-start | bytes 4194304 | tf_op jit(solution)/shard_map/all_to_all | solution.py:122
  19.5 1.4 %copy.48 = bf16[512,512]{1,0:T(8,128)(2,1)S(1)} copy(bf16[512,512]{0,1:T(8,128)(2,1)} %bitcast.113) | data formatting | bytes 1048576 | tf_op jit(solution)/shard_map/jsr,rc->jsc/dot_general | solution.py:54
  21.0 0.6 dynamic-slice.2
  22.3 0.6 fusion.57
  22.9 0.7 multiply_sine_fusion.1
  23.6 0.2 convert_reduce_fusion
  23.9 0.1 broadcast_bitcast_fusion
  24.0 0.6 fusion.35
  24.6 0.1 fusion.19
  24.6 0.5 multiply_cosine_fusion
  25.2 42.6 %all-to-all-done = bf16[1,8,2,128,512]{4,3,2,0,1:T(8,128)(2,1)S(1)} async-done(((bf16[1,8,2,128,512]{4,3,2,0,1:T(8,128)(2,1)}), bf16[1,8,2,128,512]{4,3,2,0,1:T(8,128)(2,1)S(1)}, u32[]{:S(2)}, u32[]{:S(2)}) %all-to-all-start) | async-done | bytes 2097184 | tf_op jit(solution)/shard_map/all_to_all | solution.py:122
  67.8 2.3 %copy.37 = bf16[1,4,2,128,2,512]{3,5,4,2,1,0:T(8,128)(2,1)} copy(bf16[1,4,2,128,2,512]{5,3,2,4,1,0:T(8,128)(2,1)S(1)} %bitcast.106) | data formatting | bytes 4194304 | tf_op jit(solution)/shard_map/transpose | solution.py:124
  70.1 2.3 %gather_fusion.1 = bf16[4,128,1024]{1,2,0:T(8,128)(2,1)S(1)} fusion(bf16[8,128,1024]{1,2,0:T(8,128)(2,1)} %bitcast.108, s32[1024]{0:T(1024)S(1)} %pad_clamp_fusion), kind=kCustom, calls=%fused_computation.1 | custom fusion | bytes 2097168 | tf_op jit(solution)/shard_map/jit(take_along_axis)/gather | solution.py:85
  72.5 0.8 copy.38
  73.3 0.4 gather.11
  73.7 0.1 broadcast_select_fusion
  73.8 0.1 fusion.56
  73.9 0.4 convolution_bitcast_fusion
  74.4 0.2 fusion.12
  74.5 0.4 fusion.58
  74.9 0.4 fusion.6
  75.4 13.1 %all-gather = bf16[4,1,4096]{2,1,0:T(2,128)(2,1)S(1)} all-gather(bf16[1,1,4096]{2,1,0:T(2,128)(2,1)S(1)} %reshape.857), channel_id=1, replica_groups=mesh['groups'=2,'pool'=4,'heads'=2,'rep'=2] {'pool'}, dimensions={0}, use_global_device_ids=true | all-gather | bytes 40960 | tf_op jit(solution)/shard_map/all_gather | solution.py:147
  88.5 8.0 %fusion.14 = f32[4,2048]{1,0:T(4,128)S(1)} fusion(bf16[4096,2048]{1,0:T(8,128)(2,1)} %all-gather.3.cloned.1.call-done, bf16[4,1,4096]{2,1,0:T(2,128)(2,1)S(1)} %all-gather), kind=kOutput, calls=%fused_computation.25 | convolution fusion | flops 67108864 | bytes 16842752 | tf_op jit(solution)/shard_map/dot_general | solution.py:150
  96.6 8.3 %all-reduce = bf16[4,2048]{1,0:T(4,128)(2,1)S(1)} all-reduce(f32[4,2048]{1,0:T(4,128)S(1)} %fusion.14), channel_id=2, replica_groups=mesh['groups'=2,'pool'=4,'heads'=2,'rep'=2] {'heads'}, use_global_device_ids=true, to_apply=%region_5.6.clone | all-reduce | flops 8192 | bytes 49152
  104.9 0.6 fusion.21
  (31 shorter events, 0.3 us)
Async XLA Ops:
  6.5 68.4 %copy-start = (bf16[512,512]{1,0:T(8,128)(2,1)S(1)}, bf16[512,512]{1,0:T(8,128)(2,1)}, u32[]{:S(2)}) copy-start(bf16[512,512]{1,0:T(8,128)(2,1)} %param.10) | copy-start | bytes 1572868
  6.5 0.7 copy-start.2
  6.5 82.0 %all-gather.3.cloned.1.call-start = ((), (), s32[]{:S(2)}) async-start(), calls=%async_computation.1 | async-start | bytes 25165824 | tf_op jit(solution)/shard_map/all_gather | solution.py:148
  10.7 10.3 %copy-start.1 = (bf16[1,1,4096]{2,1,0:T(2,128)(2,1)S(1)}, bf16[1,1,4096]{2,1,0:T(2,128)(2,1)}, u32[]{:S(2)}) copy-start(bf16[1,1,4096]{2,1,0:T(2,128)(2,1)} %param.7) | copy-start | bytes 24580
  10.7 10.3 %copy-start.4 = (u32[32]{0:T(128)S(1)}, u32[32]{0:T(128)}, u32[]{:S(2)}) copy-start(u32[32]{0:T(128)} %constant.101) | copy-start | bytes 388
  10.7 11.5 %copy-start.3 = (s32[1,4]{1,0:T(1,128)S(1)}, s32[1,4]{1,0:T(1,128)}, u32[]{:S(2)}) copy-start(s32[1,4]{1,0:T(1,128)} %param.12) | copy-start | bytes 52
  12.3 55.5 %all-to-all-start = ((bf16[1,8,2,128,512]{4,3,2,0,1:T(8,128)(2,1)}), bf16[1,8,2,128,512]{4,3,2,0,1:T(8,128)(2,1)S(1)}, u32[]{:S(2)}, u32[]{:S(2)}) async-start(bf16[1,8,2,128,512]{4,3,2,0,1:T(8,128)(2,1)} %bitcast.107), calls=%async_computation | async-start | bytes 4194304 | tf_op jit(solution)/shard_map/all_to_all | solution.py:122
Sparse Core Ops, SparseCore 0:
  8.9 32.7 all-gather.2
where the time goes:
time: 113 us; the launch traced here: 112 us
  waiting for transfers between devices  43.3 us (38%)
  blocking collectives  21.4 us (19%)
  between operations  14.3 us (13%)
  local copies, waits for them, and re-layouts  13.4 us (12%)
  matrix products  9.31 us (8%)
  starting transfers between devices  7.25 us (6%)
  other arithmetic  3.39 us (3%)
    all_to_all x1, waiting for transfers between devices, per_device(): lax.all_to_all(copies, ('pool', 'heads'), split_axis=1, concat_axis=1, ti...  42.6 us
    all_gather x1, blocking collectives, per_device(): gathered = lax.all_gather(heads_out, 'pool', axis=0, tiled=True)  13.1 us
    unnamed x1, blocking collectives  8.32 us
    dot_general x1, matrix products, per_device(): jnp.dot(gathered, full_weight, preferred_element_type=jnp.float32)  8.04 us
    all_to_all x1, starting transfers between devices, per_device(): lax.all_to_all(copies, ('pool', 'heads'), split_axis=1, concat_axis=1, ti...  7.25 us
    gather x3, local copies, waits for them, and re-layouts, compact_slots(): return jnp.take_along_axis(received, slot_of[:, :, None, None], axis=1)  3.59 us
    gather x1, local copies, waits for them, and re-layouts, per_device(): outgoing = block_view[dest_ids, seq_ids, source_block]  2.8 us
    transpose x1, local copies, waits for them, and re-layouts, per_device(): received.transpose(0, 1, 3, 4, 2, 5)  2.35 us
  transfers between devices with their start and end apart: 2, of which 1 were waited for; matrix products, arithmetic and copies ran while one was open for 15% of the time, Pallas kernels for 0%

commit v1 on v0

v1 whole, which is shorter than its diff:
```python
import functools

import jax
import jax.numpy as jnp
import numpy as np
from jax import lax
from jax.experimental import pallas as pl
from jax.experimental.pallas import tpu as pltpu
from jax.sharding import PartitionSpec as P

HEAD_SIZE = 128
LANE = 64
BLOCK = 128
CAP = 2
QUERY_PER_GROUP = 8

ROPE_BASE = 500000.0
MASKED = -1e30
FAR = 1 << 29

SMEM = pl.BlockSpec(memory_space=pltpu.SMEM)
VMEM = pl.BlockSpec(memory_space=pltpu.VMEM)
ANY = pl.BlockSpec(memory_space=pl.ANY)


def frequencies():
    half = HEAD_SIZE // 2
    exponents = np.arange(half, dtype=np.float32) * np.float32(2.0 / HEAD_SIZE)
    freq = np.power(np.float64(ROPE_BASE), -exponents.astype(np.float64)).astype(np.float32)
    return np.concatenate([freq, freq])


def rope_tables(positions):
    angles = positions.astype(jnp.float32)[..., None] * jnp.asarray(frequencies())
    sign = jnp.asarray(np.where(np.arange(HEAD_SIZE) < HEAD_SIZE // 2, -1.0, 1.0).astype(np.float32))
    return jnp.cos(angles), jnp.sin(angles) * sign


def shift(value, axes, size, step):
    return lax.ppermute(value, axes, [(i, (i + step) % size) for i in range(size)])


def params(mib, **more):
    return pltpu.CompilerParams(vmem_limit_bytes=mib << 20, **more)


def slot_blocks(sel_ref, seq, sel_count, shard, shard_blocks):
    first = jnp.int32(-1)
    second = jnp.int32(-1)
    for i in range(sel_count):
        block = sel_ref[seq, i]
        here = block // shard_blocks == shard
        second = jnp.where(here & (first >= 0), block, second)
        first = jnp.where(here & (first < 0), block, first)
    return first, second


def gather_kernel(pools, sel_count, sel_ref, lat_ref, keys_ref, *rest):
    value_refs = rest[:pools]
    raw, sems = rest[pools:]
    shard_blocks = lat_ref.shape[2] // BLOCK
    columns = lat_ref.shape[3]
    width = columns // 2
    me = lax.axis_index("pool")
    copies = []
    for k in range(pools):
        seq = lax.rem(me + k, pools)
        for c, block in enumerate(slot_blocks(sel_ref, seq, sel_count, me, shard_blocks)):
            local = jnp.maximum(block - me * shard_blocks, 0)
            row = pl.multiple_of(local * BLOCK, BLOCK)
            at = (k * CAP + c) * BLOCK
            copies.append(
                pltpu.make_async_copy(
                    lat_ref.at[0, seq, pl.ds(row, BLOCK), :],
                    raw.at[pl.ds(at, BLOCK), :],
                    sems.at[k * CAP + c],
                )
            )
            copies[-1].start()
    source = lax.broadcasted_iota(jnp.int32, (columns, columns), 0)
    target = lax.broadcasted_iota(jnp.int32, (columns, columns), 1)
    is_value = (target >= width).astype(jnp.int32)
    within = target - is_value * width
    wanted = (within // LANE) * (2 * LANE) + is_value * LANE + within % LANE
    pick = (source == wanted).astype(jnp.float32).astype(jnp.bfloat16)
    rows = CAP * BLOCK
    for k in range(pools):
        for c in range(CAP):
            copies[k * CAP + c].wait()
        packed = jnp.dot(
            raw[k * rows : (k + 1) * rows, :], pick, preferred_element_type=jnp.float32
        ).astype(jnp.bfloat16)
        keys_ref[k * rows : (k + 1) * rows, :] = packed[:, :width]
        value_refs[k][...] = packed[:, width:]


def score_kernel(pools, heads, sel_count, shard_blocks, sel_ref, len_ref, map_ref, cos_ref, sin_ref, *rest):
    key_refs = rest[:heads]
    query_refs = rest[heads : heads + pools]
    out_refs = rest[heads + pools :]
    me = lax.axis_index("pool")
    head = lax.axis_index("heads")
    width = key_refs[0].shape[1]
    groups = map_ref.shape[1] // HEAD_SIZE
    rows = CAP * BLOCK
    maps = []
    for j in range(heads):
        owner = lax.rem(head - j + heads, heads)
        maps.append(map_ref[pl.ds(pl.multiple_of(owner * width, width), width), :])
    column = lax.broadcasted_iota(jnp.int32, (QUERY_PER_GROUP, rows), 1)
    for k in range(pools):
        seq = lax.rem(me + k, pools)
        first, second = slot_blocks(sel_ref, seq, sel_count, me, shard_blocks)
        first = jnp.where(first < 0, FAR, first * BLOCK)
        second = jnp.where(second < 0, FAR, second * BLOCK)
        position = jnp.where(column < BLOCK, first + column, second + column - BLOCK)
        live = position < len_ref[seq]
        at = slice(k * rows, (k + 1) * rows)
        rebuilt = jnp.dot(key_refs[0][at, :], maps[0], preferred_element_type=jnp.float32)
        for j in range(1, heads):
            rebuilt += jnp.dot(key_refs[j][at, :], maps[j], preferred_element_type=jnp.float32)
        cosine = cos_ref[at, :]
        sine = sin_ref[at, :]
        for g in range(groups):
            one = rebuilt[:, g * HEAD_SIZE : (g + 1) * HEAD_SIZE]
            turned = (one * cosine + pltpu.roll(one, HEAD_SIZE // 2, 1) * sine).astype(jnp.bfloat16)
            mine = slice(g * QUERY_PER_GROUP, (g + 1) * QUERY_PER_GROUP)
            scores = lax.dot_general(
                query_refs[k][mine, :].astype(jnp.bfloat16), turned, (((1,), (1,)), ((), ())),
                preferred_element_type=jnp.float32,
            ) * (HEAD_SIZE ** -0.5)
            out_refs[k][mine, :] = jnp.where(live, scores, MASKED)


def compact_kernel(pools, sel_count, shard_blocks, sel_ref, *rest):
    value_refs = rest[:pools]
    out_ref, sem = rest[pools:]
    me = lax.axis_index("pool")
    place = jnp.int32(0)
    for k in range(pools):
        owner = lax.rem(me - k + pools, pools)
        for c, block in enumerate(slot_blocks(sel_ref, me, sel_count, owner, shard_blocks)):
            @pl.when(block >= 0)
            def _(k=k, c=c, place=place):
                pltpu.make_async_copy(
                    value_refs[k].at[pl.ds(c * BLOCK, BLOCK), :],
                    out_ref.at[pl.ds(pl.multiple_of(place * BLOCK, BLOCK), BLOCK), :],
                    sem,
                ).start()
            place = place + (block >= 0).astype(jnp.int32)
    pltpu.make_async_copy(out_ref, out_ref, sem).wait()


def attend_kernel(pools, heads, sel_count, shard_blocks, sel_ref, map_ref, *rest):
    score_refs = rest[:pools]
    value_refs = rest[pools : pools + heads]
    out_ref, dense = rest[pools + heads :]
    me = lax.axis_index("pool")
    head = lax.axis_index("heads")
    width = value_refs[0].shape[1]
    groups = map_ref.shape[1] // HEAD_SIZE
    scores = [ref[...] for ref in score_refs]
    top = functools.reduce(jnp.maximum, [jnp.max(s, axis=1, keepdims=True) for s in scores])
    weights = [jnp.exp(s - top) for s in scores]
    total = functools.reduce(jnp.add, [jnp.sum(w, axis=1, keepdims=True) for w in weights])
    place = jnp.int32(0)
    for k in range(pools):
        owner = lax.rem(me - k + pools, pools)
        attention = weights[k] / total
        for c, block in enumerate(slot_blocks(sel_ref, me, sel_count, owner, shard_blocks)):
            @pl.when(block >= 0)
            def _(c=c, place=place, attention=attention):
                dense[:, pl.ds(pl.multiple_of(place * BLOCK, BLOCK), BLOCK)] = attention[
                    :, c * BLOCK : (c + 1) * BLOCK
                ]
            place = place + (block >= 0).astype(jnp.int32)
    attention = dense[...].astype(jnp.bfloat16)
    mixed = [None] * groups
    for j in range(heads):
        owner = lax.rem(head - j + heads, heads)
        context = jnp.dot(
            attention, value_refs[j][...], preferred_element_type=jnp.float32
        ).astype(jnp.bfloat16)
        rows = pl.ds(pl.multiple_of(owner * width, width), width)
        for g in range(groups):
            part = jnp.dot(
                context[g * QUERY_PER_GROUP : (g + 1) * QUERY_PER_GROUP, :],
                map_ref[rows, g * HEAD_SIZE : (g + 1) * HEAD_SIZE],
                preferred_element_type=jnp.float32,
            )
            mixed[g] = part if j == 0 else mixed[g] + part
    for g in range(groups):
        for q in range(QUERY_PER_GROUP):
            at = (g * QUERY_PER_GROUP + q) * HEAD_SIZE
            out_ref[:, at : at + HEAD_SIZE] = mixed[g][q : q + 1, :].astype(jnp.bfloat16)


def project_kernel(pools, heads, reps, steps, *refs):
    total = pools * reps
    row_refs = refs[:total]
    weight_ref = refs[total]
    out_refs = refs[total + 1 : total + 1 + heads * reps]
    rows, acc = refs[total + 1 + heads * reps :]
    step = pl.program_id(0)
    depth = weight_ref.shape[0]

    @pl.when(step == 0)
    def _():
        for n in range(total):
            rows[n : n + 1, :] = row_refs[n][...].astype(jnp.float32)
        acc[...] = jnp.zeros_like(acc)

    left = rows[:, pl.ds(pl.multiple_of(step * depth, depth), depth)].astype(jnp.bfloat16)
    acc[...] += jnp.dot(left, weight_ref[...], preferred_element_type=jnp.float32)

    @pl.when(step == steps - 1)
    def _():
        here = lax.axis_index("pool") * reps + lax.axis_index("rep")
        at = lax.axis_index("heads") * reps + lax.axis_index("rep")
        count = heads * reps
        each = pools // heads
        for d in range(count):
            target = lax.rem(at + d, count)
            for u in range(each):
                source = ((target // reps) * each + u) * reps + lax.rem(target, reps)
                n = lax.rem(here - source + total, total)
                out_refs[d][u : u + 1, :] = acc[pl.ds(n, 1), :]


def finish_kernel(heads, reps, *refs):
    count = heads * reps
    part_refs = refs[:count]
    out_ref, acc = refs[count:]
    at = lax.axis_index("heads") * reps + lax.axis_index("rep")
    width = part_refs[0].shape[1]
    acc[...] = jnp.zeros_like(acc)
    for d in range(count):
        source = lax.rem(at - d + count, count)
        columns = pl.ds(pl.multiple_of(lax.rem(source, reps) * width, width), width)
        acc[:, columns] += part_refs[d][...]
    out_ref[0] = acc[...].astype(jnp.bfloat16)


def per_device(queries, latents, key_latent_maps, value_latent_maps, out_weight, lengths, selected):
    pools = lax.axis_size("pool")
    heads = lax.axis_size("heads")
    reps = lax.axis_size("rep")
    me = lax.axis_index("pool")
    picks = selected[0]
    spans = lengths[0]
    half_seqs, sel_count = picks.shape
    assert half_seqs == pools and pools % heads == 0
    shard_blocks = latents.shape[2] // BLOCK
    width = latents.shape[3] // 2
    rows = CAP * BLOCK
    own_width = value_latent_maps.shape[1]
    own_heads = own_width // HEAD_SIZE * QUERY_PER_GROUP
    bf16, f32 = jnp.bfloat16, jnp.float32
    shape = jax.ShapeDtypeStruct

    packed = pl.pallas_call(
        functools.partial(gather_kernel, pools, sel_count),
        out_shape=[shape((pools * rows, width), bf16)] + [shape((rows, width), bf16)] * pools,
        in_specs=[SMEM, ANY],
        out_specs=[VMEM] * (pools + 1),
        scratch_shapes=[
            pltpu.VMEM((pools * rows, 2 * width), bf16),
            pltpu.SemaphoreType.DMA((pools * CAP,)),
        ],
        compiler_params=params(40),
        name="gather",
    )(picks, latents)
    keys, values = packed[0], packed[1:]
    key_parts = [keys] + [shift(keys, "heads", heads, j) for j in range(1, heads)]
    value_parts = [values[0]] + [shift(values[k], "pool", pools, k) for k in range(1, pools)]

    query_cos, query_sin = rope_tables(spans[me])
    query = queries[0].astype(f32).reshape(own_heads, HEAD_SIZE)
    query = (query * query_cos + jnp.roll(query, HEAD_SIZE // 2, axis=1) * query_sin).astype(bf16)
    query_parts = [query] + [shift(query, "pool", pools, pools - k) for k in range(1, pools)]

    order = (me + jnp.arange(pools, dtype=jnp.int32)) % pools
    near = picks[order]
    here = near // shard_blocks == me
    rank = jnp.cumsum(here.astype(jnp.int32), axis=1) - 1
    match = here[:, :, None] & (rank[:, :, None] == jnp.arange(CAP, dtype=jnp.int32))
    slots = jnp.sum(jnp.where(match, near[:, :, None], 0), axis=1)
    positions = (slots[:, :, None] * BLOCK + jnp.arange(BLOCK, dtype=jnp.int32)).reshape(-1)
    cosine, sine = rope_tables(positions)

    dense = pl.pallas_call(
        functools.partial(compact_kernel, pools, sel_count, shard_blocks),
        out_shape=shape((sel_count * BLOCK, width), bf16),
        in_specs=[SMEM] + [ANY] * pools,
        out_specs=ANY,
        scratch_shapes=[pltpu.SemaphoreType.DMA],
        compiler_params=params(16),
        name="compact",
    )(picks, *value_parts)
    dense_parts = [dense] + [shift(dense, "heads", heads, j) for j in range(1, heads)]

    scores = pl.pallas_call(
        functools.partial(score_kernel, pools, heads, sel_count, shard_blocks),
        out_shape=[shape((own_heads, rows), f32)] * pools,
        in_specs=[SMEM, SMEM] + [VMEM] * (3 + heads + pools),
        out_specs=[VMEM] * pools,
        compiler_params=params(40),
        name="score",
    )(picks, spans, key_latent_maps, cosine, sine, *key_parts, *query_parts)
    score_parts = [scores[0]] + [shift(scores[k], "pool", pools, k) for k in range(1, pools)]

    mine = pl.pallas_call(
        functools.partial(attend_kernel, pools, heads, sel_count, shard_blocks),
        out_shape=shape((1, own_heads * HEAD_SIZE), bf16),
        in_specs=[SMEM] + [VMEM] * (1 + pools + heads),
        out_specs=VMEM,
        scratch_shapes=[pltpu.VMEM((own_heads, sel_count * BLOCK), f32)],
        compiler_params=params(40),
        name="attend",
    )(picks, value_latent_maps, *score_parts, *dense_parts)
    row_parts = [mine] + [
        shift(mine, ("pool", "rep"), pools * reps, n) for n in range(1, pools * reps)
    ]

    features, own_columns = out_weight.shape
    depth = min(features, 512)
    steps = features // depth
    each = pools // heads
    whole = lambda i: (0, 0)
    partial = pl.pallas_call(
        functools.partial(project_kernel, pools, heads, reps, steps),
        out_shape=[shape((each, own_columns), f32)] * (heads * reps),
        grid=(steps,),
        in_specs=[pl.BlockSpec((1, features), whole)] * (pools * reps)
        + [pl.BlockSpec((depth, own_columns), lambda i: (i, 0))],
        out_specs=[pl.BlockSpec((each, own_columns), whole)] * (heads * reps),
        scratch_shapes=[
            pltpu.VMEM((pools * reps, features), f32),
            pltpu.VMEM((pools * reps, own_columns), f32),
        ],
        compiler_params=params(40),
        name="project",
    )(*row_parts, out_weight)
    final_parts = [partial[0]] + [
        shift(partial[d], ("heads", "rep"), heads * reps, d) for d in range(1, heads * reps)
    ]
    return pl.pallas_call(
        functools.partial(finish_kernel, heads, reps),
        out_shape=shape((1, each, reps * own_columns), bf16),
        in_specs=[VMEM] * (heads * reps),
        out_specs=VMEM,
        scratch_shapes=[pltpu.VMEM((each, reps * own_columns), f32)],
        name="finish",
    )(*final_parts)


def solution(mesh):
    return jax.shard_map(
        per_device,
        mesh=mesh,
        in_specs=(
            P(("groups", "rep"), "pool", "heads"),
            P(("groups", "rep"), None, "pool", "heads"),
            P(None, "heads"),
            P(None, "heads"),
            P("heads", ("pool", "rep")),
            P(("groups", "rep"), None),
            P(("groups", "rep"), None, None),
        ),
        out_specs=P(("groups", "rep"), "heads", "pool"),
        check_vma=False,
    )
```

time: 113 us -> 73 us (0.65)
  waiting for transfers between devices: 43.3 us -> 9.01 us
  starting transfers between devices: 7.25 us -> 32.5 us
  blocking collectives: 21.4 us -> 0 us
  between operations: 14.3 us -> 0.16 us
  Pallas kernels: 0 us -> 11.8 us
  matrix products: 9.31 us -> 0 us
  other arithmetic: 3.39 us -> 6.43 us
  local copies, waits for them, and re-layouts: 13.4 us -> 11.9 us
    all_to_all x1 -> x0, waiting for transfers between devices: 42.6 us -> none  [per_device(): lax.all_to_all(copies, ('pool', 'heads'), split_axis=1, concat_axis=1, ti...]
    ppermute x0 -> x21, starting transfers between devices: none -> 32.5 us  [shift(): lax.ppermute(value, axes, [(i, (i + step) % size) for i in range(size)])]
    all_gather x1 -> x0, blocking collectives: 13.1 us -> none  [per_device(): gathered = lax.all_gather(heads_out, 'pool', axis=0, tiled=True)]
    pallas_call x0 -> x6, Pallas kernels: none -> 11.8 us  [the longest x1 3.51 us: per_device(): pl.pallas_call(functools.partial(gather_kernel, pools, sel_count), out_sh...]
    unnamed x12 -> x24, local copies, waits for them, and re-layouts: 0.64 us -> 10.5 us
    ppermute x0 -> x21, waiting for transfers between devices: none -> 9.01 us  [shift(): lax.ppermute(value, axes, [(i, (i + step) % size) for i in range(size)])]
    dot_general x3 -> x0, matrix products: 8.91 us -> none  [the longest x1 8.04 us: per_device(): jnp.dot(gathered, full_weight, preferred_element_type=jnp.float32)]
    unnamed x1 -> x0, blocking collectives: 8.32 us -> none
  transfers between devices with their start and end apart: 2 -> 21, of which waited for: 1 -> 7; matrix products, arithmetic and copies ran while one was open for 15% -> 6% of each run, Pallas kernels for 0% -> 10%
where the time goes in v1:
time: 73 us; the launch traced here: 71.7 us
  starting transfers between devices  32.5 us (45%)
  local copies, waits for them, and re-layouts  11.9 us (16%)
  Pallas kernels  11.8 us (16%)
  waiting for transfers between devices  9.01 us (12%)
  other arithmetic  6.43 us (9%)
    ppermute x21, starting transfers between devices, shift(): lax.ppermute(value, axes, [(i, (i + step) % size) for i in range(size)])  32.5 us
    unnamed x24, local copies, waits for them, and re-layouts  10.5 us
    ppermute x21, waiting for transfers between devices, shift(): lax.ppermute(value, axes, [(i, (i + step) % size) for i in range(size)])  9.01 us
    pallas_call x1, Pallas kernels, per_device(): pl.pallas_call(functools.partial(gather_kernel, pools, sel_count), out_sh...  3.51 us
    mul x1, other arithmetic, rope_tables(): return (jnp.cos(angles), jnp.sin(angles) * sign)  2.57 us
    pallas_call x1, Pallas kernels, per_device(): pl.pallas_call(functools.partial(score_kernel, pools, heads, sel_count, s...  2.47 us
    pallas_call x1, Pallas kernels, per_device(): pl.pallas_call(functools.partial(project_kernel, pools, heads, reps, step...  2.11 us
  transfers between devices with their start and end apart: 21, of which 7 were waited for; matrix products, arithmetic and copies ran while one was open for 6% of the time, Pallas kernels for 10%

profile of v1, /device:TPU:0, one launch (start us, length us, event | category | flops | bytes accessed | tf_op | source)
XLA Modules:
  0.0 71.7 jit_solution(1084304620654347488)
XLA Ops:
  0.0 0.7 %convert_element_type.43 = f32[1,1,4096]{2,1,0:T(1,128)S(1)} convert(bf16[1,1,4096]{2,1,0:T(2,128)(2,1)} %param.11) | non-fusion elementwise | flops 4096 | bytes 24576 | tf_op jit(solution)/shard_map/convert_element_type | solution.py:278
  0.8 1.2 %fusion.13 = f32[1,1]{1,0:T(1,128)} fusion(s32[1,4]{1,0:T(1,128)} %param.16, s32[]{:T(128)S(6)} %select_n.48), kind=kLoop, calls=%fused_computation.34 | loop fusion | flops 1 | bytes 12 | tf_op jit(solution)/shard_map/convert_element_type | solution.py:34
  2.1 1.4 %multiply_cosine_fusion.1 = (f32[128]{0:T(128)S(1)}, f32[128]{0:T(128)S(1)}) fusion(f32[128]{0:T(128)} %constant.49.clone, f32[]{:T(128)} %bitcast.5, f32[128]{0:T(128)} %constant.50.clone), kind=kLoop, calls=%fused_computation.26 | loop fusion | flops 256 | bytes 2052 | tf_op jit(solution)/shard_map/cos | solution.py:36
  3.5 3.0 %collective-permute-start.3 = (bf16[32,128]{1,0:T(8,128)(2,1)S(1)}, bf16[32,128]{1,0:T(8,128)(2,1)S(1)}, u32[]{:S(2)}, u32[]{:S(2)}) collective-permute-start(bf16[32,128]{1,0:T(8,128)(2,1)S(1)} %fusion.2.rest_2_), channel_id=1, source_target_pairs={{0,4},{4,8},{8,12},{12,0},{1,5},{5,9},{9,13},{13,1},{2,6},{6,10},{... | collective-permute-start | bytes 24584 | tf_op jit(solution)/shard_map/ppermute | solution.py:40
  6.5 2.2 %copy-done.1 = bf16[1,4,1024,512]{3,2,1,0:T(8,128)(2,1)S(1)} copy-done((bf16[1,4,1024,512]{3,2,1,0:T(8,128)(2,1)S(1)}, bf16[1,4,1024,512]{3,2,1,0:T(8,128)(2,1)}, u32[]{:S(2)}) %copy-start.1) | copy-done | bytes 4194328
  9.4 3.5 %gather.7 = (bf16[1024,256]{1,0:T(8,128)(2,1)S(1)}, bf16[256,256]{1,0:T(8,128)(2,1)S(1)}, bf16[256,256]{1,0:T(8,128)(2,1)S(1)}, bf16[256,256]{1,0:T(8,128)(2,1)S(1)}, bf16[256,256]{1,0:T(8,128)(2,1)S(1)}) custom-call(s32[4,4]{1,0:T(4,128)S(1)} %bitcast.8, bf16[1,4,1024,512]{3,2,1,0:T(8,128)(2,1)S(1)} %copy-done.1), custom_call_target="tpu_custom_call" | custom-call | tf_op jit(solution)/shard_map/gather/pallas_call | solution.py:261
  12.9 1.6 %collective-permute-start.7 = (bf16[256,256]{1,0:T(8,128)(2,1)S(1)}, bf16[256,256]{1,0:T(8,128)(2,1)S(1)}, u32[]{:S(2)}, u32[]{:S(2)}) collective-permute-start(bf16[256,256]{1,0:T(8,128)(2,1)S(1)} %get-tuple-element.24), channel_id=1, source_target_pairs={{0,4},{4,8},{8,12},{12,0},{1,5},{5,9},{9,13},{13,1},{2,6},{6,10},{... | collective-permute-start | bytes 393224 | tf_op jit(solution)/shard_map/ppermute | solution.py:40
  14.5 1.1 %collective-permute-start.8 = (bf16[256,256]{1,0:T(8,128)(2,1)S(1)}, bf16[256,256]{1,0:T(8,128)(2,1)S(1)}, u32[]{:S(2)}, u32[]{:S(2)}) collective-permute-start(bf16[256,256]{1,0:T(8,128)(2,1)S(1)} %get-tuple-element.25), channel_id=1, source_target_pairs={{0,8},{4,12},{8,0},{12,4},{1,9},{5,13},{9,1},{13,5},{2,10},{6,14},... | collective-permute-start | bytes 393224 | tf_op jit(solution)/shard_map/ppermute | solution.py:40
  15.6 2.8 %collective-permute-start.9 = (bf16[256,256]{1,0:T(8,128)(2,1)S(1)}, bf16[256,256]{1,0:T(8,128)(2,1)S(1)}, u32[]{:S(2)}, u32[]{:S(2)}) collective-permute-start(bf16[256,256]{1,0:T(8,128)(2,1)S(1)} %get-tuple-element.26), channel_id=1, source_target_pairs={{0,12},{4,0},{8,4},{12,8},{1,13},{5,1},{9,5},{13,9},{2,14},{6,2},{... | collective-permute-start | bytes 393224 | tf_op jit(solution)/shard_map/ppermute | solution.py:40
  18.5 1.5 %collective-permute-start = (bf16[1024,256]{1,0:T(8,128)(2,1)S(1)}, bf16[1024,256]{1,0:T(8,128)(2,1)S(1)}, u32[]{:S(2)}, u32[]{:S(2)}) collective-permute-start(bf16[1024,256]{1,0:T(8,128)(2,1)S(1)} %get-tuple-element.18.rest_0_), channel_id=1, source_target_pairs={{0,2},{2,0},{1,3},{3,1},{4,6},{6,4},{5,7},{7,5},{8,10},{10,8},{9,1... | collective-permute-start | bytes 1572872 | tf_op jit(solution)/shard_map/ppermute | solution.py:40
  20.0 1.2 %gather_fusion = s32[4,4]{1,0:T(4,128)S(1)} fusion(s32[4,4]{1,0:T(4,128)} %bitcast.7, s32[1024]{0:T(1024)S(1)} %pad_clamp_fusion), kind=kCustom, calls=%fused_computation | custom fusion | bytes 144 | tf_op jit(solution)/shard_map/gather | solution.py:283
  21.8 5.9 %collective-permute-start.2 = (bf16[32,128]{1,0:T(8,128)(2,1)S(1)}, bf16[32,128]{1,0:T(8,128)(2,1)S(1)}, u32[]{:S(2)}, u32[]{:S(2)}) collective-permute-start(bf16[32,128]{1,0:T(8,128)(2,1)S(1)} %fusion.2.rest_2_), channel_id=1, source_target_pairs={{0,8},{4,12},{8,0},{12,4},{1,9},{5,13},{9,1},{13,5},{2,10},{6,14},... | collective-permute-start | bytes 24584 | tf_op jit(solution)/shard_map/ppermute | solution.py:40
  27.7 2.3 %collective-permute-start.1 = (bf16[32,128]{1,0:T(8,128)(2,1)S(1)}, bf16[32,128]{1,0:T(8,128)(2,1)S(1)}, u32[]{:S(2)}, u32[]{:S(2)}) collective-permute-start(bf16[32,128]{1,0:T(8,128)(2,1)S(1)} %fusion.2.rest_2_), channel_id=1, source_target_pairs={{0,12},{4,0},{8,4},{12,8},{1,13},{5,1},{9,5},{13,9},{2,14},{6,2},{... | collective-permute-start | bytes 24584 | tf_op jit(solution)/shard_map/ppermute | solution.py:40
  30.0 0.7 copy-done.5
  30.7 1.1 %compact.1.rest_4_ = bf16[512,256]{1,0:T(8,128)(2,1)S(1)} custom-call(s32[4,4]{1,0:T(4,128)S(1)} %bitcast.9, bf16[256,256]{1,0:T(8,128)(2,1)S(1)} %get-tuple-element.23.rest_0_, bf16[256,256]{1,0:T(8,128)(2,1)S(1)} %collective-permute-done.7.rest_1_, bf16[256,256]{1,0:T(8,128)(2,1)S(1)} %collective-permute-done.8.rest_2_, ...), custom_call_target="tpu_custom_call" | custom-call | tf_op jit(solution)/shard_map/compact/pallas_call | solution.py:291
  31.8 1.6 %collective-permute-start.10 = (bf16[512,256]{1,0:T(8,128)(2,1)S(1)}, bf16[512,256]{1,0:T(8,128)(2,1)S(1)}, u32[]{:S(2)}, u32[]{:S(2)}) collective-permute-start(bf16[512,256]{1,0:T(8,128)(2,1)S(1)} %compact.1.rest_4_), channel_id=1, source_target_pairs={{0,2},{2,0},{1,3},{3,1},{4,6},{6,4},{5,7},{7,5},{8,10},{10,8},{9,1... | collective-permute-start | bytes 786440 | tf_op jit(solution)/shard_map/ppermute | solution.py:40
  33.3 2.6 %fusion = (f32[1024,128]{1,0:T(8,128)S(1)}, f32[1024,128]{1,0:T(8,128)S(1)}) fusion(f32[128]{0:T(128)} %constant.50.clone, f32[128]{0:T(128)} %constant.49.clone, f32[1024]{0:T(1024)S(1)} %bitcast.15), kind=kLoop, calls=%fused_computation.3 | loop fusion | flops 262144 | bytes 1053696 | tf_op jit(solution)/shard_map/mul | solution.py:36
  36.0 1.0 %copy-done.2 = bf16[512,512]{1,0:T(8,128)(2,1)S(1)} copy-done((bf16[512,512]{1,0:T(8,128)(2,1)S(1)}, bf16[512,512]{1,0:T(8,128)(2,1)}, u32[]{:S(2)}) %copy-start.2) | copy-done | bytes 524312
  38.3 2.5 %score.1 = (f32[32,256]{1,0:T(8,128)S(1)}, f32[32,256]{1,0:T(8,128)S(1)}, f32[32,256]{1,0:T(8,128)S(1)}, f32[32,256]{1,0:T(8,128)S(1)}) custom-call(s32[4,4]{1,0:T(4,128)S(1)} %bitcast.10, s32[4]{0:T(128)S(1)} %bitcast.12, bf16[512,512]{1,0:T(8,128)(2,1)S(1)} %copy-done.2, f32[1024,128]{1,0:T(8,128)S(1)} %get-tuple-element.36.cos_ref, ...), custom_call_target="tpu_custom_call" | custom-call | tf_op jit(solution)/shard_map/score/pallas_call | solution.py:302
  41.4 3.3 %collective-permute-start.6 = (f32[32,256]{1,0:T(8,128)S(1)}, f32[32,256]{1,0:T(8,128)S(1)}, u32[]{:S(2)}, u32[]{:S(2)}) collective-permute-start(f32[32,256]{1,0:T(8,128)S(1)} %get-tuple-element.22), channel_id=1, source_target_pairs={{0,12},{4,0},{8,4},{12,8},{1,13},{5,1},{9,5},{13,9},{2,14},{6,2},{... | collective-permute-start | bytes 98312 | tf_op jit(solution)/shard_map/ppermute | solution.py:40
  44.7 1.9 %collective-permute-done.4.rest_1_ = f32[32,256]{1,0:T(8,128)S(1)} collective-permute-done((f32[32,256]{1,0:T(8,128)S(1)}, f32[32,256]{1,0:T(8,128)S(1)}, u32[]{:S(2)}, u32[]{:S(2)}) %collective-permute-start.4) | collective-permute-done | bytes 32800 | tf_op jit(solution)/shard_map/ppermute | solution.py:40
  47.1 1.2 %attend.1.refs_0_ = bf16[1,4096]{1,0:T(2,128)(2,1)S(1)} custom-call(s32[4,4]{1,0:T(4,128)S(1)} %bitcast.11, bf16[512,512]{1,0:T(8,128)(2,1)S(1)} %copy-done.3, f32[32,256]{1,0:T(8,128)S(1)} %get-tuple-element.19.rest_0_, f32[32,256]{1,0:T(8,128)S(1)} %collective-permute-done.4.rest_1_, f32[32,256]{1,0:T(8,128)S(1)} %collective-permute-done.5.rest_2_, ...), custom_call_target="tpu_custom_call" | custom-call | tf_op jit(solution)/shard_map/attend/pallas_call | solution.py:312
  48.4 3.3 %collective-permute-start.16 = (bf16[1,4096]{1,0:T(2,128)(2,1)S(1)}, bf16[1,4096]{1,0:T(2,128)(2,1)S(1)}, u32[]{:S(2)}, u32[]{:S(2)}) collective-permute-start(bf16[1,4096]{1,0:T(2,128)(2,1)S(1)} %attend.1.refs_0_), channel_id=1, source_target_pairs={{0,12},{1,13},{4,0},{5,1},{8,4},{9,5},{12,8},{13,9},{2,14},{3,15},... | collective-permute-start | bytes 24584 | tf_op jit(solution)/shard_map/ppermute | solution.py:40
  51.7 2.7 %collective-permute-start.14 = (bf16[1,4096]{1,0:T(2,128)(2,1)S(1)}, bf16[1,4096]{1,0:T(2,128)(2,1)S(1)}, u32[]{:S(2)}, u32[]{:S(2)}) collective-permute-start(bf16[1,4096]{1,0:T(2,128)(2,1)S(1)} %attend.1.refs_0_), channel_id=1, source_target_pairs={{0,8},{1,9},{4,12},{5,13},{8,0},{9,1},{12,4},{13,5},{2,10},{3,11},... | collective-permute-start | bytes 24584 | tf_op jit(solution)/shard_map/ppermute | solution.py:40
  55.1 1.4 %collective-permute-done.14.refs_4_ = bf16[1,4096]{1,0:T(2,128)(2,1)S(1)} collective-permute-done((bf16[1,4096]{1,0:T(2,128)(2,1)S(1)}, bf16[1,4096]{1,0:T(2,128)(2,1)S(1)}, u32[]{:S(2)}, u32[]{:S(2)}) %collective-permute-start.14) | collective-permute-done | bytes 8224 | tf_op jit(solution)/shard_map/ppermute | solution.py:40
  56.6 1.9 %collective-permute-done.13.refs_3_ = bf16[1,4096]{1,0:T(2,128)(2,1)S(1)} collective-permute-done((bf16[1,4096]{1,0:T(2,128)(2,1)S(1)}, bf16[1,4096]{1,0:T(2,128)(2,1)S(1)}, u32[]{:S(2)}, u32[]{:S(2)}) %collective-permute-start.13) | collective-permute-done | bytes 8224 | tf_op jit(solution)/shard_map/ppermute | solution.py:40
  58.5 1.5 %collective-permute-done.12.refs_2_ = bf16[1,4096]{1,0:T(2,128)(2,1)S(1)} collective-permute-done((bf16[1,4096]{1,0:T(2,128)(2,1)S(1)}, bf16[1,4096]{1,0:T(2,128)(2,1)S(1)}, u32[]{:S(2)}, u32[]{:S(2)}) %collective-permute-start.12) | collective-permute-done | bytes 8224 | tf_op jit(solution)/shard_map/ppermute | solution.py:40
  60.0 3.4 %copy-done = bf16[4096,1024]{1,0:T(8,128)(2,1)S(1)} copy-done((bf16[4096,1024]{1,0:T(8,128)(2,1)S(1)}, bf16[4096,1024]{1,0:T(8,128)(2,1)}, u32[]{:S(2)}) %copy-start) | copy-done | bytes 8388632
  63.4 2.1 %project.1 = (f32[2,1024]{1,0:T(2,128)S(1)}, f32[2,1024]{1,0:T(2,128)S(1)}, f32[2,1024]{1,0:T(2,128)S(1)}, f32[2,1024]{1,0:T(2,128)S(1)}) custom-call(bf16[1,4096]{1,0:T(2,128)(2,1)S(1)} %attend.1.refs_0_, bf16[1,4096]{1,0:T(2,128)(2,1)S(1)} %collective-permute-done.11.refs_1_, bf16[1,4096]{1,0:T(2,128)(2,1)S(1)} %collective-permute-done.12.refs_2_, ...), custom_call_target="tpu_custom_call" | custom-call | tf_op jit(solution)/shard_map/project/pallas_call | solution.py:330
  66.7 1.4 %collective-permute-start.20 = (f32[2,1024]{1,0:T(2,128)S(1)}, f32[2,1024]{1,0:T(2,128)S(1)}, u32[]{:S(2)}, u32[]{:S(2)}) collective-permute-start(f32[2,1024]{1,0:T(2,128)S(1)} %get-tuple-element.30), channel_id=1, source_target_pairs={{0,3},{1,0},{2,1},{3,2},{4,7},{5,4},{6,5},{7,6},{8,11},{9,8},{10,9... | collective-permute-start | bytes 24584 | tf_op jit(solution)/shard_map/ppermute | solution.py:40
  68.1 1.1 %collective-permute-done.18.refs_1_ = f32[2,1024]{1,0:T(2,128)S(1)} collective-permute-done((f32[2,1024]{1,0:T(2,128)S(1)}, f32[2,1024]{1,0:T(2,128)S(1)}, u32[]{:S(2)}, u32[]{:S(2)}) %collective-permute-start.18) | collective-permute-done | bytes 8224 | tf_op jit(solution)/shard_map/ppermute | solution.py:40
  70.4 1.4 %finish.1 = bf16[1,2,2048]{2,1,0:T(2,128)(2,1)} custom-call(f32[2,1024]{1,0:T(2,128)} %copy-done.7, f32[2,1024]{1,0:T(2,128)} %copy-done.9, f32[2,1024]{1,0:T(2,128)} %copy-done.10, f32[2,1024]{1,0:T(2,128)} %copy-done.11), custom_call_target="tpu_custom_call" | custom-call | tf_op jit(solution)/shard_map/finish/pallas_call | solution.py:347
  (56 shorter events, 7.0 us)
Async XLA Ops:
  3.5 32.4 %collective-permute-start.3 = (bf16[32,128]{1,0:T(8,128)(2,1)S(1)}, bf16[32,128]{1,0:T(8,128)(2,1)S(1)}, u32[]{:S(2)}, u32[]{:S(2)}) collective-permute-start(bf16[32,128]{1,0:T(8,128)(2,1)S(1)} %fusion.2.rest_2_), channel_id=1, source_target_pairs={{0,4},{4,8},{8,12},{12,0},{1,5},{5,9},{9,13},{13,1},{2,6},{6,10},{... | collective-permute-start | bytes 24584 | tf_op jit(solution)/shard_map/ppermute | solution.py:40
  6.5 2.2 %copy-start.1 = (bf16[1,4,1024,512]{3,2,1,0:T(8,128)(2,1)S(1)}, bf16[1,4,1024,512]{3,2,1,0:T(8,128)(2,1)}, u32[]{:S(2)}) copy-start(bf16[1,4,1024,512]{3,2,1,0:T(8,128)(2,1)} %lat_ref.1) | copy-start | bytes 12582916
  8.7 0.7 copy-start.4
  9.4 37.7 %copy-start.3 = (bf16[512,512]{1,0:T(8,128)(2,1)S(1)}, bf16[512,512]{1,0:T(8,128)(2,1)}, u32[]{:S(2)}) copy-start(bf16[512,512]{1,0:T(8,128)(2,1)} %map_ref.3) | copy-start | bytes 1572868
  12.9 8.9 %collective-permute-start.7 = (bf16[256,256]{1,0:T(8,128)(2,1)S(1)}, bf16[256,256]{1,0:T(8,128)(2,1)S(1)}, u32[]{:S(2)}, u32[]{:S(2)}) collective-permute-start(bf16[256,256]{1,0:T(8,128)(2,1)S(1)} %get-tuple-element.24), channel_id=1, source_target_pairs={{0,4},{4,8},{8,12},{12,0},{1,5},{5,9},{9,13},{13,1},{2,6},{6,10},{... | collective-permute-start | bytes 393224 | tf_op jit(solution)/shard_map/ppermute | solution.py:40
  14.5 13.1 %collective-permute-start.8 = (bf16[256,256]{1,0:T(8,128)(2,1)S(1)}, bf16[256,256]{1,0:T(8,128)(2,1)S(1)}, u32[]{:S(2)}, u32[]{:S(2)}) collective-permute-start(bf16[256,256]{1,0:T(8,128)(2,1)S(1)} %get-tuple-element.25), channel_id=1, source_target_pairs={{0,8},{4,12},{8,0},{12,4},{1,9},{5,13},{9,1},{13,5},{2,10},{6,14},... | collective-permute-start | bytes 393224 | tf_op jit(solution)/shard_map/ppermute | solution.py:40
  15.6 14.4 %collective-permute-start.9 = (bf16[256,256]{1,0:T(8,128)(2,1)S(1)}, bf16[256,256]{1,0:T(8,128)(2,1)S(1)}, u32[]{:S(2)}, u32[]{:S(2)}) collective-permute-start(bf16[256,256]{1,0:T(8,128)(2,1)S(1)} %get-tuple-element.26), channel_id=1, source_target_pairs={{0,12},{4,0},{8,4},{12,8},{1,13},{5,1},{9,5},{13,9},{2,14},{6,2},{... | collective-permute-start | bytes 393224 | tf_op jit(solution)/shard_map/ppermute | solution.py:40
  18.5 17.5 %collective-permute-start = (bf16[1024,256]{1,0:T(8,128)(2,1)S(1)}, bf16[1024,256]{1,0:T(8,128)(2,1)S(1)}, u32[]{:S(2)}, u32[]{:S(2)}) collective-permute-start(bf16[1024,256]{1,0:T(8,128)(2,1)S(1)} %get-tuple-element.18.rest_0_), channel_id=1, source_target_pairs={{0,2},{2,0},{1,3},{3,1},{4,6},{6,4},{5,7},{7,5},{8,10},{10,8},{9,1... | collective-permute-start | bytes 1572872 | tf_op jit(solution)/shard_map/ppermute | solution.py:40
  21.8 14.1 %collective-permute-start.2 = (bf16[32,128]{1,0:T(8,128)(2,1)S(1)}, bf16[32,128]{1,0:T(8,128)(2,1)S(1)}, u32[]{:S(2)}, u32[]{:S(2)}) collective-permute-start(bf16[32,128]{1,0:T(8,128)(2,1)S(1)} %fusion.2.rest_2_), channel_id=1, source_target_pairs={{0,8},{4,12},{8,0},{12,4},{1,9},{5,13},{9,1},{13,5},{2,10},{6,14},... | collective-permute-start | bytes 24584 | tf_op jit(solution)/shard_map/ppermute | solution.py:40
  27.7 8.3 %collective-permute-start.1 = (bf16[32,128]{1,0:T(8,128)(2,1)S(1)}, bf16[32,128]{1,0:T(8,128)(2,1)S(1)}, u32[]{:S(2)}, u32[]{:S(2)}) collective-permute-start(bf16[32,128]{1,0:T(8,128)(2,1)S(1)} %fusion.2.rest_2_), channel_id=1, source_target_pairs={{0,12},{4,0},{8,4},{12,8},{1,13},{5,1},{9,5},{13,9},{2,14},{6,2},{... | collective-permute-start | bytes 24584 | tf_op jit(solution)/shard_map/ppermute | solution.py:40
  30.0 0.7 copy-start.5
  31.8 12.9 %collective-permute-start.10 = (bf16[512,256]{1,0:T(8,128)(2,1)S(1)}, bf16[512,256]{1,0:T(8,128)(2,1)S(1)}, u32[]{:S(2)}, u32[]{:S(2)}) collective-permute-start(bf16[512,256]{1,0:T(8,128)(2,1)S(1)} %compact.1.rest_4_), channel_id=1, source_target_pairs={{0,2},{2,0},{1,3},{3,1},{4,6},{6,4},{5,7},{7,5},{8,10},{10,8},{9,1... | collective-permute-start | bytes 786440 | tf_op jit(solution)/shard_map/ppermute | solution.py:40
  35.9 1.0 %copy-start.2 = (bf16[512,512]{1,0:T(8,128)(2,1)S(1)}, bf16[512,512]{1,0:T(8,128)(2,1)}, u32[]{:S(2)}) copy-start(bf16[512,512]{1,0:T(8,128)(2,1)} %map_ref.2) | copy-start | bytes 1572868
  37.0 0.7 copy-start.6
  37.7 0.7 copy-start.8
  40.8 5.7 %collective-permute-start.4 = (f32[32,256]{1,0:T(8,128)S(1)}, f32[32,256]{1,0:T(8,128)S(1)}, u32[]{:S(2)}, u32[]{:S(2)}) collective-permute-start(f32[32,256]{1,0:T(8,128)S(1)} %get-tuple-element.20), channel_id=1, source_target_pairs={{0,4},{4,8},{8,12},{12,0},{1,5},{5,9},{9,13},{13,1},{2,6},{6,10},{... | collective-permute-start | bytes 98312 | tf_op jit(solution)/shard_map/ppermute | solution.py:40
  40.8 5.7 %collective-permute-start.5 = (f32[32,256]{1,0:T(8,128)S(1)}, f32[32,256]{1,0:T(8,128)S(1)}, u32[]{:S(2)}, u32[]{:S(2)}) collective-permute-start(f32[32,256]{1,0:T(8,128)S(1)} %get-tuple-element.21), channel_id=1, source_target_pairs={{0,8},{4,12},{8,0},{12,4},{1,9},{5,13},{9,1},{13,5},{2,10},{6,14},... | collective-permute-start | bytes 98312 | tf_op jit(solution)/shard_map/ppermute | solution.py:40
  41.4 5.7 %collective-permute-start.6 = (f32[32,256]{1,0:T(8,128)S(1)}, f32[32,256]{1,0:T(8,128)S(1)}, u32[]{:S(2)}, u32[]{:S(2)}) collective-permute-start(f32[32,256]{1,0:T(8,128)S(1)} %get-tuple-element.22), channel_id=1, source_target_pairs={{0,12},{4,0},{8,4},{12,8},{1,13},{5,1},{9,5},{13,9},{2,14},{6,2},{... | collective-permute-start | bytes 98312 | tf_op jit(solution)/shard_map/ppermute | solution.py:40
  48.4 6.1 %collective-permute-start.17 = (bf16[1,4096]{1,0:T(2,128)(2,1)S(1)}, bf16[1,4096]{1,0:T(2,128)(2,1)S(1)}, u32[]{:S(2)}, u32[]{:S(2)}) collective-permute-start(bf16[1,4096]{1,0:T(2,128)(2,1)S(1)} %attend.1.refs_0_), channel_id=1, source_target_pairs={{0,13},{1,0},{4,1},{5,4},{8,5},{9,8},{12,9},{13,12},{2,15},{3,2},{... | collective-permute-start | bytes 24584 | tf_op jit(solution)/shard_map/ppermute | solution.py:40
  48.4 6.3 %collective-permute-start.16 = (bf16[1,4096]{1,0:T(2,128)(2,1)S(1)}, bf16[1,4096]{1,0:T(2,128)(2,1)S(1)}, u32[]{:S(2)}, u32[]{:S(2)}) collective-permute-start(bf16[1,4096]{1,0:T(2,128)(2,1)S(1)} %attend.1.refs_0_), channel_id=1, source_target_pairs={{0,12},{1,13},{4,0},{5,1},{8,4},{9,5},{12,8},{13,9},{2,14},{3,15},... | collective-permute-start | bytes 24584 | tf_op jit(solution)/shard_map/ppermute | solution.py:40
  51.7 3.4 %collective-permute-start.15 = (bf16[1,4096]{1,0:T(2,128)(2,1)S(1)}, bf16[1,4096]{1,0:T(2,128)(2,1)S(1)}, u32[]{:S(2)}, u32[]{:S(2)}) collective-permute-start(bf16[1,4096]{1,0:T(2,128)(2,1)S(1)} %attend.1.refs_0_), channel_id=1, source_target_pairs={{0,9},{1,12},{4,13},{5,0},{8,1},{9,4},{12,5},{13,8},{2,11},{3,14},... | collective-permute-start | bytes 24584 | tf_op jit(solution)/shard_map/ppermute | solution.py:40
  51.7 4.8 %collective-permute-start.14 = (bf16[1,4096]{1,0:T(2,128)(2,1)S(1)}, bf16[1,4096]{1,0:T(2,128)(2,1)S(1)}, u32[]{:S(2)}, u32[]{:S(2)}) collective-permute-start(bf16[1,4096]{1,0:T(2,128)(2,1)S(1)} %attend.1.refs_0_), channel_id=1, source_target_pairs={{0,8},{1,9},{4,12},{5,13},{8,0},{9,1},{12,4},{13,5},{2,10},{3,11},... | collective-permute-start | bytes 24584 | tf_op jit(solution)/shard_map/ppermute | solution.py:40
  54.4 4.1 %collective-permute-start.13 = (bf16[1,4096]{1,0:T(2,128)(2,1)S(1)}, bf16[1,4096]{1,0:T(2,128)(2,1)S(1)}, u32[]{:S(2)}, u32[]{:S(2)}) collective-permute-start(bf16[1,4096]{1,0:T(2,128)(2,1)S(1)} %attend.1.refs_0_), channel_id=1, source_target_pairs={{0,5},{1,8},{4,9},{5,12},{8,13},{9,0},{12,1},{13,4},{2,7},{3,10},{... | collective-permute-start | bytes 24584 | tf_op jit(solution)/shard_map/ppermute | solution.py:40
  54.4 5.5 %collective-permute-start.12 = (bf16[1,4096]{1,0:T(2,128)(2,1)S(1)}, bf16[1,4096]{1,0:T(2,128)(2,1)S(1)}, u32[]{:S(2)}, u32[]{:S(2)}) collective-permute-start(bf16[1,4096]{1,0:T(2,128)(2,1)S(1)} %attend.1.refs_0_), channel_id=1, source_target_pairs={{0,4},{1,5},{4,8},{5,9},{8,12},{9,13},{12,0},{13,1},{2,6},{3,7},{6... | collective-permute-start | bytes 24584 | tf_op jit(solution)/shard_map/ppermute | solution.py:40
  54.8 5.2 %collective-permute-start.11 = (bf16[1,4096]{1,0:T(2,128)(2,1)S(1)}, bf16[1,4096]{1,0:T(2,128)(2,1)S(1)}, u32[]{:S(2)}, u32[]{:S(2)}) collective-permute-start(bf16[1,4096]{1,0:T(2,128)(2,1)S(1)} %attend.1.refs_0_), channel_id=1, source_target_pairs={{0,1},{1,4},{4,5},{5,8},{8,9},{9,12},{12,13},{13,0},{2,3},{3,6},{6... | collective-permute-start | bytes 24584 | tf_op jit(solution)/shard_map/ppermute | solution.py:40
  60.0 3.4 %copy-start = (bf16[4096,1024]{1,0:T(8,128)(2,1)S(1)}, bf16[4096,1024]{1,0:T(8,128)(2,1)}, u32[]{:S(2)}) copy-start(bf16[4096,1024]{1,0:T(8,128)(2,1)} %refs_8_.1) | copy-start | bytes 25165828
  65.5 0.6 copy-start.7
  66.1 3.1 %collective-permute-start.18 = (f32[2,1024]{1,0:T(2,128)S(1)}, f32[2,1024]{1,0:T(2,128)S(1)}, u32[]{:S(2)}, u32[]{:S(2)}) collective-permute-start(f32[2,1024]{1,0:T(2,128)S(1)} %get-tuple-element.28), channel_id=1, source_target_pairs={{0,1},{1,2},{2,3},{3,0},{4,5},{5,6},{6,7},{7,4},{8,9},{9,10},{10,1... | collective-permute-start | bytes 24584 | tf_op jit(solution)/shard_map/ppermute | solution.py:40
  66.1 3.7 %collective-permute-start.19 = (f32[2,1024]{1,0:T(2,128)S(1)}, f32[2,1024]{1,0:T(2,128)S(1)}, u32[]{:S(2)}, u32[]{:S(2)}) collective-permute-start(f32[2,1024]{1,0:T(2,128)S(1)} %get-tuple-element.29), channel_id=1, source_target_pairs={{0,2},{1,3},{2,0},{3,1},{4,6},{5,7},{6,4},{7,5},{8,10},{9,11},{10,... | collective-permute-start | bytes 24584 | tf_op jit(solution)/shard_map/ppermute | solution.py:40
  66.7 3.1 %collective-permute-start.20 = (f32[2,1024]{1,0:T(2,128)S(1)}, f32[2,1024]{1,0:T(2,128)S(1)}, u32[]{:S(2)}, u32[]{:S(2)}) collective-permute-start(f32[2,1024]{1,0:T(2,128)S(1)} %get-tuple-element.30), channel_id=1, source_target_pairs={{0,3},{1,0},{2,1},{3,2},{4,7},{5,4},{6,5},{7,6},{8,11},{9,8},{10,9... | collective-permute-start | bytes 24584 | tf_op jit(solution)/shard_map/ppermute | solution.py:40
  69.2 0.6 copy-start.9
  69.8 0.6 copy-start.10
  (1 other events, 0.6 us)

commit v2 on v1

v2 whole, which is shorter than its diff:
```python
import functools

import jax
import jax.numpy as jnp
import numpy as np
from jax import lax
from jax.experimental import pallas as pl
from jax.experimental.pallas import tpu as pltpu
from jax.sharding import PartitionSpec as P

HEAD_SIZE = 128
LANE = 64
BLOCK = 128
CAP = 2
QUERY_PER_GROUP = 8

ROPE_BASE = 500000.0
MASKED = -1e30
FAR = 1 << 29

SMEM = pl.BlockSpec(memory_space=pltpu.SMEM)
VMEM = pl.BlockSpec(memory_space=pltpu.VMEM)
ANY = pl.BlockSpec(memory_space=pl.ANY)
HBM = pl.BlockSpec(memory_space=pltpu.HBM)


def frequencies():
    half = HEAD_SIZE // 2
    exponents = np.arange(half, dtype=np.float32) * np.float32(2.0 / HEAD_SIZE)
    freq = np.power(np.float64(ROPE_BASE), -exponents.astype(np.float64)).astype(np.float32)
    return np.concatenate([freq, freq])[None, :]


def swap(value, axes, size, step):
    return lax.ppermute(value, axes, [(i, i ^ step) for i in range(size)])


def in_hbm(value):
    return pltpu.with_memory_space_constraint(value, pltpu.HBM)


def in_vmem(value):
    return pltpu.with_memory_space_constraint(value, pltpu.VMEM)


def params(mib, **more):
    return pltpu.CompilerParams(vmem_limit_bytes=mib << 20, **more)


def slot_blocks(sel_ref, seq, shard, shard_blocks):
    first = jnp.int32(-1)
    second = jnp.int32(-1)
    for i in range(sel_ref.shape[2]):
        block = sel_ref[0, seq, i]
        here = (block >= shard * shard_blocks) & (block < (shard + 1) * shard_blocks)
        second = jnp.where(here & (first >= 0), block, second)
        first = jnp.where(here & (first < 0), block, first)
    return first, second


def pack_queries(rows, width):
    if width >= HEAD_SIZE:
        each = rows.shape[0] // (width // HEAD_SIZE)
        return [rows[i * each : (i + 1) * each, :] for i in range(width // HEAD_SIZE)], 1
    return [rows[:, i * width : (i + 1) * width] for i in range(HEAD_SIZE // width)], 0


def unpack_queries(packed, width):
    if width >= HEAD_SIZE:
        return jnp.concatenate(
            [packed[:, i * HEAD_SIZE : (i + 1) * HEAD_SIZE] for i in range(width // HEAD_SIZE)], axis=0
        )
    each = packed.shape[0] // (HEAD_SIZE // width)
    return jnp.concatenate(
        [packed[i * each : (i + 1) * each, :] for i in range(HEAD_SIZE // width)], axis=1
    )


def gather_kernel(pools, sel_ref, len_ref, lat_ref, query_ref, freq_ref, near_ref, far_ref, *rest):
    pay_refs = rest[:pools]
    raw, query, sems = rest[pools:]
    shard_blocks = lat_ref.shape[2] // BLOCK
    columns = lat_ref.shape[3]
    width = columns // 2
    rows = CAP * BLOCK
    me = lax.axis_index("pool")
    copies = []
    for k in range(pools):
        seq = me ^ k
        for c, block in enumerate(slot_blocks(sel_ref, seq, me, shard_blocks)):
            local = jnp.maximum(block - me * shard_blocks, 0)
            copies.append(
                pltpu.make_async_copy(
                    lat_ref.at[0, seq, pl.ds(pl.multiple_of(local * BLOCK, BLOCK), BLOCK), :],
                    raw.at[pl.ds((k * CAP + c) * BLOCK, BLOCK), :],
                    sems.at[k * CAP + c],
                )
            )
            copies[-1].start()
    lane = lax.broadcasted_iota(jnp.int32, (1, HEAD_SIZE), 1)
    angle = len_ref[0, me].astype(jnp.float32) * freq_ref[...]
    cosine = jnp.cos(angle)
    sine = jnp.where(lane < HEAD_SIZE // 2, -jnp.sin(angle), jnp.sin(angle))
    for n in range(query.shape[0]):
        query[n : n + 1, :] = query_ref[0, :, n * HEAD_SIZE : (n + 1) * HEAD_SIZE].astype(jnp.float32)
    turned = query[...] * cosine + pltpu.roll(query[...], HEAD_SIZE // 2, 1) * sine
    pieces, axis = pack_queries(turned, width)
    packed_query = jnp.concatenate(pieces, axis=axis).astype(jnp.bfloat16)
    chunk = min(4 * LANE, columns)
    half = chunk // 2
    source = lax.broadcasted_iota(jnp.int32, (chunk, chunk), 0)
    target = lax.broadcasted_iota(jnp.int32, (chunk, chunk), 1)
    within = target & (half - 1)
    wanted = ((within >> 6) << 7) + (within & (LANE - 1)) + jnp.where(target >= half, LANE, 0)
    pick = (source == wanted).astype(jnp.float32).astype(jnp.bfloat16)
    for k in range(pools - 1, -1, -1):
        for c in range(CAP):
            copies[k * CAP + c].wait()
        keys_ref, at = (far_ref, k - pools // 2) if k >= pools // 2 else (near_ref, k)
        for j in range(columns // chunk):
            packed = jnp.dot(
                raw[k * rows : (k + 1) * rows, j * chunk : (j + 1) * chunk], pick,
                preferred_element_type=jnp.float32,
            ).astype(jnp.bfloat16)
            keys_ref[at * rows : (at + 1) * rows, j * half : (j + 1) * half] = packed[:, :half]
            pay_refs[k][:rows, j * half : (j + 1) * half] = packed[:, half:]
        pay_refs[k][rows:, :] = packed_query


def table_kernel(
    pools, shard_blocks, sel_ref, len_ref, freq_ref, after_ref, key_map_ref, value_map_ref,
    cos_ref, sin_ref, live_ref, place_ref, key_out_ref, value_out_ref, sems,
):
    del after_ref
    loads = [
        pltpu.make_async_copy(key_map_ref, key_out_ref, sems.at[0]),
        pltpu.make_async_copy(value_map_ref, value_out_ref, sems.at[1]),
    ]
    for load in loads:
        load.start()
    me = lax.axis_index("pool")
    lane = lax.broadcasted_iota(jnp.int32, (BLOCK, HEAD_SIZE), 1)
    row = lax.broadcasted_iota(jnp.int32, (BLOCK, HEAD_SIZE), 0)
    front = lane < HEAD_SIZE // 2
    across = lax.broadcasted_iota(jnp.int32, (1, BLOCK), 1)
    place = jnp.int32(0)
    for k in range(pools):
        seq = me ^ k
        found = slot_blocks(sel_ref, seq, me, shard_blocks)
        one, two = [jnp.maximum(block, 0) * BLOCK for block in found]
        angle = (jnp.where(front, one, two) + row).astype(jnp.float32) * freq_ref[...]
        for ref, table, sign in ((cos_ref, jnp.cos(angle), 1.0), (sin_ref, jnp.sin(angle), -1.0)):
            turned = pltpu.roll(table, HEAD_SIZE // 2, 1)
            at = k * CAP * BLOCK
            ref[at : at + BLOCK, :] = jnp.where(front, sign * table, turned)
            ref[at + BLOCK : at + 2 * BLOCK, :] = jnp.where(front, sign * turned, table)
        mine = slot_blocks(sel_ref, me, seq, shard_blocks)
        for c in range(CAP):
            start = jnp.where(found[c] < 0, FAR, found[c] * BLOCK)
            live_ref[k : k + 1, c * BLOCK : (c + 1) * BLOCK] = (start + across < len_ref[0, seq]).astype(jnp.int32)
            at = (k * CAP + c) * BLOCK
            used = mine[c] >= 0
            place_ref[:, at : at + BLOCK] = jnp.where(used, place, -1) + 0 * across
            place = place + used.astype(jnp.int32)
    for load in loads:
        load.wait()


def score_kernel(first, count, heads, map_ref, cos_ref, sin_ref, live_ref, *rest):
    key_refs = rest[:heads]
    pay_refs = rest[heads : heads + count]
    out_refs = rest[heads + count :]
    head = lax.axis_index("heads")
    width = key_refs[0].shape[1]
    groups = map_ref.shape[1] // HEAD_SIZE
    rows = CAP * BLOCK
    maps = []
    for j in range(heads):
        owner = head ^ j
        maps.append(map_ref[pl.ds(pl.multiple_of(owner * width, width), width), :])
    for i in range(count):
        k = first + i
        live = live_ref[k : k + 1, :] > 0
        queries = unpack_queries(pay_refs[i][rows:, :], width)
        at = slice(i * rows, (i + 1) * rows)
        rebuilt = jnp.dot(key_refs[0][at, :], maps[0], preferred_element_type=jnp.float32)
        for j in range(1, heads):
            rebuilt += jnp.dot(key_refs[j][at, :], maps[j], preferred_element_type=jnp.float32)
        cosine = cos_ref[k * rows : (k + 1) * rows, :]
        sine = sin_ref[k * rows : (k + 1) * rows, :]
        for g in range(groups):
            one = rebuilt[:, g * HEAD_SIZE : (g + 1) * HEAD_SIZE]
            turned = (one * cosine + pltpu.roll(one, HEAD_SIZE // 2, 1) * sine).astype(jnp.bfloat16)
            mine = slice(g * QUERY_PER_GROUP, (g + 1) * QUERY_PER_GROUP)
            scores = lax.dot_general(
                queries[mine, :], turned, (((1,), (1,)), ((), ())), preferred_element_type=jnp.float32
            ) * (HEAD_SIZE ** -0.5)
            out_refs[i][mine, :] = jnp.where(live, scores, MASKED)


def compact_kernel(pools, shard_blocks, sel_ref, after_ref, *rest):
    del after_ref
    pay_refs = rest[:pools]
    out_ref, sem = rest[pools:]
    me = lax.axis_index("pool")
    place = jnp.int32(0)
    for k in range(pools):
        for c, block in enumerate(slot_blocks(sel_ref, me, me ^ k, shard_blocks)):
            @pl.when(block >= 0)
            def _(k=k, c=c, place=place):
                pltpu.make_async_copy(
                    pay_refs[k].at[pl.ds(c * BLOCK, BLOCK), :],
                    out_ref.at[pl.ds(pl.multiple_of(place * BLOCK, BLOCK), BLOCK), :],
                    sem,
                ).start()
            place = place + (block >= 0).astype(jnp.int32)
    pltpu.make_async_copy(out_ref, out_ref, sem).wait()


def attend_kernel(pools, heads, map_ref, place_ref, *rest):
    score_refs = rest[:pools]
    value_refs = rest[pools : pools + heads]
    out_ref = rest[pools + heads]
    head = lax.axis_index("heads")
    width = value_refs[0].shape[1]
    groups = map_ref.shape[1] // HEAD_SIZE
    scores = [ref[...] for ref in score_refs]
    top = functools.reduce(jnp.maximum, [jnp.max(s, axis=1, keepdims=True) for s in scores])
    weights = [jnp.exp(s - top) for s in scores]
    total = functools.reduce(jnp.add, [jnp.sum(w, axis=1, keepdims=True) for w in weights])
    slots = []
    for k in range(pools):
        attention = weights[k] / total
        for c in range(CAP):
            at = (k * CAP + c) * BLOCK
            slots.append((place_ref[:, at : at + BLOCK], attention[:, c * BLOCK : (c + 1) * BLOCK]))
    dense = []
    for i in range(value_refs[0].shape[0] // BLOCK):
        chosen = jnp.zeros_like(slots[0][1])
        for place, attention in slots:
            chosen = jnp.where(place == i, attention, chosen)
        dense.append(chosen)
    attention = jnp.concatenate(dense, axis=1).astype(jnp.bfloat16)
    mixed = [None] * groups
    for j in range(heads):
        owner = head ^ j
        context = jnp.dot(
            attention, value_refs[j][...], preferred_element_type=jnp.float32
        ).astype(jnp.bfloat16)
        rows = pl.ds(pl.multiple_of(owner * width, width), width)
        for g in range(groups):
            part = jnp.dot(
                context[g * QUERY_PER_GROUP : (g + 1) * QUERY_PER_GROUP, :],
                map_ref[rows, g * HEAD_SIZE : (g + 1) * HEAD_SIZE],
                preferred_element_type=jnp.float32,
            )
            mixed[g] = part if j == 0 else mixed[g] + part
    for g in range(groups):
        for q in range(QUERY_PER_GROUP):
            at = (g * QUERY_PER_GROUP + q) * HEAD_SIZE
            out_ref[:, at : at + HEAD_SIZE] = mixed[g][q : q + 1, :].astype(jnp.bfloat16)


def pair_kernel(*refs):
    for i, ref in enumerate(refs[:-1]):
        refs[-1][i : i + 1, :] = ref[...].astype(jnp.float32).astype(jnp.bfloat16)


def project_kernel(pools, heads, reps, *refs):
    row_refs = refs[:pools]
    weight_ref = refs[pools]
    out_refs = refs[pools + 1 : pools + 1 + heads * reps]
    acc = refs[pools + 1 + heads * reps]
    left = jnp.concatenate([ref[...].astype(jnp.float32) for ref in row_refs], axis=0).astype(jnp.bfloat16)
    acc[...] = jnp.dot(left, weight_ref[...], preferred_element_type=jnp.float32)
    here = lax.axis_index("pool") * reps + lax.axis_index("rep")
    at = lax.axis_index("heads") * reps + lax.axis_index("rep")
    each = pools // heads
    for d in range(heads * reps):
        target = at ^ d
        for u in range(each):
            source = ((target // reps) * each + u) * reps + target % reps
            out_refs[d][u : u + 1, :] = acc[pl.ds(here ^ source, 1), :]


def per_device(queries, latents, key_latent_maps, value_latent_maps, out_weight, lengths, selected):
    pools = lax.axis_size("pool")
    heads = lax.axis_size("heads")
    reps = lax.axis_size("rep")
    half_seqs, sel_count = selected.shape[1:]
    assert half_seqs == pools and pools % heads == 0
    shard_blocks = latents.shape[2] // BLOCK
    width = latents.shape[3] // 2
    rows = CAP * BLOCK
    own_heads = queries.shape[2] // HEAD_SIZE
    query_rows = queries.shape[2] // width
    bf16, f32, i32 = jnp.bfloat16, jnp.float32, jnp.int32
    shape = jax.ShapeDtypeStruct
    freq = jnp.asarray(frequencies())

    packed = pl.pallas_call(
        functools.partial(gather_kernel, pools),
        out_shape=[shape((pools // 2 * rows, width), bf16)] * 2
        + [shape((rows + query_rows, width), bf16)] * pools,
        in_specs=[SMEM, SMEM, HBM, VMEM, VMEM],
        out_specs=[VMEM] * (pools + 2),
        scratch_shapes=[
            pltpu.VMEM((pools * rows, 2 * width), bf16),
            pltpu.VMEM((own_heads, HEAD_SIZE), f32),
            pltpu.SemaphoreType.DMA((pools * CAP,)),
        ],
        compiler_params=params(16),
        name="gather",
    )(in_hbm(selected), in_hbm(lengths), in_hbm(latents), in_hbm(queries), in_hbm(freq))
    near, far, pays = packed[0], packed[1], packed[2:]
    pay_parts = [pays[0]] + [swap(pays[k], "pool", pools, k) for k in range(1, pools)]
    far_parts = [far] + [swap(far, "heads", heads, j) for j in range(1, heads)]
    near_parts = [near] + [swap(near, "heads", heads, j) for j in range(1, heads)]

    cosine, sine, live, place, key_maps, value_maps = pl.pallas_call(
        functools.partial(table_kernel, pools, shard_blocks),
        out_shape=[shape((pools * rows, HEAD_SIZE), f32)] * 2
        + [shape((pools, rows), i32), shape((1, pools * rows), i32)]
        + [shape(key_latent_maps.shape, bf16), shape(value_latent_maps.shape, bf16)],
        in_specs=[SMEM, SMEM, VMEM, ANY, ANY, ANY],
        out_specs=[VMEM] * 6,
        scratch_shapes=[pltpu.SemaphoreType.DMA((2,))],
        compiler_params=params(16),
        name="tables",
    )(in_hbm(selected), in_hbm(lengths), in_hbm(freq), far, in_hbm(key_latent_maps), in_hbm(value_latent_maps))

    dense = pl.pallas_call(
        functools.partial(compact_kernel, pools, shard_blocks),
        out_shape=shape((sel_count * BLOCK, width), bf16),
        in_specs=[SMEM] + [ANY] * (pools + 1),
        out_specs=ANY,
        scratch_shapes=[pltpu.SemaphoreType.DMA],
        compiler_params=params(8),
        name="compact",
    )(in_hbm(selected), place, *pay_parts)
    dense_parts = [dense] + [swap(dense, "heads", heads, j) for j in range(1, heads)]

    def score(first, count, key_parts):
        return pl.pallas_call(
            functools.partial(score_kernel, first, count, heads),
            out_shape=[shape((own_heads, rows), f32)] * count,
            in_specs=[VMEM] * (4 + heads + count),
            out_specs=[VMEM] * count,
            compiler_params=params(20),
            name="score",
        )(key_maps, cosine, sine, live, *key_parts, *pay_parts[first : first + count])

    middle = pools // 2
    far_scores = score(middle, middle, far_parts)
    near_scores = score(0, middle, near_parts)
    scores = [*near_scores, *far_scores]
    score_parts = [scores[0]] + [swap(scores[k], "pool", pools, k) for k in range(1, pools)]

    mine = pl.pallas_call(
        functools.partial(attend_kernel, pools, heads),
        out_shape=shape((1, own_heads * HEAD_SIZE), bf16),
        in_specs=[VMEM] * (2 + pools + heads),
        out_specs=VMEM,
        compiler_params=params(16),
        name="attend",
    )(value_maps, place, *score_parts, *dense_parts)
    pair = pl.pallas_call(
        pair_kernel,
        out_shape=shape((reps, own_heads * HEAD_SIZE), bf16),
        in_specs=[VMEM] * reps,
        out_specs=VMEM,
        compiler_params=params(4),
        name="pair",
    )(mine, *[swap(mine, "rep", reps, r) for r in range(1, reps)])
    row_parts = [pair] + [swap(pair, "pool", pools, k) for k in range(1, pools)]

    features, own_columns = out_weight.shape
    each = pools // heads
    partial = pl.pallas_call(
        functools.partial(project_kernel, pools, heads, reps),
        out_shape=[shape((each, own_columns), f32)] * (heads * reps),
        in_specs=[VMEM] * (pools + 1),
        out_specs=[VMEM] * (heads * reps),
        scratch_shapes=[pltpu.VMEM((pools * reps, own_columns), f32)],
        compiler_params=params(24),
        name="project",
    )(*row_parts, in_vmem(out_weight))
    parts = [partial[0]] + [
        swap(partial[d], ("heads", "rep"), heads * reps, d) for d in range(1, heads * reps)
    ]
    blocks = [sum(parts[h * reps + r] for h in range(heads)) for r in range(reps)]
    rep = lax.axis_index("rep")
    columns = []
    for r in range(reps):
        columns.append(functools.reduce(
            lambda kept, d: jnp.where(rep ^ d == r, blocks[d], kept), range(1, reps), blocks[0]))
    return jnp.concatenate(columns, axis=1).astype(bf16)[None]


def solution(mesh):
    return jax.shard_map(
        per_device,
        mesh=mesh,
        in_specs=(
            P(("groups", "rep"), "pool", "heads"),
            P(("groups", "rep"), None, "pool", "heads"),
            P(None, "heads"),
            P(None, "heads"),
            P("heads", ("pool", "rep")),
            P(("groups", "rep"), None),
            P(("groups", "rep"), None, None),
        ),
        out_specs=P(("groups", "rep"), "heads", "pool"),
        check_vma=False,
    )
```

time: 73 us -> 49.7 us (0.68); the launches traced: 71.7 us -> 49.5 us
  local copies, waits for them, and re-layouts: 11.9 us -> 0.01 us
  starting transfers between devices: 32.5 us -> 21 us
  waiting for transfers between devices: 9.01 us -> 16.7 us
  other arithmetic: 6.43 us -> 0.62 us
    ppermute x21 -> x16, starting transfers between devices: 32.5 us -> 21 us  [swap(): return lax.ppermute(value, axes, [(i, i ^ step) for i in range(size)])]
    unnamed x24 -> x2, local copies, waits for them, and re-layouts: 10.5 us -> 0.01 us
    ppermute x21 -> x16, waiting for transfers between devices: 9.01 us -> 16.7 us  [swap(): return lax.ppermute(value, axes, [(i, i ^ step) for i in range(size)])]
    mul x2 -> x0, other arithmetic: 2.57 us -> none  [the longest x1 2.57 us: rope_tables(): return (jnp.cos(angles), jnp.sin(angles) * sign)]
    convert_element_type x5 -> x0, other arithmetic: 2.14 us -> none  [the longest x2 1.31 us: rope_tables(): positions.astype(jnp.float32)[..., None] * jnp.asarray(frequencies())]
    cos x1 -> x0, other arithmetic: 1.36 us -> none  [rope_tables(): return (jnp.cos(angles), jnp.sin(angles) * sign)]
    gather x1 -> x0, local copies, waits for them, and re-layouts: 1.25 us -> none  [per_device(): near = picks[order]]
    pallas_call x6 -> x8, Pallas kernels: 11.8 us -> 11.1 us  [the longest x1 3.33 us: per_device(): pl.pallas_call(functools.partial(gather_kernel, pools), out_shape=[shape(...]
  transfers between devices with their start and end apart: 21 -> 16, of which waited for: 7 -> 9; matrix products, arithmetic and copies ran while one was open for 6% -> 0% of each run, Pallas kernels for 10% -> 12%
where the time goes in v2:
time: 49.7 us; the launch traced here: 49.5 us
  starting transfers between devices  21 us (42%)
  waiting for transfers between devices  16.7 us (34%)
  Pallas kernels  11.1 us (22%)
  other arithmetic  0.62 us (1%)
    ppermute x16, starting transfers between devices, swap(): return lax.ppermute(value, axes, [(i, i ^ step) for i in range(size)])  21 us
    ppermute x16, waiting for transfers between devices, swap(): return lax.ppermute(value, axes, [(i, i ^ step) for i in range(size)])  16.7 us
    pallas_call x1, Pallas kernels, per_device(): pl.pallas_call(functools.partial(gather_kernel, pools), out_shape=[shape(...  3.33 us
    pallas_call x1, Pallas kernels, per_device(): pl.pallas_call(functools.partial(table_kernel, pools, shard_blocks), out_...  2.84 us
    pallas_call x2, Pallas kernels, score(): pl.pallas_call(functools.partial(score_kernel, first, count, heads), out_...  2.03 us
    pallas_call x1, Pallas kernels, per_device(): pl.pallas_call(functools.partial(project_kernel, pools, heads, reps), out...  1.21 us
    pallas_call x1, Pallas kernels, per_device(): pl.pallas_call(functools.partial(compact_kernel, pools, shard_blocks), ou...  1.14 us
  transfers between devices with their start and end apart: 16, of which 9 were waited for; matrix products, arithmetic and copies ran while one was open for 0% of the time, Pallas kernels for 12%

profile of v2, /device:TPU:0, one launch (start us, length us, event | category | flops | bytes accessed | tf_op | source)
XLA Modules:
  0.0 49.5 jit_solution(13366314316496067024)
XLA Ops:
  0.0 3.3 %gather.1 = (bf16[512,256]{1,0:T(8,128)(2,1)S(1)}, bf16[512,256]{1,0:T(8,128)(2,1)S(1)}, bf16[272,256]{1,0:T(8,128)(2,1)S(1)}, bf16[272,256]{1,0:T(8,128)(2,1)S(...) custom-call(s32[1,4,4]{2,1,0:T(4,128)} %sel_ref.5, s32[1,4]{1,0:T(1,128)} %len_ref.3, ...), custom_call_target="tpu_custom_call" | custom-call | tf_op jit(solution)/shard_map/gather/pallas_call | solution.py:301
  3.3 4.1 %collective-permute-start.4 = (bf16[272,256]{1,0:T(8,128)(2,1)S(1)}, bf16[272,256]{1,0:T(8,128)(2,1)S(1)}, u32[]{:S(2)}, u32[]{:S(2)}) collective-permute-start(bf16[272,256]{1,0:T(8,128)(2,1)S(1)} %get-tuple-element.37), channel_id=1, source_target_pairs={{0,8},{4,12},{8,0},{12,4},{1,9},{5,13},{9,1},{13,5},{2,10},{6,14},... | collective-permute-start | bytes 417800 | tf_op jit(solution)/shard_map/ppermute | solution.py:35
  7.4 1.3 %collective-permute-start.5 = (bf16[272,256]{1,0:T(8,128)(2,1)S(1)}, bf16[272,256]{1,0:T(8,128)(2,1)S(1)}, u32[]{:S(2)}, u32[]{:S(2)}) collective-permute-start(bf16[272,256]{1,0:T(8,128)(2,1)S(1)} %get-tuple-element.38), channel_id=1, source_target_pairs={{0,12},{4,8},{8,4},{12,0},{1,13},{5,9},{9,5},{13,1},{2,14},{6,10},... | collective-permute-start | bytes 417800 | tf_op jit(solution)/shard_map/ppermute | solution.py:35
  8.8 0.2 collective-permute-start.1
  9.0 1.5 %collective-permute-start.3 = (bf16[512,256]{1,0:T(8,128)(2,1)S(1)}, bf16[512,256]{1,0:T(8,128)(2,1)S(1)}, u32[]{:S(2)}, u32[]{:S(2)}) collective-permute-start(bf16[512,256]{1,0:T(8,128)(2,1)S(1)} %get-tuple-element.25.after_ref.rest_0_), channel_id=1, source_target_pairs={{0,2},{2,0},{1,3},{3,1},{4,6},{6,4},{5,7},{7,5},{8,10},{10,8},{9,1... | collective-permute-start | bytes 786440 | tf_op jit(solution)/shard_map/ppermute | solution.py:35
  10.5 0.5 %collective-permute-start = (bf16[512,256]{1,0:T(8,128)(2,1)S(1)}, bf16[512,256]{1,0:T(8,128)(2,1)S(1)}, u32[]{:S(2)}, u32[]{:S(2)}) collective-permute-start(bf16[512,256]{1,0:T(8,128)(2,1)S(1)} %get-tuple-element.32.rest_0_), channel_id=1, source_target_pairs={{0,2},{2,0},{1,3},{3,1},{4,6},{6,4},{5,7},{7,5},{8,10},{10,8},{9,1... | collective-permute-start | bytes 786440 | tf_op jit(solution)/shard_map/ppermute | solution.py:35
  11.0 2.8 %tables.1 = (f32[1024,128]{1,0:T(8,128)S(1)}, f32[1024,128]{1,0:T(8,128)S(1)}, s32[4,256]{1,0:T(4,128)S(1)}, s32[1,1024]{1,0:T(1,128)S(1)}, bf16[512,512]{1,0:T(8,128)(2,1)S(1)}, /*index=5*/bf16[512,512]{1,0:T(8,128)(2,1)S(1)}) custom-call(s32[1,4,4]{2,1,0:T(4,128)} %sel_ref.5, s32[1,4]{1,0:T(1,128)} %len_ref.3, f32[1,128]{1,0:T(1,128)} %constant.10.clone.freq_ref, ...), custom_call_target="tpu_custom_call" | custom-call | tf_op jit(solution)/shard_map/tables/pallas_call | solution.py:320
  13.9 4.1 %collective-permute-done.4.rest_2_ = bf16[272,256]{1,0:T(8,128)(2,1)S(1)} collective-permute-done((bf16[272,256]{1,0:T(8,128)(2,1)S(1)}, bf16[272,256]{1,0:T(8,128)(2,1)S(1)}, u32[]{:S(2)}, u32[]{:S(2)}) %collective-permute-start.4) | collective-permute-done | bytes 139296 | tf_op jit(solution)/shard_map/ppermute | solution.py:35
  18.0 0.5 %collective-permute-done.1.rest_3_.rest_1_ = bf16[272,256]{1,0:T(8,128)(2,1)S(1)} collective-permute-done((bf16[272,256]{1,0:T(8,128)(2,1)S(1)}, bf16[272,256]{1,0:T(8,128)(2,1)S(1)}, u32[]{:S(2)}, u32[]{:S(2)}) %collective-permute-start.1) | collective-permute-done | bytes 139296 | tf_op jit(solution)/shard_map/ppermute | solution.py:35
  18.5 1.1 %compact.1.rest_4_ = bf16[512,256]{1,0:T(8,128)(2,1)S(1)} custom-call(s32[1,4,4]{2,1,0:T(4,128)} %sel_ref.5, s32[1,1024]{1,0:T(1,128)S(1)} %get-tuple-element.27.after_ref.place_ref, bf16[272,256]{1,0:T(8,128)(2,1)S(1)} %get-tuple-element.33.rest_2_.rest_0_, bf16[272,256]{1,0:T(8,128)(2,1)S(1)} %collective-permute-done.1.rest_3_.rest_1_, ...), custom_call_target="tpu_custom_call" | custom-call | tf_op jit(solution)/shard_map/compact/pallas_call | solution.py:332
  19.6 1.6 %collective-permute-start.8 = (bf16[512,256]{1,0:T(8,128)(2,1)S(1)}, bf16[512,256]{1,0:T(8,128)(2,1)S(1)}, u32[]{:S(2)}, u32[]{:S(2)}) collective-permute-start(bf16[512,256]{1,0:T(8,128)(2,1)S(1)} %compact.1.rest_4_), channel_id=1, source_target_pairs={{0,2},{2,0},{1,3},{3,1},{4,6},{6,4},{5,7},{7,5},{8,10},{10,8},{9,1... | collective-permute-start | bytes 786440 | tf_op jit(solution)/shard_map/ppermute | solution.py:35
  21.2 1.0 %score.3 = (f32[32,256]{1,0:T(8,128)S(1)}, f32[32,256]{1,0:T(8,128)S(1)}) custom-call(bf16[512,512]{1,0:T(8,128)(2,1)S(1)} %get-tuple-element.28.map_ref, f32[1024,128]{1,0:T(8,128)S(1)} %get-tuple-element.29.cos_ref, f32[1024,128]{1,0:T(8,128)S(1)} %get-tuple-element.30.sin_ref, s32[4,256]{1,0:T(4,128)S(1)} %get-tuple-element.31.live_ref, ...), custom_call_target="tpu_custom_call" | custom-call | tf_op jit(solution)/shard_map/score/pallas_call | solution.py:344
  22.2 4.3 %collective-permute-start.6 = (f32[32,256]{1,0:T(8,128)S(1)}, f32[32,256]{1,0:T(8,128)S(1)}, u32[]{:S(2)}, u32[]{:S(2)}) collective-permute-start(f32[32,256]{1,0:T(8,128)S(1)} %get-tuple-element.39), channel_id=1, source_target_pairs={{0,8},{4,12},{8,0},{12,4},{1,9},{5,13},{9,1},{13,5},{2,10},{6,14},... | collective-permute-start | bytes 98312 | tf_op jit(solution)/shard_map/ppermute | solution.py:35
  26.5 0.4 collective-permute-start.7
  27.0 1.0 %score.2 = (f32[32,256]{1,0:T(8,128)S(1)}, f32[32,256]{1,0:T(8,128)S(1)}) custom-call(bf16[512,512]{1,0:T(8,128)(2,1)S(1)} %get-tuple-element.28.map_ref, f32[1024,128]{1,0:T(8,128)S(1)} %get-tuple-element.29.cos_ref, f32[1024,128]{1,0:T(8,128)S(1)} %get-tuple-element.30.sin_ref, s32[4,256]{1,0:T(4,128)S(1)} %get-tuple-element.31.live_ref, ...), custom_call_target="tpu_custom_call" | custom-call | tf_op jit(solution)/shard_map/score/pallas_call | solution.py:344
  28.0 0.2 collective-permute-start.2
  28.2 0.3 collective-permute-done.6.rest_2_
  28.5 3.8 %collective-permute-done.7.rest_3_ = f32[32,256]{1,0:T(8,128)S(1)} collective-permute-done((f32[32,256]{1,0:T(8,128)S(1)}, f32[32,256]{1,0:T(8,128)S(1)}, u32[]{:S(2)}, u32[]{:S(2)}) %collective-permute-start.7) | collective-permute-done | bytes 32800 | tf_op jit(solution)/shard_map/ppermute | solution.py:35
  32.3 0.5 %attend.1.refs_0_ = bf16[1,4096]{1,0:T(2,128)(2,1)S(1)} custom-call(bf16[512,512]{1,0:T(8,128)(2,1)S(1)} %get-tuple-element.26.map_ref, s32[1,1024]{1,0:T(1,128)S(1)} %get-tuple-element.27.after_ref.place_ref, f32[32,256]{1,0:T(8,128)S(1)} %get-tuple-element.35.rest_0_, f32[32,256]{1,0:T(8,128)S(1)} %collective-permute-done.2.rest_1_, ...), custom_call_target="tpu_custom_call" | custom-call | tf_op jit(solution)/shard_map/attend/pallas_call | solution.py:359
  32.8 0.1 collective-permute-start.9
  32.9 1.2 %collective-permute-done.9.refs_1_ = bf16[1,4096]{1,0:T(2,128)(2,1)S(1)} collective-permute-done((bf16[1,4096]{1,0:T(2,128)(2,1)S(1)}, bf16[1,4096]{1,0:T(2,128)(2,1)S(1)}, u32[]{:S(2)}, u32[]{:S(2)}) %collective-permute-start.9) | collective-permute-done | bytes 8224 | tf_op jit(solution)/shard_map/ppermute | solution.py:35
  34.1 0.1 collective-permute-start.10
  34.2 3.6 %collective-permute-start.11 = (bf16[2,4096]{1,0:T(2,128)(2,1)S(1)}, bf16[2,4096]{1,0:T(2,128)(2,1)S(1)}, u32[]{:S(2)}, u32[]{:S(2)}) collective-permute-start(bf16[2,4096]{1,0:T(2,128)(2,1)S(1)} %pair.1.refs_0_), channel_id=1, source_target_pairs={{0,8},{4,12},{8,0},{12,4},{1,9},{5,13},{9,1},{13,5},{2,10},{6,14},... | collective-permute-start | bytes 49160 | tf_op jit(solution)/shard_map/ppermute | solution.py:35
  37.8 0.8 %collective-permute-start.12 = (bf16[2,4096]{1,0:T(2,128)(2,1)S(1)}, bf16[2,4096]{1,0:T(2,128)(2,1)S(1)}, u32[]{:S(2)}, u32[]{:S(2)}) collective-permute-start(bf16[2,4096]{1,0:T(2,128)(2,1)S(1)} %pair.1.refs_0_), channel_id=1, source_target_pairs={{0,12},{4,8},{8,4},{12,0},{1,13},{5,9},{9,5},{13,1},{2,14},{6,10},... | collective-permute-start | bytes 49160 | tf_op jit(solution)/shard_map/ppermute | solution.py:35
  38.6 0.9 %collective-permute-done.11.refs_2_ = bf16[2,4096]{1,0:T(2,128)(2,1)S(1)} collective-permute-done((bf16[2,4096]{1,0:T(2,128)(2,1)S(1)}, bf16[2,4096]{1,0:T(2,128)(2,1)S(1)}, u32[]{:S(2)}, u32[]{:S(2)}) %collective-permute-start.11) | collective-permute-done | bytes 16416 | tf_op jit(solution)/shard_map/ppermute | solution.py:35
  39.5 3.8 %collective-permute-done.12.refs_3_ = bf16[2,4096]{1,0:T(2,128)(2,1)S(1)} collective-permute-done((bf16[2,4096]{1,0:T(2,128)(2,1)S(1)}, bf16[2,4096]{1,0:T(2,128)(2,1)S(1)}, u32[]{:S(2)}, u32[]{:S(2)}) %collective-permute-start.12) | collective-permute-done | bytes 16416 | tf_op jit(solution)/shard_map/ppermute | solution.py:35
  43.3 1.2 %project.1 = (f32[2,1024]{1,0:T(2,128)S(1)}, f32[2,1024]{1,0:T(2,128)S(1)}, f32[2,1024]{1,0:T(2,128)S(1)}, f32[2,1024]{1,0:T(2,128)S(1)}) custom-call(bf16[2,4096]{1,0:T(2,128)(2,1)S(1)} %pair.1.refs_0_, bf16[2,4096]{1,0:T(2,128)(2,1)S(1)} %collective-permute-done.10.refs_1_, bf16[2,4096]{1,0:T(2,128)(2,1)S(1)} %collective-permute-done.11.refs_2_, ...), custom_call_target="tpu_custom_call" | custom-call | tf_op jit(solution)/shard_map/project/pallas_call | solution.py:379
  44.6 0.7 %collective-permute-start.14 = (f32[2,1024]{1,0:T(2,128)S(1)}, f32[2,1024]{1,0:T(2,128)S(1)}, u32[]{:S(2)}, u32[]{:S(2)}) collective-permute-start(f32[2,1024]{1,0:T(2,128)S(1)} %get-tuple-element.42), channel_id=1, source_target_pairs={{0,3},{1,2},{2,1},{3,0},{4,7},{5,6},{6,5},{7,4},{8,11},{9,10},{10,... | collective-permute-start | bytes 24584 | tf_op jit(solution)/shard_map/ppermute | solution.py:35
  45.3 1.5 %collective-permute-start.15 = (f32[2,1024]{1,0:T(2,128)S(1)}, f32[2,1024]{1,0:T(2,128)S(1)}, u32[]{:S(2)}, u32[]{:S(2)}) collective-permute-start(f32[2,1024]{1,0:T(2,128)S(1)} %get-tuple-element.44), channel_id=1, source_target_pairs={{0,2},{1,3},{2,0},{3,1},{4,6},{5,7},{6,4},{7,5},{8,10},{9,11},{10,... | collective-permute-start | bytes 24584 | tf_op jit(solution)/shard_map/ppermute | solution.py:35
  46.7 1.0 %collective-permute-done.14 = f32[2,1024]{1,0:T(2,128)S(1)} collective-permute-done((f32[2,1024]{1,0:T(2,128)S(1)}, f32[2,1024]{1,0:T(2,128)S(1)}, u32[]{:S(2)}, u32[]{:S(2)}) %collective-permute-start.14) | collective-permute-done | bytes 8224 | tf_op jit(solution)/shard_map/ppermute | solution.py:35
  47.7 1.2 %collective-permute-done.15 = f32[2,1024]{1,0:T(2,128)S(1)} collective-permute-done((f32[2,1024]{1,0:T(2,128)S(1)}, f32[2,1024]{1,0:T(2,128)S(1)}, u32[]{:S(2)}, u32[]{:S(2)}) %collective-permute-start.15) | collective-permute-done | bytes 8224 | tf_op jit(solution)/shard_map/ppermute | solution.py:35
  48.9 0.6 %pad_maximum_fusion = bf16[1,2,2048]{2,1,0:T(2,128)(2,1)} fusion(bf16[1,2,1024]{2,1,0:T(2,128)(2,1)S(1)} %get-tuple-element.46, bf16[1,2,1024]{2,1,0:T(2,128)(2,1)S(1)} %get-tuple-element.45), kind=kLoop, calls=%fused_computation | loop fusion | flops 16384 | bytes 16384 | tf_op jit(solution)/shard_map/concatenate | solution.py:397
  (12 shorter events, 0.1 us)
Async XLA Ops:
  0.0 43.3 %copy-start = (bf16[4096,1024]{1,0:T(8,128)(2,1)S(1)}, bf16[4096,1024]{1,0:T(8,128)(2,1)}, u32[]{:S(2)}) copy-start(bf16[4096,1024]{1,0:T(8,128)(2,1)} %refs_4_.1) | copy-start | bytes 25165828
  3.3 14.6 %collective-permute-start.4 = (bf16[272,256]{1,0:T(8,128)(2,1)S(1)}, bf16[272,256]{1,0:T(8,128)(2,1)S(1)}, u32[]{:S(2)}, u32[]{:S(2)}) collective-permute-start(bf16[272,256]{1,0:T(8,128)(2,1)S(1)} %get-tuple-element.37), channel_id=1, source_target_pairs={{0,8},{4,12},{8,0},{12,4},{1,9},{5,13},{9,1},{13,5},{2,10},{6,14},... | collective-permute-start | bytes 417800 | tf_op jit(solution)/shard_map/ppermute | solution.py:35
  7.4 10.5 %collective-permute-start.5 = (bf16[272,256]{1,0:T(8,128)(2,1)S(1)}, bf16[272,256]{1,0:T(8,128)(2,1)S(1)}, u32[]{:S(2)}, u32[]{:S(2)}) collective-permute-start(bf16[272,256]{1,0:T(8,128)(2,1)S(1)} %get-tuple-element.38), channel_id=1, source_target_pairs={{0,12},{4,8},{8,4},{12,0},{1,13},{5,9},{9,5},{13,1},{2,14},{6,10},... | collective-permute-start | bytes 417800 | tf_op jit(solution)/shard_map/ppermute | solution.py:35
  8.8 9.7 %collective-permute-start.1 = (bf16[272,256]{1,0:T(8,128)(2,1)S(1)}, bf16[272,256]{1,0:T(8,128)(2,1)S(1)}, u32[]{:S(2)}, u32[]{:S(2)}) collective-permute-start(bf16[272,256]{1,0:T(8,128)(2,1)S(1)} %get-tuple-element.34), channel_id=1, source_target_pairs={{0,4},{4,0},{8,12},{12,8},{1,5},{5,1},{9,13},{13,9},{2,6},{6,2},{1... | collective-permute-start | bytes 417800 | tf_op jit(solution)/shard_map/ppermute | solution.py:35
  9.0 12.2 %collective-permute-start.3 = (bf16[512,256]{1,0:T(8,128)(2,1)S(1)}, bf16[512,256]{1,0:T(8,128)(2,1)S(1)}, u32[]{:S(2)}, u32[]{:S(2)}) collective-permute-start(bf16[512,256]{1,0:T(8,128)(2,1)S(1)} %get-tuple-element.25.after_ref.rest_0_), channel_id=1, source_target_pairs={{0,2},{2,0},{1,3},{3,1},{4,6},{6,4},{5,7},{7,5},{8,10},{10,8},{9,1... | collective-permute-start | bytes 786440 | tf_op jit(solution)/shard_map/ppermute | solution.py:35
  10.5 16.5 %collective-permute-start = (bf16[512,256]{1,0:T(8,128)(2,1)S(1)}, bf16[512,256]{1,0:T(8,128)(2,1)S(1)}, u32[]{:S(2)}, u32[]{:S(2)}) collective-permute-start(bf16[512,256]{1,0:T(8,128)(2,1)S(1)} %get-tuple-element.32.rest_0_), channel_id=1, source_target_pairs={{0,2},{2,0},{1,3},{3,1},{4,6},{6,4},{5,7},{7,5},{8,10},{10,8},{9,1... | collective-permute-start | bytes 786440 | tf_op jit(solution)/shard_map/ppermute | solution.py:35
  19.6 12.7 %collective-permute-start.8 = (bf16[512,256]{1,0:T(8,128)(2,1)S(1)}, bf16[512,256]{1,0:T(8,128)(2,1)S(1)}, u32[]{:S(2)}, u32[]{:S(2)}) collective-permute-start(bf16[512,256]{1,0:T(8,128)(2,1)S(1)} %compact.1.rest_4_), channel_id=1, source_target_pairs={{0,2},{2,0},{1,3},{3,1},{4,6},{6,4},{5,7},{7,5},{8,10},{10,8},{9,1... | collective-permute-start | bytes 786440 | tf_op jit(solution)/shard_map/ppermute | solution.py:35
  22.2 6.3 %collective-permute-start.6 = (f32[32,256]{1,0:T(8,128)S(1)}, f32[32,256]{1,0:T(8,128)S(1)}, u32[]{:S(2)}, u32[]{:S(2)}) collective-permute-start(f32[32,256]{1,0:T(8,128)S(1)} %get-tuple-element.39), channel_id=1, source_target_pairs={{0,8},{4,12},{8,0},{12,4},{1,9},{5,13},{9,1},{13,5},{2,10},{6,14},... | collective-permute-start | bytes 98312 | tf_op jit(solution)/shard_map/ppermute | solution.py:35
  26.5 5.8 %collective-permute-start.7 = (f32[32,256]{1,0:T(8,128)S(1)}, f32[32,256]{1,0:T(8,128)S(1)}, u32[]{:S(2)}, u32[]{:S(2)}) collective-permute-start(f32[32,256]{1,0:T(8,128)S(1)} %get-tuple-element.40), channel_id=1, source_target_pairs={{0,12},{4,8},{8,4},{12,0},{1,13},{5,9},{9,5},{13,1},{2,14},{6,10},... | collective-permute-start | bytes 98312 | tf_op jit(solution)/shard_map/ppermute | solution.py:35
  28.0 4.3 %collective-permute-start.2 = (f32[32,256]{1,0:T(8,128)S(1)}, f32[32,256]{1,0:T(8,128)S(1)}, u32[]{:S(2)}, u32[]{:S(2)}) collective-permute-start(f32[32,256]{1,0:T(8,128)S(1)} %get-tuple-element.36), channel_id=1, source_target_pairs={{0,4},{4,0},{8,12},{12,8},{1,5},{5,1},{9,13},{13,9},{2,6},{6,2},{1... | collective-permute-start | bytes 98312 | tf_op jit(solution)/shard_map/ppermute | solution.py:35
  32.8 1.2 %collective-permute-start.9 = (bf16[1,4096]{1,0:T(2,128)(2,1)S(1)}, bf16[1,4096]{1,0:T(2,128)(2,1)S(1)}, u32[]{:S(2)}, u32[]{:S(2)}) collective-permute-start(bf16[1,4096]{1,0:T(2,128)(2,1)S(1)} %attend.1.refs_0_), channel_id=1, source_target_pairs={{0,1},{1,0},{2,3},{3,2},{4,5},{5,4},{6,7},{7,6},{8,9},{9,8},{10,11... | collective-permute-start | bytes 24584 | tf_op jit(solution)/shard_map/ppermute | solution.py:35
  34.1 4.5 %collective-permute-start.10 = (bf16[2,4096]{1,0:T(2,128)(2,1)S(1)}, bf16[2,4096]{1,0:T(2,128)(2,1)S(1)}, u32[]{:S(2)}, u32[]{:S(2)}) collective-permute-start(bf16[2,4096]{1,0:T(2,128)(2,1)S(1)} %pair.1.refs_0_), channel_id=1, source_target_pairs={{0,4},{4,0},{8,12},{12,8},{1,5},{5,1},{9,13},{13,9},{2,6},{6,2},{1... | collective-permute-start | bytes 49160 | tf_op jit(solution)/shard_map/ppermute | solution.py:35
  34.2 5.3 %collective-permute-start.11 = (bf16[2,4096]{1,0:T(2,128)(2,1)S(1)}, bf16[2,4096]{1,0:T(2,128)(2,1)S(1)}, u32[]{:S(2)}, u32[]{:S(2)}) collective-permute-start(bf16[2,4096]{1,0:T(2,128)(2,1)S(1)} %pair.1.refs_0_), channel_id=1, source_target_pairs={{0,8},{4,12},{8,0},{12,4},{1,9},{5,13},{9,1},{13,5},{2,10},{6,14},... | collective-permute-start | bytes 49160 | tf_op jit(solution)/shard_map/ppermute | solution.py:35
  37.8 5.5 %collective-permute-start.12 = (bf16[2,4096]{1,0:T(2,128)(2,1)S(1)}, bf16[2,4096]{1,0:T(2,128)(2,1)S(1)}, u32[]{:S(2)}, u32[]{:S(2)}) collective-permute-start(bf16[2,4096]{1,0:T(2,128)(2,1)S(1)} %pair.1.refs_0_), channel_id=1, source_target_pairs={{0,12},{4,8},{8,4},{12,0},{1,13},{5,9},{9,5},{13,1},{2,14},{6,10},... | collective-permute-start | bytes 49160 | tf_op jit(solution)/shard_map/ppermute | solution.py:35
  44.5 2.2 %collective-permute-start.13 = (f32[2,1024]{1,0:T(2,128)S(1)}, f32[2,1024]{1,0:T(2,128)S(1)}, u32[]{:S(2)}, u32[]{:S(2)}) collective-permute-start(f32[2,1024]{1,0:T(2,128)S(1)} %get-tuple-element.41), channel_id=1, source_target_pairs={{0,1},{1,0},{2,3},{3,2},{4,5},{5,4},{6,7},{7,6},{8,9},{9,8},{10,11... | collective-permute-start | bytes 24584 | tf_op jit(solution)/shard_map/ppermute | solution.py:35
  44.6 3.1 %collective-permute-start.14 = (f32[2,1024]{1,0:T(2,128)S(1)}, f32[2,1024]{1,0:T(2,128)S(1)}, u32[]{:S(2)}, u32[]{:S(2)}) collective-permute-start(f32[2,1024]{1,0:T(2,128)S(1)} %get-tuple-element.42), channel_id=1, source_target_pairs={{0,3},{1,2},{2,1},{3,0},{4,7},{5,6},{6,5},{7,4},{8,11},{9,10},{10,... | collective-permute-start | bytes 24584 | tf_op jit(solution)/shard_map/ppermute | solution.py:35
  45.3 3.7 %collective-permute-start.15 = (f32[2,1024]{1,0:T(2,128)S(1)}, f32[2,1024]{1,0:T(2,128)S(1)}, u32[]{:S(2)}, u32[]{:S(2)}) collective-permute-start(f32[2,1024]{1,0:T(2,128)S(1)} %get-tuple-element.44), channel_id=1, source_target_pairs={{0,2},{1,3},{2,0},{3,1},{4,6},{5,7},{6,4},{7,5},{8,10},{9,11},{10,... | collective-permute-start | bytes 24584 | tf_op jit(solution)/shard_map/ppermute | solution.py:35

commit v3 on v2

v3 whole, which is shorter than its diff:
```python
import functools

import jax
import jax.numpy as jnp
import numpy as np
from jax import lax
from jax.experimental import pallas as pl
from jax.experimental.pallas import tpu as pltpu
from jax.sharding import PartitionSpec as P

HEAD_SIZE = 128
LANE = 64
BLOCK = 128
CAP = 2
QUERY_PER_GROUP = 8

ROPE_BASE = 500000.0
MASKED = -1e30
FAR = 1 << 29

SMEM = pl.BlockSpec(memory_space=pltpu.SMEM)
VMEM = pl.BlockSpec(memory_space=pltpu.VMEM)
ANY = pl.BlockSpec(memory_space=pl.ANY)
HBM = pl.BlockSpec(memory_space=pltpu.HBM)


def frequencies():
    half = HEAD_SIZE // 2
    exponents = np.arange(half, dtype=np.float32) * np.float32(2.0 / HEAD_SIZE)
    freq = np.power(np.float64(ROPE_BASE), -exponents.astype(np.float64)).astype(np.float32)
    return np.concatenate([freq, freq])[None, :]


def swap(value, axes, size, step):
    return lax.ppermute(value, axes, [(i, i ^ step) for i in range(size)])


def in_hbm(value):
    return pltpu.with_memory_space_constraint(value, pltpu.HBM)


def in_vmem(value):
    return pltpu.with_memory_space_constraint(value, pltpu.VMEM)


def params(mib, **more):
    return pltpu.CompilerParams(vmem_limit_bytes=mib << 20, **more)


def slot_blocks(sel_ref, seq, shard, shard_blocks):
    first = jnp.int32(-1)
    second = jnp.int32(-1)
    for i in range(sel_ref.shape[2]):
        block = sel_ref[0, seq, i]
        here = (block >= shard * shard_blocks) & (block < (shard + 1) * shard_blocks)
        second = jnp.where(here & (first >= 0), block, second)
        first = jnp.where(here & (first < 0), block, first)
    return first, second


def gather_kernel(pools, sel_ref, lat_ref, query_ref, line_ref, near_ref, far_ref, *rest):
    value_refs = rest[:pools]
    raw, sems = rest[pools:]
    shard_blocks = lat_ref.shape[2] // BLOCK
    columns = lat_ref.shape[3]
    width = columns // 2
    rows = CAP * BLOCK
    me = lax.axis_index("pool")
    copies = {}
    for k in range(pools - 1, -1, -1):
        seq = me ^ k
        for c, block in enumerate(slot_blocks(sel_ref, seq, me, shard_blocks)):
            local = jnp.maximum(block - me * shard_blocks, 0)
            copies[k, c] = pltpu.make_async_copy(
                lat_ref.at[0, seq, pl.ds(pl.multiple_of(local * BLOCK, BLOCK), BLOCK), :],
                raw.at[pl.ds((k * CAP + c) * BLOCK, BLOCK), :],
                sems.at[k * CAP + c],
            )
            copies[k, c].start()
    line_ref[...] = query_ref[0]
    chunk = min(4 * LANE, columns)
    half = chunk // 2
    source = lax.broadcasted_iota(jnp.int32, (chunk, chunk), 0)
    target = lax.broadcasted_iota(jnp.int32, (chunk, chunk), 1)
    within = target & (half - 1)
    wanted = ((within >> 6) << 7) + (within & (LANE - 1)) + jnp.where(target >= half, LANE, 0)
    pick = (source == wanted).astype(jnp.float32).astype(jnp.bfloat16)
    for k in range(pools - 1, -1, -1):
        for c in range(CAP):
            copies[k, c].wait()
        keys_ref, at = (far_ref, k - pools // 2) if k >= pools // 2 else (near_ref, k)
        for j in range(columns // chunk):
            packed = jnp.dot(
                raw[k * rows : (k + 1) * rows, j * chunk : (j + 1) * chunk], pick,
                preferred_element_type=jnp.float32,
            ).astype(jnp.bfloat16)
            keys_ref[at * rows : (at + 1) * rows, j * half : (j + 1) * half] = packed[:, :half]
            value_refs[k][:, j * half : (j + 1) * half] = packed[:, half:]


def table_kernel(
    pools, shard_blocks, sel_ref, len_ref, freq_ref, after_ref, key_map_ref, value_map_ref,
    cos_ref, sin_ref, turn_ref, live_ref, place_ref, key_out_ref, value_out_ref, sems,
):
    del after_ref
    loads = [
        pltpu.make_async_copy(key_map_ref, key_out_ref, sems.at[0]),
        pltpu.make_async_copy(value_map_ref, value_out_ref, sems.at[1]),
    ]
    for load in loads:
        load.start()
    me = lax.axis_index("pool")
    lane = lax.broadcasted_iota(jnp.int32, (BLOCK, HEAD_SIZE), 1)
    row = lax.broadcasted_iota(jnp.int32, (BLOCK, HEAD_SIZE), 0)
    front = lane < HEAD_SIZE // 2
    across = lax.broadcasted_iota(jnp.int32, (1, BLOCK), 1)
    place = jnp.int32(0)
    for k in range(pools):
        turn_ref[k : k + 1, :] = len_ref[0, me ^ k].astype(jnp.float32) * freq_ref[...]
    angle = turn_ref[0:pools, :]
    turn_ref[0:pools, :] = jnp.cos(angle)
    turn_ref[pools:, :] = jnp.where(front[:1, :], -jnp.sin(angle), jnp.sin(angle))
    for k in range(pools):
        seq = me ^ k
        found = slot_blocks(sel_ref, seq, me, shard_blocks)
        one, two = [jnp.maximum(block, 0) * BLOCK for block in found]
        angle = (jnp.where(front, one, two) + row).astype(jnp.float32) * freq_ref[...]
        for ref, table, sign in ((cos_ref, jnp.cos(angle), 1.0), (sin_ref, jnp.sin(angle), -1.0)):
            turned = pltpu.roll(table, HEAD_SIZE // 2, 1)
            at = k * CAP * BLOCK
            ref[at : at + BLOCK, :] = jnp.where(front, sign * table, turned)
            ref[at + BLOCK : at + 2 * BLOCK, :] = jnp.where(front, sign * turned, table)
        mine = slot_blocks(sel_ref, me, seq, shard_blocks)
        for c in range(CAP):
            start = jnp.where(found[c] < 0, FAR, found[c] * BLOCK)
            live_ref[k : k + 1, c * BLOCK : (c + 1) * BLOCK] = (start + across < len_ref[0, seq]).astype(jnp.int32)
            at = (k * CAP + c) * BLOCK
            used = mine[c] >= 0
            place_ref[:, at : at + BLOCK] = jnp.where(used, place, -1) + 0 * across
            place = place + used.astype(jnp.int32)
    for load in loads:
        load.wait()


def score_kernel(first, count, heads, pools, map_ref, cos_ref, sin_ref, turn_ref, live_ref, query_ref, after_ref, *rest):
    del after_ref
    key_refs = rest[:heads]
    out_refs = rest[heads : heads + count]
    head = lax.axis_index("heads")
    width = key_refs[0].shape[1]
    groups = map_ref.shape[1] // HEAD_SIZE
    rows = CAP * BLOCK
    maps = []
    for j in range(heads):
        owner = head ^ j
        maps.append(map_ref[pl.ds(pl.multiple_of(owner * width, width), width), :])
    for i in range(count):
        k = first + i
        live = live_ref[k : k + 1, :] > 0
        line = query_ref[i : i + 1, :].astype(jnp.float32)
        query = jnp.concatenate(
            [line[:, n * HEAD_SIZE : (n + 1) * HEAD_SIZE] for n in range(groups * QUERY_PER_GROUP)], axis=0
        )
        query = query * turn_ref[k : k + 1, :] + pltpu.roll(query, HEAD_SIZE // 2, 1) * turn_ref[
            pools + k : pools + k + 1, :
        ]
        queries = query.astype(jnp.bfloat16)
        at = slice(i * rows, (i + 1) * rows)
        rebuilt = jnp.dot(key_refs[0][at, :], maps[0], preferred_element_type=jnp.float32)
        for j in range(1, heads):
            rebuilt += jnp.dot(key_refs[j][at, :], maps[j], preferred_element_type=jnp.float32)
        cosine = cos_ref[k * rows : (k + 1) * rows, :]
        sine = sin_ref[k * rows : (k + 1) * rows, :]
        for g in range(groups):
            one = rebuilt[:, g * HEAD_SIZE : (g + 1) * HEAD_SIZE]
            turned = (one * cosine + pltpu.roll(one, HEAD_SIZE // 2, 1) * sine).astype(jnp.bfloat16)
            mine = slice(g * QUERY_PER_GROUP, (g + 1) * QUERY_PER_GROUP)
            scores = lax.dot_general(
                queries[mine, :], turned, (((1,), (1,)), ((), ())), preferred_element_type=jnp.float32
            ) * (HEAD_SIZE ** -0.5)
            out_refs[i][mine, :] = jnp.where(live, scores, MASKED)


def compact_kernel(pools, shard_blocks, sel_ref, *rest):
    value_refs = rest[:pools][::-1]
    out_ref, sem = rest[-2:]
    me = lax.axis_index("pool")
    place = jnp.int32(0)
    for k in range(pools):
        for c, block in enumerate(slot_blocks(sel_ref, me, me ^ k, shard_blocks)):
            @pl.when(block >= 0)
            def _(k=k, c=c, place=place):
                pltpu.make_async_copy(
                    value_refs[k].at[pl.ds(c * BLOCK, BLOCK), :],
                    out_ref.at[pl.ds(pl.multiple_of(place * BLOCK, BLOCK), BLOCK), :],
                    sem,
                ).start()
            place = place + (block >= 0).astype(jnp.int32)
    pltpu.make_async_copy(out_ref, out_ref, sem).wait()


def attend_kernel(pools, heads, map_ref, place_ref, *rest):
    score_refs = rest[:pools][::-1]
    value_refs = rest[pools : pools + heads]
    out_ref = rest[pools + heads]
    head = lax.axis_index("heads")
    width = value_refs[0].shape[1]
    groups = map_ref.shape[1] // HEAD_SIZE
    scores = [ref[...] for ref in score_refs]
    top = functools.reduce(jnp.maximum, [jnp.max(s, axis=1, keepdims=True) for s in scores])
    weights = [jnp.exp(s - top) for s in scores]
    total = functools.reduce(jnp.add, [jnp.sum(w, axis=1, keepdims=True) for w in weights])
    slots = []
    for k in range(pools):
        attention = weights[k] / total
        for c in range(CAP):
            at = (k * CAP + c) * BLOCK
            slots.append((place_ref[:, at : at + BLOCK], attention[:, c * BLOCK : (c + 1) * BLOCK]))
    dense = []
    for i in range(value_refs[0].shape[0] // BLOCK):
        chosen = jnp.zeros_like(slots[0][1])
        for place, attention in slots:
            chosen = jnp.where(place == i, attention, chosen)
        dense.append(chosen)
    attention = jnp.concatenate(dense, axis=1).astype(jnp.bfloat16)
    mixed = [None] * groups
    for j in range(heads):
        owner = head ^ j
        context = jnp.dot(
            attention, value_refs[j][...], preferred_element_type=jnp.float32
        ).astype(jnp.bfloat16)
        rows = pl.ds(pl.multiple_of(owner * width, width), width)
        for g in range(groups):
            part = jnp.dot(
                context[g * QUERY_PER_GROUP : (g + 1) * QUERY_PER_GROUP, :],
                map_ref[rows, g * HEAD_SIZE : (g + 1) * HEAD_SIZE],
                preferred_element_type=jnp.float32,
            )
            mixed[g] = part if j == 0 else mixed[g] + part
    for g in range(groups):
        for q in range(QUERY_PER_GROUP):
            at = (g * QUERY_PER_GROUP + q) * HEAD_SIZE
            out_ref[:, at : at + HEAD_SIZE] = mixed[g][q : q + 1, :].astype(jnp.bfloat16)


def join_kernel(*refs):
    rows = [ref[...].reshape(-1, ref.shape[-1]).astype(jnp.float32) for ref in refs[:-1]]
    refs[-1][...] = jnp.concatenate(rows, axis=0).astype(jnp.bfloat16)


def project_kernel(pools, heads, reps, own_ref, far_ref, weight_ref, *rest):
    out_refs = rest[:heads]
    acc = rest[heads]
    left = jnp.concatenate(
        [own_ref[...].astype(jnp.float32), far_ref[...].astype(jnp.float32)], axis=0
    ).astype(jnp.bfloat16)
    acc[...] = jnp.dot(left, weight_ref[...], preferred_element_type=jnp.float32)
    pool = lax.axis_index("pool")
    head = lax.axis_index("heads")
    each = pools // heads
    for j in range(heads):
        for t in range(reps):
            for u in range(each):
                n = (pool ^ ((head ^ j) * each + u)) * reps + t
                out_refs[j][t * each + u : t * each + u + 1, :] = acc[pl.ds(n, 1), :]


def sum_kernel(reps, *refs):
    part_refs, out_refs = refs[:-reps], refs[-reps:]
    total = functools.reduce(jnp.add, [ref[...] for ref in part_refs])
    each = total.shape[0] // reps
    for t in range(reps):
        out_refs[t][...] = total[t * each : (t + 1) * each, :].astype(jnp.bfloat16)


def place_kernel(reps, *refs):
    out_ref = refs[reps]
    rep = lax.axis_index("rep")
    width = refs[0].shape[1]
    for t in range(reps):
        out_ref[0, :, pl.ds(pl.multiple_of((rep ^ t) * width, width), width)] = refs[t][...]


def per_device(queries, latents, key_latent_maps, value_latent_maps, out_weight, lengths, selected):
    pools = lax.axis_size("pool")
    heads = lax.axis_size("heads")
    reps = lax.axis_size("rep")
    half_seqs, sel_count = selected.shape[1:]
    assert half_seqs == pools and pools % heads == 0
    shard_blocks = latents.shape[2] // BLOCK
    width = latents.shape[3] // 2
    rows = CAP * BLOCK
    own_heads = queries.shape[2] // HEAD_SIZE
    bf16, f32, i32 = jnp.bfloat16, jnp.float32, jnp.int32
    shape = jax.ShapeDtypeStruct
    freq = jnp.asarray(frequencies())

    def join(*blocks):
        return pl.pallas_call(
            join_kernel,
            out_shape=shape((sum(block.size for block in blocks) // queries.shape[2], queries.shape[2]), bf16),
            in_specs=[VMEM] * len(blocks),
            out_specs=VMEM,
            compiler_params=params(4),
            name="join",
        )(*blocks)

    packed = pl.pallas_call(
        functools.partial(gather_kernel, pools),
        out_shape=[shape((1, queries.shape[2]), bf16)]
        + [shape((pools // 2 * rows, width), bf16)] * 2
        + [shape((rows, width), bf16)] * pools,
        in_specs=[SMEM, HBM, VMEM],
        out_specs=[VMEM] * (pools + 3),
        scratch_shapes=[
            pltpu.VMEM((pools * rows, 2 * width), bf16),
            pltpu.SemaphoreType.DMA((pools * CAP,)),
        ],
        compiler_params=params(16),
        name="gather",
    )(in_hbm(selected), in_hbm(latents), in_hbm(queries))
    line, near, far, values = packed[0], packed[1], packed[2], packed[3:]
    value_parts = {k: swap(values[k], "pool", pools, k) for k in range(pools - 1, 0, -1)}
    value_parts = [values[0]] + [value_parts[k] for k in range(1, pools)]
    far_parts = [far] + [swap(far, "heads", heads, j) for j in range(1, heads)]
    near_parts = [near] + [swap(near, "heads", heads, j) for j in range(1, heads)]
    middle = pools // 2
    near_queries = line
    step = 1
    while step < middle:
        near_queries = join(near_queries, swap(near_queries, "pool", pools, step))
        step *= 2
    far_queries = swap(near_queries, "pool", pools, middle)

    cosine, sine, turn, live, place, key_maps, value_maps = pl.pallas_call(
        functools.partial(table_kernel, pools, shard_blocks),
        out_shape=[shape((pools * rows, HEAD_SIZE), f32)] * 2
        + [shape((2 * pools, HEAD_SIZE), f32), shape((pools, rows), i32), shape((1, pools * rows), i32)]
        + [shape(key_latent_maps.shape, bf16), shape(value_latent_maps.shape, bf16)],
        in_specs=[SMEM, SMEM, VMEM, ANY, ANY, ANY],
        out_specs=[VMEM] * 7,
        scratch_shapes=[pltpu.SemaphoreType.DMA((2,))],
        compiler_params=params(16),
        name="tables",
    )(in_hbm(selected), in_hbm(lengths), in_hbm(freq), near_queries, in_hbm(key_latent_maps), in_hbm(value_latent_maps))

    def score(first, count, key_parts, query_parts, after):
        return pl.pallas_call(
            functools.partial(score_kernel, first, count, heads, pools),
            out_shape=[shape((own_heads, rows), f32)] * count,
            in_specs=[VMEM] * 6 + [ANY] + [VMEM] * heads,
            out_specs=[VMEM] * count,
            compiler_params=params(20),
            name="score",
        )(key_maps, cosine, sine, turn, live, query_parts, after, *key_parts)

    far_scores = score(middle, middle, far_parts, far_queries, near_queries)
    near_scores = score(0, middle, near_parts, near_queries, far_scores[0])
    scores = [*near_scores, *far_scores]
    score_parts = {k: swap(scores[k], "pool", pools, k) for k in range(pools - 1, 0, -1)}
    score_parts = [scores[0]] + [score_parts[k] for k in range(1, pools)]
    dense = pl.pallas_call(
        functools.partial(compact_kernel, pools, shard_blocks),
        out_shape=shape((sel_count * BLOCK, width), bf16),
        in_specs=[SMEM] + [ANY] * (2 * pools - middle),
        out_specs=ANY,
        scratch_shapes=[pltpu.SemaphoreType.DMA],
        compiler_params=params(8),
        name="compact",
    )(in_hbm(selected), *value_parts[::-1], *score_parts[:middle - 1 : -1])
    dense_parts = [dense] + [swap(dense, "heads", heads, j) for j in range(1, heads)]


    mine = pl.pallas_call(
        functools.partial(attend_kernel, pools, heads),
        out_shape=shape((1, own_heads * HEAD_SIZE), bf16),
        in_specs=[VMEM] * (2 + pools + heads),
        out_specs=VMEM,
        compiler_params=params(16),
        name="attend",
    )(value_maps, place, *score_parts[::-1], *dense_parts)
    own_rows = join(mine, *[swap(mine, "rep", reps, r) for r in range(1, reps)])
    step = 1
    while step < middle:
        own_rows = join(own_rows, swap(own_rows, "pool", pools, step))
        step *= 2
    far_rows = swap(own_rows, "pool", pools, middle)

    own_columns = out_weight.shape[1]
    each = pools // heads
    parts = pl.pallas_call(
        functools.partial(project_kernel, pools, heads, reps),
        out_shape=[shape((reps * each, own_columns), f32)] * heads,
        in_specs=[VMEM] * 3,
        out_specs=[VMEM] * heads,
        scratch_shapes=[pltpu.VMEM((pools * reps, own_columns), f32)],
        compiler_params=params(24),
        name="project",
    )(own_rows, far_rows, in_vmem(out_weight))
    sums = pl.pallas_call(
        functools.partial(sum_kernel, reps),
        out_shape=[shape((each, own_columns), bf16)] * reps,
        in_specs=[VMEM] * heads,
        out_specs=[VMEM] * reps,
        compiler_params=params(4),
        name="sum",
    )(parts[0], *[swap(parts[j], "heads", heads, j) for j in range(1, heads)])
    return pl.pallas_call(
        functools.partial(place_kernel, reps),
        out_shape=shape((1, each, reps * own_columns), bf16),
        in_specs=[VMEM] * reps,
        out_specs=VMEM,
        compiler_params=params(4),
        name="place",
    )(sums[0], *[swap(sums[t], "rep", reps, t) for t in range(1, reps)])


def solution(mesh):
    return jax.shard_map(
        per_device,
        mesh=mesh,
        in_specs=(
            P(("groups", "rep"), "pool", "heads"),
            P(("groups", "rep"), None, "pool", "heads"),
            P(None, "heads"),
            P(None, "heads"),
            P("heads", ("pool", "rep")),
            P(("groups", "rep"), None),
            P(("groups", "rep"), None, None),
        ),
        out_specs=P(("groups", "rep"), "heads", "pool"),
        check_vma=False,
    )
```

time: 49.7 us -> 57.8 us (1.16)
  waiting for transfers between devices: 16.7 us -> 27.4 us
  starting transfers between devices: 21 us -> 18.6 us
  other arithmetic: 0.62 us -> 0 us
    ppermute x16, waiting for transfers between devices: 16.7 us -> 27.4 us  [swap(): return lax.ppermute(value, axes, [(i, i ^ step) for i in range(size)])]
    ppermute x16, starting transfers between devices: 21 us -> 18.6 us  [swap(): return lax.ppermute(value, axes, [(i, i ^ step) for i in range(size)])]
    pallas_call x3 -> x7, Pallas kernels: 2.06 us -> 2.7 us  [the longest x2 2 us: score(): pl.pallas_call(functools.partial(score_kernel, first, count, heads, pools...]
    concatenate x2 -> x0, other arithmetic: 0.62 us -> none  [per_device(): return jnp.concatenate(columns, axis=1).astype(bf16)[None]]
  transfers between devices with their start and end apart: 16 -> 16, of which waited for: 9 -> 10; matrix products, arithmetic and copies ran while one was open for 0% -> 0% of each run, Pallas kernels for 12% -> 11%
where the time goes in v3:
time: 57.8 us; the launch traced here: 57.6 us
  waiting for transfers between devices  27.4 us (47%)
  starting transfers between devices  18.6 us (32%)
  Pallas kernels  11.5 us (20%)
    ppermute x16, waiting for transfers between devices, swap(): return lax.ppermute(value, axes, [(i, i ^ step) for i in range(size)])  27.4 us
    ppermute x16, starting transfers between devices, swap(): return lax.ppermute(value, axes, [(i, i ^ step) for i in range(size)])  18.6 us
    pallas_call x1, Pallas kernels, per_device(): pl.pallas_call(functools.partial(gather_kernel, pools), out_shape=[shape(...  3 us
    pallas_call x1, Pallas kernels, per_device(): pl.pallas_call(functools.partial(table_kernel, pools, shard_blocks), out_...  2.97 us
    pallas_call x2, Pallas kernels, score(): pl.pallas_call(functools.partial(score_kernel, first, count, heads, pools...  2 us
    pallas_call x1, Pallas kernels, per_device(): pl.pallas_call(functools.partial(project_kernel, pools, heads, reps), out...  1.2 us
  transfers between devices with their start and end apart: 16, of which 10 were waited for; matrix products, arithmetic and copies ran while one was open for 0% of the time, Pallas kernels for 11%

profile of v3, /device:TPU:0, one launch (start us, length us, event | category | flops | bytes accessed | tf_op | source)
XLA Modules:
  0.0 57.6 jit_solution(481513746761662203)
XLA Ops:
  0.0 3.0 %gather.1 = (bf16[1,4096]{1,0:T(2,128)(2,1)S(1)}, bf16[512,256]{1,0:T(8,128)(2,1)S(1)}, bf16[512,256]{1,0:T(8,128)(2,1)S(1)}, bf16[256,256]{1,0:T(8,128)(2,1)S(1...) custom-call(s32[1,4,4]{2,1,0:T(4,128)} %sel_ref.5, ...), custom_call_target="tpu_custom_call" | custom-call | tf_op jit(solution)/shard_map/gather/pallas_call | solution.py:308
  3.0 3.0 %collective-permute-start.2 = (bf16[512,256]{1,0:T(8,128)(2,1)S(1)}, bf16[512,256]{1,0:T(8,128)(2,1)S(1)}, u32[]{:S(2)}, u32[]{:S(2)}) collective-permute-start(bf16[512,256]{1,0:T(8,128)(2,1)S(1)} %get-tuple-element.35.rest_0_), channel_id=1, source_target_pairs={{0,2},{2,0},{1,3},{3,1},{4,6},{6,4},{5,7},{7,5},{8,10},{10,8},{9,1... | collective-permute-start | bytes 786440 | tf_op jit(solution)/shard_map/ppermute | solution.py:35
  6.0 3.6 %collective-permute-start.7 = (bf16[256,256]{1,0:T(8,128)(2,1)S(1)}, bf16[256,256]{1,0:T(8,128)(2,1)S(1)}, u32[]{:S(2)}, u32[]{:S(2)}) collective-permute-start(bf16[256,256]{1,0:T(8,128)(2,1)S(1)} %get-tuple-element.41), channel_id=1, source_target_pairs={{0,12},{4,8},{8,4},{12,0},{1,13},{5,9},{9,5},{13,1},{2,14},{6,10},... | collective-permute-start | bytes 393224 | tf_op jit(solution)/shard_map/ppermute | solution.py:35
  9.6 0.8 %collective-permute-start.9 = (bf16[256,256]{1,0:T(8,128)(2,1)S(1)}, bf16[256,256]{1,0:T(8,128)(2,1)S(1)}, u32[]{:S(2)}, u32[]{:S(2)}) collective-permute-start(bf16[256,256]{1,0:T(8,128)(2,1)S(1)} %get-tuple-element.43), channel_id=1, source_target_pairs={{0,4},{4,0},{8,12},{12,8},{1,5},{5,1},{9,13},{13,9},{2,6},{6,2},{1... | collective-permute-start | bytes 393224 | tf_op jit(solution)/shard_map/ppermute | solution.py:35
  10.4 1.3 %collective-permute-start = (bf16[1,4096]{1,0:T(2,128)(2,1)S(1)}, bf16[1,4096]{1,0:T(2,128)(2,1)S(1)}, u32[]{:S(2)}, u32[]{:S(2)}) collective-permute-start(bf16[1,4096]{1,0:T(2,128)(2,1)S(1)} %get-tuple-element.27.refs_0_), channel_id=1, source_target_pairs={{0,4},{4,0},{8,12},{12,8},{1,5},{5,1},{9,13},{13,9},{2,6},{6,2},{1... | collective-permute-start | bytes 24584 | tf_op jit(solution)/shard_map/ppermute | solution.py:35
  11.7 6.5 %collective-permute-done.refs_1_ = bf16[1,4096]{1,0:T(2,128)(2,1)S(1)} collective-permute-done((bf16[1,4096]{1,0:T(2,128)(2,1)S(1)}, bf16[1,4096]{1,0:T(2,128)(2,1)S(1)}, u32[]{:S(2)}, u32[]{:S(2)}) %collective-permute-start) | collective-permute-done | bytes 8224 | tf_op jit(solution)/shard_map/ppermute | solution.py:35
  18.2 1.4 %collective-permute-start.1 = (bf16[2,4096]{1,0:T(2,128)(2,1)S(1)}, bf16[2,4096]{1,0:T(2,128)(2,1)S(1)}, u32[]{:S(2)}, u32[]{:S(2)}) collective-permute-start(bf16[2,4096]{1,0:T(2,128)(2,1)S(1)} %join.3.after_ref.query_ref), channel_id=1, source_target_pairs={{0,8},{4,12},{8,0},{12,4},{1,9},{5,13},{9,1},{13,5},{2,10},{6,14},... | collective-permute-start | bytes 49160 | tf_op jit(solution)/shard_map/ppermute | solution.py:35
  19.5 3.0 %tables.1 = (f32[1024,128]{1,0:T(8,128)S(1)}, f32[1024,128]{1,0:T(8,128)S(1)}, f32[8,128]{1,0:T(8,128)S(1)}, s32[4,256]{1,0:T(4,128)S(1)}, s32[1,1024]{1,0:T(1,1...) custom-call(s32[1,4,4]{2,1,0:T(4,128)} %sel_ref.5, s32[1,4]{1,0:T(1,128)} %len_ref.1, ...), custom_call_target="tpu_custom_call" | custom-call | tf_op jit(solution)/shard_map/tables/pallas_call | solution.py:335
  22.5 0.4 collective-permute-done.1.query_ref
  22.9 0.5 collective-permute-start.5
  23.4 1.0 %score.2 = (f32[32,256]{1,0:T(8,128)S(1)}, f32[32,256]{1,0:T(8,128)S(1)}) custom-call(bf16[512,512]{1,0:T(8,128)(2,1)S(1)} %get-tuple-element.30.map_ref, f32[1024,128]{1,0:T(8,128)S(1)} %get-tuple-element.31.cos_ref, f32[1024,128]{1,0:T(8,128)S(1)} %get-tuple-element.32.sin_ref, f32[8,128]{1,0:T(8,128)S(1)} %get-tuple-element.33.turn_ref, ...), custom_call_target="tpu_custom_call" | custom-call | tf_op jit(solution)/shard_map/score/pallas_call | solution.py:348
  24.4 3.3 %collective-permute-start.3 = (f32[32,256]{1,0:T(8,128)S(1)}, f32[32,256]{1,0:T(8,128)S(1)}, u32[]{:S(2)}, u32[]{:S(2)}) collective-permute-start(f32[32,256]{1,0:T(8,128)S(1)} %get-tuple-element.36), channel_id=1, source_target_pairs={{0,12},{4,8},{8,4},{12,0},{1,13},{5,9},{9,5},{13,1},{2,14},{6,10},... | collective-permute-start | bytes 98312 | tf_op jit(solution)/shard_map/ppermute | solution.py:35
  27.7 0.7 %collective-permute-start.4 = (f32[32,256]{1,0:T(8,128)S(1)}, f32[32,256]{1,0:T(8,128)S(1)}, u32[]{:S(2)}, u32[]{:S(2)}) collective-permute-start(f32[32,256]{1,0:T(8,128)S(1)} %get-tuple-element.37.after_ref), channel_id=1, source_target_pairs={{0,8},{4,12},{8,0},{12,4},{1,9},{5,13},{9,1},{13,5},{2,10},{6,14},... | collective-permute-start | bytes 98312 | tf_op jit(solution)/shard_map/ppermute | solution.py:35
  28.4 1.8 %collective-permute-done.3.rest_4_.rest_0_ = f32[32,256]{1,0:T(8,128)S(1)} collective-permute-done((f32[32,256]{1,0:T(8,128)S(1)}, f32[32,256]{1,0:T(8,128)S(1)}, u32[]{:S(2)}, u32[]{:S(2)}) %collective-permute-start.3) | collective-permute-done | bytes 32800 | tf_op jit(solution)/shard_map/ppermute | solution.py:35
  30.2 2.3 %collective-permute-done.4.rest_5_.rest_1_ = f32[32,256]{1,0:T(8,128)S(1)} collective-permute-done((f32[32,256]{1,0:T(8,128)S(1)}, f32[32,256]{1,0:T(8,128)S(1)}, u32[]{:S(2)}, u32[]{:S(2)}) %collective-permute-start.4) | collective-permute-done | bytes 32800 | tf_op jit(solution)/shard_map/ppermute | solution.py:35
  32.5 1.1 %compact.1.rest_4_ = bf16[512,256]{1,0:T(8,128)(2,1)S(1)} custom-call(s32[1,4,4]{2,1,0:T(4,128)} %sel_ref.5, bf16[256,256]{1,0:T(8,128)(2,1)S(1)} %collective-permute-done.7.rest_0_, bf16[256,256]{1,0:T(8,128)(2,1)S(1)} %collective-permute-done.8.rest_1_, bf16[256,256]{1,0:T(8,128)(2,1)S(1)} %collective-permute-done.9.rest_2_, ...), custom_call_target="tpu_custom_call" | custom-call | tf_op jit(solution)/shard_map/compact/pallas_call | solution.py:362
  33.7 1.6 %collective-permute-start.10 = (bf16[512,256]{1,0:T(8,128)(2,1)S(1)}, bf16[512,256]{1,0:T(8,128)(2,1)S(1)}, u32[]{:S(2)}, u32[]{:S(2)}) collective-permute-start(bf16[512,256]{1,0:T(8,128)(2,1)S(1)} %compact.1.rest_4_), channel_id=1, source_target_pairs={{0,2},{2,0},{1,3},{3,1},{4,6},{6,4},{5,7},{7,5},{8,10},{10,8},{9,1... | collective-permute-start | bytes 786440 | tf_op jit(solution)/shard_map/ppermute | solution.py:35
  35.2 1.0 %score.3 = (f32[32,256]{1,0:T(8,128)S(1)}, f32[32,256]{1,0:T(8,128)S(1)}) custom-call(bf16[512,512]{1,0:T(8,128)(2,1)S(1)} %get-tuple-element.30.map_ref, f32[1024,128]{1,0:T(8,128)S(1)} %get-tuple-element.31.cos_ref, f32[1024,128]{1,0:T(8,128)S(1)} %get-tuple-element.32.sin_ref, f32[8,128]{1,0:T(8,128)S(1)} %get-tuple-element.33.turn_ref, ...), custom_call_target="tpu_custom_call" | custom-call | tf_op jit(solution)/shard_map/score/pallas_call | solution.py:348
  36.3 3.9 %collective-permute-done.6.rest_2_ = f32[32,256]{1,0:T(8,128)S(1)} collective-permute-done((f32[32,256]{1,0:T(8,128)S(1)}, f32[32,256]{1,0:T(8,128)S(1)}, u32[]{:S(2)}, u32[]{:S(2)}) %collective-permute-start.6) | collective-permute-done | bytes 32800 | tf_op jit(solution)/shard_map/ppermute | solution.py:35
  40.2 0.5 attend.1.refs_0_
  40.7 0.1 collective-permute-start.11
  40.8 1.2 %collective-permute-done.11.refs_1_ = bf16[1,4096]{1,0:T(2,128)(2,1)S(1)} collective-permute-done((bf16[1,4096]{1,0:T(2,128)(2,1)S(1)}, bf16[1,4096]{1,0:T(2,128)(2,1)S(1)}, u32[]{:S(2)}, u32[]{:S(2)}) %collective-permute-start.11) | collective-permute-done | bytes 8224 | tf_op jit(solution)/shard_map/ppermute | solution.py:35
  42.0 0.1 collective-permute-start.12
  42.1 3.7 %collective-permute-done.12.refs_1_ = bf16[2,4096]{1,0:T(2,128)(2,1)S(1)} collective-permute-done((bf16[2,4096]{1,0:T(2,128)(2,1)S(1)}, bf16[2,4096]{1,0:T(2,128)(2,1)S(1)}, u32[]{:S(2)}, u32[]{:S(2)}) %collective-permute-start.12) | collective-permute-done | bytes 16416 | tf_op jit(solution)/shard_map/ppermute | solution.py:35
  45.8 0.7 %collective-permute-start.13 = (bf16[4,4096]{1,0:T(4,128)(2,1)S(1)}, bf16[4,4096]{1,0:T(4,128)(2,1)S(1)}, u32[]{:S(2)}, u32[]{:S(2)}) collective-permute-start(bf16[4,4096]{1,0:T(4,128)(2,1)S(1)} %join.5.own_ref), channel_id=1, source_target_pairs={{0,8},{4,12},{8,0},{12,4},{1,9},{5,13},{9,1},{13,5},{2,10},{6,14},... | collective-permute-start | bytes 98312 | tf_op jit(solution)/shard_map/ppermute | solution.py:35
  46.6 4.1 %collective-permute-done.13.far_ref = bf16[4,4096]{1,0:T(4,128)(2,1)S(1)} collective-permute-done((bf16[4,4096]{1,0:T(4,128)(2,1)S(1)}, bf16[4,4096]{1,0:T(4,128)(2,1)S(1)}, u32[]{:S(2)}, u32[]{:S(2)}) %collective-permute-start.13) | collective-permute-done | bytes 32800 | tf_op jit(solution)/shard_map/ppermute | solution.py:35
  50.7 1.2 %project.1 = (f32[4,1024]{1,0:T(4,128)S(1)}, f32[4,1024]{1,0:T(4,128)S(1)}) custom-call(bf16[4,4096]{1,0:T(4,128)(2,1)S(1)} %join.5.own_ref, bf16[4,4096]{1,0:T(4,128)(2,1)S(1)} %collective-permute-done.13.far_ref, bf16[4096,1024]{1,0:T(8,128)(2,1)S(1)} %copy-done), custom_call_target="tpu_custom_call" | custom-call | tf_op jit(solution)/shard_map/project/pallas_call | solution.py:391
  51.9 1.5 %collective-permute-start.14 = (f32[4,1024]{1,0:T(4,128)S(1)}, f32[4,1024]{1,0:T(4,128)S(1)}, u32[]{:S(2)}, u32[]{:S(2)}) collective-permute-start(f32[4,1024]{1,0:T(4,128)S(1)} %get-tuple-element.46), channel_id=1, source_target_pairs={{0,2},{2,0},{1,3},{3,1},{4,6},{6,4},{5,7},{7,5},{8,10},{10,8},{9,1... | collective-permute-start | bytes 49160 | tf_op jit(solution)/shard_map/ppermute | solution.py:35
  53.4 2.3 %collective-permute-done.14.refs_1_ = f32[4,1024]{1,0:T(4,128)S(1)} collective-permute-done((f32[4,1024]{1,0:T(4,128)S(1)}, f32[4,1024]{1,0:T(4,128)S(1)}, u32[]{:S(2)}, u32[]{:S(2)}) %collective-permute-start.14) | collective-permute-done | bytes 16416 | tf_op jit(solution)/shard_map/ppermute | solution.py:35
  55.7 0.1 collective-permute-start.15
  55.8 1.2 %collective-permute-done.15.refs_1_ = bf16[2,1024]{1,0:T(2,128)(2,1)S(1)} collective-permute-done((bf16[2,1024]{1,0:T(2,128)(2,1)S(1)}, bf16[2,1024]{1,0:T(2,128)(2,1)S(1)}, u32[]{:S(2)}, u32[]{:S(2)}) %collective-permute-start.15) | collective-permute-done | bytes 4128 | tf_op jit(solution)/shard_map/ppermute | solution.py:35
  57.0 0.6 %place.1 = bf16[1,2,2048]{2,1,0:T(2,128)(2,1)} custom-call(bf16[2,1024]{1,0:T(2,128)(2,1)S(1)} %get-tuple-element.47.refs_0_, bf16[2,1024]{1,0:T(2,128)(2,1)S(1)} %collective-permute-done.15.refs_1_), custom_call_target="tpu_custom_call" | custom-call | tf_op jit(solution)/shard_map/place/pallas_call | solution.py:408
  (14 shorter events, 0.2 us)
Async XLA Ops:
  0.0 50.7 %copy-start = (bf16[4096,1024]{1,0:T(8,128)(2,1)S(1)}, bf16[4096,1024]{1,0:T(8,128)(2,1)}, u32[]{:S(2)}) copy-start(bf16[4096,1024]{1,0:T(8,128)(2,1)} %weight_ref.1) | copy-start | bytes 25165828
  3.0 20.4 %collective-permute-start.2 = (bf16[512,256]{1,0:T(8,128)(2,1)S(1)}, bf16[512,256]{1,0:T(8,128)(2,1)S(1)}, u32[]{:S(2)}, u32[]{:S(2)}) collective-permute-start(bf16[512,256]{1,0:T(8,128)(2,1)S(1)} %get-tuple-element.35.rest_0_), channel_id=1, source_target_pairs={{0,2},{2,0},{1,3},{3,1},{4,6},{6,4},{5,7},{7,5},{8,10},{10,8},{9,1... | collective-permute-start | bytes 786440 | tf_op jit(solution)/shard_map/ppermute | solution.py:35
  6.0 21.7 %collective-permute-start.7 = (bf16[256,256]{1,0:T(8,128)(2,1)S(1)}, bf16[256,256]{1,0:T(8,128)(2,1)S(1)}, u32[]{:S(2)}, u32[]{:S(2)}) collective-permute-start(bf16[256,256]{1,0:T(8,128)(2,1)S(1)} %get-tuple-element.41), channel_id=1, source_target_pairs={{0,12},{4,8},{8,4},{12,0},{1,13},{5,9},{9,5},{13,1},{2,14},{6,10},... | collective-permute-start | bytes 393224 | tf_op jit(solution)/shard_map/ppermute | solution.py:35
  9.6 18.7 %collective-permute-start.8 = (bf16[256,256]{1,0:T(8,128)(2,1)S(1)}, bf16[256,256]{1,0:T(8,128)(2,1)S(1)}, u32[]{:S(2)}, u32[]{:S(2)}) collective-permute-start(bf16[256,256]{1,0:T(8,128)(2,1)S(1)} %get-tuple-element.42), channel_id=1, source_target_pairs={{0,8},{4,12},{8,0},{12,4},{1,9},{5,13},{9,1},{13,5},{2,10},{6,14},... | collective-permute-start | bytes 393224 | tf_op jit(solution)/shard_map/ppermute | solution.py:35
  9.6 18.7 %collective-permute-start.9 = (bf16[256,256]{1,0:T(8,128)(2,1)S(1)}, bf16[256,256]{1,0:T(8,128)(2,1)S(1)}, u32[]{:S(2)}, u32[]{:S(2)}) collective-permute-start(bf16[256,256]{1,0:T(8,128)(2,1)S(1)} %get-tuple-element.43), channel_id=1, source_target_pairs={{0,4},{4,0},{8,12},{12,8},{1,5},{5,1},{9,13},{13,9},{2,6},{6,2},{1... | collective-permute-start | bytes 393224 | tf_op jit(solution)/shard_map/ppermute | solution.py:35
  10.4 7.7 %collective-permute-start = (bf16[1,4096]{1,0:T(2,128)(2,1)S(1)}, bf16[1,4096]{1,0:T(2,128)(2,1)S(1)}, u32[]{:S(2)}, u32[]{:S(2)}) collective-permute-start(bf16[1,4096]{1,0:T(2,128)(2,1)S(1)} %get-tuple-element.27.refs_0_), channel_id=1, source_target_pairs={{0,4},{4,0},{8,12},{12,8},{1,5},{5,1},{9,13},{13,9},{2,6},{6,2},{1... | collective-permute-start | bytes 24584 | tf_op jit(solution)/shard_map/ppermute | solution.py:35
  18.2 4.7 %collective-permute-start.1 = (bf16[2,4096]{1,0:T(2,128)(2,1)S(1)}, bf16[2,4096]{1,0:T(2,128)(2,1)S(1)}, u32[]{:S(2)}, u32[]{:S(2)}) collective-permute-start(bf16[2,4096]{1,0:T(2,128)(2,1)S(1)} %join.3.after_ref.query_ref), channel_id=1, source_target_pairs={{0,8},{4,12},{8,0},{12,4},{1,9},{5,13},{9,1},{13,5},{2,10},{6,14},... | collective-permute-start | bytes 49160 | tf_op jit(solution)/shard_map/ppermute | solution.py:35
  22.9 12.4 %collective-permute-start.5 = (bf16[512,256]{1,0:T(8,128)(2,1)S(1)}, bf16[512,256]{1,0:T(8,128)(2,1)S(1)}, u32[]{:S(2)}, u32[]{:S(2)}) collective-permute-start(bf16[512,256]{1,0:T(8,128)(2,1)S(1)} %get-tuple-element.38.rest_0_), channel_id=1, source_target_pairs={{0,2},{2,0},{1,3},{3,1},{4,6},{6,4},{5,7},{7,5},{8,10},{10,8},{9,1... | collective-permute-start | bytes 786440 | tf_op jit(solution)/shard_map/ppermute | solution.py:35
  24.4 5.8 %collective-permute-start.3 = (f32[32,256]{1,0:T(8,128)S(1)}, f32[32,256]{1,0:T(8,128)S(1)}, u32[]{:S(2)}, u32[]{:S(2)}) collective-permute-start(f32[32,256]{1,0:T(8,128)S(1)} %get-tuple-element.36), channel_id=1, source_target_pairs={{0,12},{4,8},{8,4},{12,0},{1,13},{5,9},{9,5},{13,1},{2,14},{6,10},... | collective-permute-start | bytes 98312 | tf_op jit(solution)/shard_map/ppermute | solution.py:35
  27.7 4.8 %collective-permute-start.4 = (f32[32,256]{1,0:T(8,128)S(1)}, f32[32,256]{1,0:T(8,128)S(1)}, u32[]{:S(2)}, u32[]{:S(2)}) collective-permute-start(f32[32,256]{1,0:T(8,128)S(1)} %get-tuple-element.37.after_ref), channel_id=1, source_target_pairs={{0,8},{4,12},{8,0},{12,4},{1,9},{5,13},{9,1},{13,5},{2,10},{6,14},... | collective-permute-start | bytes 98312 | tf_op jit(solution)/shard_map/ppermute | solution.py:35
  33.7 6.5 %collective-permute-start.10 = (bf16[512,256]{1,0:T(8,128)(2,1)S(1)}, bf16[512,256]{1,0:T(8,128)(2,1)S(1)}, u32[]{:S(2)}, u32[]{:S(2)}) collective-permute-start(bf16[512,256]{1,0:T(8,128)(2,1)S(1)} %compact.1.rest_4_), channel_id=1, source_target_pairs={{0,2},{2,0},{1,3},{3,1},{4,6},{6,4},{5,7},{7,5},{8,10},{10,8},{9,1... | collective-permute-start | bytes 786440 | tf_op jit(solution)/shard_map/ppermute | solution.py:35
  36.2 3.9 %collective-permute-start.6 = (f32[32,256]{1,0:T(8,128)S(1)}, f32[32,256]{1,0:T(8,128)S(1)}, u32[]{:S(2)}, u32[]{:S(2)}) collective-permute-start(f32[32,256]{1,0:T(8,128)S(1)} %get-tuple-element.39), channel_id=1, source_target_pairs={{0,4},{4,0},{8,12},{12,8},{1,5},{5,1},{9,13},{13,9},{2,6},{6,2},{1... | collective-permute-start | bytes 98312 | tf_op jit(solution)/shard_map/ppermute | solution.py:35
  40.7 1.2 %collective-permute-start.11 = (bf16[1,4096]{1,0:T(2,128)(2,1)S(1)}, bf16[1,4096]{1,0:T(2,128)(2,1)S(1)}, u32[]{:S(2)}, u32[]{:S(2)}) collective-permute-start(bf16[1,4096]{1,0:T(2,128)(2,1)S(1)} %attend.1.refs_0_), channel_id=1, source_target_pairs={{0,1},{1,0},{2,3},{3,2},{4,5},{5,4},{6,7},{7,6},{8,9},{9,8},{10,11... | collective-permute-start | bytes 24584 | tf_op jit(solution)/shard_map/ppermute | solution.py:35
  42.0 3.8 %collective-permute-start.12 = (bf16[2,4096]{1,0:T(2,128)(2,1)S(1)}, bf16[2,4096]{1,0:T(2,128)(2,1)S(1)}, u32[]{:S(2)}, u32[]{:S(2)}) collective-permute-start(bf16[2,4096]{1,0:T(2,128)(2,1)S(1)} %join.4.refs_0_), channel_id=1, source_target_pairs={{0,4},{4,0},{8,12},{12,8},{1,5},{5,1},{9,13},{13,9},{2,6},{6,2},{1... | collective-permute-start | bytes 49160 | tf_op jit(solution)/shard_map/ppermute | solution.py:35
  45.8 4.9 %collective-permute-start.13 = (bf16[4,4096]{1,0:T(4,128)(2,1)S(1)}, bf16[4,4096]{1,0:T(4,128)(2,1)S(1)}, u32[]{:S(2)}, u32[]{:S(2)}) collective-permute-start(bf16[4,4096]{1,0:T(4,128)(2,1)S(1)} %join.5.own_ref), channel_id=1, source_target_pairs={{0,8},{4,12},{8,0},{12,4},{1,9},{5,13},{9,1},{13,5},{2,10},{6,14},... | collective-permute-start | bytes 98312 | tf_op jit(solution)/shard_map/ppermute | solution.py:35
  51.9 3.8 %collective-permute-start.14 = (f32[4,1024]{1,0:T(4,128)S(1)}, f32[4,1024]{1,0:T(4,128)S(1)}, u32[]{:S(2)}, u32[]{:S(2)}) collective-permute-start(f32[4,1024]{1,0:T(4,128)S(1)} %get-tuple-element.46), channel_id=1, source_target_pairs={{0,2},{2,0},{1,3},{3,1},{4,6},{6,4},{5,7},{7,5},{8,10},{10,8},{9,1... | collective-permute-start | bytes 49160 | tf_op jit(solution)/shard_map/ppermute | solution.py:35
  55.7 1.2 %collective-permute-start.15 = (bf16[2,1024]{1,0:T(2,128)(2,1)S(1)}, bf16[2,1024]{1,0:T(2,128)(2,1)S(1)}, u32[]{:S(2)}, u32[]{:S(2)}) collective-permute-start(bf16[2,1024]{1,0:T(2,128)(2,1)S(1)} %get-tuple-element.48), channel_id=1, source_target_pairs={{0,1},{1,0},{2,3},{3,2},{4,5},{5,4},{6,7},{7,6},{8,9},{9,8},{10,11... | collective-permute-start | bytes 12296 | tf_op jit(solution)/shard_map/ppermute | solution.py:35

commit v4 on v3

--- a/solution.py
+++ b/solution.py
@@ -58,9 +58,21 @@
     return first, second
 
 
-def gather_kernel(pools, sel_ref, lat_ref, query_ref, line_ref, near_ref, far_ref, *rest):
-    value_refs = rest[:pools]
-    raw, sems = rest[pools:]
+def heads_to_rows(line, lanes):
+    count = line.shape[1] // HEAD_SIZE
+    rows = jnp.concatenate([line[:, n * HEAD_SIZE : (n + 1) * HEAD_SIZE] for n in range(count)], axis=0)
+    return jnp.concatenate([rows[:, i : i + lanes] for i in range(0, HEAD_SIZE, lanes)], axis=0)
+
+
+def rows_to_heads(rows):
+    pieces = HEAD_SIZE // rows.shape[1]
+    count = rows.shape[0] // pieces
+    return jnp.concatenate([rows[i * count : (i + 1) * count, :] for i in range(pieces)], axis=1)
+
+
+def gather_kernel(pools, sel_ref, lat_ref, query_ref, near_ref, far_ref, *rest):
+    value_refs = rest[:-2]
+    raw, sems = rest[-2:]
     shard_blocks = lat_ref.shape[2] // BLOCK
     columns = lat_ref.shape[3]
     width = columns // 2
@@ -77,7 +89,7 @@
                 sems.at[k * CAP + c],
             )
             copies[k, c].start()
-    line_ref[...] = query_ref[0]
+    queries = heads_to_rows(query_ref[0].astype(jnp.float32), value_refs[0].shape[1]).astype(jnp.bfloat16)
     chunk = min(4 * LANE, columns)
     half = chunk // 2
     source = lax.broadcasted_iota(jnp.int32, (chunk, chunk), 0)
@@ -95,14 +107,14 @@
                 preferred_element_type=jnp.float32,
             ).astype(jnp.bfloat16)
             keys_ref[at * rows : (at + 1) * rows, j * half : (j + 1) * half] = packed[:, :half]
-            value_refs[k][:, j * half : (j + 1) * half] = packed[:, half:]
-
-
-def table_kernel(
-    pools, shard_blocks, sel_ref, len_ref, freq_ref, after_ref, key_map_ref, value_map_ref,
-    cos_ref, sin_ref, turn_ref, live_ref, place_ref, key_out_ref, value_out_ref, sems,
-):
-    del after_ref
+            value_refs[j * pools + k][:rows, :] = packed[:, half:]
+        value_refs[k][rows:, :] = queries
+
+
+def table_kernel(pools, shard_blocks, sel_ref, len_ref, freq_ref, key_map_ref, value_map_ref, *rest):
+    held = (len(rest) - 8) // 2
+    cos_ref, sin_ref, turn_ref, live_ref, place_ref, key_out_ref, value_out_ref = rest[held : held + 7]
+    sems = rest[-1]
     loads = [
         pltpu.make_async_copy(key_map_ref, key_out_ref, sems.at[0]),
         pltpu.make_async_copy(value_map_ref, value_out_ref, sems.at[1]),
@@ -142,10 +154,11 @@
         load.wait()
 
 
-def score_kernel(first, count, heads, pools, map_ref, cos_ref, sin_ref, turn_ref, live_ref, query_ref, after_ref, *rest):
+def score_kernel(first, count, heads, pools, map_ref, cos_ref, sin_ref, turn_ref, live_ref, after_ref, *rest):
     del after_ref
     key_refs = rest[:heads]
-    out_refs = rest[heads : heads + count]
+    pay_refs = rest[heads : heads + count][::-1]
+    out_refs = rest[heads + count :]
     head = lax.axis_index("heads")
     width = key_refs[0].shape[1]
     groups = map_ref.shape[1] // HEAD_SIZE
@@ -157,10 +170,7 @@
     for i in range(count):
         k = first + i
         live = live_ref[k : k + 1, :] > 0
-        line = query_ref[i : i + 1, :].astype(jnp.float32)
-        query = jnp.concatenate(
-            [line[:, n * HEAD_SIZE : (n + 1) * HEAD_SIZE] for n in range(groups * QUERY_PER_GROUP)], axis=0
-        )
+        query = rows_to_heads(pay_refs[i][rows:, :].astype(jnp.float32))
         query = query * turn_ref[k : k + 1, :] + pltpu.roll(query, HEAD_SIZE // 2, 1) * turn_ref[
             pools + k : pools + k + 1, :
         ]
@@ -199,10 +209,10 @@
     pltpu.make_async_copy(out_ref, out_ref, sem).wait()
 
 
-def attend_kernel(pools, heads, map_ref, place_ref, *rest):
+def attend_kernel(pools, heads, chunks, map_ref, place_ref, *rest):
     score_refs = rest[:pools][::-1]
-    value_refs = rest[pools : pools + heads]
-    out_ref = rest[pools + heads]
+    value_refs = rest[pools : pools + heads * chunks]
+    out_ref = rest[-1]
     head = lax.axis_index("heads")
     width = value_refs[0].shape[1]
     groups = map_ref.shape[1] // HEAD_SIZE
@@ -224,8 +234,8 @@
         dense.append(chosen)
     attention = jnp.concatenate(dense, axis=1).astype(jnp.bfloat16)
     mixed = [None] * groups
-    for j in range(heads):
-        owner = head ^ j
+    for j in range(heads * chunks):
+        owner = (head ^ (j // chunks)) * chunks + j % chunks
         context = jnp.dot(
             attention, value_refs[j][...], preferred_element_type=jnp.float32
         ).astype(jnp.bfloat16)
@@ -248,37 +258,30 @@
     refs[-1][...] = jnp.concatenate(rows, axis=0).astype(jnp.bfloat16)
 
 
-def project_kernel(pools, heads, reps, own_ref, far_ref, weight_ref, *rest):
-    out_refs = rest[:heads]
-    acc = rest[heads]
-    left = jnp.concatenate(
-        [own_ref[...].astype(jnp.float32), far_ref[...].astype(jnp.float32)], axis=0
-    ).astype(jnp.bfloat16)
+def project_kernel(pools, heads, reps, weight_ref, *rest):
+    row_refs = rest[:pools][::-1]
+    out_refs = rest[pools:-1]
+    acc = rest[-1]
+    left = jnp.concatenate([ref[...].astype(jnp.float32) for ref in row_refs], axis=0).astype(jnp.bfloat16)
     acc[...] = jnp.dot(left, weight_ref[...], preferred_element_type=jnp.float32)
     pool = lax.axis_index("pool")
     head = lax.axis_index("heads")
     each = pools // heads
-    for j in range(heads):
-        for t in range(reps):
-            for u in range(each):
-                n = (pool ^ ((head ^ j) * each + u)) * reps + t
-                out_refs[j][t * each + u : t * each + u + 1, :] = acc[pl.ds(n, 1), :]
-
-
-def sum_kernel(reps, *refs):
-    part_refs, out_refs = refs[:-reps], refs[-reps:]
-    total = functools.reduce(jnp.add, [ref[...] for ref in part_refs])
-    each = total.shape[0] // reps
-    for t in range(reps):
-        out_refs[t][...] = total[t * each : (t + 1) * each, :].astype(jnp.bfloat16)
-
-
-def place_kernel(reps, *refs):
-    out_ref = refs[reps]
+    for d in range(heads * reps):
+        for u in range(each):
+            n = (pool ^ ((head ^ (d // reps)) * each + u)) * reps + d % reps
+            out_refs[d][u : u + 1, :] = acc[pl.ds(n, 1), :]
+
+
+def finish_kernel(heads, reps, *refs):
+    out_ref = refs[-1]
+    refs = refs[:-1][::-1]
     rep = lax.axis_index("rep")
     width = refs[0].shape[1]
     for t in range(reps):
-        out_ref[0, :, pl.ds(pl.multiple_of((rep ^ t) * width, width), width)] = refs[t][...]
+        total = functools.reduce(jnp.add, [refs[j * reps + t][...] for j in range(heads)])
+        columns = pl.ds(pl.multiple_of((rep ^ t) * width, width), width)
+        out_ref[0, :, columns] = total.astype(jnp.bfloat16)
 
 
 def per_device(queries, latents, key_latent_maps, value_latent_maps, out_weight, lengths, selected):
@@ -305,13 +308,24 @@
             name="join",
         )(*blocks)
 
+    def exchange(value, axis, size):
+        taken = {step: swap(value, axis, size, step) for step in range(size - 1, 0, -1)}
+        return [value] + [taken[step] for step in range(1, size)]
+
+    def scatter(blocks, axis, size):
+        taken = {step: swap(blocks[step], axis, size, step) for step in range(size - 1, 0, -1)}
+        return [blocks[0]] + [taken[step] for step in range(1, size)]
+
+    middle = pools // 2
+    chunks = max(1, width // (2 * LANE))
+    query_rows = queries.shape[2] // (width // chunks)
     packed = pl.pallas_call(
         functools.partial(gather_kernel, pools),
-        out_shape=[shape((1, queries.shape[2]), bf16)]
-        + [shape((pools // 2 * rows, width), bf16)] * 2
-        + [shape((rows, width), bf16)] * pools,
+        out_shape=[shape((middle * rows, width), bf16)] * 2
+        + [shape((rows + query_rows, width // chunks), bf16)] * pools
+        + [shape((rows, width // chunks), bf16)] * (pools * (chunks - 1)),
         in_specs=[SMEM, HBM, VMEM],
-        out_specs=[VMEM] * (pools + 3),
+        out_specs=[VMEM] * (pools * chunks + 2),
         scratch_shapes=[
             pltpu.VMEM((pools * rows, 2 * width), bf16),
             pltpu.SemaphoreType.DMA((pools * CAP,)),
@@ -319,100 +333,94 @@
         compiler_params=params(16),
         name="gather",
     )(in_hbm(selected), in_hbm(latents), in_hbm(queries))
-    line, near, far, values = packed[0], packed[1], packed[2], packed[3:]
-    value_parts = {k: swap(values[k], "pool", pools, k) for k in range(pools - 1, 0, -1)}
-    value_parts = [values[0]] + [value_parts[k] for k in range(1, pools)]
-    far_parts = [far] + [swap(far, "heads", heads, j) for j in range(1, heads)]
-    near_parts = [near] + [swap(near, "heads", heads, j) for j in range(1, heads)]
-    middle = pools // 2
-    near_queries = line
-    step = 1
-    while step < middle:
-        near_queries = join(near_queries, swap(near_queries, "pool", pools, step))
-        step *= 2
-    far_queries = swap(near_queries, "pool", pools, middle)
-
-    cosine, sine, turn, live, place, key_maps, value_maps = pl.pallas_call(
+    near, far, values = packed[0], packed[1], packed[2:]
+    far_parts = exchange(far, "heads", heads)
+    near_parts = exchange(near, "heads", heads)
+
+    later = values[pools * (chunks - 1) :]
+    cosine, sine, turn, live, place, key_maps, value_maps, *later = pl.pallas_call(
         functools.partial(table_kernel, pools, shard_blocks),
         out_shape=[shape((pools * rows, HEAD_SIZE), f32)] * 2
         + [shape((2 * pools, HEAD_SIZE), f32), shape((pools, rows), i32), shape((1, pools * rows), i32)]
-        + [shape(key_latent_maps.shape, bf16), shape(value_latent_maps.shape, bf16)],
-        in_specs=[SMEM, SMEM, VMEM, ANY, ANY, ANY],
-        out_specs=[VMEM] * 7,
+        + [shape(key_latent_maps.shape, bf16), shape(value_latent_maps.shape, bf16)]
+        + [shape(block.shape, bf16) for block in later],
+        in_specs=[SMEM, SMEM, VMEM] + [ANY] * (2 + pools),
+        out_specs=[VMEM] * 7 + [ANY] * pools,
         scratch_shapes=[pltpu.SemaphoreType.DMA((2,))],
+        input_output_aliases={5 + k: 7 + k for k in range(pools)},
         compiler_params=params(16),
         name="tables",
-    )(in_hbm(selected), in_hbm(lengths), in_hbm(freq), near_queries, in_hbm(key_latent_maps), in_hbm(value_latent_maps))
-
-    def score(first, count, key_parts, query_parts, after):
+    )(
+        in_hbm(selected), in_hbm(lengths), in_hbm(freq), in_hbm(key_latent_maps),
+        in_hbm(value_latent_maps), *later,
+    )
+    values = [*values[: pools * (chunks - 1)], *later]
+    value_parts = [scatter(values[c * pools : (c + 1) * pools], "pool", pools) for c in range(chunks)]
+
+    def score(first, count, key_parts, after):
+        pays = value_parts[0][first : first + count]
         return pl.pallas_call(
             functools.partial(score_kernel, first, count, heads, pools),
             out_shape=[shape((own_heads, rows), f32)] * count,
-            in_specs=[VMEM] * 6 + [ANY] + [VMEM] * heads,
+            in_specs=[VMEM] * 5 + [ANY] + [VMEM] * (heads + count),
             out_specs=[VMEM] * count,
             compiler_params=params(20),
+            cost_estimate=pl.CostEstimate(flops=0, transcendentals=0, bytes_accessed=3 << 20),
             name="score",
-        )(key_maps, cosine, sine, turn, live, query_parts, after, *key_parts)
-
-    far_scores = score(middle, middle, far_parts, far_queries, near_queries)
-    near_scores = score(0, middle, near_parts, near_queries, far_scores[0])
-    scores = [*near_scores, *far_scores]
-    score_parts = {k: swap(scores[k], "pool", pools, k) for k in range(pools - 1, 0, -1)}
-    score_parts = [scores[0]] + [score_parts[k] for k in range(1, pools)]
-    dense = pl.pallas_call(
-        functools.partial(compact_kernel, pools, shard_blocks),
-        out_shape=shape((sel_count * BLOCK, width), bf16),
-        in_specs=[SMEM] + [ANY] * (2 * pools - middle),
-        out_specs=ANY,
-        scratch_shapes=[pltpu.SemaphoreType.DMA],
-        compiler_params=params(8),
-        name="compact",
-    )(in_hbm(selected), *value_parts[::-1], *score_parts[:middle - 1 : -1])
-    dense_parts = [dense] + [swap(dense, "heads", heads, j) for j in range(1, heads)]
-
+        )(key_maps, cosine, sine, turn, live, after, *key_parts, *pays[::-1])
+
+    def compact(parts, *after):
+        return pl.pallas_call(
+            functools.partial(compact_kernel, pools, shard_blocks),
+            out_shape=shape((sel_count * BLOCK, width // chunks), bf16),
+            in_specs=[SMEM] + [ANY] * (pools + len(after)),
+            out_specs=ANY,
+            scratch_shapes=[pltpu.SemaphoreType.DMA],
+            compiler_params=params(8),
+            cost_estimate=pl.CostEstimate(flops=0, transcendentals=0, bytes_accessed=3 << 20),
+            name="compact",
+        )(in_hbm(selected), *parts[::-1], *after)
+
+    far_scores = score(middle, middle, far_parts, place)
+    dense = []
+    for c in range(chunks - 1):
+        dense.append(compact(value_parts[c], far_scores[0]))
+    near_scores = score(0, middle, near_parts, dense[0] if dense else far_scores[0])
+    score_parts = scatter([*near_scores, *far_scores], "pool", pools)
+    dense.append(compact(value_parts[-1], near_scores[0], *score_parts[middle:]))
+    dense = [exchange(block, "heads", heads) for block in dense]
+    dense_parts = [dense[c][j] for j in range(heads) for c in range(chunks)]
 
     mine = pl.pallas_call(
-        functools.partial(attend_kernel, pools, heads),
+        functools.partial(attend_kernel, pools, heads, chunks),
         out_shape=shape((1, own_heads * HEAD_SIZE), bf16),
-        in_specs=[VMEM] * (2 + pools + heads),
+        in_specs=[VMEM] * (2 + pools + heads * chunks),
         out_specs=VMEM,
         compiler_params=params(16),
         name="attend",
     )(value_maps, place, *score_parts[::-1], *dense_parts)
-    own_rows = join(mine, *[swap(mine, "rep", reps, r) for r in range(1, reps)])
-    step = 1
-    while step < middle:
-        own_rows = join(own_rows, swap(own_rows, "pool", pools, step))
-        step *= 2
-    far_rows = swap(own_rows, "pool", pools, middle)
+    own_rows = join(*exchange(mine, "rep", reps))
+    row_parts = exchange(own_rows, "pool", pools)
 
     own_columns = out_weight.shape[1]
     each = pools // heads
     parts = pl.pallas_call(
         functools.partial(project_kernel, pools, heads, reps),
-        out_shape=[shape((reps * each, own_columns), f32)] * heads,
-        in_specs=[VMEM] * 3,
-        out_specs=[VMEM] * heads,
+        out_shape=[shape((each, own_columns), f32)] * (heads * reps),
+        in_specs=[VMEM] * (pools + 1),
+        out_specs=[VMEM] * (heads * reps),
         scratch_shapes=[pltpu.VMEM((pools * reps, own_columns), f32)],
         compiler_params=params(24),
         name="project",
-    )(own_rows, far_rows, in_vmem(out_weight))
-    sums = pl.pallas_call(
-        functools.partial(sum_kernel, reps),
-        out_shape=[shape((each, own_columns), bf16)] * reps,
-        in_specs=[VMEM] * heads,
-        out_specs=[VMEM] * reps,
-        compiler_params=params(4),
-        name="sum",
-    )(parts[0], *[swap(parts[j], "heads", heads, j) for j in range(1, heads)])
+    )(in_vmem(out_weight), *row_parts[::-1])
     return pl.pallas_call(
-        functools.partial(place_kernel, reps),
+        functools.partial(finish_kernel, heads, reps),
         out_shape=shape((1, each, reps * own_columns), bf16),
-        in_specs=[VMEM] * reps,
+        in_specs=[VMEM] * (heads * reps),
         out_specs=VMEM,
         compiler_params=params(4),
-        name="place",
-    )(sums[0], *[swap(sums[t], "rep", reps, t) for t in range(1, reps)])
+        name="finish",
+    )(*scatter(parts, ("heads", "rep"), heads * reps)[::-1])
 
 
 def solution(mesh):

time: 57.8 us -> 48.2 us (0.83)
  waiting for transfers between devices: 27.4 us -> 9.58 us
  starting transfers between devices: 18.6 us -> 25.5 us
  Pallas kernels: 11.5 us -> 12.6 us
    ppermute x16 -> x20, waiting for transfers between devices: 27.4 us -> 9.58 us  [swap(): return lax.ppermute(value, axes, [(i, i ^ step) for i in range(size)])]
    ppermute x16 -> x20, starting transfers between devices: 18.6 us -> 25.5 us  [swap(): return lax.ppermute(value, axes, [(i, i ^ step) for i in range(size)])]
    pallas_call x4, Pallas kernels: 2.27 us -> 3.38 us  [the longest x2 1.94 us: compact(): pl.pallas_call(functools.partial(compact_kernel, pools, shard_blocks), ou...]
  transfers between devices with their start and end apart: 16 -> 20, of which waited for: 10 -> 8; matrix products, arithmetic and copies ran while one was open for 0% -> 0% of each run, Pallas kernels for 11% -> 15%
where the time goes in v4:
time: 48.2 us; the launch traced here: 47.9 us
  starting transfers between devices  25.5 us (53%)
  Pallas kernels  12.6 us (26%)
  waiting for transfers between devices  9.58 us (20%)
    ppermute x20, starting transfers between devices, swap(): return lax.ppermute(value, axes, [(i, i ^ step) for i in range(size)])  25.5 us
    ppermute x20, waiting for transfers between devices, swap(): return lax.ppermute(value, axes, [(i, i ^ step) for i in range(size)])  9.58 us
    pallas_call x1, Pallas kernels, per_device(): pl.pallas_call(functools.partial(gather_kernel, pools), out_shape=[shape(...  3 us
    pallas_call x1, Pallas kernels, per_device(): pl.pallas_call(functools.partial(table_kernel, pools, shard_blocks), out_...  2.97 us
    pallas_call x2, Pallas kernels, score(): pl.pallas_call(functools.partial(score_kernel, first, count, heads, pools...  2.05 us
    pallas_call x2, Pallas kernels, compact(): pl.pallas_call(functools.partial(compact_kernel, pools, shard_blocks), ou...  1.94 us
    pallas_call x1, Pallas kernels, per_device(): pl.pallas_call(functools.partial(project_kernel, pools, heads, reps), out...  1.21 us
  transfers between devices with their start and end apart: 20, of which 8 were waited for; matrix products, arithmetic and copies ran while one was open for 0% of the time, Pallas kernels for 15%

profile of v4, /device:TPU:0, one launch (start us, length us, event | category | flops | bytes accessed | tf_op | source)
XLA Modules:
  0.0 47.9 jit_solution(5766579422151474293)
XLA Ops:
  0.0 3.0 %gather.1 = (bf16[512,256]{1,0:T(8,128)(2,1)S(1)}, bf16[512,256]{1,0:T(8,128)(2,1)S(1)}, bf16[288,128]{1,0:T(8,128)(2,1)S(1)}, bf16[288,128]{1,0:T(8,128)(2,1)S(...) custom-call(s32[1,4,4]{2,1,0:T(4,128)} %sel_ref.7, ...), custom_call_target="tpu_custom_call" | custom-call | tf_op jit(solution)/shard_map/gather/pallas_call | solution.py:322
  3.0 3.0 %collective-permute-start = (bf16[512,256]{1,0:T(8,128)(2,1)S(1)}, bf16[512,256]{1,0:T(8,128)(2,1)S(1)}, u32[]{:S(2)}, u32[]{:S(2)}) collective-permute-start(bf16[512,256]{1,0:T(8,128)(2,1)S(1)} %get-tuple-element.45.rest_0_), channel_id=1, source_target_pairs={{0,2},{2,0},{1,3},{3,1},{4,6},{6,4},{5,7},{7,5},{8,10},{10,8},{9,1... | collective-permute-start | bytes 786440 | tf_op jit(solution)/shard_map/ppermute | solution.py:35
  6.1 4.1 %collective-permute-start.1 = (bf16[288,128]{1,0:T(8,128)(2,1)S(1)}, bf16[288,128]{1,0:T(8,128)(2,1)S(1)}, u32[]{:S(2)}, u32[]{:S(2)}) collective-permute-start(bf16[288,128]{1,0:T(8,128)(2,1)S(1)} %get-tuple-element.46), channel_id=1, source_target_pairs={{0,12},{4,8},{8,4},{12,0},{1,13},{5,9},{9,5},{13,1},{2,14},{6,10},... | collective-permute-start | bytes 221192 | tf_op jit(solution)/shard_map/ppermute | solution.py:35
  10.2 0.6 %collective-permute-start.5 = (bf16[288,128]{1,0:T(8,128)(2,1)S(1)}, bf16[288,128]{1,0:T(8,128)(2,1)S(1)}, u32[]{:S(2)}, u32[]{:S(2)}) collective-permute-start(bf16[288,128]{1,0:T(8,128)(2,1)S(1)} %get-tuple-element.50), channel_id=1, source_target_pairs={{0,4},{4,0},{8,12},{12,8},{1,5},{5,1},{9,13},{13,9},{2,6},{6,2},{1... | collective-permute-start | bytes 221192 | tf_op jit(solution)/shard_map/ppermute | solution.py:35
  10.7 3.0 %tables.1 = (f32[1024,128]{1,0:T(8,128)S(1)}, f32[1024,128]{1,0:T(8,128)S(1)}, f32[8,128]{1,0:T(8,128)S(1)}, s32[4,256]{1,0:T(4,128)S(1)}, s32[1,1024]{1,0:T(1,1...) custom-call(s32[1,4,4]{2,1,0:T(4,128)} %sel_ref.7, ...), custom_call_target="tpu_custom_call", output_to_operand_aliasing={{7}: (5, {}), {8}: (6, {}), {9}: (7, {}), {10}: (8, {})} | custom-call | tf_op jit(solution)/shard_map/tables/pallas_call | solution.py:341
  13.7 1.5 %collective-permute-start.10 = (bf16[256,128]{1,0:T(8,128)(2,1)S(1)}, bf16[256,128]{1,0:T(8,128)(2,1)S(1)}, u32[]{:S(2)}, u32[]{:S(2)}) collective-permute-start(bf16[256,128]{1,0:T(8,128)(2,1)S(1)} %get-tuple-element.57), channel_id=1, source_target_pairs={{0,4},{4,0},{8,12},{12,8},{1,5},{5,1},{9,13},{13,9},{2,6},{6,2},{1... | collective-permute-start | bytes 196616 | tf_op jit(solution)/shard_map/ppermute | solution.py:35
  15.3 0.7 %collective-permute-done.2.rest_3_.rest_1_ = bf16[288,128]{1,0:T(8,128)(2,1)S(1)} collective-permute-done((bf16[288,128]{1,0:T(8,128)(2,1)S(1)}, bf16[288,128]{1,0:T(8,128)(2,1)S(1)}, u32[]{:S(2)}, u32[]{:S(2)}) %collective-permute-start.2) | collective-permute-done | bytes 73760 | tf_op jit(solution)/shard_map/ppermute | solution.py:35
  15.9 2.5 %collective-permute-start.8 = (bf16[256,128]{1,0:T(8,128)(2,1)S(1)}, bf16[256,128]{1,0:T(8,128)(2,1)S(1)}, u32[]{:S(2)}, u32[]{:S(2)}) collective-permute-start(bf16[256,128]{1,0:T(8,128)(2,1)S(1)} %get-tuple-element.55), channel_id=1, source_target_pairs={{0,12},{4,8},{8,4},{12,0},{1,13},{5,9},{9,5},{13,1},{2,14},{6,10},... | collective-permute-start | bytes 196616 | tf_op jit(solution)/shard_map/ppermute | solution.py:35
  18.5 1.0 %score.2 = (f32[32,256]{1,0:T(8,128)S(1)}, f32[32,256]{1,0:T(8,128)S(1)}) custom-call(bf16[512,512]{1,0:T(8,128)(2,1)S(1)} %get-tuple-element.40.map_ref, f32[1024,128]{1,0:T(8,128)S(1)} %get-tuple-element.41.cos_ref, f32[1024,128]{1,0:T(8,128)S(1)} %get-tuple-element.42.sin_ref, f32[8,128]{1,0:T(8,128)S(1)} %get-tuple-element.43.turn_ref, ...), custom_call_target="tpu_custom_call" | custom-call | bytes 3145728 | tf_op jit(solution)/shard_map/score/pallas_call | solution.py:362
  19.5 2.7 %collective-permute-start.3 = (f32[32,256]{1,0:T(8,128)S(1)}, f32[32,256]{1,0:T(8,128)S(1)}, u32[]{:S(2)}, u32[]{:S(2)}) collective-permute-start(f32[32,256]{1,0:T(8,128)S(1)} %get-tuple-element.48), channel_id=1, source_target_pairs={{0,12},{4,8},{8,4},{12,0},{1,13},{5,9},{9,5},{13,1},{2,14},{6,10},... | collective-permute-start | bytes 98312 | tf_op jit(solution)/shard_map/ppermute | solution.py:35
  22.2 0.7 %collective-permute-start.4 = (f32[32,256]{1,0:T(8,128)S(1)}, f32[32,256]{1,0:T(8,128)S(1)}, u32[]{:S(2)}, u32[]{:S(2)}) collective-permute-start(f32[32,256]{1,0:T(8,128)S(1)} %get-tuple-element.49.rest_4_), channel_id=1, source_target_pairs={{0,8},{4,12},{8,0},{12,4},{1,9},{5,13},{9,1},{13,5},{2,10},{6,14},... | collective-permute-start | bytes 98312 | tf_op jit(solution)/shard_map/ppermute | solution.py:35
  22.9 1.0 %compact.2.after_ref.rest_4_ = bf16[512,128]{1,0:T(8,128)(2,1)S(1)} custom-call(s32[1,4,4]{2,1,0:T(4,128)} %sel_ref.7, bf16[288,128]{1,0:T(8,128)(2,1)S(1)} %collective-permute-done.1.rest_2_.rest_0_, bf16[288,128]{1,0:T(8,128)(2,1)S(1)} %collective-permute-done.2.rest_3_.rest_1_, bf16[288,128]{1,0:T(8,128)(2,1)S(1)} %collective-permute-done.5.rest_2_, ...), custom_call_target="tpu_custom_call" | custom-call | bytes 3145728 | tf_op jit(solution)/shard_map/compact/pallas_call | solution.py:373
  23.8 1.0 %score.3 = (f32[32,256]{1,0:T(8,128)S(1)}, f32[32,256]{1,0:T(8,128)S(1)}) custom-call(bf16[512,512]{1,0:T(8,128)(2,1)S(1)} %get-tuple-element.40.map_ref, f32[1024,128]{1,0:T(8,128)S(1)} %get-tuple-element.41.cos_ref, f32[1024,128]{1,0:T(8,128)S(1)} %get-tuple-element.42.sin_ref, f32[8,128]{1,0:T(8,128)S(1)} %get-tuple-element.43.turn_ref, ...), custom_call_target="tpu_custom_call" | custom-call | bytes 3145728 | tf_op jit(solution)/shard_map/score/pallas_call | solution.py:362
  24.9 1.5 %collective-permute-start.11 = (bf16[512,128]{1,0:T(8,128)(2,1)S(1)}, bf16[512,128]{1,0:T(8,128)(2,1)S(1)}, u32[]{:S(2)}, u32[]{:S(2)}) collective-permute-start(bf16[512,128]{1,0:T(8,128)(2,1)S(1)} %compact.2.after_ref.rest_4_), channel_id=1, source_target_pairs={{0,2},{2,0},{1,3},{3,1},{4,6},{6,4},{5,7},{7,5},{8,10},{10,8},{9,1... | collective-permute-start | bytes 393224 | tf_op jit(solution)/shard_map/ppermute | solution.py:35
  26.4 0.6 %collective-permute-done.4.rest_5_.rest_1_ = f32[32,256]{1,0:T(8,128)S(1)} collective-permute-done((f32[32,256]{1,0:T(8,128)S(1)}, f32[32,256]{1,0:T(8,128)S(1)}, u32[]{:S(2)}, u32[]{:S(2)}) %collective-permute-start.4) | collective-permute-done | bytes 32800 | tf_op jit(solution)/shard_map/ppermute | solution.py:35
  27.0 1.0 %compact.3.rest_5_ = bf16[512,128]{1,0:T(8,128)(2,1)S(1)} custom-call(s32[1,4,4]{2,1,0:T(4,128)} %sel_ref.7, bf16[256,128]{1,0:T(8,128)(2,1)S(1)} %collective-permute-done.8.rest_0_, bf16[256,128]{1,0:T(8,128)(2,1)S(1)} %collective-permute-done.9.rest_1_, bf16[256,128]{1,0:T(8,128)(2,1)S(1)} %collective-permute-done.10.rest_2_, ...), custom_call_target="tpu_custom_call" | custom-call | bytes 3145728 | tf_op jit(solution)/shard_map/compact/pallas_call | solution.py:373
  28.0 1.6 %collective-permute-start.12 = (bf16[512,128]{1,0:T(8,128)(2,1)S(1)}, bf16[512,128]{1,0:T(8,128)(2,1)S(1)}, u32[]{:S(2)}, u32[]{:S(2)}) collective-permute-start(bf16[512,128]{1,0:T(8,128)(2,1)S(1)} %compact.3.rest_5_), channel_id=1, source_target_pairs={{0,2},{2,0},{1,3},{3,1},{4,6},{6,4},{5,7},{7,5},{8,10},{10,8},{9,1... | collective-permute-start | bytes 393224 | tf_op jit(solution)/shard_map/ppermute | solution.py:35
  29.5 0.9 %collective-permute-start.7 = (f32[32,256]{1,0:T(8,128)S(1)}, f32[32,256]{1,0:T(8,128)S(1)}, u32[]{:S(2)}, u32[]{:S(2)}) collective-permute-start(f32[32,256]{1,0:T(8,128)S(1)} %get-tuple-element.53), channel_id=1, source_target_pairs={{0,4},{4,0},{8,12},{12,8},{1,5},{5,1},{9,13},{13,9},{2,6},{6,2},{1... | collective-permute-start | bytes 98312 | tf_op jit(solution)/shard_map/ppermute | solution.py:35
  30.4 3.0 %collective-permute-done.7.rest_2_ = f32[32,256]{1,0:T(8,128)S(1)} collective-permute-done((f32[32,256]{1,0:T(8,128)S(1)}, f32[32,256]{1,0:T(8,128)S(1)}, u32[]{:S(2)}, u32[]{:S(2)}) %collective-permute-start.7) | collective-permute-done | bytes 32800 | tf_op jit(solution)/shard_map/ppermute | solution.py:35
  33.5 0.8 %attend.1.refs_0_ = bf16[1,4096]{1,0:T(2,128)(2,1)S(1)} custom-call(bf16[512,512]{1,0:T(8,128)(2,1)S(1)} %get-tuple-element.38.map_ref, s32[1,1024]{1,0:T(1,128)S(1)} %get-tuple-element.39.after_ref.place_ref, f32[32,256]{1,0:T(8,128)S(1)} %collective-permute-done.3.rest_6_.rest_0_, f32[32,256]{1,0:T(8,128)S(1)} %collective-permute-done.4.rest_5_.rest_1_, ...), custom_call_target="tpu_custom_call" | custom-call | tf_op jit(solution)/shard_map/attend/pallas_call | solution.py:394
  34.4 1.2 %collective-permute-done.13.refs_1_ = bf16[1,4096]{1,0:T(2,128)(2,1)S(1)} collective-permute-done((bf16[1,4096]{1,0:T(2,128)(2,1)S(1)}, bf16[1,4096]{1,0:T(2,128)(2,1)S(1)}, u32[]{:S(2)}, u32[]{:S(2)}) %collective-permute-start.13) | collective-permute-done | bytes 8224 | tf_op jit(solution)/shard_map/ppermute | solution.py:35
  35.6 2.0 %collective-permute-start.14 = (bf16[2,4096]{1,0:T(2,128)(2,1)S(1)}, bf16[2,4096]{1,0:T(2,128)(2,1)S(1)}, u32[]{:S(2)}, u32[]{:S(2)}) collective-permute-start(bf16[2,4096]{1,0:T(2,128)(2,1)S(1)} %join.1.rest_3_), channel_id=1, source_target_pairs={{0,12},{4,8},{8,4},{12,0},{1,13},{5,9},{9,5},{13,1},{2,14},{6,10},... | collective-permute-start | bytes 49160 | tf_op jit(solution)/shard_map/ppermute | solution.py:35
  37.6 0.4 collective-permute-start.15
  38.0 2.0 %collective-permute-start.16 = (bf16[2,4096]{1,0:T(2,128)(2,1)S(1)}, bf16[2,4096]{1,0:T(2,128)(2,1)S(1)}, u32[]{:S(2)}, u32[]{:S(2)}) collective-permute-start(bf16[2,4096]{1,0:T(2,128)(2,1)S(1)} %join.1.rest_3_), channel_id=1, source_target_pairs={{0,4},{4,0},{8,12},{12,8},{1,5},{5,1},{9,13},{13,9},{2,6},{6,2},{1... | collective-permute-start | bytes 49160 | tf_op jit(solution)/shard_map/ppermute | solution.py:35
  40.0 1.2 %collective-permute-done.14.rest_0_ = bf16[2,4096]{1,0:T(2,128)(2,1)S(1)} collective-permute-done((bf16[2,4096]{1,0:T(2,128)(2,1)S(1)}, bf16[2,4096]{1,0:T(2,128)(2,1)S(1)}, u32[]{:S(2)}, u32[]{:S(2)}) %collective-permute-start.14) | collective-permute-done | bytes 16416 | tf_op jit(solution)/shard_map/ppermute | solution.py:35
  41.3 1.0 %collective-permute-done.15.rest_1_ = bf16[2,4096]{1,0:T(2,128)(2,1)S(1)} collective-permute-done((bf16[2,4096]{1,0:T(2,128)(2,1)S(1)}, bf16[2,4096]{1,0:T(2,128)(2,1)S(1)}, u32[]{:S(2)}, u32[]{:S(2)}) %collective-permute-start.15) | collective-permute-done | bytes 16416 | tf_op jit(solution)/shard_map/ppermute | solution.py:35
  42.2 1.2 %project.1 = (f32[2,1024]{1,0:T(2,128)S(1)}, f32[2,1024]{1,0:T(2,128)S(1)}, f32[2,1024]{1,0:T(2,128)S(1)}, f32[2,1024]{1,0:T(2,128)S(1)}) custom-call(bf16[4096,1024]{1,0:T(8,128)(2,1)S(1)} %copy-done, bf16[2,4096]{1,0:T(2,128)(2,1)S(1)} %collective-permute-done.14.rest_0_, bf16[2,4096]{1,0:T(2,128)(2,1)S(1)} %collective-permute-done.15.rest_1_, ...), custom_call_target="tpu_custom_call" | custom-call | tf_op jit(solution)/shard_map/project/pallas_call | solution.py:407
  43.5 1.4 %collective-permute-start.18 = (f32[2,1024]{1,0:T(2,128)S(1)}, f32[2,1024]{1,0:T(2,128)S(1)}, u32[]{:S(2)}, u32[]{:S(2)}) collective-permute-start(f32[2,1024]{1,0:T(2,128)S(1)} %get-tuple-element.60), channel_id=1, source_target_pairs={{0,2},{1,3},{2,0},{3,1},{4,6},{5,7},{6,4},{7,5},{8,10},{9,11},{10,... | collective-permute-start | bytes 24584 | tf_op jit(solution)/shard_map/ppermute | solution.py:35
  44.9 0.5 %collective-permute-start.19 = (f32[2,1024]{1,0:T(2,128)S(1)}, f32[2,1024]{1,0:T(2,128)S(1)}, u32[]{:S(2)}, u32[]{:S(2)}) collective-permute-start(f32[2,1024]{1,0:T(2,128)S(1)} %get-tuple-element.61), channel_id=1, source_target_pairs={{0,1},{1,0},{2,3},{3,2},{4,5},{5,4},{6,7},{7,6},{8,9},{9,8},{10,11... | collective-permute-start | bytes 24584 | tf_op jit(solution)/shard_map/ppermute | solution.py:35
  45.4 1.2 %collective-permute-done.17.refs_0_ = f32[2,1024]{1,0:T(2,128)S(1)} collective-permute-done((f32[2,1024]{1,0:T(2,128)S(1)}, f32[2,1024]{1,0:T(2,128)S(1)}, u32[]{:S(2)}, u32[]{:S(2)}) %collective-permute-start.17) | collective-permute-done | bytes 8224 | tf_op jit(solution)/shard_map/ppermute | solution.py:35
  46.6 0.7 %collective-permute-done.18.refs_1_ = f32[2,1024]{1,0:T(2,128)S(1)} collective-permute-done((f32[2,1024]{1,0:T(2,128)S(1)}, f32[2,1024]{1,0:T(2,128)S(1)}, u32[]{:S(2)}, u32[]{:S(2)}) %collective-permute-start.18) | collective-permute-done | bytes 8224 | tf_op jit(solution)/shard_map/ppermute | solution.py:35
  47.3 0.6 %finish.1 = bf16[1,2,2048]{2,1,0:T(2,128)(2,1)} custom-call(f32[2,1024]{1,0:T(2,128)S(1)} %collective-permute-done.17.refs_0_, f32[2,1024]{1,0:T(2,128)S(1)} %collective-permute-done.18.refs_1_, f32[2,1024]{1,0:T(2,128)S(1)} %collective-permute-done.19.refs_2_, f32[2,1024]{1,0:T(2,128)S(1)} %get-tuple-element.62.refs_3_), custom_call_target="tpu_custom_call" | custom-call | tf_op jit(solution)/shard_map/finish/pallas_call | solution.py:416
  (20 shorter events, 0.3 us)
Async XLA Ops:
  0.0 42.2 %copy-start = (bf16[4096,1024]{1,0:T(8,128)(2,1)S(1)}, bf16[4096,1024]{1,0:T(8,128)(2,1)}, u32[]{:S(2)}) copy-start(bf16[4096,1024]{1,0:T(8,128)(2,1)} %weight_ref.1) | copy-start | bytes 25165828
  3.0 15.5 %collective-permute-start = (bf16[512,256]{1,0:T(8,128)(2,1)S(1)}, bf16[512,256]{1,0:T(8,128)(2,1)S(1)}, u32[]{:S(2)}, u32[]{:S(2)}) collective-permute-start(bf16[512,256]{1,0:T(8,128)(2,1)S(1)} %get-tuple-element.45.rest_0_), channel_id=1, source_target_pairs={{0,2},{2,0},{1,3},{3,1},{4,6},{6,4},{5,7},{7,5},{8,10},{10,8},{9,1... | collective-permute-start | bytes 786440 | tf_op jit(solution)/shard_map/ppermute | solution.py:35
  6.0 16.2 %collective-permute-start.6 = (bf16[512,256]{1,0:T(8,128)(2,1)S(1)}, bf16[512,256]{1,0:T(8,128)(2,1)S(1)}, u32[]{:S(2)}, u32[]{:S(2)}) collective-permute-start(bf16[512,256]{1,0:T(8,128)(2,1)S(1)} %get-tuple-element.52.rest_0_), channel_id=1, source_target_pairs={{0,2},{2,0},{1,3},{3,1},{4,6},{6,4},{5,7},{7,5},{8,10},{10,8},{9,1... | collective-permute-start | bytes 786440 | tf_op jit(solution)/shard_map/ppermute | solution.py:35
  6.1 7.6 %collective-permute-start.1 = (bf16[288,128]{1,0:T(8,128)(2,1)S(1)}, bf16[288,128]{1,0:T(8,128)(2,1)S(1)}, u32[]{:S(2)}, u32[]{:S(2)}) collective-permute-start(bf16[288,128]{1,0:T(8,128)(2,1)S(1)} %get-tuple-element.46), channel_id=1, source_target_pairs={{0,12},{4,8},{8,4},{12,0},{1,13},{5,9},{9,5},{13,1},{2,14},{6,10},... | collective-permute-start | bytes 221192 | tf_op jit(solution)/shard_map/ppermute | solution.py:35
  10.2 5.8 %collective-permute-start.2 = (bf16[288,128]{1,0:T(8,128)(2,1)S(1)}, bf16[288,128]{1,0:T(8,128)(2,1)S(1)}, u32[]{:S(2)}, u32[]{:S(2)}) collective-permute-start(bf16[288,128]{1,0:T(8,128)(2,1)S(1)} %get-tuple-element.47), channel_id=1, source_target_pairs={{0,8},{4,12},{8,0},{12,4},{1,9},{5,13},{9,1},{13,5},{2,10},{6,14},... | collective-permute-start | bytes 221192 | tf_op jit(solution)/shard_map/ppermute | solution.py:35
  10.2 9.3 %collective-permute-start.5 = (bf16[288,128]{1,0:T(8,128)(2,1)S(1)}, bf16[288,128]{1,0:T(8,128)(2,1)S(1)}, u32[]{:S(2)}, u32[]{:S(2)}) collective-permute-start(bf16[288,128]{1,0:T(8,128)(2,1)S(1)} %get-tuple-element.50), channel_id=1, source_target_pairs={{0,4},{4,0},{8,12},{12,8},{1,5},{5,1},{9,13},{13,9},{2,6},{6,2},{1... | collective-permute-start | bytes 221192 | tf_op jit(solution)/shard_map/ppermute | solution.py:35
  13.7 11.2 %collective-permute-start.10 = (bf16[256,128]{1,0:T(8,128)(2,1)S(1)}, bf16[256,128]{1,0:T(8,128)(2,1)S(1)}, u32[]{:S(2)}, u32[]{:S(2)}) collective-permute-start(bf16[256,128]{1,0:T(8,128)(2,1)S(1)} %get-tuple-element.57), channel_id=1, source_target_pairs={{0,4},{4,0},{8,12},{12,8},{1,5},{5,1},{9,13},{13,9},{2,6},{6,2},{1... | collective-permute-start | bytes 196616 | tf_op jit(solution)/shard_map/ppermute | solution.py:35
  15.9 10.5 %collective-permute-start.8 = (bf16[256,128]{1,0:T(8,128)(2,1)S(1)}, bf16[256,128]{1,0:T(8,128)(2,1)S(1)}, u32[]{:S(2)}, u32[]{:S(2)}) collective-permute-start(bf16[256,128]{1,0:T(8,128)(2,1)S(1)} %get-tuple-element.55), channel_id=1, source_target_pairs={{0,12},{4,8},{8,4},{12,0},{1,13},{5,9},{9,5},{13,1},{2,14},{6,10},... | collective-permute-start | bytes 196616 | tf_op jit(solution)/shard_map/ppermute | solution.py:35
  18.5 7.9 %collective-permute-start.9 = (bf16[256,128]{1,0:T(8,128)(2,1)S(1)}, bf16[256,128]{1,0:T(8,128)(2,1)S(1)}, u32[]{:S(2)}, u32[]{:S(2)}) collective-permute-start(bf16[256,128]{1,0:T(8,128)(2,1)S(1)} %get-tuple-element.56), channel_id=1, source_target_pairs={{0,8},{4,12},{8,0},{12,4},{1,9},{5,13},{9,1},{13,5},{2,10},{6,14},... | collective-permute-start | bytes 196616 | tf_op jit(solution)/shard_map/ppermute | solution.py:35
  19.5 6.9 %collective-permute-start.3 = (f32[32,256]{1,0:T(8,128)S(1)}, f32[32,256]{1,0:T(8,128)S(1)}, u32[]{:S(2)}, u32[]{:S(2)}) collective-permute-start(f32[32,256]{1,0:T(8,128)S(1)} %get-tuple-element.48), channel_id=1, source_target_pairs={{0,12},{4,8},{8,4},{12,0},{1,13},{5,9},{9,5},{13,1},{2,14},{6,10},... | collective-permute-start | bytes 98312 | tf_op jit(solution)/shard_map/ppermute | solution.py:35
  22.2 4.8 %collective-permute-start.4 = (f32[32,256]{1,0:T(8,128)S(1)}, f32[32,256]{1,0:T(8,128)S(1)}, u32[]{:S(2)}, u32[]{:S(2)}) collective-permute-start(f32[32,256]{1,0:T(8,128)S(1)} %get-tuple-element.49.rest_4_), channel_id=1, source_target_pairs={{0,8},{4,12},{8,0},{12,4},{1,9},{5,13},{9,1},{13,5},{2,10},{6,14},... | collective-permute-start | bytes 98312 | tf_op jit(solution)/shard_map/ppermute | solution.py:35
  24.9 8.6 %collective-permute-start.11 = (bf16[512,128]{1,0:T(8,128)(2,1)S(1)}, bf16[512,128]{1,0:T(8,128)(2,1)S(1)}, u32[]{:S(2)}, u32[]{:S(2)}) collective-permute-start(bf16[512,128]{1,0:T(8,128)(2,1)S(1)} %compact.2.after_ref.rest_4_), channel_id=1, source_target_pairs={{0,2},{2,0},{1,3},{3,1},{4,6},{6,4},{5,7},{7,5},{8,10},{10,8},{9,1... | collective-permute-start | bytes 393224 | tf_op jit(solution)/shard_map/ppermute | solution.py:35
  28.0 5.5 %collective-permute-start.12 = (bf16[512,128]{1,0:T(8,128)(2,1)S(1)}, bf16[512,128]{1,0:T(8,128)(2,1)S(1)}, u32[]{:S(2)}, u32[]{:S(2)}) collective-permute-start(bf16[512,128]{1,0:T(8,128)(2,1)S(1)} %compact.3.rest_5_), channel_id=1, source_target_pairs={{0,2},{2,0},{1,3},{3,1},{4,6},{6,4},{5,7},{7,5},{8,10},{10,8},{9,1... | collective-permute-start | bytes 393224 | tf_op jit(solution)/shard_map/ppermute | solution.py:35
  29.5 3.9 %collective-permute-start.7 = (f32[32,256]{1,0:T(8,128)S(1)}, f32[32,256]{1,0:T(8,128)S(1)}, u32[]{:S(2)}, u32[]{:S(2)}) collective-permute-start(f32[32,256]{1,0:T(8,128)S(1)} %get-tuple-element.53), channel_id=1, source_target_pairs={{0,4},{4,0},{8,12},{12,8},{1,5},{5,1},{9,13},{13,9},{2,6},{6,2},{1... | collective-permute-start | bytes 98312 | tf_op jit(solution)/shard_map/ppermute | solution.py:35
  34.3 1.2 %collective-permute-start.13 = (bf16[1,4096]{1,0:T(2,128)(2,1)S(1)}, bf16[1,4096]{1,0:T(2,128)(2,1)S(1)}, u32[]{:S(2)}, u32[]{:S(2)}) collective-permute-start(bf16[1,4096]{1,0:T(2,128)(2,1)S(1)} %attend.1.refs_0_), channel_id=1, source_target_pairs={{0,1},{1,0},{2,3},{3,2},{4,5},{5,4},{6,7},{7,6},{8,9},{9,8},{10,11... | collective-permute-start | bytes 24584 | tf_op jit(solution)/shard_map/ppermute | solution.py:35
  35.6 5.7 %collective-permute-start.14 = (bf16[2,4096]{1,0:T(2,128)(2,1)S(1)}, bf16[2,4096]{1,0:T(2,128)(2,1)S(1)}, u32[]{:S(2)}, u32[]{:S(2)}) collective-permute-start(bf16[2,4096]{1,0:T(2,128)(2,1)S(1)} %join.1.rest_3_), channel_id=1, source_target_pairs={{0,12},{4,8},{8,4},{12,0},{1,13},{5,9},{9,5},{13,1},{2,14},{6,10},... | collective-permute-start | bytes 49160 | tf_op jit(solution)/shard_map/ppermute | solution.py:35
  37.6 4.6 %collective-permute-start.15 = (bf16[2,4096]{1,0:T(2,128)(2,1)S(1)}, bf16[2,4096]{1,0:T(2,128)(2,1)S(1)}, u32[]{:S(2)}, u32[]{:S(2)}) collective-permute-start(bf16[2,4096]{1,0:T(2,128)(2,1)S(1)} %join.1.rest_3_), channel_id=1, source_target_pairs={{0,8},{4,12},{8,0},{12,4},{1,9},{5,13},{9,1},{13,5},{2,10},{6,14},... | collective-permute-start | bytes 49160 | tf_op jit(solution)/shard_map/ppermute | solution.py:35
  38.0 4.2 %collective-permute-start.16 = (bf16[2,4096]{1,0:T(2,128)(2,1)S(1)}, bf16[2,4096]{1,0:T(2,128)(2,1)S(1)}, u32[]{:S(2)}, u32[]{:S(2)}) collective-permute-start(bf16[2,4096]{1,0:T(2,128)(2,1)S(1)} %join.1.rest_3_), channel_id=1, source_target_pairs={{0,4},{4,0},{8,12},{12,8},{1,5},{5,1},{9,13},{13,9},{2,6},{6,2},{1... | collective-permute-start | bytes 49160 | tf_op jit(solution)/shard_map/ppermute | solution.py:35
  43.5 3.1 %collective-permute-start.17 = (f32[2,1024]{1,0:T(2,128)S(1)}, f32[2,1024]{1,0:T(2,128)S(1)}, u32[]{:S(2)}, u32[]{:S(2)}) collective-permute-start(f32[2,1024]{1,0:T(2,128)S(1)} %get-tuple-element.59), channel_id=1, source_target_pairs={{0,3},{1,2},{2,1},{3,0},{4,7},{5,6},{6,5},{7,4},{8,11},{9,10},{10,... | collective-permute-start | bytes 24584 | tf_op jit(solution)/shard_map/ppermute | solution.py:35
  43.5 3.7 %collective-permute-start.18 = (f32[2,1024]{1,0:T(2,128)S(1)}, f32[2,1024]{1,0:T(2,128)S(1)}, u32[]{:S(2)}, u32[]{:S(2)}) collective-permute-start(f32[2,1024]{1,0:T(2,128)S(1)} %get-tuple-element.60), channel_id=1, source_target_pairs={{0,2},{1,3},{2,0},{3,1},{4,6},{5,7},{6,4},{7,5},{8,10},{9,11},{10,... | collective-permute-start | bytes 24584 | tf_op jit(solution)/shard_map/ppermute | solution.py:35
  44.9 2.4 %collective-permute-start.19 = (f32[2,1024]{1,0:T(2,128)S(1)}, f32[2,1024]{1,0:T(2,128)S(1)}, u32[]{:S(2)}, u32[]{:S(2)}) collective-permute-start(f32[2,1024]{1,0:T(2,128)S(1)} %get-tuple-element.61), channel_id=1, source_target_pairs={{0,1},{1,0},{2,3},{3,2},{4,5},{5,4},{6,7},{7,6},{8,9},{9,8},{10,11... | collective-permute-start | bytes 24584 | tf_op jit(solution)/shard_map/ppermute | solution.py:35

commit v5 on v4

--- a/solution.py
+++ b/solution.py
@@ -61,13 +61,18 @@
 def heads_to_rows(line, lanes):
     count = line.shape[1] // HEAD_SIZE
     rows = jnp.concatenate([line[:, n * HEAD_SIZE : (n + 1) * HEAD_SIZE] for n in range(count)], axis=0)
-    return jnp.concatenate([rows[:, i : i + lanes] for i in range(0, HEAD_SIZE, lanes)], axis=0)
+    if lanes < HEAD_SIZE:
+        return jnp.concatenate([rows[:, i : i + lanes] for i in range(0, HEAD_SIZE, lanes)], axis=0)
+    each = count * HEAD_SIZE // lanes
+    return jnp.concatenate([rows[i : i + each, :] for i in range(0, count, each)], axis=1)
 
 
 def rows_to_heads(rows):
-    pieces = HEAD_SIZE // rows.shape[1]
-    count = rows.shape[0] // pieces
-    return jnp.concatenate([rows[i * count : (i + 1) * count, :] for i in range(pieces)], axis=1)
+    count, lanes = rows.shape
+    if lanes < HEAD_SIZE:
+        each = count * lanes // HEAD_SIZE
+        return jnp.concatenate([rows[i : i + each, :] for i in range(0, count, each)], axis=1)
+    return jnp.concatenate([rows[:, i : i + HEAD_SIZE] for i in range(0, lanes, HEAD_SIZE)], axis=0)
 
 
 def gather_kernel(pools, sel_ref, lat_ref, query_ref, near_ref, far_ref, *rest):
@@ -107,13 +112,12 @@
                 preferred_element_type=jnp.float32,
             ).astype(jnp.bfloat16)
             keys_ref[at * rows : (at + 1) * rows, j * half : (j + 1) * half] = packed[:, :half]
-            value_refs[j * pools + k][:rows, :] = packed[:, half:]
+            value_refs[k][:rows, j * half : (j + 1) * half] = packed[:, half:]
         value_refs[k][rows:, :] = queries
 
 
-def table_kernel(pools, shard_blocks, sel_ref, len_ref, freq_ref, key_map_ref, value_map_ref, *rest):
-    held = (len(rest) - 8) // 2
-    cos_ref, sin_ref, turn_ref, live_ref, place_ref, key_out_ref, value_out_ref = rest[held : held + 7]
+def table_kernel(pools, shard_blocks, sel_ref, len_ref, freq_ref, key_map_ref, value_map_ref, held_ref, *rest):
+    cos_ref, sin_ref, turn_ref, live_ref, place_ref, key_out_ref, value_out_ref = rest[:7]
     sems = rest[-1]
     loads = [
         pltpu.make_async_copy(key_map_ref, key_out_ref, sems.at[0]),
@@ -191,27 +195,26 @@
             out_refs[i][mine, :] = jnp.where(live, scores, MASKED)
 
 
-def compact_kernel(pools, shard_blocks, sel_ref, *rest):
+def compact_kernel(pools, place_ref, after_ref, *rest):
+    del after_ref
     value_refs = rest[:pools][::-1]
-    out_ref, sem = rest[-2:]
-    me = lax.axis_index("pool")
-    place = jnp.int32(0)
-    for k in range(pools):
-        for c, block in enumerate(slot_blocks(sel_ref, me, me ^ k, shard_blocks)):
-            @pl.when(block >= 0)
-            def _(k=k, c=c, place=place):
-                pltpu.make_async_copy(
-                    value_refs[k].at[pl.ds(c * BLOCK, BLOCK), :],
-                    out_ref.at[pl.ds(pl.multiple_of(place * BLOCK, BLOCK), BLOCK), :],
-                    sem,
-                ).start()
-            place = place + (block >= 0).astype(jnp.int32)
-    pltpu.make_async_copy(out_ref, out_ref, sem).wait()
-
-
-def attend_kernel(pools, heads, chunks, map_ref, place_ref, *rest):
+    out_ref = rest[pools]
+    width = out_ref.shape[1]
+    spare = pools * CAP - out_ref.shape[0] // BLOCK
+    for i in range(out_ref.shape[0] // BLOCK):
+        chosen = jnp.zeros((BLOCK, width), jnp.float32)
+        for slot in range(i, i + spare + 1):
+            place = place_ref[:, slot * BLOCK : slot * BLOCK + LANE]
+            place = jnp.concatenate([place] * (width // LANE), axis=1)
+            k, c = slot // CAP, slot % CAP
+            block = value_refs[k][c * BLOCK : (c + 1) * BLOCK, :].astype(jnp.float32)
+            chosen = jnp.where(place == i, block, chosen)
+        out_ref[i * BLOCK : (i + 1) * BLOCK, :] = chosen.astype(jnp.bfloat16)
+
+
+def attend_kernel(pools, heads, map_ref, place_ref, *rest):
     score_refs = rest[:pools][::-1]
-    value_refs = rest[pools : pools + heads * chunks]
+    value_refs = rest[pools : pools + heads]
     out_ref = rest[-1]
     head = lax.axis_index("heads")
     width = value_refs[0].shape[1]
@@ -227,15 +230,16 @@
             at = (k * CAP + c) * BLOCK
             slots.append((place_ref[:, at : at + BLOCK], attention[:, c * BLOCK : (c + 1) * BLOCK]))
     dense = []
-    for i in range(value_refs[0].shape[0] // BLOCK):
+    kept = value_refs[0].shape[0] // BLOCK
+    for i in range(kept):
         chosen = jnp.zeros_like(slots[0][1])
-        for place, attention in slots:
+        for place, attention in slots[i : i + len(slots) - kept + 1]:
             chosen = jnp.where(place == i, attention, chosen)
         dense.append(chosen)
     attention = jnp.concatenate(dense, axis=1).astype(jnp.bfloat16)
     mixed = [None] * groups
-    for j in range(heads * chunks):
-        owner = (head ^ (j // chunks)) * chunks + j % chunks
+    for j in range(heads):
+        owner = head ^ j
         context = jnp.dot(
             attention, value_refs[j][...], preferred_element_type=jnp.float32
         ).astype(jnp.bfloat16)
@@ -317,15 +321,13 @@
         return [blocks[0]] + [taken[step] for step in range(1, size)]
 
     middle = pools // 2
-    chunks = max(1, width // (2 * LANE))
-    query_rows = queries.shape[2] // (width // chunks)
+    query_rows = queries.shape[2] // width
     packed = pl.pallas_call(
         functools.partial(gather_kernel, pools),
         out_shape=[shape((middle * rows, width), bf16)] * 2
-        + [shape((rows + query_rows, width // chunks), bf16)] * pools
-        + [shape((rows, width // chunks), bf16)] * (pools * (chunks - 1)),
+        + [shape((rows + query_rows, width), bf16)] * pools,
         in_specs=[SMEM, HBM, VMEM],
-        out_specs=[VMEM] * (pools * chunks + 2),
+        out_specs=[VMEM] * (pools + 2),
         scratch_shapes=[
             pltpu.VMEM((pools * rows, 2 * width), bf16),
             pltpu.SemaphoreType.DMA((pools * CAP,)),
@@ -337,28 +339,27 @@
     far_parts = exchange(far, "heads", heads)
     near_parts = exchange(near, "heads", heads)
 
-    later = values[pools * (chunks - 1) :]
-    cosine, sine, turn, live, place, key_maps, value_maps, *later = pl.pallas_call(
+    cosine, sine, turn, live, place, key_maps, value_maps, held = pl.pallas_call(
         functools.partial(table_kernel, pools, shard_blocks),
         out_shape=[shape((pools * rows, HEAD_SIZE), f32)] * 2
         + [shape((2 * pools, HEAD_SIZE), f32), shape((pools, rows), i32), shape((1, pools * rows), i32)]
         + [shape(key_latent_maps.shape, bf16), shape(value_latent_maps.shape, bf16)]
-        + [shape(block.shape, bf16) for block in later],
-        in_specs=[SMEM, SMEM, VMEM] + [ANY] * (2 + pools),
-        out_specs=[VMEM] * 7 + [ANY] * pools,
+        + [shape(values[1].shape, bf16)],
+        in_specs=[SMEM, SMEM, VMEM] + [ANY] * 3,
+        out_specs=[VMEM] * 7 + [ANY],
         scratch_shapes=[pltpu.SemaphoreType.DMA((2,))],
-        input_output_aliases={5 + k: 7 + k for k in range(pools)},
+        input_output_aliases={5: 7},
         compiler_params=params(16),
+        cost_estimate=pl.CostEstimate(flops=0, transcendentals=0, bytes_accessed=10 << 20),
         name="tables",
     )(
         in_hbm(selected), in_hbm(lengths), in_hbm(freq), in_hbm(key_latent_maps),
-        in_hbm(value_latent_maps), *later,
+        in_hbm(value_latent_maps), values[1],
     )
-    values = [*values[: pools * (chunks - 1)], *later]
-    value_parts = [scatter(values[c * pools : (c + 1) * pools], "pool", pools) for c in range(chunks)]
+    value_parts = scatter([values[0], held, *values[2:]], "pool", pools)
 
     def score(first, count, key_parts, after):
-        pays = value_parts[0][first : first + count]
+        pays = value_parts[first : first + count]
         return pl.pallas_call(
             functools.partial(score_kernel, first, count, heads, pools),
             out_shape=[shape((own_heads, rows), f32)] * count,
@@ -369,32 +370,24 @@
             name="score",
         )(key_maps, cosine, sine, turn, live, after, *key_parts, *pays[::-1])
 
-    def compact(parts, *after):
-        return pl.pallas_call(
-            functools.partial(compact_kernel, pools, shard_blocks),
-            out_shape=shape((sel_count * BLOCK, width // chunks), bf16),
-            in_specs=[SMEM] + [ANY] * (pools + len(after)),
-            out_specs=ANY,
-            scratch_shapes=[pltpu.SemaphoreType.DMA],
-            compiler_params=params(8),
-            cost_estimate=pl.CostEstimate(flops=0, transcendentals=0, bytes_accessed=3 << 20),
-            name="compact",
-        )(in_hbm(selected), *parts[::-1], *after)
-
     far_scores = score(middle, middle, far_parts, place)
-    dense = []
-    for c in range(chunks - 1):
-        dense.append(compact(value_parts[c], far_scores[0]))
-    near_scores = score(0, middle, near_parts, dense[0] if dense else far_scores[0])
+    dense = pl.pallas_call(
+        functools.partial(compact_kernel, pools),
+        out_shape=shape((sel_count * BLOCK, width), bf16),
+        in_specs=[VMEM, ANY] + [VMEM] * pools,
+        out_specs=VMEM,
+        compiler_params=params(16),
+        cost_estimate=pl.CostEstimate(flops=0, transcendentals=0, bytes_accessed=3 << 20),
+        name="compact",
+    )(place, far_scores[0], *value_parts[::-1])
+    near_scores = score(0, middle, near_parts, dense)
+    dense_parts = exchange(dense, "heads", heads)
     score_parts = scatter([*near_scores, *far_scores], "pool", pools)
-    dense.append(compact(value_parts[-1], near_scores[0], *score_parts[middle:]))
-    dense = [exchange(block, "heads", heads) for block in dense]
-    dense_parts = [dense[c][j] for j in range(heads) for c in range(chunks)]
 
     mine = pl.pallas_call(
-        functools.partial(attend_kernel, pools, heads, chunks),
+        functools.partial(attend_kernel, pools, heads),
         out_shape=shape((1, own_heads * HEAD_SIZE), bf16),
-        in_specs=[VMEM] * (2 + pools + heads * chunks),
+        in_specs=[VMEM] * (2 + pools + heads),
         out_specs=VMEM,
         compiler_params=params(16),
         name="attend",

time: 48.2 us -> 45.5 us (0.944)
  starting transfers between devices: 25.5 us -> 18.4 us
  waiting for transfers between devices: 9.58 us -> 16.1 us
  Pallas kernels: 12.6 us -> 10.7 us
    ppermute x20 -> x16, starting transfers between devices: 25.5 us -> 18.4 us  [swap(): return lax.ppermute(value, axes, [(i, i ^ step) for i in range(size)])]
    ppermute x20 -> x16, waiting for transfers between devices: 9.58 us -> 16.1 us  [swap(): return lax.ppermute(value, axes, [(i, i ^ step) for i in range(size)])]
    pallas_call x3 -> x2, Pallas kernels: 2.76 us -> 0.84 us  [the longest x1 0.52 us: per_device(): pl.pallas_call(functools.partial(attend_kernel, pools, heads), out_shape=...]
  transfers between devices with their start and end apart: 20 -> 16, of which waited for: 8 -> 11; matrix products, arithmetic and copies ran while one was open for 0% -> 0% of each run, Pallas kernels for 15% -> 12%
where the time goes in v5:
time: 45.5 us; the launch traced here: 45.3 us
  starting transfers between devices  18.4 us (40%)
  waiting for transfers between devices  16.1 us (35%)
  Pallas kernels  10.7 us (24%)
    ppermute x16, starting transfers between devices, swap(): return lax.ppermute(value, axes, [(i, i ^ step) for i in range(size)])  18.4 us
    ppermute x16, waiting for transfers between devices, swap(): return lax.ppermute(value, axes, [(i, i ^ step) for i in range(size)])  16.1 us
    pallas_call x1, Pallas kernels, per_device(): pl.pallas_call(functools.partial(gather_kernel, pools), out_shape=[shape(...  3 us
    pallas_call x1, Pallas kernels, per_device(): pl.pallas_call(functools.partial(table_kernel, pools, shard_blocks), out_...  2.97 us
    pallas_call x2, Pallas kernels, score(): pl.pallas_call(functools.partial(score_kernel, first, count, heads, pools...  2.04 us
    pallas_call x1, Pallas kernels, per_device(): pl.pallas_call(functools.partial(project_kernel, pools, heads, reps), out...  1.2 us
  transfers between devices with their start and end apart: 16, of which 11 were waited for; matrix products, arithmetic and copies ran while one was open for 0% of the time, Pallas kernels for 12%

profile of v5, /device:TPU:0, one launch (start us, length us, event | category | flops | bytes accessed | tf_op | source)
XLA Modules:
  0.0 45.3 jit_solution(17159504984455180505)
XLA Ops:
  0.0 3.0 %gather.1 = (bf16[512,256]{1,0:T(8,128)(2,1)S(1)}, bf16[512,256]{1,0:T(8,128)(2,1)S(1)}, bf16[272,256]{1,0:T(8,128)(2,1)S(1)}, bf16[272,256]{1,0:T(8,128)(2,1)S(...) custom-call(s32[1,4,4]{2,1,0:T(4,128)} %sel_ref.3, bf16[1,4,1024,512]{3,2,1,0:T(8,128)(2,1)} %lat_ref.1, ...), custom_call_target="tpu_custom_call" | custom-call | tf_op jit(solution)/shard_map/gather/pallas_call | solution.py:325
  3.0 3.0 %collective-permute-start = (bf16[512,256]{1,0:T(8,128)(2,1)S(1)}, bf16[512,256]{1,0:T(8,128)(2,1)S(1)}, u32[]{:S(2)}, u32[]{:S(2)}) collective-permute-start(bf16[512,256]{1,0:T(8,128)(2,1)S(1)} %get-tuple-element.35.rest_0_), channel_id=1, source_target_pairs={{0,2},{2,0},{1,3},{3,1},{4,6},{6,4},{5,7},{7,5},{8,10},{10,8},{9,1... | collective-permute-start | bytes 786440 | tf_op jit(solution)/shard_map/ppermute | solution.py:35
  6.0 3.6 %collective-permute-start.1 = (bf16[272,256]{1,0:T(8,128)(2,1)S(1)}, bf16[272,256]{1,0:T(8,128)(2,1)S(1)}, u32[]{:S(2)}, u32[]{:S(2)}) collective-permute-start(bf16[272,256]{1,0:T(8,128)(2,1)S(1)} %get-tuple-element.36), channel_id=1, source_target_pairs={{0,12},{4,8},{8,4},{12,0},{1,13},{5,9},{9,5},{13,1},{2,14},{6,10},... | collective-permute-start | bytes 417800 | tf_op jit(solution)/shard_map/ppermute | solution.py:35
  9.6 3.0 %tables.1 = (f32[1024,128]{1,0:T(8,128)S(1)}, f32[1024,128]{1,0:T(8,128)S(1)}, f32[8,128]{1,0:T(8,128)S(1)}, s32[4,256]{1,0:T(4,128)S(1)}, s32[1,1024]{1,0:T(1,1...) custom-call(s32[1,4,4]{2,1,0:T(4,128)} %sel_ref.3, ...), custom_call_target="tpu_custom_call", output_to_operand_aliasing={{7}: (5, {})} | custom-call | bytes 10485760 | tf_op jit(solution)/shard_map/tables/pallas_call | solution.py:342
  12.6 0.8 %collective-permute-start.5 = (bf16[272,256]{1,0:T(8,128)(2,1)S(1)}, bf16[272,256]{1,0:T(8,128)(2,1)S(1)}, u32[]{:S(2)}, u32[]{:S(2)}) collective-permute-start(bf16[272,256]{1,0:T(8,128)(2,1)S(1)} %get-tuple-element.40), channel_id=1, source_target_pairs={{0,4},{4,0},{8,12},{12,8},{1,5},{5,1},{9,13},{13,9},{2,6},{6,2},{1... | collective-permute-start | bytes 417800 | tf_op jit(solution)/shard_map/ppermute | solution.py:35
  13.5 0.3 collective-permute-start.6
  13.8 0.7 %collective-permute-done.1.rest_2_.rest_0_ = bf16[272,256]{1,0:T(8,128)(2,1)S(1)} collective-permute-done((bf16[272,256]{1,0:T(8,128)(2,1)S(1)}, bf16[272,256]{1,0:T(8,128)(2,1)S(1)}, u32[]{:S(2)}, u32[]{:S(2)}) %collective-permute-start.1) | collective-permute-done | bytes 139296 | tf_op jit(solution)/shard_map/ppermute | solution.py:35
  14.5 6.7 %collective-permute-done.2.rest_3_.rest_1_ = bf16[272,256]{1,0:T(8,128)(2,1)S(1)} collective-permute-done((bf16[272,256]{1,0:T(8,128)(2,1)S(1)}, bf16[272,256]{1,0:T(8,128)(2,1)S(1)}, u32[]{:S(2)}, u32[]{:S(2)}) %collective-permute-start.2) | collective-permute-done | bytes 139296 | tf_op jit(solution)/shard_map/ppermute | solution.py:35
  21.1 1.0 %score.2 = (f32[32,256]{1,0:T(8,128)S(1)}, f32[32,256]{1,0:T(8,128)S(1)}) custom-call(bf16[512,512]{1,0:T(8,128)(2,1)S(1)} %get-tuple-element.30.map_ref, f32[1024,128]{1,0:T(8,128)S(1)} %get-tuple-element.31.cos_ref, f32[1024,128]{1,0:T(8,128)S(1)} %get-tuple-element.32.sin_ref, f32[8,128]{1,0:T(8,128)S(1)} %get-tuple-element.33.turn_ref, ...), custom_call_target="tpu_custom_call" | custom-call | bytes 3145728 | tf_op jit(solution)/shard_map/score/pallas_call | solution.py:363
  22.2 0.3 compact.1.after_ref.rest_4_
  22.5 0.6 %collective-permute-start.8 = (bf16[512,256]{1,0:T(8,128)(2,1)S(1)}, bf16[512,256]{1,0:T(8,128)(2,1)S(1)}, u32[]{:S(2)}, u32[]{:S(2)}) collective-permute-start(bf16[512,256]{1,0:T(8,128)(2,1)S(1)} %compact.1.after_ref.rest_4_), channel_id=1, source_target_pairs={{0,2},{2,0},{1,3},{3,1},{4,6},{6,4},{5,7},{7,5},{8,10},{10,8},{9,1... | collective-permute-start | bytes 786440 | tf_op jit(solution)/shard_map/ppermute | solution.py:35
  23.1 1.0 %score.3 = (f32[32,256]{1,0:T(8,128)S(1)}, f32[32,256]{1,0:T(8,128)S(1)}) custom-call(bf16[512,512]{1,0:T(8,128)(2,1)S(1)} %get-tuple-element.30.map_ref, f32[1024,128]{1,0:T(8,128)S(1)} %get-tuple-element.31.cos_ref, f32[1024,128]{1,0:T(8,128)S(1)} %get-tuple-element.32.sin_ref, f32[8,128]{1,0:T(8,128)S(1)} %get-tuple-element.33.turn_ref, ...), custom_call_target="tpu_custom_call" | custom-call | bytes 3145728 | tf_op jit(solution)/shard_map/score/pallas_call | solution.py:363
  24.2 2.5 %collective-permute-start.3 = (f32[32,256]{1,0:T(8,128)S(1)}, f32[32,256]{1,0:T(8,128)S(1)}, u32[]{:S(2)}, u32[]{:S(2)}) collective-permute-start(f32[32,256]{1,0:T(8,128)S(1)} %get-tuple-element.38), channel_id=1, source_target_pairs={{0,12},{4,8},{8,4},{12,0},{1,13},{5,9},{9,5},{13,1},{2,14},{6,10},... | collective-permute-start | bytes 98312 | tf_op jit(solution)/shard_map/ppermute | solution.py:35
  26.7 0.9 %collective-permute-start.4 = (f32[32,256]{1,0:T(8,128)S(1)}, f32[32,256]{1,0:T(8,128)S(1)}, u32[]{:S(2)}, u32[]{:S(2)}) collective-permute-start(f32[32,256]{1,0:T(8,128)S(1)} %get-tuple-element.39.after_ref), channel_id=1, source_target_pairs={{0,8},{4,12},{8,0},{12,4},{1,9},{5,13},{9,1},{13,5},{2,10},{6,14},... | collective-permute-start | bytes 98312 | tf_op jit(solution)/shard_map/ppermute | solution.py:35
  27.6 0.8 %collective-permute-done.7.rest_2_ = f32[32,256]{1,0:T(8,128)S(1)} collective-permute-done((f32[32,256]{1,0:T(8,128)S(1)}, f32[32,256]{1,0:T(8,128)S(1)}, u32[]{:S(2)}, u32[]{:S(2)}) %collective-permute-start.7) | collective-permute-done | bytes 32800 | tf_op jit(solution)/shard_map/ppermute | solution.py:35
  28.4 1.5 %collective-permute-done.3.rest_0_ = f32[32,256]{1,0:T(8,128)S(1)} collective-permute-done((f32[32,256]{1,0:T(8,128)S(1)}, f32[32,256]{1,0:T(8,128)S(1)}, u32[]{:S(2)}, u32[]{:S(2)}) %collective-permute-start.3) | collective-permute-done | bytes 32800 | tf_op jit(solution)/shard_map/ppermute | solution.py:35
  29.9 1.6 %collective-permute-done.4.rest_1_ = f32[32,256]{1,0:T(8,128)S(1)} collective-permute-done((f32[32,256]{1,0:T(8,128)S(1)}, f32[32,256]{1,0:T(8,128)S(1)}, u32[]{:S(2)}, u32[]{:S(2)}) %collective-permute-start.4) | collective-permute-done | bytes 32800 | tf_op jit(solution)/shard_map/ppermute | solution.py:35
  31.5 0.5 %attend.1.refs_0_ = bf16[1,4096]{1,0:T(2,128)(2,1)S(1)} custom-call(bf16[512,512]{1,0:T(8,128)(2,1)S(1)} %get-tuple-element.28.map_ref, s32[1,1024]{1,0:T(1,128)S(1)} %get-tuple-element.29.after_ref.place_ref, f32[32,256]{1,0:T(8,128)S(1)} %collective-permute-done.3.rest_0_, f32[32,256]{1,0:T(8,128)S(1)} %collective-permute-done.4.rest_1_, ...), custom_call_target="tpu_custom_call" | custom-call | tf_op jit(solution)/shard_map/attend/pallas_call | solution.py:387
  32.1 1.2 %collective-permute-done.9.refs_1_ = bf16[1,4096]{1,0:T(2,128)(2,1)S(1)} collective-permute-done((bf16[1,4096]{1,0:T(2,128)(2,1)S(1)}, bf16[1,4096]{1,0:T(2,128)(2,1)S(1)}, u32[]{:S(2)}, u32[]{:S(2)}) %collective-permute-start.9) | collective-permute-done | bytes 8224 | tf_op jit(solution)/shard_map/ppermute | solution.py:35
  33.3 1.4 %collective-permute-start.10 = (bf16[2,4096]{1,0:T(2,128)(2,1)S(1)}, bf16[2,4096]{1,0:T(2,128)(2,1)S(1)}, u32[]{:S(2)}, u32[]{:S(2)}) collective-permute-start(bf16[2,4096]{1,0:T(2,128)(2,1)S(1)} %join.1.rest_3_), channel_id=1, source_target_pairs={{0,12},{4,8},{8,4},{12,0},{1,13},{5,9},{9,5},{13,1},{2,14},{6,10},... | collective-permute-start | bytes 49160 | tf_op jit(solution)/shard_map/ppermute | solution.py:35
  34.7 1.1 %collective-permute-start.11 = (bf16[2,4096]{1,0:T(2,128)(2,1)S(1)}, bf16[2,4096]{1,0:T(2,128)(2,1)S(1)}, u32[]{:S(2)}, u32[]{:S(2)}) collective-permute-start(bf16[2,4096]{1,0:T(2,128)(2,1)S(1)} %join.1.rest_3_), channel_id=1, source_target_pairs={{0,8},{4,12},{8,0},{12,4},{1,9},{5,13},{9,1},{13,5},{2,10},{6,14},... | collective-permute-start | bytes 49160 | tf_op jit(solution)/shard_map/ppermute | solution.py:35
  35.9 1.9 %collective-permute-start.12 = (bf16[2,4096]{1,0:T(2,128)(2,1)S(1)}, bf16[2,4096]{1,0:T(2,128)(2,1)S(1)}, u32[]{:S(2)}, u32[]{:S(2)}) collective-permute-start(bf16[2,4096]{1,0:T(2,128)(2,1)S(1)} %join.1.rest_3_), channel_id=1, source_target_pairs={{0,4},{4,0},{8,12},{12,8},{1,5},{5,1},{9,13},{13,9},{2,6},{6,2},{1... | collective-permute-start | bytes 49160 | tf_op jit(solution)/shard_map/ppermute | solution.py:35
  37.8 1.1 %collective-permute-done.10.rest_0_ = bf16[2,4096]{1,0:T(2,128)(2,1)S(1)} collective-permute-done((bf16[2,4096]{1,0:T(2,128)(2,1)S(1)}, bf16[2,4096]{1,0:T(2,128)(2,1)S(1)}, u32[]{:S(2)}, u32[]{:S(2)}) %collective-permute-start.10) | collective-permute-done | bytes 16416 | tf_op jit(solution)/shard_map/ppermute | solution.py:35
  38.9 0.5 %collective-permute-done.11.rest_1_ = bf16[2,4096]{1,0:T(2,128)(2,1)S(1)} collective-permute-done((bf16[2,4096]{1,0:T(2,128)(2,1)S(1)}, bf16[2,4096]{1,0:T(2,128)(2,1)S(1)}, u32[]{:S(2)}, u32[]{:S(2)}) %collective-permute-start.11) | collective-permute-done | bytes 16416 | tf_op jit(solution)/shard_map/ppermute | solution.py:35
  39.4 0.2 collective-permute-done.12.rest_2_
  39.6 1.2 %project.1 = (f32[2,1024]{1,0:T(2,128)S(1)}, f32[2,1024]{1,0:T(2,128)S(1)}, f32[2,1024]{1,0:T(2,128)S(1)}, f32[2,1024]{1,0:T(2,128)S(1)}) custom-call(bf16[4096,1024]{1,0:T(8,128)(2,1)S(1)} %copy-done, bf16[2,4096]{1,0:T(2,128)(2,1)S(1)} %collective-permute-done.10.rest_0_, bf16[2,4096]{1,0:T(2,128)(2,1)S(1)} %collective-permute-done.11.rest_1_, ...), custom_call_target="tpu_custom_call" | custom-call | tf_op jit(solution)/shard_map/project/pallas_call | solution.py:400
  40.8 0.1 collective-permute-start.13
  40.9 1.6 %collective-permute-start.14 = (f32[2,1024]{1,0:T(2,128)S(1)}, f32[2,1024]{1,0:T(2,128)S(1)}, u32[]{:S(2)}, u32[]{:S(2)}) collective-permute-start(f32[2,1024]{1,0:T(2,128)S(1)} %get-tuple-element.46), channel_id=1, source_target_pairs={{0,2},{1,3},{2,0},{3,1},{4,6},{5,7},{6,4},{7,5},{8,10},{9,11},{10,... | collective-permute-start | bytes 24584 | tf_op jit(solution)/shard_map/ppermute | solution.py:35
  42.5 0.3 collective-permute-start.15
  42.8 1.2 %collective-permute-done.13.refs_0_ = f32[2,1024]{1,0:T(2,128)S(1)} collective-permute-done((f32[2,1024]{1,0:T(2,128)S(1)}, f32[2,1024]{1,0:T(2,128)S(1)}, u32[]{:S(2)}, u32[]{:S(2)}) %collective-permute-start.13) | collective-permute-done | bytes 8224 | tf_op jit(solution)/shard_map/ppermute | solution.py:35
  44.0 0.6 %collective-permute-done.14.refs_1_ = f32[2,1024]{1,0:T(2,128)S(1)} collective-permute-done((f32[2,1024]{1,0:T(2,128)S(1)}, f32[2,1024]{1,0:T(2,128)S(1)}, u32[]{:S(2)}, u32[]{:S(2)}) %collective-permute-start.14) | collective-permute-done | bytes 8224 | tf_op jit(solution)/shard_map/ppermute | solution.py:35
  44.6 0.6 %finish.1 = bf16[1,2,2048]{2,1,0:T(2,128)(2,1)} custom-call(f32[2,1024]{1,0:T(2,128)S(1)} %collective-permute-done.13.refs_0_, f32[2,1024]{1,0:T(2,128)S(1)} %collective-permute-done.14.refs_1_, f32[2,1024]{1,0:T(2,128)S(1)} %collective-permute-done.15.refs_2_, f32[2,1024]{1,0:T(2,128)S(1)} %get-tuple-element.48.refs_3_), custom_call_target="tpu_custom_call" | custom-call | tf_op jit(solution)/shard_map/finish/pallas_call | solution.py:409
  (11 shorter events, 0.2 us)
Async XLA Ops:
  0.0 39.6 %copy-start = (bf16[4096,1024]{1,0:T(8,128)(2,1)S(1)}, bf16[4096,1024]{1,0:T(8,128)(2,1)}, u32[]{:S(2)}) copy-start(bf16[4096,1024]{1,0:T(8,128)(2,1)} %weight_ref.1) | copy-start | bytes 25165828
  3.0 18.1 %collective-permute-start = (bf16[512,256]{1,0:T(8,128)(2,1)S(1)}, bf16[512,256]{1,0:T(8,128)(2,1)S(1)}, u32[]{:S(2)}, u32[]{:S(2)}) collective-permute-start(bf16[512,256]{1,0:T(8,128)(2,1)S(1)} %get-tuple-element.35.rest_0_), channel_id=1, source_target_pairs={{0,2},{2,0},{1,3},{3,1},{4,6},{6,4},{5,7},{7,5},{8,10},{10,8},{9,1... | collective-permute-start | bytes 786440 | tf_op jit(solution)/shard_map/ppermute | solution.py:35
  6.0 8.4 %collective-permute-start.1 = (bf16[272,256]{1,0:T(8,128)(2,1)S(1)}, bf16[272,256]{1,0:T(8,128)(2,1)S(1)}, u32[]{:S(2)}, u32[]{:S(2)}) collective-permute-start(bf16[272,256]{1,0:T(8,128)(2,1)S(1)} %get-tuple-element.36), channel_id=1, source_target_pairs={{0,12},{4,8},{8,4},{12,0},{1,13},{5,9},{9,5},{13,1},{2,14},{6,10},... | collective-permute-start | bytes 417800 | tf_op jit(solution)/shard_map/ppermute | solution.py:35
  9.6 11.5 %collective-permute-start.2 = (bf16[272,256]{1,0:T(8,128)(2,1)S(1)}, bf16[272,256]{1,0:T(8,128)(2,1)S(1)}, u32[]{:S(2)}, u32[]{:S(2)}) collective-permute-start(bf16[272,256]{1,0:T(8,128)(2,1)S(1)} %get-tuple-element.37), channel_id=1, source_target_pairs={{0,8},{4,12},{8,0},{12,4},{1,9},{5,13},{9,1},{13,5},{2,10},{6,14},... | collective-permute-start | bytes 417800 | tf_op jit(solution)/shard_map/ppermute | solution.py:35
  12.6 9.5 %collective-permute-start.5 = (bf16[272,256]{1,0:T(8,128)(2,1)S(1)}, bf16[272,256]{1,0:T(8,128)(2,1)S(1)}, u32[]{:S(2)}, u32[]{:S(2)}) collective-permute-start(bf16[272,256]{1,0:T(8,128)(2,1)S(1)} %get-tuple-element.40), channel_id=1, source_target_pairs={{0,4},{4,0},{8,12},{12,8},{1,5},{5,1},{9,13},{13,9},{2,6},{6,2},{1... | collective-permute-start | bytes 417800 | tf_op jit(solution)/shard_map/ppermute | solution.py:35
  13.5 9.6 %collective-permute-start.6 = (bf16[512,256]{1,0:T(8,128)(2,1)S(1)}, bf16[512,256]{1,0:T(8,128)(2,1)S(1)}, u32[]{:S(2)}, u32[]{:S(2)}) collective-permute-start(bf16[512,256]{1,0:T(8,128)(2,1)S(1)} %get-tuple-element.42.rest_0_), channel_id=1, source_target_pairs={{0,2},{2,0},{1,3},{3,1},{4,6},{6,4},{5,7},{7,5},{8,10},{10,8},{9,1... | collective-permute-start | bytes 786440 | tf_op jit(solution)/shard_map/ppermute | solution.py:35
  22.5 9.0 %collective-permute-start.8 = (bf16[512,256]{1,0:T(8,128)(2,1)S(1)}, bf16[512,256]{1,0:T(8,128)(2,1)S(1)}, u32[]{:S(2)}, u32[]{:S(2)}) collective-permute-start(bf16[512,256]{1,0:T(8,128)(2,1)S(1)} %compact.1.after_ref.rest_4_), channel_id=1, source_target_pairs={{0,2},{2,0},{1,3},{3,1},{4,6},{6,4},{5,7},{7,5},{8,10},{10,8},{9,1... | collective-permute-start | bytes 786440 | tf_op jit(solution)/shard_map/ppermute | solution.py:35
  24.1 4.3 %collective-permute-start.7 = (f32[32,256]{1,0:T(8,128)S(1)}, f32[32,256]{1,0:T(8,128)S(1)}, u32[]{:S(2)}, u32[]{:S(2)}) collective-permute-start(f32[32,256]{1,0:T(8,128)S(1)} %get-tuple-element.43), channel_id=1, source_target_pairs={{0,4},{4,0},{8,12},{12,8},{1,5},{5,1},{9,13},{13,9},{2,6},{6,2},{1... | collective-permute-start | bytes 98312 | tf_op jit(solution)/shard_map/ppermute | solution.py:35
  24.2 5.8 %collective-permute-start.3 = (f32[32,256]{1,0:T(8,128)S(1)}, f32[32,256]{1,0:T(8,128)S(1)}, u32[]{:S(2)}, u32[]{:S(2)}) collective-permute-start(f32[32,256]{1,0:T(8,128)S(1)} %get-tuple-element.38), channel_id=1, source_target_pairs={{0,12},{4,8},{8,4},{12,0},{1,13},{5,9},{9,5},{13,1},{2,14},{6,10},... | collective-permute-start | bytes 98312 | tf_op jit(solution)/shard_map/ppermute | solution.py:35
  26.7 4.8 %collective-permute-start.4 = (f32[32,256]{1,0:T(8,128)S(1)}, f32[32,256]{1,0:T(8,128)S(1)}, u32[]{:S(2)}, u32[]{:S(2)}) collective-permute-start(f32[32,256]{1,0:T(8,128)S(1)} %get-tuple-element.39.after_ref), channel_id=1, source_target_pairs={{0,8},{4,12},{8,0},{12,4},{1,9},{5,13},{9,1},{13,5},{2,10},{6,14},... | collective-permute-start | bytes 98312 | tf_op jit(solution)/shard_map/ppermute | solution.py:35
  32.0 1.2 %collective-permute-start.9 = (bf16[1,4096]{1,0:T(2,128)(2,1)S(1)}, bf16[1,4096]{1,0:T(2,128)(2,1)S(1)}, u32[]{:S(2)}, u32[]{:S(2)}) collective-permute-start(bf16[1,4096]{1,0:T(2,128)(2,1)S(1)} %attend.1.refs_0_), channel_id=1, source_target_pairs={{0,1},{1,0},{2,3},{3,2},{4,5},{5,4},{6,7},{7,6},{8,9},{9,8},{10,11... | collective-permute-start | bytes 24584 | tf_op jit(solution)/shard_map/ppermute | solution.py:35
  33.3 5.6 %collective-permute-start.10 = (bf16[2,4096]{1,0:T(2,128)(2,1)S(1)}, bf16[2,4096]{1,0:T(2,128)(2,1)S(1)}, u32[]{:S(2)}, u32[]{:S(2)}) collective-permute-start(bf16[2,4096]{1,0:T(2,128)(2,1)S(1)} %join.1.rest_3_), channel_id=1, source_target_pairs={{0,12},{4,8},{8,4},{12,0},{1,13},{5,9},{9,5},{13,1},{2,14},{6,10},... | collective-permute-start | bytes 49160 | tf_op jit(solution)/shard_map/ppermute | solution.py:35
  34.7 4.6 %collective-permute-start.11 = (bf16[2,4096]{1,0:T(2,128)(2,1)S(1)}, bf16[2,4096]{1,0:T(2,128)(2,1)S(1)}, u32[]{:S(2)}, u32[]{:S(2)}) collective-permute-start(bf16[2,4096]{1,0:T(2,128)(2,1)S(1)} %join.1.rest_3_), channel_id=1, source_target_pairs={{0,8},{4,12},{8,0},{12,4},{1,9},{5,13},{9,1},{13,5},{2,10},{6,14},... | collective-permute-start | bytes 49160 | tf_op jit(solution)/shard_map/ppermute | solution.py:35
  35.9 3.7 %collective-permute-start.12 = (bf16[2,4096]{1,0:T(2,128)(2,1)S(1)}, bf16[2,4096]{1,0:T(2,128)(2,1)S(1)}, u32[]{:S(2)}, u32[]{:S(2)}) collective-permute-start(bf16[2,4096]{1,0:T(2,128)(2,1)S(1)} %join.1.rest_3_), channel_id=1, source_target_pairs={{0,4},{4,0},{8,12},{12,8},{1,5},{5,1},{9,13},{13,9},{2,6},{6,2},{1... | collective-permute-start | bytes 49160 | tf_op jit(solution)/shard_map/ppermute | solution.py:35
  40.8 3.2 %collective-permute-start.13 = (f32[2,1024]{1,0:T(2,128)S(1)}, f32[2,1024]{1,0:T(2,128)S(1)}, u32[]{:S(2)}, u32[]{:S(2)}) collective-permute-start(f32[2,1024]{1,0:T(2,128)S(1)} %get-tuple-element.45), channel_id=1, source_target_pairs={{0,3},{1,2},{2,1},{3,0},{4,7},{5,6},{6,5},{7,4},{8,11},{9,10},{10,... | collective-permute-start | bytes 24584 | tf_op jit(solution)/shard_map/ppermute | solution.py:35
  40.9 3.7 %collective-permute-start.14 = (f32[2,1024]{1,0:T(2,128)S(1)}, f32[2,1024]{1,0:T(2,128)S(1)}, u32[]{:S(2)}, u32[]{:S(2)}) collective-permute-start(f32[2,1024]{1,0:T(2,128)S(1)} %get-tuple-element.46), channel_id=1, source_target_pairs={{0,2},{1,3},{2,0},{3,1},{4,6},{5,7},{6,4},{7,5},{8,10},{9,11},{10,... | collective-permute-start | bytes 24584 | tf_op jit(solution)/shard_map/ppermute | solution.py:35
  42.5 2.1 %collective-permute-start.15 = (f32[2,1024]{1,0:T(2,128)S(1)}, f32[2,1024]{1,0:T(2,128)S(1)}, u32[]{:S(2)}, u32[]{:S(2)}) collective-permute-start(f32[2,1024]{1,0:T(2,128)S(1)} %get-tuple-element.47), channel_id=1, source_target_pairs={{0,1},{1,0},{2,3},{3,2},{4,5},{5,4},{6,7},{7,6},{8,9},{9,8},{10,11... | collective-permute-start | bytes 24584 | tf_op jit(solution)/shard_map/ppermute | solution.py:35

commit v6 on v5

--- a/solution.py
+++ b/solution.py
@@ -24,11 +24,14 @@
 HBM = pl.BlockSpec(memory_space=pltpu.HBM)
 
 
-def frequencies():
+def rotary_tables(blocks):
     half = HEAD_SIZE // 2
     exponents = np.arange(half, dtype=np.float32) * np.float32(2.0 / HEAD_SIZE)
     freq = np.power(np.float64(ROPE_BASE), -exponents.astype(np.float64)).astype(np.float32)
-    return np.concatenate([freq, freq])[None, :]
+    freq = np.concatenate([freq, freq]).astype(np.float64)[None, :]
+    coarse = np.arange(-(-(blocks + 1) // 8) * 8)[:, None] * BLOCK * freq
+    fine = np.arange(BLOCK)[:, None] * freq
+    return [f(angle).astype(np.float32) for angle in (coarse, fine) for f in (np.cos, np.sin)]
 
 
 def swap(value, axes, size, step):
@@ -102,9 +105,9 @@
     within = target & (half - 1)
     wanted = ((within >> 6) << 7) + (within & (LANE - 1)) + jnp.where(target >= half, LANE, 0)
     pick = (source == wanted).astype(jnp.float32).astype(jnp.bfloat16)
+    for copy in copies.values():
+        copy.wait()
     for k in range(pools - 1, -1, -1):
-        for c in range(CAP):
-            copies[k, c].wait()
         keys_ref, at = (far_ref, k - pools // 2) if k >= pools // 2 else (near_ref, k)
         for j in range(columns // chunk):
             packed = jnp.dot(
@@ -116,8 +119,11 @@
         value_refs[k][rows:, :] = queries
 
 
-def table_kernel(pools, shard_blocks, sel_ref, len_ref, freq_ref, key_map_ref, value_map_ref, held_ref, *rest):
-    cos_ref, sin_ref, turn_ref, live_ref, place_ref, key_out_ref, value_out_ref = rest[:7]
+def table_kernel(
+    pools, shard_blocks, sel_ref, len_ref, coarse_cos_ref, coarse_sin_ref, fine_cos_ref, fine_sin_ref,
+    key_map_ref, value_map_ref, *rest,
+):
+    cos_ref, sin_ref, turn_ref, live_ref, place_ref, key_out_ref, value_out_ref = rest[2:9]
     sems = rest[-1]
     loads = [
         pltpu.make_async_copy(key_map_ref, key_out_ref, sems.at[0]),
@@ -126,31 +132,34 @@
     for load in loads:
         load.start()
     me = lax.axis_index("pool")
-    lane = lax.broadcasted_iota(jnp.int32, (BLOCK, HEAD_SIZE), 1)
-    row = lax.broadcasted_iota(jnp.int32, (BLOCK, HEAD_SIZE), 0)
-    front = lane < HEAD_SIZE // 2
+    front = lax.broadcasted_iota(jnp.int32, (1, HEAD_SIZE), 1) < HEAD_SIZE // 2
     across = lax.broadcasted_iota(jnp.int32, (1, BLOCK), 1)
+
+    def turned(block, fine_cos, fine_sin):
+        coarse_cos = coarse_cos_ref[pl.ds(block, 1), :]
+        coarse_sin = coarse_sin_ref[pl.ds(block, 1), :]
+        sine = coarse_sin * fine_cos + coarse_cos * fine_sin
+        return coarse_cos * fine_cos - coarse_sin * fine_sin, jnp.where(front, -sine, sine)
+
     place = jnp.int32(0)
     for k in range(pools):
-        turn_ref[k : k + 1, :] = len_ref[0, me ^ k].astype(jnp.float32) * freq_ref[...]
-    angle = turn_ref[0:pools, :]
-    turn_ref[0:pools, :] = jnp.cos(angle)
-    turn_ref[pools:, :] = jnp.where(front[:1, :], -jnp.sin(angle), jnp.sin(angle))
-    for k in range(pools):
         seq = me ^ k
+        length = len_ref[0, seq]
+        rest_of = length & (BLOCK - 1)
+        cosine, sine = turned(
+            length >> 7, fine_cos_ref[pl.ds(rest_of, 1), :], fine_sin_ref[pl.ds(rest_of, 1), :]
+        )
+        turn_ref[k : k + 1, :] = cosine
+        turn_ref[pools + k : pools + k + 1, :] = sine
         found = slot_blocks(sel_ref, seq, me, shard_blocks)
-        one, two = [jnp.maximum(block, 0) * BLOCK for block in found]
-        angle = (jnp.where(front, one, two) + row).astype(jnp.float32) * freq_ref[...]
-        for ref, table, sign in ((cos_ref, jnp.cos(angle), 1.0), (sin_ref, jnp.sin(angle), -1.0)):
-            turned = pltpu.roll(table, HEAD_SIZE // 2, 1)
-            at = k * CAP * BLOCK
-            ref[at : at + BLOCK, :] = jnp.where(front, sign * table, turned)
-            ref[at + BLOCK : at + 2 * BLOCK, :] = jnp.where(front, sign * turned, table)
         mine = slot_blocks(sel_ref, me, seq, shard_blocks)
         for c in range(CAP):
+            at = (k * CAP + c) * BLOCK
+            cosine, sine = turned(jnp.maximum(found[c], 0), fine_cos_ref[...], fine_sin_ref[...])
+            cos_ref[at : at + BLOCK, :] = cosine
+            sin_ref[at : at + BLOCK, :] = sine
             start = jnp.where(found[c] < 0, FAR, found[c] * BLOCK)
-            live_ref[k : k + 1, c * BLOCK : (c + 1) * BLOCK] = (start + across < len_ref[0, seq]).astype(jnp.int32)
-            at = (k * CAP + c) * BLOCK
+            live_ref[k : k + 1, c * BLOCK : (c + 1) * BLOCK] = (start + across < length).astype(jnp.int32)
             used = mine[c] >= 0
             place_ref[:, at : at + BLOCK] = jnp.where(used, place, -1) + 0 * across
             place = place + used.astype(jnp.int32)
@@ -160,8 +169,8 @@
 
 def score_kernel(first, count, heads, pools, map_ref, cos_ref, sin_ref, turn_ref, live_ref, after_ref, *rest):
     del after_ref
-    key_refs = rest[:heads]
-    pay_refs = rest[heads : heads + count][::-1]
+    pay_refs = rest[:count][::-1]
+    key_refs = rest[count : count + heads]
     out_refs = rest[heads + count :]
     head = lax.axis_index("heads")
     width = key_refs[0].shape[1]
@@ -300,7 +309,7 @@
     own_heads = queries.shape[2] // HEAD_SIZE
     bf16, f32, i32 = jnp.bfloat16, jnp.float32, jnp.int32
     shape = jax.ShapeDtypeStruct
-    freq = jnp.asarray(frequencies())
+    constants = [jnp.asarray(table) for table in rotary_tables(shard_blocks * pools)]
 
     def join(*blocks):
         return pl.pallas_call(
@@ -336,27 +345,29 @@
         name="gather",
     )(in_hbm(selected), in_hbm(latents), in_hbm(queries))
     near, far, values = packed[0], packed[1], packed[2:]
-    far_parts = exchange(far, "heads", heads)
-    near_parts = exchange(near, "heads", heads)
-
-    cosine, sine, turn, live, place, key_maps, value_maps, held = pl.pallas_call(
+
+    passed = [values[1], near]
+    cosine, sine, turn, live, place, key_maps, value_maps, *passed = pl.pallas_call(
         functools.partial(table_kernel, pools, shard_blocks),
         out_shape=[shape((pools * rows, HEAD_SIZE), f32)] * 2
         + [shape((2 * pools, HEAD_SIZE), f32), shape((pools, rows), i32), shape((1, pools * rows), i32)]
         + [shape(key_latent_maps.shape, bf16), shape(value_latent_maps.shape, bf16)]
-        + [shape(values[1].shape, bf16)],
-        in_specs=[SMEM, SMEM, VMEM] + [ANY] * 3,
-        out_specs=[VMEM] * 7 + [ANY],
+        + [shape(block.shape, bf16) for block in passed],
+        in_specs=[SMEM, SMEM] + [VMEM] * 4 + [ANY] * 4,
+        out_specs=[VMEM] * 7 + [ANY] * 2,
         scratch_shapes=[pltpu.SemaphoreType.DMA((2,))],
-        input_output_aliases={5: 7},
+        input_output_aliases={8 + i: 7 + i for i in range(2)},
         compiler_params=params(16),
-        cost_estimate=pl.CostEstimate(flops=0, transcendentals=0, bytes_accessed=10 << 20),
+        cost_estimate=pl.CostEstimate(flops=0, transcendentals=0, bytes_accessed=5 << 20),
         name="tables",
     )(
-        in_hbm(selected), in_hbm(lengths), in_hbm(freq), in_hbm(key_latent_maps),
-        in_hbm(value_latent_maps), values[1],
+        in_hbm(selected), in_hbm(lengths), *[in_hbm(table) for table in constants],
+        in_hbm(key_latent_maps), in_hbm(value_latent_maps), *passed,
     )
+    held, near = passed
     value_parts = scatter([values[0], held, *values[2:]], "pool", pools)
+    far_parts = exchange(far, "heads", heads)
+    near_parts = exchange(near, "heads", heads)
 
     def score(first, count, key_parts, after):
         pays = value_parts[first : first + count]
@@ -368,7 +379,7 @@
             compiler_params=params(20),
             cost_estimate=pl.CostEstimate(flops=0, transcendentals=0, bytes_accessed=3 << 20),
             name="score",
-        )(key_maps, cosine, sine, turn, live, after, *key_parts, *pays[::-1])
+        )(key_maps, cosine, sine, turn, live, after, *pays[::-1], *key_parts)
 
     far_scores = score(middle, middle, far_parts, place)
     dense = pl.pallas_call(
@@ -380,7 +391,7 @@
         cost_estimate=pl.CostEstimate(flops=0, transcendentals=0, bytes_accessed=3 << 20),
         name="compact",
     )(place, far_scores[0], *value_parts[::-1])
-    near_scores = score(0, middle, near_parts, dense)
+    near_scores = score(0, middle, near_parts, far_scores[0])
     dense_parts = exchange(dense, "heads", heads)
     score_parts = scatter([*near_scores, *far_scores], "pool", pools)
 

time: 45.5 us -> 44.4 us (0.976)
  Pallas kernels: 10.7 us -> 9.67 us
    pallas_call x1, Pallas kernels: 2.97 us -> 2.11 us  [per_device(): pl.pallas_call(functools.partial(table_kernel, pools, shard_blocks), out_...]
  transfers between devices with their start and end apart: 16 -> 16, of which waited for: 11 -> 10; matrix products, arithmetic and copies ran while one was open for 0% -> 0% of each run, Pallas kernels for 12% -> 10%
where the time goes in v6:
time: 44.4 us; the launch traced here: 44.2 us
  starting transfers between devices  18.3 us (41%)
  waiting for transfers between devices  16.1 us (36%)
  Pallas kernels  9.67 us (22%)
    ppermute x16, starting transfers between devices, swap(): return lax.ppermute(value, axes, [(i, i ^ step) for i in range(size)])  18.3 us
    ppermute x16, waiting for transfers between devices, swap(): return lax.ppermute(value, axes, [(i, i ^ step) for i in range(size)])  16.1 us
    pallas_call x1, Pallas kernels, per_device(): pl.pallas_call(functools.partial(gather_kernel, pools), out_shape=[shape(...  2.83 us
    pallas_call x1, Pallas kernels, per_device(): pl.pallas_call(functools.partial(table_kernel, pools, shard_blocks), out_...  2.11 us
    pallas_call x2, Pallas kernels, score(): pl.pallas_call(functools.partial(score_kernel, first, count, heads, pools...  2.04 us
    pallas_call x1, Pallas kernels, per_device(): pl.pallas_call(functools.partial(project_kernel, pools, heads, reps), out...  1.2 us
  transfers between devices with their start and end apart: 16, of which 10 were waited for; matrix products, arithmetic and copies ran while one was open for 0% of the time, Pallas kernels for 10%

profile of v6, /device:TPU:0, one launch (start us, length us, event | category | flops | bytes accessed | tf_op | source)
XLA Modules:
  0.0 44.2 jit_solution(1821929985107270061)
XLA Ops:
  0.0 2.8 %gather.1 = (bf16[512,256]{1,0:T(8,128)(2,1)S(1)}, bf16[512,256]{1,0:T(8,128)(2,1)S(1)}, bf16[272,256]{1,0:T(8,128)(2,1)S(1)}, bf16[272,256]{1,0:T(8,128)(2,1)S(...) custom-call(s32[1,4,4]{2,1,0:T(4,128)} %sel_ref.3, bf16[1,4,1024,512]{3,2,1,0:T(8,128)(2,1)} %lat_ref.1, ...), custom_call_target="tpu_custom_call" | custom-call | tf_op jit(solution)/shard_map/gather/pallas_call | solution.py:334
  2.8 3.0 %collective-permute-start.2 = (bf16[512,256]{1,0:T(8,128)(2,1)S(1)}, bf16[512,256]{1,0:T(8,128)(2,1)S(1)}, u32[]{:S(2)}, u32[]{:S(2)}) collective-permute-start(bf16[512,256]{1,0:T(8,128)(2,1)S(1)} %get-tuple-element.39.rest_2_), channel_id=1, source_target_pairs={{0,2},{2,0},{1,3},{3,1},{4,6},{6,4},{5,7},{7,5},{8,10},{10,8},{9,1... | collective-permute-start | bytes 786440 | tf_op jit(solution)/shard_map/ppermute | solution.py:38
  5.8 3.6 %collective-permute-start = (bf16[272,256]{1,0:T(8,128)(2,1)S(1)}, bf16[272,256]{1,0:T(8,128)(2,1)S(1)}, u32[]{:S(2)}, u32[]{:S(2)}) collective-permute-start(bf16[272,256]{1,0:T(8,128)(2,1)S(1)} %get-tuple-element.37), channel_id=1, source_target_pairs={{0,12},{4,8},{8,4},{12,0},{1,13},{5,9},{9,5},{13,1},{2,14},{6,10},... | collective-permute-start | bytes 417800 | tf_op jit(solution)/shard_map/ppermute | solution.py:38
  9.4 2.1 %tables.1 = (f32[1024,128]{1,0:T(8,128)S(1)}, f32[1024,128]{1,0:T(8,128)S(1)}, f32[8,128]{1,0:T(8,128)S(1)}, s32[4,256]{1,0:T(4,128)S(1)}, s32[1,1024]{1,0:T(1,1...) custom-call(s32[1,4,4]{2,1,0:T(4,128)} %sel_ref.3, ...), custom_call_target="tpu_custom_call", output_to_operand_aliasing={{7}: (8, {}), {8}: (9, {})} | custom-call | bytes 5242880 | tf_op jit(solution)/shard_map/tables/pallas_call | solution.py:350
  11.6 0.8 %collective-permute-start.5 = (bf16[272,256]{1,0:T(8,128)(2,1)S(1)}, bf16[272,256]{1,0:T(8,128)(2,1)S(1)}, u32[]{:S(2)}, u32[]{:S(2)}) collective-permute-start(bf16[272,256]{1,0:T(8,128)(2,1)S(1)} %get-tuple-element.42), channel_id=1, source_target_pairs={{0,4},{4,0},{8,12},{12,8},{1,5},{5,1},{9,13},{13,9},{2,6},{6,2},{1... | collective-permute-start | bytes 417800 | tf_op jit(solution)/shard_map/ppermute | solution.py:38
  12.4 0.3 collective-permute-start.6
  12.7 1.6 %collective-permute-done.rest_0_ = bf16[272,256]{1,0:T(8,128)(2,1)S(1)} collective-permute-done((bf16[272,256]{1,0:T(8,128)(2,1)S(1)}, bf16[272,256]{1,0:T(8,128)(2,1)S(1)}, u32[]{:S(2)}, u32[]{:S(2)}) %collective-permute-start) | collective-permute-done | bytes 139296 | tf_op jit(solution)/shard_map/ppermute | solution.py:38
  14.3 6.6 %collective-permute-done.1.rest_1_ = bf16[272,256]{1,0:T(8,128)(2,1)S(1)} collective-permute-done((bf16[272,256]{1,0:T(8,128)(2,1)S(1)}, bf16[272,256]{1,0:T(8,128)(2,1)S(1)}, u32[]{:S(2)}, u32[]{:S(2)}) %collective-permute-start.1) | collective-permute-done | bytes 139296 | tf_op jit(solution)/shard_map/ppermute | solution.py:38
  20.9 1.0 %score.2 = (f32[32,256]{1,0:T(8,128)S(1)}, f32[32,256]{1,0:T(8,128)S(1)}) custom-call(bf16[512,512]{1,0:T(8,128)(2,1)S(1)} %get-tuple-element.32.map_ref, f32[1024,128]{1,0:T(8,128)S(1)} %get-tuple-element.33.cos_ref, f32[1024,128]{1,0:T(8,128)S(1)} %get-tuple-element.34.sin_ref, f32[8,128]{1,0:T(8,128)S(1)} %get-tuple-element.35.turn_ref, ...), custom_call_target="tpu_custom_call" | custom-call | bytes 3145728 | tf_op jit(solution)/shard_map/score/pallas_call | solution.py:374
  22.0 0.3 compact.1.rest_4_
  22.3 0.6 %collective-permute-start.8 = (bf16[512,256]{1,0:T(8,128)(2,1)S(1)}, bf16[512,256]{1,0:T(8,128)(2,1)S(1)}, u32[]{:S(2)}, u32[]{:S(2)}) collective-permute-start(bf16[512,256]{1,0:T(8,128)(2,1)S(1)} %compact.1.rest_4_), channel_id=1, source_target_pairs={{0,2},{2,0},{1,3},{3,1},{4,6},{6,4},{5,7},{7,5},{8,10},{10,8},{9,1... | collective-permute-start | bytes 786440 | tf_op jit(solution)/shard_map/ppermute | solution.py:38
  23.0 2.4 %collective-permute-start.3 = (f32[32,256]{1,0:T(8,128)S(1)}, f32[32,256]{1,0:T(8,128)S(1)}, u32[]{:S(2)}, u32[]{:S(2)}) collective-permute-start(f32[32,256]{1,0:T(8,128)S(1)} %get-tuple-element.40), channel_id=1, source_target_pairs={{0,12},{4,8},{8,4},{12,0},{1,13},{5,9},{9,5},{13,1},{2,14},{6,10},... | collective-permute-start | bytes 98312 | tf_op jit(solution)/shard_map/ppermute | solution.py:38
  25.4 1.0 %score.3 = (f32[32,256]{1,0:T(8,128)S(1)}, f32[32,256]{1,0:T(8,128)S(1)}) custom-call(bf16[512,512]{1,0:T(8,128)(2,1)S(1)} %get-tuple-element.32.map_ref, f32[1024,128]{1,0:T(8,128)S(1)} %get-tuple-element.33.cos_ref, f32[1024,128]{1,0:T(8,128)S(1)} %get-tuple-element.34.sin_ref, f32[8,128]{1,0:T(8,128)S(1)} %get-tuple-element.35.turn_ref, ...), custom_call_target="tpu_custom_call" | custom-call | bytes 3145728 | tf_op jit(solution)/shard_map/score/pallas_call | solution.py:374
  26.4 1.0 %collective-permute-start.7 = (f32[32,256]{1,0:T(8,128)S(1)}, f32[32,256]{1,0:T(8,128)S(1)}, u32[]{:S(2)}, u32[]{:S(2)}) collective-permute-start(f32[32,256]{1,0:T(8,128)S(1)} %get-tuple-element.45), channel_id=1, source_target_pairs={{0,4},{4,0},{8,12},{12,8},{1,5},{5,1},{9,13},{13,9},{2,6},{6,2},{1... | collective-permute-start | bytes 98312 | tf_op jit(solution)/shard_map/ppermute | solution.py:38
  27.4 1.6 %collective-permute-done.3.rest_0_ = f32[32,256]{1,0:T(8,128)S(1)} collective-permute-done((f32[32,256]{1,0:T(8,128)S(1)}, f32[32,256]{1,0:T(8,128)S(1)}, u32[]{:S(2)}, u32[]{:S(2)}) %collective-permute-start.3) | collective-permute-done | bytes 32800 | tf_op jit(solution)/shard_map/ppermute | solution.py:38
  29.1 1.3 %collective-permute-done.7.rest_2_ = f32[32,256]{1,0:T(8,128)S(1)} collective-permute-done((f32[32,256]{1,0:T(8,128)S(1)}, f32[32,256]{1,0:T(8,128)S(1)}, u32[]{:S(2)}, u32[]{:S(2)}) %collective-permute-start.7) | collective-permute-done | bytes 32800 | tf_op jit(solution)/shard_map/ppermute | solution.py:38
  30.3 0.5 %attend.1.refs_0_ = bf16[1,4096]{1,0:T(2,128)(2,1)S(1)} custom-call(bf16[512,512]{1,0:T(8,128)(2,1)S(1)} %get-tuple-element.30.map_ref, s32[1,1024]{1,0:T(1,128)S(1)} %get-tuple-element.31.after_ref.place_ref, f32[32,256]{1,0:T(8,128)S(1)} %collective-permute-done.3.rest_0_, f32[32,256]{1,0:T(8,128)S(1)} %collective-permute-done.4.rest_1_, ...), custom_call_target="tpu_custom_call" | custom-call | tf_op jit(solution)/shard_map/attend/pallas_call | solution.py:398
  30.9 0.1 collective-permute-start.9
  31.0 1.2 %collective-permute-done.9.refs_1_ = bf16[1,4096]{1,0:T(2,128)(2,1)S(1)} collective-permute-done((bf16[1,4096]{1,0:T(2,128)(2,1)S(1)}, bf16[1,4096]{1,0:T(2,128)(2,1)S(1)}, u32[]{:S(2)}, u32[]{:S(2)}) %collective-permute-start.9) | collective-permute-done | bytes 8224 | tf_op jit(solution)/shard_map/ppermute | solution.py:38
  32.2 1.5 %collective-permute-start.10 = (bf16[2,4096]{1,0:T(2,128)(2,1)S(1)}, bf16[2,4096]{1,0:T(2,128)(2,1)S(1)}, u32[]{:S(2)}, u32[]{:S(2)}) collective-permute-start(bf16[2,4096]{1,0:T(2,128)(2,1)S(1)} %join.1.rest_3_), channel_id=1, source_target_pairs={{0,12},{4,8},{8,4},{12,0},{1,13},{5,9},{9,5},{13,1},{2,14},{6,10},... | collective-permute-start | bytes 49160 | tf_op jit(solution)/shard_map/ppermute | solution.py:38
  33.7 1.0 %collective-permute-start.11 = (bf16[2,4096]{1,0:T(2,128)(2,1)S(1)}, bf16[2,4096]{1,0:T(2,128)(2,1)S(1)}, u32[]{:S(2)}, u32[]{:S(2)}) collective-permute-start(bf16[2,4096]{1,0:T(2,128)(2,1)S(1)} %join.1.rest_3_), channel_id=1, source_target_pairs={{0,8},{4,12},{8,0},{12,4},{1,9},{5,13},{9,1},{13,5},{2,10},{6,14},... | collective-permute-start | bytes 49160 | tf_op jit(solution)/shard_map/ppermute | solution.py:38
  34.7 1.9 %collective-permute-start.12 = (bf16[2,4096]{1,0:T(2,128)(2,1)S(1)}, bf16[2,4096]{1,0:T(2,128)(2,1)S(1)}, u32[]{:S(2)}, u32[]{:S(2)}) collective-permute-start(bf16[2,4096]{1,0:T(2,128)(2,1)S(1)} %join.1.rest_3_), channel_id=1, source_target_pairs={{0,4},{4,0},{8,12},{12,8},{1,5},{5,1},{9,13},{13,9},{2,6},{6,2},{1... | collective-permute-start | bytes 49160 | tf_op jit(solution)/shard_map/ppermute | solution.py:38
  36.6 1.3 %collective-permute-done.10.rest_0_ = bf16[2,4096]{1,0:T(2,128)(2,1)S(1)} collective-permute-done((bf16[2,4096]{1,0:T(2,128)(2,1)S(1)}, bf16[2,4096]{1,0:T(2,128)(2,1)S(1)}, u32[]{:S(2)}, u32[]{:S(2)}) %collective-permute-start.10) | collective-permute-done | bytes 16416 | tf_op jit(solution)/shard_map/ppermute | solution.py:38
  37.9 0.5 %collective-permute-done.11.rest_1_ = bf16[2,4096]{1,0:T(2,128)(2,1)S(1)} collective-permute-done((bf16[2,4096]{1,0:T(2,128)(2,1)S(1)}, bf16[2,4096]{1,0:T(2,128)(2,1)S(1)}, u32[]{:S(2)}, u32[]{:S(2)}) %collective-permute-start.11) | collective-permute-done | bytes 16416 | tf_op jit(solution)/shard_map/ppermute | solution.py:38
  38.3 0.2 collective-permute-done.12.rest_2_
  38.5 1.2 %project.1 = (f32[2,1024]{1,0:T(2,128)S(1)}, f32[2,1024]{1,0:T(2,128)S(1)}, f32[2,1024]{1,0:T(2,128)S(1)}, f32[2,1024]{1,0:T(2,128)S(1)}) custom-call(bf16[4096,1024]{1,0:T(8,128)(2,1)S(1)} %copy-done, bf16[2,4096]{1,0:T(2,128)(2,1)S(1)} %collective-permute-done.10.rest_0_, bf16[2,4096]{1,0:T(2,128)(2,1)S(1)} %collective-permute-done.11.rest_1_, ...), custom_call_target="tpu_custom_call" | custom-call | tf_op jit(solution)/shard_map/project/pallas_call | solution.py:411
  39.7 0.2 collective-permute-start.13
  39.9 1.4 %collective-permute-start.14 = (f32[2,1024]{1,0:T(2,128)S(1)}, f32[2,1024]{1,0:T(2,128)S(1)}, u32[]{:S(2)}, u32[]{:S(2)}) collective-permute-start(f32[2,1024]{1,0:T(2,128)S(1)} %get-tuple-element.48), channel_id=1, source_target_pairs={{0,2},{1,3},{2,0},{3,1},{4,6},{5,7},{6,4},{7,5},{8,10},{9,11},{10,... | collective-permute-start | bytes 24584 | tf_op jit(solution)/shard_map/ppermute | solution.py:38
  41.4 0.3 collective-permute-start.15
  41.7 1.3 %collective-permute-done.13.refs_0_ = f32[2,1024]{1,0:T(2,128)S(1)} collective-permute-done((f32[2,1024]{1,0:T(2,128)S(1)}, f32[2,1024]{1,0:T(2,128)S(1)}, u32[]{:S(2)}, u32[]{:S(2)}) %collective-permute-start.13) | collective-permute-done | bytes 8224 | tf_op jit(solution)/shard_map/ppermute | solution.py:38
  42.9 0.6 %collective-permute-done.14.refs_1_ = f32[2,1024]{1,0:T(2,128)S(1)} collective-permute-done((f32[2,1024]{1,0:T(2,128)S(1)}, f32[2,1024]{1,0:T(2,128)S(1)}, u32[]{:S(2)}, u32[]{:S(2)}) %collective-permute-start.14) | collective-permute-done | bytes 8224 | tf_op jit(solution)/shard_map/ppermute | solution.py:38
  43.6 0.6 %finish.1 = bf16[1,2,2048]{2,1,0:T(2,128)(2,1)} custom-call(f32[2,1024]{1,0:T(2,128)S(1)} %collective-permute-done.13.refs_0_, f32[2,1024]{1,0:T(2,128)S(1)} %collective-permute-done.14.refs_1_, f32[2,1024]{1,0:T(2,128)S(1)} %collective-permute-done.15.refs_2_, f32[2,1024]{1,0:T(2,128)S(1)} %get-tuple-element.50.refs_3_), custom_call_target="tpu_custom_call" | custom-call | tf_op jit(solution)/shard_map/finish/pallas_call | solution.py:420
  (11 shorter events, 0.1 us)
Async XLA Ops:
  0.0 38.5 %copy-start = (bf16[4096,1024]{1,0:T(8,128)(2,1)S(1)}, bf16[4096,1024]{1,0:T(8,128)(2,1)}, u32[]{:S(2)}) copy-start(bf16[4096,1024]{1,0:T(8,128)(2,1)} %weight_ref.1) | copy-start | bytes 25165828
  2.8 18.1 %collective-permute-start.2 = (bf16[512,256]{1,0:T(8,128)(2,1)S(1)}, bf16[512,256]{1,0:T(8,128)(2,1)S(1)}, u32[]{:S(2)}, u32[]{:S(2)}) collective-permute-start(bf16[512,256]{1,0:T(8,128)(2,1)S(1)} %get-tuple-element.39.rest_2_), channel_id=1, source_target_pairs={{0,2},{2,0},{1,3},{3,1},{4,6},{6,4},{5,7},{7,5},{8,10},{10,8},{9,1... | collective-permute-start | bytes 786440 | tf_op jit(solution)/shard_map/ppermute | solution.py:38
  5.8 8.4 %collective-permute-start = (bf16[272,256]{1,0:T(8,128)(2,1)S(1)}, bf16[272,256]{1,0:T(8,128)(2,1)S(1)}, u32[]{:S(2)}, u32[]{:S(2)}) collective-permute-start(bf16[272,256]{1,0:T(8,128)(2,1)S(1)} %get-tuple-element.37), channel_id=1, source_target_pairs={{0,12},{4,8},{8,4},{12,0},{1,13},{5,9},{9,5},{13,1},{2,14},{6,10},... | collective-permute-start | bytes 417800 | tf_op jit(solution)/shard_map/ppermute | solution.py:38
  9.4 11.5 %collective-permute-start.1 = (bf16[272,256]{1,0:T(8,128)(2,1)S(1)}, bf16[272,256]{1,0:T(8,128)(2,1)S(1)}, u32[]{:S(2)}, u32[]{:S(2)}) collective-permute-start(bf16[272,256]{1,0:T(8,128)(2,1)S(1)} %get-tuple-element.38), channel_id=1, source_target_pairs={{0,8},{4,12},{8,0},{12,4},{1,9},{5,13},{9,1},{13,5},{2,10},{6,14},... | collective-permute-start | bytes 417800 | tf_op jit(solution)/shard_map/ppermute | solution.py:38
  11.6 10.4 %collective-permute-start.5 = (bf16[272,256]{1,0:T(8,128)(2,1)S(1)}, bf16[272,256]{1,0:T(8,128)(2,1)S(1)}, u32[]{:S(2)}, u32[]{:S(2)}) collective-permute-start(bf16[272,256]{1,0:T(8,128)(2,1)S(1)} %get-tuple-element.42), channel_id=1, source_target_pairs={{0,4},{4,0},{8,12},{12,8},{1,5},{5,1},{9,13},{13,9},{2,6},{6,2},{1... | collective-permute-start | bytes 417800 | tf_op jit(solution)/shard_map/ppermute | solution.py:38
  12.4 13.0 %collective-permute-start.6 = (bf16[512,256]{1,0:T(8,128)(2,1)S(1)}, bf16[512,256]{1,0:T(8,128)(2,1)S(1)}, u32[]{:S(2)}, u32[]{:S(2)}) collective-permute-start(bf16[512,256]{1,0:T(8,128)(2,1)S(1)} %get-tuple-element.44.rest_2_), channel_id=1, source_target_pairs={{0,2},{2,0},{1,3},{3,1},{4,6},{6,4},{5,7},{7,5},{8,10},{10,8},{9,1... | collective-permute-start | bytes 786440 | tf_op jit(solution)/shard_map/ppermute | solution.py:38
  22.3 8.0 %collective-permute-start.8 = (bf16[512,256]{1,0:T(8,128)(2,1)S(1)}, bf16[512,256]{1,0:T(8,128)(2,1)S(1)}, u32[]{:S(2)}, u32[]{:S(2)}) collective-permute-start(bf16[512,256]{1,0:T(8,128)(2,1)S(1)} %compact.1.rest_4_), channel_id=1, source_target_pairs={{0,2},{2,0},{1,3},{3,1},{4,6},{6,4},{5,7},{7,5},{8,10},{10,8},{9,1... | collective-permute-start | bytes 786440 | tf_op jit(solution)/shard_map/ppermute | solution.py:38
  22.9 6.2 %collective-permute-start.4 = (f32[32,256]{1,0:T(8,128)S(1)}, f32[32,256]{1,0:T(8,128)S(1)}, u32[]{:S(2)}, u32[]{:S(2)}) collective-permute-start(f32[32,256]{1,0:T(8,128)S(1)} %get-tuple-element.41.after_ref), channel_id=1, source_target_pairs={{0,8},{4,12},{8,0},{12,4},{1,9},{5,13},{9,1},{13,5},{2,10},{6,14},... | collective-permute-start | bytes 98312 | tf_op jit(solution)/shard_map/ppermute | solution.py:38
  23.0 6.1 %collective-permute-start.3 = (f32[32,256]{1,0:T(8,128)S(1)}, f32[32,256]{1,0:T(8,128)S(1)}, u32[]{:S(2)}, u32[]{:S(2)}) collective-permute-start(f32[32,256]{1,0:T(8,128)S(1)} %get-tuple-element.40), channel_id=1, source_target_pairs={{0,12},{4,8},{8,4},{12,0},{1,13},{5,9},{9,5},{13,1},{2,14},{6,10},... | collective-permute-start | bytes 98312 | tf_op jit(solution)/shard_map/ppermute | solution.py:38
  26.4 3.9 %collective-permute-start.7 = (f32[32,256]{1,0:T(8,128)S(1)}, f32[32,256]{1,0:T(8,128)S(1)}, u32[]{:S(2)}, u32[]{:S(2)}) collective-permute-start(f32[32,256]{1,0:T(8,128)S(1)} %get-tuple-element.45), channel_id=1, source_target_pairs={{0,4},{4,0},{8,12},{12,8},{1,5},{5,1},{9,13},{13,9},{2,6},{6,2},{1... | collective-permute-start | bytes 98312 | tf_op jit(solution)/shard_map/ppermute | solution.py:38
  30.9 1.2 %collective-permute-start.9 = (bf16[1,4096]{1,0:T(2,128)(2,1)S(1)}, bf16[1,4096]{1,0:T(2,128)(2,1)S(1)}, u32[]{:S(2)}, u32[]{:S(2)}) collective-permute-start(bf16[1,4096]{1,0:T(2,128)(2,1)S(1)} %attend.1.refs_0_), channel_id=1, source_target_pairs={{0,1},{1,0},{2,3},{3,2},{4,5},{5,4},{6,7},{7,6},{8,9},{9,8},{10,11... | collective-permute-start | bytes 24584 | tf_op jit(solution)/shard_map/ppermute | solution.py:38
  32.2 5.7 %collective-permute-start.10 = (bf16[2,4096]{1,0:T(2,128)(2,1)S(1)}, bf16[2,4096]{1,0:T(2,128)(2,1)S(1)}, u32[]{:S(2)}, u32[]{:S(2)}) collective-permute-start(bf16[2,4096]{1,0:T(2,128)(2,1)S(1)} %join.1.rest_3_), channel_id=1, source_target_pairs={{0,12},{4,8},{8,4},{12,0},{1,13},{5,9},{9,5},{13,1},{2,14},{6,10},... | collective-permute-start | bytes 49160 | tf_op jit(solution)/shard_map/ppermute | solution.py:38
  33.7 4.6 %collective-permute-start.11 = (bf16[2,4096]{1,0:T(2,128)(2,1)S(1)}, bf16[2,4096]{1,0:T(2,128)(2,1)S(1)}, u32[]{:S(2)}, u32[]{:S(2)}) collective-permute-start(bf16[2,4096]{1,0:T(2,128)(2,1)S(1)} %join.1.rest_3_), channel_id=1, source_target_pairs={{0,8},{4,12},{8,0},{12,4},{1,9},{5,13},{9,1},{13,5},{2,10},{6,14},... | collective-permute-start | bytes 49160 | tf_op jit(solution)/shard_map/ppermute | solution.py:38
  34.7 3.8 %collective-permute-start.12 = (bf16[2,4096]{1,0:T(2,128)(2,1)S(1)}, bf16[2,4096]{1,0:T(2,128)(2,1)S(1)}, u32[]{:S(2)}, u32[]{:S(2)}) collective-permute-start(bf16[2,4096]{1,0:T(2,128)(2,1)S(1)} %join.1.rest_3_), channel_id=1, source_target_pairs={{0,4},{4,0},{8,12},{12,8},{1,5},{5,1},{9,13},{13,9},{2,6},{6,2},{1... | collective-permute-start | bytes 49160 | tf_op jit(solution)/shard_map/ppermute | solution.py:38
  39.7 3.2 %collective-permute-start.13 = (f32[2,1024]{1,0:T(2,128)S(1)}, f32[2,1024]{1,0:T(2,128)S(1)}, u32[]{:S(2)}, u32[]{:S(2)}) collective-permute-start(f32[2,1024]{1,0:T(2,128)S(1)} %get-tuple-element.47), channel_id=1, source_target_pairs={{0,3},{1,2},{2,1},{3,0},{4,7},{5,6},{6,5},{7,4},{8,11},{9,10},{10,... | collective-permute-start | bytes 24584 | tf_op jit(solution)/shard_map/ppermute | solution.py:38
  39.9 3.7 %collective-permute-start.14 = (f32[2,1024]{1,0:T(2,128)S(1)}, f32[2,1024]{1,0:T(2,128)S(1)}, u32[]{:S(2)}, u32[]{:S(2)}) collective-permute-start(f32[2,1024]{1,0:T(2,128)S(1)} %get-tuple-element.48), channel_id=1, source_target_pairs={{0,2},{1,3},{2,0},{3,1},{4,6},{5,7},{6,4},{7,5},{8,10},{9,11},{10,... | collective-permute-start | bytes 24584 | tf_op jit(solution)/shard_map/ppermute | solution.py:38
  41.4 2.2 %collective-permute-start.15 = (f32[2,1024]{1,0:T(2,128)S(1)}, f32[2,1024]{1,0:T(2,128)S(1)}, u32[]{:S(2)}, u32[]{:S(2)}) collective-permute-start(f32[2,1024]{1,0:T(2,128)S(1)} %get-tuple-element.49), channel_id=1, source_target_pairs={{0,1},{1,0},{2,3},{3,2},{4,5},{5,4},{6,7},{7,6},{8,9},{9,8},{10,11... | collective-permute-start | bytes 24584 | tf_op jit(solution)/shard_map/ppermute | solution.py:38

commit v7 on v5

--- a/solution.py
+++ b/solution.py
@@ -75,9 +75,11 @@
     return jnp.concatenate([rows[:, i : i + HEAD_SIZE] for i in range(0, lanes, HEAD_SIZE)], axis=0)
 
 
-def gather_kernel(pools, sel_ref, lat_ref, query_ref, near_ref, far_ref, *rest):
-    value_refs = rest[:-2]
-    raw, sems = rest[-2:]
+def gather_kernel(pools, sel_ref, lat_ref, query_ref, keys_ref, *rest):
+    value_refs = rest[:pools]
+    raw, line, sems = rest[pools:]
+    load = pltpu.make_async_copy(query_ref.at[0], line, sems.at[pools * CAP])
+    load.start()
     shard_blocks = lat_ref.shape[2] // BLOCK
     columns = lat_ref.shape[3]
     width = columns // 2
@@ -94,7 +96,6 @@
                 sems.at[k * CAP + c],
             )
             copies[k, c].start()
-    queries = heads_to_rows(query_ref[0].astype(jnp.float32), value_refs[0].shape[1]).astype(jnp.bfloat16)
     chunk = min(4 * LANE, columns)
     half = chunk // 2
     source = lax.broadcasted_iota(jnp.int32, (chunk, chunk), 0)
@@ -102,16 +103,17 @@
     within = target & (half - 1)
     wanted = ((within >> 6) << 7) + (within & (LANE - 1)) + jnp.where(target >= half, LANE, 0)
     pick = (source == wanted).astype(jnp.float32).astype(jnp.bfloat16)
+    load.wait()
+    queries = heads_to_rows(line[...].astype(jnp.float32), width).astype(jnp.bfloat16)
+    for copy in copies.values():
+        copy.wait()
     for k in range(pools - 1, -1, -1):
-        for c in range(CAP):
-            copies[k, c].wait()
-        keys_ref, at = (far_ref, k - pools // 2) if k >= pools // 2 else (near_ref, k)
         for j in range(columns // chunk):
             packed = jnp.dot(
                 raw[k * rows : (k + 1) * rows, j * chunk : (j + 1) * chunk], pick,
                 preferred_element_type=jnp.float32,
             ).astype(jnp.bfloat16)
-            keys_ref[at * rows : (at + 1) * rows, j * half : (j + 1) * half] = packed[:, :half]
+            keys_ref[k * rows : (k + 1) * rows, j * half : (j + 1) * half] = packed[:, :half]
             value_refs[k][:rows, j * half : (j + 1) * half] = packed[:, half:]
         value_refs[k][rows:, :] = queries
 
@@ -158,58 +160,61 @@
         load.wait()
 
 
-def score_kernel(first, count, heads, pools, map_ref, cos_ref, sin_ref, turn_ref, live_ref, after_ref, *rest):
-    del after_ref
+def rebuild_kernel(pools, heads, map_ref, cos_ref, sin_ref, *rest):
     key_refs = rest[:heads]
-    pay_refs = rest[heads : heads + count][::-1]
-    out_refs = rest[heads + count :]
+    out_ref = rest[heads]
     head = lax.axis_index("heads")
     width = key_refs[0].shape[1]
-    groups = map_ref.shape[1] // HEAD_SIZE
     rows = CAP * BLOCK
     maps = []
     for j in range(heads):
         owner = head ^ j
         maps.append(map_ref[pl.ds(pl.multiple_of(owner * width, width), width), :])
-    for i in range(count):
-        k = first + i
+    for k in range(pools):
+        at = slice(k * rows, (k + 1) * rows)
+        rebuilt = jnp.dot(key_refs[0][at, :], maps[0], preferred_element_type=jnp.float32)
+        for j in range(1, heads):
+            rebuilt += jnp.dot(key_refs[j][at, :], maps[j], preferred_element_type=jnp.float32)
+        cosine = cos_ref[at, :]
+        sine = sin_ref[at, :]
+        for g in range(map_ref.shape[1] // HEAD_SIZE):
+            lanes = slice(g * HEAD_SIZE, (g + 1) * HEAD_SIZE)
+            one = rebuilt[:, lanes]
+            out_ref[at, lanes] = (one * cosine + pltpu.roll(one, HEAD_SIZE // 2, 1) * sine).astype(jnp.bfloat16)
+
+
+def score_kernel(pools, turn_ref, live_ref, place_ref, key_ref, *rest):
+    pay_refs = rest[:pools][::-1]
+    dense_ref = rest[pools]
+    out_refs = rest[pools + 1 :]
+    groups = key_ref.shape[1] // HEAD_SIZE
+    rows = CAP * BLOCK
+    width = dense_ref.shape[1]
+    kept = dense_ref.shape[0] // BLOCK
+    for k in range(pools - 1, -1, -1):
         live = live_ref[k : k + 1, :] > 0
-        query = rows_to_heads(pay_refs[i][rows:, :].astype(jnp.float32))
+        query = rows_to_heads(pay_refs[k][rows:, :].astype(jnp.float32))
         query = query * turn_ref[k : k + 1, :] + pltpu.roll(query, HEAD_SIZE // 2, 1) * turn_ref[
             pools + k : pools + k + 1, :
         ]
-        queries = query.astype(jnp.bfloat16)
-        at = slice(i * rows, (i + 1) * rows)
-        rebuilt = jnp.dot(key_refs[0][at, :], maps[0], preferred_element_type=jnp.float32)
-        for j in range(1, heads):
-            rebuilt += jnp.dot(key_refs[j][at, :], maps[j], preferred_element_type=jnp.float32)
-        cosine = cos_ref[k * rows : (k + 1) * rows, :]
-        sine = sin_ref[k * rows : (k + 1) * rows, :]
+        query = query.astype(jnp.bfloat16)
         for g in range(groups):
-            one = rebuilt[:, g * HEAD_SIZE : (g + 1) * HEAD_SIZE]
-            turned = (one * cosine + pltpu.roll(one, HEAD_SIZE // 2, 1) * sine).astype(jnp.bfloat16)
             mine = slice(g * QUERY_PER_GROUP, (g + 1) * QUERY_PER_GROUP)
             scores = lax.dot_general(
-                queries[mine, :], turned, (((1,), (1,)), ((), ())), preferred_element_type=jnp.float32
+                query[mine, :], key_ref[k * rows : (k + 1) * rows, g * HEAD_SIZE : (g + 1) * HEAD_SIZE],
+                (((1,), (1,)), ((), ())), preferred_element_type=jnp.float32,
             ) * (HEAD_SIZE ** -0.5)
-            out_refs[i][mine, :] = jnp.where(live, scores, MASKED)
-
-
-def compact_kernel(pools, place_ref, after_ref, *rest):
-    del after_ref
-    value_refs = rest[:pools][::-1]
-    out_ref = rest[pools]
-    width = out_ref.shape[1]
-    spare = pools * CAP - out_ref.shape[0] // BLOCK
-    for i in range(out_ref.shape[0] // BLOCK):
+            out_refs[k][mine, :] = jnp.where(live, scores, MASKED)
+    spare = pools * CAP - kept
+    for i in range(kept):
         chosen = jnp.zeros((BLOCK, width), jnp.float32)
         for slot in range(i, i + spare + 1):
             place = place_ref[:, slot * BLOCK : slot * BLOCK + LANE]
             place = jnp.concatenate([place] * (width // LANE), axis=1)
             k, c = slot // CAP, slot % CAP
-            block = value_refs[k][c * BLOCK : (c + 1) * BLOCK, :].astype(jnp.float32)
+            block = pay_refs[k][c * BLOCK : (c + 1) * BLOCK, :].astype(jnp.float32)
             chosen = jnp.where(place == i, block, chosen)
-        out_ref[i * BLOCK : (i + 1) * BLOCK, :] = chosen.astype(jnp.bfloat16)
+        dense_ref[i * BLOCK : (i + 1) * BLOCK, :] = chosen.astype(jnp.bfloat16)
 
 
 def attend_kernel(pools, heads, map_ref, place_ref, *rest):
@@ -263,7 +268,7 @@
 
 
 def project_kernel(pools, heads, reps, weight_ref, *rest):
-    row_refs = rest[:pools][::-1]
+    row_refs = rest[:pools]
     out_refs = rest[pools:-1]
     acc = rest[-1]
     left = jnp.concatenate([ref[...].astype(jnp.float32) for ref in row_refs], axis=0).astype(jnp.bfloat16)
@@ -320,24 +325,22 @@
         taken = {step: swap(blocks[step], axis, size, step) for step in range(size - 1, 0, -1)}
         return [blocks[0]] + [taken[step] for step in range(1, size)]
 
-    middle = pools // 2
     query_rows = queries.shape[2] // width
     packed = pl.pallas_call(
         functools.partial(gather_kernel, pools),
-        out_shape=[shape((middle * rows, width), bf16)] * 2
+        out_shape=[shape((pools * rows, width), bf16)]
         + [shape((rows + query_rows, width), bf16)] * pools,
-        in_specs=[SMEM, HBM, VMEM],
-        out_specs=[VMEM] * (pools + 2),
+        in_specs=[SMEM, HBM, HBM],
+        out_specs=[VMEM] * (pools + 1),
         scratch_shapes=[
             pltpu.VMEM((pools * rows, 2 * width), bf16),
-            pltpu.SemaphoreType.DMA((pools * CAP,)),
+            pltpu.VMEM((1, queries.shape[2]), bf16),
+            pltpu.SemaphoreType.DMA((pools * CAP + 1,)),
         ],
         compiler_params=params(16),
         name="gather",
     )(in_hbm(selected), in_hbm(latents), in_hbm(queries))
-    near, far, values = packed[0], packed[1], packed[2:]
-    far_parts = exchange(far, "heads", heads)
-    near_parts = exchange(near, "heads", heads)
+    keys, values = packed[0], packed[1:]
 
     cosine, sine, turn, live, place, key_maps, value_maps, held = pl.pallas_call(
         functools.partial(table_kernel, pools, shard_blocks),
@@ -350,39 +353,32 @@
         scratch_shapes=[pltpu.SemaphoreType.DMA((2,))],
         input_output_aliases={5: 7},
         compiler_params=params(16),
-        cost_estimate=pl.CostEstimate(flops=0, transcendentals=0, bytes_accessed=10 << 20),
         name="tables",
     )(
         in_hbm(selected), in_hbm(lengths), in_hbm(freq), in_hbm(key_latent_maps),
         in_hbm(value_latent_maps), values[1],
     )
+    key_parts = exchange(keys, "heads", heads)
     value_parts = scatter([values[0], held, *values[2:]], "pool", pools)
 
-    def score(first, count, key_parts, after):
-        pays = value_parts[first : first + count]
-        return pl.pallas_call(
-            functools.partial(score_kernel, first, count, heads, pools),
-            out_shape=[shape((own_heads, rows), f32)] * count,
-            in_specs=[VMEM] * 5 + [ANY] + [VMEM] * (heads + count),
-            out_specs=[VMEM] * count,
-            compiler_params=params(20),
-            cost_estimate=pl.CostEstimate(flops=0, transcendentals=0, bytes_accessed=3 << 20),
-            name="score",
-        )(key_maps, cosine, sine, turn, live, after, *key_parts, *pays[::-1])
-
-    far_scores = score(middle, middle, far_parts, place)
-    dense = pl.pallas_call(
-        functools.partial(compact_kernel, pools),
-        out_shape=shape((sel_count * BLOCK, width), bf16),
-        in_specs=[VMEM, ANY] + [VMEM] * pools,
+    turned = pl.pallas_call(
+        functools.partial(rebuild_kernel, pools, heads),
+        out_shape=shape((pools * rows, own_heads // QUERY_PER_GROUP * HEAD_SIZE), bf16),
+        in_specs=[VMEM] * (3 + heads),
         out_specs=VMEM,
+        compiler_params=params(20),
+        name="rebuild",
+    )(key_maps, cosine, sine, *key_parts)
+    dense, *scores = pl.pallas_call(
+        functools.partial(score_kernel, pools),
+        out_shape=[shape((sel_count * BLOCK, width), bf16)] + [shape((own_heads, rows), f32)] * pools,
+        in_specs=[VMEM] * (4 + pools),
+        out_specs=[VMEM] * (1 + pools),
         compiler_params=params(16),
-        cost_estimate=pl.CostEstimate(flops=0, transcendentals=0, bytes_accessed=3 << 20),
-        name="compact",
-    )(place, far_scores[0], *value_parts[::-1])
-    near_scores = score(0, middle, near_parts, dense)
+        name="score",
+    )(turn, live, place, turned, *value_parts[::-1])
     dense_parts = exchange(dense, "heads", heads)
-    score_parts = scatter([*near_scores, *far_scores], "pool", pools)
+    score_parts = scatter(scores, "pool", pools)
 
     mine = pl.pallas_call(
         functools.partial(attend_kernel, pools, heads),
@@ -405,7 +401,7 @@
         scratch_shapes=[pltpu.VMEM((pools * reps, own_columns), f32)],
         compiler_params=params(24),
         name="project",
-    )(in_vmem(out_weight), *row_parts[::-1])
+    )(in_vmem(out_weight), *row_parts)
     return pl.pallas_call(
         functools.partial(finish_kernel, heads, reps),
         out_shape=shape((1, each, reps * own_columns), bf16),

time: 45.5 us -> 43.8 us (0.963)
  waiting for transfers between devices: 16.1 us -> 14.8 us
  Pallas kernels: 10.7 us -> 9.71 us
  starting transfers between devices: 18.4 us -> 18.9 us
    ppermute x16 -> x15, waiting for transfers between devices: 16.1 us -> 14.8 us  [swap(): return lax.ppermute(value, axes, [(i, i ^ step) for i in range(size)])]
    pallas_call x3 -> x2, Pallas kernels: 2.36 us -> 1.42 us  [the longest x1 0.85 us: per_device(): pl.pallas_call(functools.partial(rebuild_kernel, pools, heads), out_shape...]
    ppermute x16 -> x15, starting transfers between devices: 18.4 us -> 18.9 us  [swap(): return lax.ppermute(value, axes, [(i, i ^ step) for i in range(size)])]
  transfers between devices with their start and end apart: 16 -> 15, of which waited for: 11 -> 9; matrix products, arithmetic and copies ran while one was open for 0% -> 0% of each run, Pallas kernels for 12% -> 9%
where the time goes in v7:
time: 43.8 us; the launch traced here: 43.5 us
  starting transfers between devices  18.9 us (43%)
  waiting for transfers between devices  14.8 us (34%)
  Pallas kernels  9.71 us (22%)
    ppermute x15, starting transfers between devices, swap(): return lax.ppermute(value, axes, [(i, i ^ step) for i in range(size)])  18.9 us
    ppermute x15, waiting for transfers between devices, swap(): return lax.ppermute(value, axes, [(i, i ^ step) for i in range(size)])  14.8 us
    pallas_call x1, Pallas kernels, per_device(): pl.pallas_call(functools.partial(table_kernel, pools, shard_blocks), out_...  2.97 us
    pallas_call x1, Pallas kernels, per_device(): pl.pallas_call(functools.partial(gather_kernel, pools), out_shape=[shape(...  2.94 us
    pallas_call x1, Pallas kernels, per_device(): pl.pallas_call(functools.partial(project_kernel, pools, heads, reps), out...  1.21 us
  transfers between devices with their start and end apart: 15, of which 9 were waited for; matrix products, arithmetic and copies ran while one was open for 0% of the time, Pallas kernels for 9%

profile of v7, /device:TPU:0, one launch (start us, length us, event | category | flops | bytes accessed | tf_op | source)
XLA Modules:
  0.0 43.5 jit_solution(15467174913566691883)
XLA Ops:
  0.0 2.9 %gather.1 = (bf16[1024,256]{1,0:T(8,128)(2,1)S(1)}, bf16[272,256]{1,0:T(8,128)(2,1)S(1)}, bf16[272,256]{1,0:T(8,128)(2,1)S(1)}, bf16[272,256]{1,0:T(8,128)(2,1)S(1)}, bf16[272,256]{1,0:T(8,128)(2,1)S(1)}) custom-call(s32[1,4,4]{2,1,0:T(4,128)} %sel_ref.3, bf16[1,4,1024,512]{3,2,1,0:T(8,128)(2,1)} %lat_ref.1, bf16[1,1,4096]{2,1,0:T(2,128)(2,1)} %query_ref.1), custom_call_target="tpu_custom_call" | custom-call | tf_op jit(solution)/shard_map/gather/pallas_call | solution.py:329
  3.0 3.0 %collective-permute-start = (bf16[1024,256]{1,0:T(8,128)(2,1)S(1)}, bf16[1024,256]{1,0:T(8,128)(2,1)S(1)}, u32[]{:S(2)}, u32[]{:S(2)}) collective-permute-start(bf16[1024,256]{1,0:T(8,128)(2,1)S(1)} %get-tuple-element.35.rest_0_), channel_id=1, source_target_pairs={{0,2},{2,0},{1,3},{3,1},{4,6},{6,4},{5,7},{7,5},{8,10},{10,8},{9,1... | collective-permute-start | bytes 1572872 | tf_op jit(solution)/shard_map/ppermute | solution.py:35
  6.0 3.6 %collective-permute-start.1 = (bf16[272,256]{1,0:T(8,128)(2,1)S(1)}, bf16[272,256]{1,0:T(8,128)(2,1)S(1)}, u32[]{:S(2)}, u32[]{:S(2)}) collective-permute-start(bf16[272,256]{1,0:T(8,128)(2,1)S(1)} %get-tuple-element.36), channel_id=1, source_target_pairs={{0,12},{4,8},{8,4},{12,0},{1,13},{5,9},{9,5},{13,1},{2,14},{6,10},... | collective-permute-start | bytes 417800 | tf_op jit(solution)/shard_map/ppermute | solution.py:35
  9.6 0.0 collective-permute-start.2
  9.6 3.0 %tables.1 = (f32[1024,128]{1,0:T(8,128)S(1)}, f32[1024,128]{1,0:T(8,128)S(1)}, f32[8,128]{1,0:T(8,128)S(1)}, s32[4,256]{1,0:T(4,128)S(1)}, s32[1,1024]{1,0:T(1,1...) custom-call(s32[1,4,4]{2,1,0:T(4,128)} %sel_ref.3, ...), custom_call_target="tpu_custom_call", output_to_operand_aliasing={{7}: (5, {})} | custom-call | tf_op jit(solution)/shard_map/tables/pallas_call | solution.py:345
  12.5 0.8 %collective-permute-start.3 = (bf16[272,256]{1,0:T(8,128)(2,1)S(1)}, bf16[272,256]{1,0:T(8,128)(2,1)S(1)}, u32[]{:S(2)}, u32[]{:S(2)}) collective-permute-start(bf16[272,256]{1,0:T(8,128)(2,1)S(1)} %get-tuple-element.38), channel_id=1, source_target_pairs={{0,4},{4,0},{8,12},{12,8},{1,5},{5,1},{9,13},{13,9},{2,6},{6,2},{1... | collective-permute-start | bytes 417800 | tf_op jit(solution)/shard_map/ppermute | solution.py:35
  13.4 4.5 %collective-permute-done.rest_1_ = bf16[1024,256]{1,0:T(8,128)(2,1)S(1)} collective-permute-done((bf16[1024,256]{1,0:T(8,128)(2,1)S(1)}, bf16[1024,256]{1,0:T(8,128)(2,1)S(1)}, u32[]{:S(2)}, u32[]{:S(2)}) %collective-permute-start) | collective-permute-done | bytes 524320 | tf_op jit(solution)/shard_map/ppermute | solution.py:35
  17.9 0.9 %rebuild.1.key_ref = bf16[1024,512]{1,0:T(8,128)(2,1)S(1)} custom-call(bf16[512,512]{1,0:T(8,128)(2,1)S(1)} %get-tuple-element.32.map_ref, f32[1024,128]{1,0:T(8,128)S(1)} %get-tuple-element.33.cos_ref, f32[1024,128]{1,0:T(8,128)S(1)} %get-tuple-element.34.sin_ref, bf16[1024,256]{1,0:T(8,128)(2,1)S(1)} %get-tuple-element.35.rest_0_, ...), custom_call_target="tpu_custom_call" | custom-call | tf_op jit(solution)/shard_map/rebuild/pallas_call | solution.py:364
  18.7 0.0 collective-permute-done.1.rest_0_
  18.8 2.3 %collective-permute-done.2.rest_1_ = bf16[272,256]{1,0:T(8,128)(2,1)S(1)} collective-permute-done((bf16[272,256]{1,0:T(8,128)(2,1)S(1)}, bf16[272,256]{1,0:T(8,128)(2,1)S(1)}, u32[]{:S(2)}, u32[]{:S(2)}) %collective-permute-start.2) | collective-permute-done | bytes 139296 | tf_op jit(solution)/shard_map/ppermute | solution.py:35
  21.1 0.6 %score.1 = (bf16[512,256]{1,0:T(8,128)(2,1)S(1)}, f32[32,256]{1,0:T(8,128)S(1)}, f32[32,256]{1,0:T(8,128)S(1)}, f32[32,256]{1,0:T(8,128)S(1)}, f32[32,256]{1,0:T(8,128)S(1)}) custom-call(f32[8,128]{1,0:T(8,128)S(1)} %get-tuple-element.30.turn_ref, s32[4,256]{1,0:T(4,128)S(1)} %get-tuple-element.31.live_ref, s32[1,1024]{1,0:T(1,128)S(1)} %get-tuple-element.29.place_ref, ...), custom_call_target="tpu_custom_call" | custom-call | tf_op jit(solution)/shard_map/score/pallas_call | solution.py:372
  21.6 0.6 %collective-permute-start.7 = (bf16[512,256]{1,0:T(8,128)(2,1)S(1)}, bf16[512,256]{1,0:T(8,128)(2,1)S(1)}, u32[]{:S(2)}, u32[]{:S(2)}) collective-permute-start(bf16[512,256]{1,0:T(8,128)(2,1)S(1)} %get-tuple-element.44.rest_4_), channel_id=1, source_target_pairs={{0,2},{2,0},{1,3},{3,1},{4,6},{6,4},{5,7},{7,5},{8,10},{10,8},{9,1... | collective-permute-start | bytes 786440 | tf_op jit(solution)/shard_map/ppermute | solution.py:35
  22.2 2.5 %collective-permute-start.4 = (f32[32,256]{1,0:T(8,128)S(1)}, f32[32,256]{1,0:T(8,128)S(1)}, u32[]{:S(2)}, u32[]{:S(2)}) collective-permute-start(f32[32,256]{1,0:T(8,128)S(1)} %get-tuple-element.40), channel_id=1, source_target_pairs={{0,12},{4,8},{8,4},{12,0},{1,13},{5,9},{9,5},{13,1},{2,14},{6,10},... | collective-permute-start | bytes 98312 | tf_op jit(solution)/shard_map/ppermute | solution.py:35
  24.8 0.0 collective-permute-start.5
  24.8 1.9 %collective-permute-start.6 = (f32[32,256]{1,0:T(8,128)S(1)}, f32[32,256]{1,0:T(8,128)S(1)}, u32[]{:S(2)}, u32[]{:S(2)}) collective-permute-start(f32[32,256]{1,0:T(8,128)S(1)} %get-tuple-element.42), channel_id=1, source_target_pairs={{0,4},{4,0},{8,12},{12,8},{1,5},{5,1},{9,13},{13,9},{2,6},{6,2},{1... | collective-permute-start | bytes 98312 | tf_op jit(solution)/shard_map/ppermute | solution.py:35
  26.6 1.4 %collective-permute-done.4.rest_0_ = f32[32,256]{1,0:T(8,128)S(1)} collective-permute-done((f32[32,256]{1,0:T(8,128)S(1)}, f32[32,256]{1,0:T(8,128)S(1)}, u32[]{:S(2)}, u32[]{:S(2)}) %collective-permute-start.4) | collective-permute-done | bytes 32800 | tf_op jit(solution)/shard_map/ppermute | solution.py:35
  28.1 1.5 %collective-permute-done.5.rest_1_ = f32[32,256]{1,0:T(8,128)S(1)} collective-permute-done((f32[32,256]{1,0:T(8,128)S(1)}, f32[32,256]{1,0:T(8,128)S(1)}, u32[]{:S(2)}, u32[]{:S(2)}) %collective-permute-start.5) | collective-permute-done | bytes 32800 | tf_op jit(solution)/shard_map/ppermute | solution.py:35
  29.6 0.5 %attend.1.refs_0_ = bf16[1,4096]{1,0:T(2,128)(2,1)S(1)} custom-call(bf16[512,512]{1,0:T(8,128)(2,1)S(1)} %get-tuple-element.28.map_ref, s32[1,1024]{1,0:T(1,128)S(1)} %get-tuple-element.29.place_ref, f32[32,256]{1,0:T(8,128)S(1)} %collective-permute-done.4.rest_0_, f32[32,256]{1,0:T(8,128)S(1)} %collective-permute-done.5.rest_1_, ...), custom_call_target="tpu_custom_call" | custom-call | tf_op jit(solution)/shard_map/attend/pallas_call | solution.py:383
  30.1 0.1 collective-permute-start.8
  30.2 1.2 %collective-permute-done.8.refs_1_ = bf16[1,4096]{1,0:T(2,128)(2,1)S(1)} collective-permute-done((bf16[1,4096]{1,0:T(2,128)(2,1)S(1)}, bf16[1,4096]{1,0:T(2,128)(2,1)S(1)}, u32[]{:S(2)}, u32[]{:S(2)}) %collective-permute-start.8) | collective-permute-done | bytes 8224 | tf_op jit(solution)/shard_map/ppermute | solution.py:35
  31.4 1.9 %collective-permute-start.11 = (bf16[2,4096]{1,0:T(2,128)(2,1)S(1)}, bf16[2,4096]{1,0:T(2,128)(2,1)S(1)}, u32[]{:S(2)}, u32[]{:S(2)}) collective-permute-start(bf16[2,4096]{1,0:T(2,128)(2,1)S(1)} %join.1.rest_0_), channel_id=1, source_target_pairs={{0,12},{4,8},{8,4},{12,0},{1,13},{5,9},{9,5},{13,1},{2,14},{6,10},... | collective-permute-start | bytes 49160 | tf_op jit(solution)/shard_map/ppermute | solution.py:35
  33.3 0.6 %collective-permute-start.10 = (bf16[2,4096]{1,0:T(2,128)(2,1)S(1)}, bf16[2,4096]{1,0:T(2,128)(2,1)S(1)}, u32[]{:S(2)}, u32[]{:S(2)}) collective-permute-start(bf16[2,4096]{1,0:T(2,128)(2,1)S(1)} %join.1.rest_0_), channel_id=1, source_target_pairs={{0,8},{4,12},{8,0},{12,4},{1,9},{5,13},{9,1},{13,5},{2,10},{6,14},... | collective-permute-start | bytes 49160 | tf_op jit(solution)/shard_map/ppermute | solution.py:35
  33.9 2.0 %collective-permute-start.9 = (bf16[2,4096]{1,0:T(2,128)(2,1)S(1)}, bf16[2,4096]{1,0:T(2,128)(2,1)S(1)}, u32[]{:S(2)}, u32[]{:S(2)}) collective-permute-start(bf16[2,4096]{1,0:T(2,128)(2,1)S(1)} %join.1.rest_0_), channel_id=1, source_target_pairs={{0,4},{4,0},{8,12},{12,8},{1,5},{5,1},{9,13},{13,9},{2,6},{6,2},{1... | collective-permute-start | bytes 49160 | tf_op jit(solution)/shard_map/ppermute | solution.py:35
  35.8 1.3 %collective-permute-done.11.rest_3_ = bf16[2,4096]{1,0:T(2,128)(2,1)S(1)} collective-permute-done((bf16[2,4096]{1,0:T(2,128)(2,1)S(1)}, bf16[2,4096]{1,0:T(2,128)(2,1)S(1)}, u32[]{:S(2)}, u32[]{:S(2)}) %collective-permute-start.11) | collective-permute-done | bytes 16416 | tf_op jit(solution)/shard_map/ppermute | solution.py:35
  37.1 0.8 %collective-permute-done.10.rest_2_ = bf16[2,4096]{1,0:T(2,128)(2,1)S(1)} collective-permute-done((bf16[2,4096]{1,0:T(2,128)(2,1)S(1)}, bf16[2,4096]{1,0:T(2,128)(2,1)S(1)}, u32[]{:S(2)}, u32[]{:S(2)}) %collective-permute-start.10) | collective-permute-done | bytes 16416 | tf_op jit(solution)/shard_map/ppermute | solution.py:35
  37.9 1.2 %project.1 = (f32[2,1024]{1,0:T(2,128)S(1)}, f32[2,1024]{1,0:T(2,128)S(1)}, f32[2,1024]{1,0:T(2,128)S(1)}, f32[2,1024]{1,0:T(2,128)S(1)}) custom-call(bf16[4096,1024]{1,0:T(8,128)(2,1)S(1)} %copy-done, bf16[2,4096]{1,0:T(2,128)(2,1)S(1)} %join.1.rest_0_, bf16[2,4096]{1,0:T(2,128)(2,1)S(1)} %collective-permute-done.9.rest_1_, ...), custom_call_target="tpu_custom_call" | custom-call | tf_op jit(solution)/shard_map/project/pallas_call | solution.py:396
  39.1 0.1 collective-permute-start.12
  39.3 1.4 %collective-permute-start.13 = (f32[2,1024]{1,0:T(2,128)S(1)}, f32[2,1024]{1,0:T(2,128)S(1)}, u32[]{:S(2)}, u32[]{:S(2)}) collective-permute-start(f32[2,1024]{1,0:T(2,128)S(1)} %get-tuple-element.46), channel_id=1, source_target_pairs={{0,2},{1,3},{2,0},{3,1},{4,6},{5,7},{6,4},{7,5},{8,10},{9,11},{10,... | collective-permute-start | bytes 24584 | tf_op jit(solution)/shard_map/ppermute | solution.py:35
  40.7 0.3 collective-permute-start.14
  41.0 1.3 %collective-permute-done.12.refs_0_ = f32[2,1024]{1,0:T(2,128)S(1)} collective-permute-done((f32[2,1024]{1,0:T(2,128)S(1)}, f32[2,1024]{1,0:T(2,128)S(1)}, u32[]{:S(2)}, u32[]{:S(2)}) %collective-permute-start.12) | collective-permute-done | bytes 8224 | tf_op jit(solution)/shard_map/ppermute | solution.py:35
  42.3 0.6 %collective-permute-done.13.refs_1_ = f32[2,1024]{1,0:T(2,128)S(1)} collective-permute-done((f32[2,1024]{1,0:T(2,128)S(1)}, f32[2,1024]{1,0:T(2,128)S(1)}, u32[]{:S(2)}, u32[]{:S(2)}) %collective-permute-start.13) | collective-permute-done | bytes 8224 | tf_op jit(solution)/shard_map/ppermute | solution.py:35
  42.9 0.6 %finish.1 = bf16[1,2,2048]{2,1,0:T(2,128)(2,1)} custom-call(f32[2,1024]{1,0:T(2,128)S(1)} %collective-permute-done.12.refs_0_, f32[2,1024]{1,0:T(2,128)S(1)} %collective-permute-done.13.refs_1_, f32[2,1024]{1,0:T(2,128)S(1)} %collective-permute-done.14.refs_2_, f32[2,1024]{1,0:T(2,128)S(1)} %get-tuple-element.48.refs_3_), custom_call_target="tpu_custom_call" | custom-call | tf_op jit(solution)/shard_map/finish/pallas_call | solution.py:405
  (8 shorter events, 0.0 us)
Async XLA Ops:
  0.0 37.9 %copy-start = (bf16[4096,1024]{1,0:T(8,128)(2,1)S(1)}, bf16[4096,1024]{1,0:T(8,128)(2,1)}, u32[]{:S(2)}) copy-start(bf16[4096,1024]{1,0:T(8,128)(2,1)} %weight_ref.1) | copy-start | bytes 25165828
  3.0 14.9 %collective-permute-start = (bf16[1024,256]{1,0:T(8,128)(2,1)S(1)}, bf16[1024,256]{1,0:T(8,128)(2,1)S(1)}, u32[]{:S(2)}, u32[]{:S(2)}) collective-permute-start(bf16[1024,256]{1,0:T(8,128)(2,1)S(1)} %get-tuple-element.35.rest_0_), channel_id=1, source_target_pairs={{0,2},{2,0},{1,3},{3,1},{4,6},{6,4},{5,7},{7,5},{8,10},{10,8},{9,1... | collective-permute-start | bytes 1572872 | tf_op jit(solution)/shard_map/ppermute | solution.py:35
  6.0 12.8 %collective-permute-start.1 = (bf16[272,256]{1,0:T(8,128)(2,1)S(1)}, bf16[272,256]{1,0:T(8,128)(2,1)S(1)}, u32[]{:S(2)}, u32[]{:S(2)}) collective-permute-start(bf16[272,256]{1,0:T(8,128)(2,1)S(1)} %get-tuple-element.36), channel_id=1, source_target_pairs={{0,12},{4,8},{8,4},{12,0},{1,13},{5,9},{9,5},{13,1},{2,14},{6,10},... | collective-permute-start | bytes 417800 | tf_op jit(solution)/shard_map/ppermute | solution.py:35
  9.6 11.5 %collective-permute-start.2 = (bf16[272,256]{1,0:T(8,128)(2,1)S(1)}, bf16[272,256]{1,0:T(8,128)(2,1)S(1)}, u32[]{:S(2)}, u32[]{:S(2)}) collective-permute-start(bf16[272,256]{1,0:T(8,128)(2,1)S(1)} %get-tuple-element.37), channel_id=1, source_target_pairs={{0,8},{4,12},{8,0},{12,4},{1,9},{5,13},{9,1},{13,5},{2,10},{6,14},... | collective-permute-start | bytes 417800 | tf_op jit(solution)/shard_map/ppermute | solution.py:35
  12.5 8.5 %collective-permute-start.3 = (bf16[272,256]{1,0:T(8,128)(2,1)S(1)}, bf16[272,256]{1,0:T(8,128)(2,1)S(1)}, u32[]{:S(2)}, u32[]{:S(2)}) collective-permute-start(bf16[272,256]{1,0:T(8,128)(2,1)S(1)} %get-tuple-element.38), channel_id=1, source_target_pairs={{0,4},{4,0},{8,12},{12,8},{1,5},{5,1},{9,13},{13,9},{2,6},{6,2},{1... | collective-permute-start | bytes 417800 | tf_op jit(solution)/shard_map/ppermute | solution.py:35
  21.6 7.9 %collective-permute-start.7 = (bf16[512,256]{1,0:T(8,128)(2,1)S(1)}, bf16[512,256]{1,0:T(8,128)(2,1)S(1)}, u32[]{:S(2)}, u32[]{:S(2)}) collective-permute-start(bf16[512,256]{1,0:T(8,128)(2,1)S(1)} %get-tuple-element.44.rest_4_), channel_id=1, source_target_pairs={{0,2},{2,0},{1,3},{3,1},{4,6},{6,4},{5,7},{7,5},{8,10},{10,8},{9,1... | collective-permute-start | bytes 786440 | tf_op jit(solution)/shard_map/ppermute | solution.py:35
  22.2 5.8 %collective-permute-start.4 = (f32[32,256]{1,0:T(8,128)S(1)}, f32[32,256]{1,0:T(8,128)S(1)}, u32[]{:S(2)}, u32[]{:S(2)}) collective-permute-start(f32[32,256]{1,0:T(8,128)S(1)} %get-tuple-element.40), channel_id=1, source_target_pairs={{0,12},{4,8},{8,4},{12,0},{1,13},{5,9},{9,5},{13,1},{2,14},{6,10},... | collective-permute-start | bytes 98312 | tf_op jit(solution)/shard_map/ppermute | solution.py:35
  24.8 4.8 %collective-permute-start.5 = (f32[32,256]{1,0:T(8,128)S(1)}, f32[32,256]{1,0:T(8,128)S(1)}, u32[]{:S(2)}, u32[]{:S(2)}) collective-permute-start(f32[32,256]{1,0:T(8,128)S(1)} %get-tuple-element.41), channel_id=1, source_target_pairs={{0,8},{4,12},{8,0},{12,4},{1,9},{5,13},{9,1},{13,5},{2,10},{6,14},... | collective-permute-start | bytes 98312 | tf_op jit(solution)/shard_map/ppermute | solution.py:35
  24.8 4.8 %collective-permute-start.6 = (f32[32,256]{1,0:T(8,128)S(1)}, f32[32,256]{1,0:T(8,128)S(1)}, u32[]{:S(2)}, u32[]{:S(2)}) collective-permute-start(f32[32,256]{1,0:T(8,128)S(1)} %get-tuple-element.42), channel_id=1, source_target_pairs={{0,4},{4,0},{8,12},{12,8},{1,5},{5,1},{9,13},{13,9},{2,6},{6,2},{1... | collective-permute-start | bytes 98312 | tf_op jit(solution)/shard_map/ppermute | solution.py:35
  30.1 1.2 %collective-permute-start.8 = (bf16[1,4096]{1,0:T(2,128)(2,1)S(1)}, bf16[1,4096]{1,0:T(2,128)(2,1)S(1)}, u32[]{:S(2)}, u32[]{:S(2)}) collective-permute-start(bf16[1,4096]{1,0:T(2,128)(2,1)S(1)} %attend.1.refs_0_), channel_id=1, source_target_pairs={{0,1},{1,0},{2,3},{3,2},{4,5},{5,4},{6,7},{7,6},{8,9},{9,8},{10,11... | collective-permute-start | bytes 24584 | tf_op jit(solution)/shard_map/ppermute | solution.py:35
  31.4 5.7 %collective-permute-start.11 = (bf16[2,4096]{1,0:T(2,128)(2,1)S(1)}, bf16[2,4096]{1,0:T(2,128)(2,1)S(1)}, u32[]{:S(2)}, u32[]{:S(2)}) collective-permute-start(bf16[2,4096]{1,0:T(2,128)(2,1)S(1)} %join.1.rest_0_), channel_id=1, source_target_pairs={{0,12},{4,8},{8,4},{12,0},{1,13},{5,9},{9,5},{13,1},{2,14},{6,10},... | collective-permute-start | bytes 49160 | tf_op jit(solution)/shard_map/ppermute | solution.py:35
  33.3 4.6 %collective-permute-start.10 = (bf16[2,4096]{1,0:T(2,128)(2,1)S(1)}, bf16[2,4096]{1,0:T(2,128)(2,1)S(1)}, u32[]{:S(2)}, u32[]{:S(2)}) collective-permute-start(bf16[2,4096]{1,0:T(2,128)(2,1)S(1)} %join.1.rest_0_), channel_id=1, source_target_pairs={{0,8},{4,12},{8,0},{12,4},{1,9},{5,13},{9,1},{13,5},{2,10},{6,14},... | collective-permute-start | bytes 49160 | tf_op jit(solution)/shard_map/ppermute | solution.py:35
  33.9 4.0 %collective-permute-start.9 = (bf16[2,4096]{1,0:T(2,128)(2,1)S(1)}, bf16[2,4096]{1,0:T(2,128)(2,1)S(1)}, u32[]{:S(2)}, u32[]{:S(2)}) collective-permute-start(bf16[2,4096]{1,0:T(2,128)(2,1)S(1)} %join.1.rest_0_), channel_id=1, source_target_pairs={{0,4},{4,0},{8,12},{12,8},{1,5},{5,1},{9,13},{13,9},{2,6},{6,2},{1... | collective-permute-start | bytes 49160 | tf_op jit(solution)/shard_map/ppermute | solution.py:35
  39.1 3.2 %collective-permute-start.12 = (f32[2,1024]{1,0:T(2,128)S(1)}, f32[2,1024]{1,0:T(2,128)S(1)}, u32[]{:S(2)}, u32[]{:S(2)}) collective-permute-start(f32[2,1024]{1,0:T(2,128)S(1)} %get-tuple-element.45), channel_id=1, source_target_pairs={{0,3},{1,2},{2,1},{3,0},{4,7},{5,6},{6,5},{7,4},{8,11},{9,10},{10,... | collective-permute-start | bytes 24584 | tf_op jit(solution)/shard_map/ppermute | solution.py:35
  39.3 3.7 %collective-permute-start.13 = (f32[2,1024]{1,0:T(2,128)S(1)}, f32[2,1024]{1,0:T(2,128)S(1)}, u32[]{:S(2)}, u32[]{:S(2)}) collective-permute-start(f32[2,1024]{1,0:T(2,128)S(1)} %get-tuple-element.46), channel_id=1, source_target_pairs={{0,2},{1,3},{2,0},{3,1},{4,6},{5,7},{6,4},{7,5},{8,10},{9,11},{10,... | collective-permute-start | bytes 24584 | tf_op jit(solution)/shard_map/ppermute | solution.py:35
  40.7 2.2 %collective-permute-start.14 = (f32[2,1024]{1,0:T(2,128)S(1)}, f32[2,1024]{1,0:T(2,128)S(1)}, u32[]{:S(2)}, u32[]{:S(2)}) collective-permute-start(f32[2,1024]{1,0:T(2,128)S(1)} %get-tuple-element.47), channel_id=1, source_target_pairs={{0,1},{1,0},{2,3},{3,2},{4,5},{5,4},{6,7},{7,6},{8,9},{9,8},{10,11... | collective-permute-start | bytes 24584 | tf_op jit(solution)/shard_map/ppermute | solution.py:35

commit v8 on v7

--- a/solution.py
+++ b/solution.py
@@ -262,35 +262,29 @@
             out_ref[:, at : at + HEAD_SIZE] = mixed[g][q : q + 1, :].astype(jnp.bfloat16)
 
 
-def join_kernel(*refs):
-    rows = [ref[...].reshape(-1, ref.shape[-1]).astype(jnp.float32) for ref in refs[:-1]]
-    refs[-1][...] = jnp.concatenate(rows, axis=0).astype(jnp.bfloat16)
-
-
-def project_kernel(pools, heads, reps, weight_ref, *rest):
-    row_refs = rest[:pools]
-    out_refs = rest[pools:-1]
+def project_kernel(pools, heads, reps, *rest):
+    weight_refs = rest[:reps]
+    row_refs = rest[reps : reps + pools]
+    out_refs = rest[reps + pools : -1]
     acc = rest[-1]
+    rep = lax.axis_index("rep")
+    width = weight_refs[0].shape[1]
     left = jnp.concatenate([ref[...].astype(jnp.float32) for ref in row_refs], axis=0).astype(jnp.bfloat16)
-    acc[...] = jnp.dot(left, weight_ref[...], preferred_element_type=jnp.float32)
+    for t in range(reps):
+        columns = pl.ds(pl.multiple_of((rep ^ t) * width, width), width)
+        acc[:, columns] = jnp.dot(left, weight_refs[t][...], preferred_element_type=jnp.float32)
     pool = lax.axis_index("pool")
     head = lax.axis_index("heads")
     each = pools // heads
-    for d in range(heads * reps):
+    for j in range(heads):
         for u in range(each):
-            n = (pool ^ ((head ^ (d // reps)) * each + u)) * reps + d % reps
-            out_refs[d][u : u + 1, :] = acc[pl.ds(n, 1), :]
-
-
-def finish_kernel(heads, reps, *refs):
-    out_ref = refs[-1]
-    refs = refs[:-1][::-1]
-    rep = lax.axis_index("rep")
-    width = refs[0].shape[1]
-    for t in range(reps):
-        total = functools.reduce(jnp.add, [refs[j * reps + t][...] for j in range(heads)])
-        columns = pl.ds(pl.multiple_of((rep ^ t) * width, width), width)
-        out_ref[0, :, columns] = total.astype(jnp.bfloat16)
+            n = pool ^ ((head ^ j) * each + u)
+            out_refs[j][u : u + 1, :] = acc[pl.ds(n, 1), :]
+
+
+def finish_kernel(*refs):
+    total = functools.reduce(jnp.add, [ref[...] for ref in refs[:-1][::-1]])
+    refs[-1][0] = total.astype(jnp.bfloat16)
 
 
 def per_device(queries, latents, key_latent_maps, value_latent_maps, out_weight, lengths, selected):
@@ -306,16 +300,6 @@
     bf16, f32, i32 = jnp.bfloat16, jnp.float32, jnp.int32
     shape = jax.ShapeDtypeStruct
     freq = jnp.asarray(frequencies())
-
-    def join(*blocks):
-        return pl.pallas_call(
-            join_kernel,
-            out_shape=shape((sum(block.size for block in blocks) // queries.shape[2], queries.shape[2]), bf16),
-            in_specs=[VMEM] * len(blocks),
-            out_specs=VMEM,
-            compiler_params=params(4),
-            name="join",
-        )(*blocks)
 
     def exchange(value, axis, size):
         taken = {step: swap(value, axis, size, step) for step in range(size - 1, 0, -1)}
@@ -388,28 +372,28 @@
         compiler_params=params(16),
         name="attend",
     )(value_maps, place, *score_parts[::-1], *dense_parts)
-    own_rows = join(*exchange(mine, "rep", reps))
-    row_parts = exchange(own_rows, "pool", pools)
+    row_parts = exchange(mine, "pool", pools)
 
     own_columns = out_weight.shape[1]
     each = pools // heads
+    weights = exchange(out_weight, "rep", reps)
     parts = pl.pallas_call(
         functools.partial(project_kernel, pools, heads, reps),
-        out_shape=[shape((each, own_columns), f32)] * (heads * reps),
-        in_specs=[VMEM] * (pools + 1),
-        out_specs=[VMEM] * (heads * reps),
-        scratch_shapes=[pltpu.VMEM((pools * reps, own_columns), f32)],
+        out_shape=[shape((each, reps * own_columns), f32)] * heads,
+        in_specs=[VMEM] * (reps + pools),
+        out_specs=[VMEM] * heads,
+        scratch_shapes=[pltpu.VMEM((pools, reps * own_columns), f32)],
         compiler_params=params(24),
         name="project",
-    )(in_vmem(out_weight), *row_parts)
+    )(*[in_vmem(weight) for weight in weights], *row_parts)
     return pl.pallas_call(
-        functools.partial(finish_kernel, heads, reps),
+        finish_kernel,
         out_shape=shape((1, each, reps * own_columns), bf16),
-        in_specs=[VMEM] * (heads * reps),
+        in_specs=[VMEM] * heads,
         out_specs=VMEM,
         compiler_params=params(4),
         name="finish",
-    )(*scatter(parts, ("heads", "rep"), heads * reps)[::-1])
+    )(*scatter(parts, "heads", heads)[::-1])
 
 
 def solution(mesh):

time: 43.8 us -> 45.2 us (1.032)
  waiting for transfers between devices: 14.8 us -> 16.4 us
  starting transfers between devices: 18.9 us -> 17.5 us
  Pallas kernels: 9.71 us -> 10.9 us
    ppermute x15 -> x13, waiting for transfers between devices: 14.8 us -> 16.4 us  [swap(): return lax.ppermute(value, axes, [(i, i ^ step) for i in range(size)])]
    ppermute x15 -> x13, starting transfers between devices: 18.9 us -> 17.5 us  [swap(): return lax.ppermute(value, axes, [(i, i ^ step) for i in range(size)])]
    pallas_call x1, Pallas kernels: 1.21 us -> 2.27 us  [per_device(): pl.pallas_call(functools.partial(project_kernel, pools, heads, reps), out...]
  transfers between devices with their start and end apart: 15 -> 13, of which waited for: 9 -> 8; matrix products, arithmetic and copies ran while one was open for 0% -> 0% of each run, Pallas kernels for 9% -> 18%
where the time goes in v8:
time: 45.2 us; the launch traced here: 45 us
  starting transfers between devices  17.5 us (39%)
  waiting for transfers between devices  16.4 us (36%)
  Pallas kernels  10.9 us (24%)
    ppermute x13, starting transfers between devices, swap(): return lax.ppermute(value, axes, [(i, i ^ step) for i in range(size)])  17.5 us
    ppermute x13, waiting for transfers between devices, swap(): return lax.ppermute(value, axes, [(i, i ^ step) for i in range(size)])  16.4 us
    pallas_call x1, Pallas kernels, per_device(): pl.pallas_call(functools.partial(gather_kernel, pools), out_shape=[shape(...  3.13 us
    pallas_call x1, Pallas kernels, per_device(): pl.pallas_call(functools.partial(table_kernel, pools, shard_blocks), out_...  2.97 us
    pallas_call x1, Pallas kernels, per_device(): pl.pallas_call(functools.partial(project_kernel, pools, heads, reps), out...  2.27 us
  transfers between devices with their start and end apart: 13, of which 8 were waited for; matrix products, arithmetic and copies ran while one was open for 0% of the time, Pallas kernels for 18%

profile of v8, /device:TPU:0, one launch (start us, length us, event | category | flops | bytes accessed | tf_op | source)
XLA Modules:
  0.0 45.0 jit_solution(5195043432348602660)
XLA Ops:
  0.0 0.5 %collective-permute-start = (bf16[4096,1024]{1,0:T(8,128)(2,1)}, bf16[4096,1024]{1,0:T(8,128)(2,1)S(1)}, u32[]{:S(2)}, u32[]{:S(2)}) collective-permute-start(bf16[4096,1024]{1,0:T(8,128)(2,1)} %rest_0_.1), channel_id=1, source_target_pairs={{0,1},{1,0},{2,3},{3,2},{4,5},{5,4},{6,7},{7,6},{8,9},{9,8},{10,11... | collective-permute-start | bytes 25165832 | tf_op jit(solution)/shard_map/ppermute | solution.py:35
  0.5 3.1 %gather.1 = (bf16[1024,256]{1,0:T(8,128)(2,1)S(1)}, bf16[272,256]{1,0:T(8,128)(2,1)S(1)}, bf16[272,256]{1,0:T(8,128)(2,1)S(1)}, bf16[272,256]{1,0:T(8,128)(2,1)S(1)}, bf16[272,256]{1,0:T(8,128)(2,1)S(1)}) custom-call(s32[1,4,4]{2,1,0:T(4,128)} %sel_ref.3, bf16[1,4,1024,512]{3,2,1,0:T(8,128)(2,1)} %lat_ref.1, bf16[1,1,4096]{2,1,0:T(2,128)(2,1)} %query_ref.1), custom_call_target="tpu_custom_call" | custom-call | tf_op jit(solution)/shard_map/gather/pallas_call | solution.py:313
  3.6 2.4 %collective-permute-start.1 = (bf16[1024,256]{1,0:T(8,128)(2,1)S(1)}, bf16[1024,256]{1,0:T(8,128)(2,1)S(1)}, u32[]{:S(2)}, u32[]{:S(2)}) collective-permute-start(bf16[1024,256]{1,0:T(8,128)(2,1)S(1)} %get-tuple-element.33.rest_0_), channel_id=1, source_target_pairs={{0,2},{2,0},{1,3},{3,1},{4,6},{6,4},{5,7},{7,5},{8,10},{10,8},{9,1... | collective-permute-start | bytes 1572872 | tf_op jit(solution)/shard_map/ppermute | solution.py:35
  6.0 3.6 %collective-permute-start.2 = (bf16[272,256]{1,0:T(8,128)(2,1)S(1)}, bf16[272,256]{1,0:T(8,128)(2,1)S(1)}, u32[]{:S(2)}, u32[]{:S(2)}) collective-permute-start(bf16[272,256]{1,0:T(8,128)(2,1)S(1)} %get-tuple-element.34), channel_id=1, source_target_pairs={{0,12},{4,8},{8,4},{12,0},{1,13},{5,9},{9,5},{13,1},{2,14},{6,10},... | collective-permute-start | bytes 417800 | tf_op jit(solution)/shard_map/ppermute | solution.py:35
  9.6 0.0 collective-permute-start.3
  9.6 3.0 %tables.1 = (f32[1024,128]{1,0:T(8,128)S(1)}, f32[1024,128]{1,0:T(8,128)S(1)}, f32[8,128]{1,0:T(8,128)S(1)}, s32[4,256]{1,0:T(4,128)S(1)}, s32[1,1024]{1,0:T(1,1...) custom-call(s32[1,4,4]{2,1,0:T(4,128)} %sel_ref.3, ...), custom_call_target="tpu_custom_call", output_to_operand_aliasing={{7}: (5, {})} | custom-call | tf_op jit(solution)/shard_map/tables/pallas_call | solution.py:329
  12.6 0.8 %collective-permute-start.4 = (bf16[272,256]{1,0:T(8,128)(2,1)S(1)}, bf16[272,256]{1,0:T(8,128)(2,1)S(1)}, u32[]{:S(2)}, u32[]{:S(2)}) collective-permute-start(bf16[272,256]{1,0:T(8,128)(2,1)S(1)} %get-tuple-element.36), channel_id=1, source_target_pairs={{0,4},{4,0},{8,12},{12,8},{1,5},{5,1},{9,13},{13,9},{2,6},{6,2},{1... | collective-permute-start | bytes 417800 | tf_op jit(solution)/shard_map/ppermute | solution.py:35
  13.4 5.2 %collective-permute-done.1.rest_1_ = bf16[1024,256]{1,0:T(8,128)(2,1)S(1)} collective-permute-done((bf16[1024,256]{1,0:T(8,128)(2,1)S(1)}, bf16[1024,256]{1,0:T(8,128)(2,1)S(1)}, u32[]{:S(2)}, u32[]{:S(2)}) %collective-permute-start.1) | collective-permute-done | bytes 524320 | tf_op jit(solution)/shard_map/ppermute | solution.py:35
  18.7 0.9 %rebuild.1.key_ref = bf16[1024,512]{1,0:T(8,128)(2,1)S(1)} custom-call(bf16[512,512]{1,0:T(8,128)(2,1)S(1)} %get-tuple-element.30.map_ref, f32[1024,128]{1,0:T(8,128)S(1)} %get-tuple-element.31.cos_ref, f32[1024,128]{1,0:T(8,128)S(1)} %get-tuple-element.32.sin_ref, bf16[1024,256]{1,0:T(8,128)(2,1)S(1)} %get-tuple-element.33.rest_0_, ...), custom_call_target="tpu_custom_call" | custom-call | tf_op jit(solution)/shard_map/rebuild/pallas_call | solution.py:348
  19.5 0.0 collective-permute-done.2.rest_0_
  19.5 2.5 %collective-permute-done.3.rest_1_ = bf16[272,256]{1,0:T(8,128)(2,1)S(1)} collective-permute-done((bf16[272,256]{1,0:T(8,128)(2,1)S(1)}, bf16[272,256]{1,0:T(8,128)(2,1)S(1)}, u32[]{:S(2)}, u32[]{:S(2)}) %collective-permute-start.3) | collective-permute-done | bytes 139296 | tf_op jit(solution)/shard_map/ppermute | solution.py:35
  22.0 0.6 %score.1 = (bf16[512,256]{1,0:T(8,128)(2,1)S(1)}, f32[32,256]{1,0:T(8,128)S(1)}, f32[32,256]{1,0:T(8,128)S(1)}, f32[32,256]{1,0:T(8,128)S(1)}, f32[32,256]{1,0:T(8,128)S(1)}) custom-call(f32[8,128]{1,0:T(8,128)S(1)} %get-tuple-element.28.turn_ref, s32[4,256]{1,0:T(4,128)S(1)} %get-tuple-element.29.live_ref, s32[1,1024]{1,0:T(1,128)S(1)} %get-tuple-element.27.place_ref, ...), custom_call_target="tpu_custom_call" | custom-call | tf_op jit(solution)/shard_map/score/pallas_call | solution.py:356
  22.6 0.6 %collective-permute-start.8 = (bf16[512,256]{1,0:T(8,128)(2,1)S(1)}, bf16[512,256]{1,0:T(8,128)(2,1)S(1)}, u32[]{:S(2)}, u32[]{:S(2)}) collective-permute-start(bf16[512,256]{1,0:T(8,128)(2,1)S(1)} %get-tuple-element.42.rest_4_), channel_id=1, source_target_pairs={{0,2},{2,0},{1,3},{3,1},{4,6},{6,4},{5,7},{7,5},{8,10},{10,8},{9,1... | collective-permute-start | bytes 786440 | tf_op jit(solution)/shard_map/ppermute | solution.py:35
  23.2 2.5 %collective-permute-start.5 = (f32[32,256]{1,0:T(8,128)S(1)}, f32[32,256]{1,0:T(8,128)S(1)}, u32[]{:S(2)}, u32[]{:S(2)}) collective-permute-start(f32[32,256]{1,0:T(8,128)S(1)} %get-tuple-element.38), channel_id=1, source_target_pairs={{0,12},{4,8},{8,4},{12,0},{1,13},{5,9},{9,5},{13,1},{2,14},{6,10},... | collective-permute-start | bytes 98312 | tf_op jit(solution)/shard_map/ppermute | solution.py:35
  25.7 0.0 collective-permute-start.6
  25.7 1.9 %collective-permute-start.7 = (f32[32,256]{1,0:T(8,128)S(1)}, f32[32,256]{1,0:T(8,128)S(1)}, u32[]{:S(2)}, u32[]{:S(2)}) collective-permute-start(f32[32,256]{1,0:T(8,128)S(1)} %get-tuple-element.40), channel_id=1, source_target_pairs={{0,4},{4,0},{8,12},{12,8},{1,5},{5,1},{9,13},{13,9},{2,6},{6,2},{1... | collective-permute-start | bytes 98312 | tf_op jit(solution)/shard_map/ppermute | solution.py:35
  27.6 1.4 %collective-permute-done.5.rest_0_ = f32[32,256]{1,0:T(8,128)S(1)} collective-permute-done((f32[32,256]{1,0:T(8,128)S(1)}, f32[32,256]{1,0:T(8,128)S(1)}, u32[]{:S(2)}, u32[]{:S(2)}) %collective-permute-start.5) | collective-permute-done | bytes 32800 | tf_op jit(solution)/shard_map/ppermute | solution.py:35
  28.9 1.6 %collective-permute-done.6.rest_1_ = f32[32,256]{1,0:T(8,128)S(1)} collective-permute-done((f32[32,256]{1,0:T(8,128)S(1)}, f32[32,256]{1,0:T(8,128)S(1)}, u32[]{:S(2)}, u32[]{:S(2)}) %collective-permute-start.6) | collective-permute-done | bytes 32800 | tf_op jit(solution)/shard_map/ppermute | solution.py:35
  30.5 0.0 collective-permute-done.7.rest_2_
  30.5 0.1 collective-permute-done.8.rest_5_
  30.6 0.5 %attend.1.rest_2_ = bf16[1,4096]{1,0:T(2,128)(2,1)S(1)} custom-call(bf16[512,512]{1,0:T(8,128)(2,1)S(1)} %get-tuple-element.26.map_ref, s32[1,1024]{1,0:T(1,128)S(1)} %get-tuple-element.27.place_ref, f32[32,256]{1,0:T(8,128)S(1)} %collective-permute-done.5.rest_0_, f32[32,256]{1,0:T(8,128)S(1)} %collective-permute-done.6.rest_1_, ...), custom_call_target="tpu_custom_call" | custom-call | tf_op jit(solution)/shard_map/attend/pallas_call | solution.py:367
  31.1 2.5 %collective-permute-start.11 = (bf16[1,4096]{1,0:T(2,128)(2,1)S(1)}, bf16[1,4096]{1,0:T(2,128)(2,1)S(1)}, u32[]{:S(2)}, u32[]{:S(2)}) collective-permute-start(bf16[1,4096]{1,0:T(2,128)(2,1)S(1)} %attend.1.rest_2_), channel_id=1, source_target_pairs={{0,12},{4,8},{8,4},{12,0},{1,13},{5,9},{9,5},{13,1},{2,14},{6,10},... | collective-permute-start | bytes 24584 | tf_op jit(solution)/shard_map/ppermute | solution.py:35
  33.7 0.0 collective-permute-start.10
  33.7 1.9 %collective-permute-start.9 = (bf16[1,4096]{1,0:T(2,128)(2,1)S(1)}, bf16[1,4096]{1,0:T(2,128)(2,1)S(1)}, u32[]{:S(2)}, u32[]{:S(2)}) collective-permute-start(bf16[1,4096]{1,0:T(2,128)(2,1)S(1)} %attend.1.rest_2_), channel_id=1, source_target_pairs={{0,4},{4,0},{8,12},{12,8},{1,5},{5,1},{9,13},{13,9},{2,6},{6,2},{1... | collective-permute-start | bytes 24584 | tf_op jit(solution)/shard_map/ppermute | solution.py:35
  35.6 1.1 %collective-permute-done.11.rest_5_ = bf16[1,4096]{1,0:T(2,128)(2,1)S(1)} collective-permute-done((bf16[1,4096]{1,0:T(2,128)(2,1)S(1)}, bf16[1,4096]{1,0:T(2,128)(2,1)S(1)}, u32[]{:S(2)}, u32[]{:S(2)}) %collective-permute-start.11) | collective-permute-done | bytes 8224 | tf_op jit(solution)/shard_map/ppermute | solution.py:35
  36.7 1.6 %collective-permute-done.10.rest_4_ = bf16[1,4096]{1,0:T(2,128)(2,1)S(1)} collective-permute-done((bf16[1,4096]{1,0:T(2,128)(2,1)S(1)}, bf16[1,4096]{1,0:T(2,128)(2,1)S(1)}, u32[]{:S(2)}, u32[]{:S(2)}) %collective-permute-start.10) | collective-permute-done | bytes 8224 | tf_op jit(solution)/shard_map/ppermute | solution.py:35
  38.3 0.0 collective-permute-done.9.rest_3_
  38.3 0.0 collective-permute-done.rest_1_
  38.3 2.3 %project.1 = (f32[2,2048]{1,0:T(2,128)S(1)}, f32[2,2048]{1,0:T(2,128)S(1)}) custom-call(bf16[4096,1024]{1,0:T(8,128)(2,1)S(1)} %copy-done, bf16[4096,1024]{1,0:T(8,128)(2,1)S(1)} %collective-permute-done.rest_1_, bf16[1,4096]{1,0:T(2,128)(2,1)S(1)} %attend.1.rest_2_, bf16[1,4096]{1,0:T(2,128)(2,1)S(1)} %collective-permute-done.9.rest_3_, ...), custom_call_target="tpu_custom_call" | custom-call | tf_op jit(solution)/shard_map/project/pallas_call | solution.py:380
  40.6 0.8 %collective-permute-start.12 = (f32[2,2048]{1,0:T(2,128)S(1)}, f32[2,2048]{1,0:T(2,128)S(1)}, u32[]{:S(2)}, u32[]{:S(2)}) collective-permute-start(f32[2,2048]{1,0:T(2,128)S(1)} %get-tuple-element.43), channel_id=1, source_target_pairs={{0,2},{2,0},{1,3},{3,1},{4,6},{6,4},{5,7},{7,5},{8,10},{10,8},{9,1... | collective-permute-start | bytes 49160 | tf_op jit(solution)/shard_map/ppermute | solution.py:35
  41.4 2.9 %collective-permute-done.12.refs_0_ = f32[2,2048]{1,0:T(2,128)S(1)} collective-permute-done((f32[2,2048]{1,0:T(2,128)S(1)}, f32[2,2048]{1,0:T(2,128)S(1)}, u32[]{:S(2)}, u32[]{:S(2)}) %collective-permute-start.12) | collective-permute-done | bytes 16416 | tf_op jit(solution)/shard_map/ppermute | solution.py:35
  44.3 0.6 %finish.1 = bf16[1,2,2048]{2,1,0:T(2,128)(2,1)} custom-call(f32[2,2048]{1,0:T(2,128)S(1)} %collective-permute-done.12.refs_0_, f32[2,2048]{1,0:T(2,128)S(1)} %get-tuple-element.44.refs_1_), custom_call_target="tpu_custom_call" | custom-call | tf_op jit(solution)/shard_map/finish/pallas_call | solution.py:389
  (3 shorter events, 0.0 us)
Async XLA Ops:
  0.0 38.3 %copy-start = (bf16[4096,1024]{1,0:T(8,128)(2,1)S(1)}, bf16[4096,1024]{1,0:T(8,128)(2,1)}, u32[]{:S(2)}) copy-start(bf16[4096,1024]{1,0:T(8,128)(2,1)} %rest_0_.1) | copy-start | bytes 25165828
  0.0 38.3 %collective-permute-start = (bf16[4096,1024]{1,0:T(8,128)(2,1)}, bf16[4096,1024]{1,0:T(8,128)(2,1)S(1)}, u32[]{:S(2)}, u32[]{:S(2)}) collective-permute-start(bf16[4096,1024]{1,0:T(8,128)(2,1)} %rest_0_.1), channel_id=1, source_target_pairs={{0,1},{1,0},{2,3},{3,2},{4,5},{5,4},{6,7},{7,6},{8,9},{9,8},{10,11... | collective-permute-start | bytes 25165832 | tf_op jit(solution)/shard_map/ppermute | solution.py:35
  3.6 15.1 %collective-permute-start.1 = (bf16[1024,256]{1,0:T(8,128)(2,1)S(1)}, bf16[1024,256]{1,0:T(8,128)(2,1)S(1)}, u32[]{:S(2)}, u32[]{:S(2)}) collective-permute-start(bf16[1024,256]{1,0:T(8,128)(2,1)S(1)} %get-tuple-element.33.rest_0_), channel_id=1, source_target_pairs={{0,2},{2,0},{1,3},{3,1},{4,6},{6,4},{5,7},{7,5},{8,10},{10,8},{9,1... | collective-permute-start | bytes 1572872 | tf_op jit(solution)/shard_map/ppermute | solution.py:35
  6.0 13.5 %collective-permute-start.2 = (bf16[272,256]{1,0:T(8,128)(2,1)S(1)}, bf16[272,256]{1,0:T(8,128)(2,1)S(1)}, u32[]{:S(2)}, u32[]{:S(2)}) collective-permute-start(bf16[272,256]{1,0:T(8,128)(2,1)S(1)} %get-tuple-element.34), channel_id=1, source_target_pairs={{0,12},{4,8},{8,4},{12,0},{1,13},{5,9},{9,5},{13,1},{2,14},{6,10},... | collective-permute-start | bytes 417800 | tf_op jit(solution)/shard_map/ppermute | solution.py:35
  9.6 12.4 %collective-permute-start.3 = (bf16[272,256]{1,0:T(8,128)(2,1)S(1)}, bf16[272,256]{1,0:T(8,128)(2,1)S(1)}, u32[]{:S(2)}, u32[]{:S(2)}) collective-permute-start(bf16[272,256]{1,0:T(8,128)(2,1)S(1)} %get-tuple-element.35), channel_id=1, source_target_pairs={{0,8},{4,12},{8,0},{12,4},{1,9},{5,13},{9,1},{13,5},{2,10},{6,14},... | collective-permute-start | bytes 417800 | tf_op jit(solution)/shard_map/ppermute | solution.py:35
  12.6 9.5 %collective-permute-start.4 = (bf16[272,256]{1,0:T(8,128)(2,1)S(1)}, bf16[272,256]{1,0:T(8,128)(2,1)S(1)}, u32[]{:S(2)}, u32[]{:S(2)}) collective-permute-start(bf16[272,256]{1,0:T(8,128)(2,1)S(1)} %get-tuple-element.36), channel_id=1, source_target_pairs={{0,4},{4,0},{8,12},{12,8},{1,5},{5,1},{9,13},{13,9},{2,6},{6,2},{1... | collective-permute-start | bytes 417800 | tf_op jit(solution)/shard_map/ppermute | solution.py:35
  22.6 8.0 %collective-permute-start.8 = (bf16[512,256]{1,0:T(8,128)(2,1)S(1)}, bf16[512,256]{1,0:T(8,128)(2,1)S(1)}, u32[]{:S(2)}, u32[]{:S(2)}) collective-permute-start(bf16[512,256]{1,0:T(8,128)(2,1)S(1)} %get-tuple-element.42.rest_4_), channel_id=1, source_target_pairs={{0,2},{2,0},{1,3},{3,1},{4,6},{6,4},{5,7},{7,5},{8,10},{10,8},{9,1... | collective-permute-start | bytes 786440 | tf_op jit(solution)/shard_map/ppermute | solution.py:35
  23.2 5.7 %collective-permute-start.5 = (f32[32,256]{1,0:T(8,128)S(1)}, f32[32,256]{1,0:T(8,128)S(1)}, u32[]{:S(2)}, u32[]{:S(2)}) collective-permute-start(f32[32,256]{1,0:T(8,128)S(1)} %get-tuple-element.38), channel_id=1, source_target_pairs={{0,12},{4,8},{8,4},{12,0},{1,13},{5,9},{9,5},{13,1},{2,14},{6,10},... | collective-permute-start | bytes 98312 | tf_op jit(solution)/shard_map/ppermute | solution.py:35
  25.7 4.8 %collective-permute-start.6 = (f32[32,256]{1,0:T(8,128)S(1)}, f32[32,256]{1,0:T(8,128)S(1)}, u32[]{:S(2)}, u32[]{:S(2)}) collective-permute-start(f32[32,256]{1,0:T(8,128)S(1)} %get-tuple-element.39), channel_id=1, source_target_pairs={{0,8},{4,12},{8,0},{12,4},{1,9},{5,13},{9,1},{13,5},{2,10},{6,14},... | collective-permute-start | bytes 98312 | tf_op jit(solution)/shard_map/ppermute | solution.py:35
  25.7 4.8 %collective-permute-start.7 = (f32[32,256]{1,0:T(8,128)S(1)}, f32[32,256]{1,0:T(8,128)S(1)}, u32[]{:S(2)}, u32[]{:S(2)}) collective-permute-start(f32[32,256]{1,0:T(8,128)S(1)} %get-tuple-element.40), channel_id=1, source_target_pairs={{0,4},{4,0},{8,12},{12,8},{1,5},{5,1},{9,13},{13,9},{2,6},{6,2},{1... | collective-permute-start | bytes 98312 | tf_op jit(solution)/shard_map/ppermute | solution.py:35
  31.1 5.6 %collective-permute-start.11 = (bf16[1,4096]{1,0:T(2,128)(2,1)S(1)}, bf16[1,4096]{1,0:T(2,128)(2,1)S(1)}, u32[]{:S(2)}, u32[]{:S(2)}) collective-permute-start(bf16[1,4096]{1,0:T(2,128)(2,1)S(1)} %attend.1.rest_2_), channel_id=1, source_target_pairs={{0,12},{4,8},{8,4},{12,0},{1,13},{5,9},{9,5},{13,1},{2,14},{6,10},... | collective-permute-start | bytes 24584 | tf_op jit(solution)/shard_map/ppermute | solution.py:35
  33.7 4.6 %collective-permute-start.10 = (bf16[1,4096]{1,0:T(2,128)(2,1)S(1)}, bf16[1,4096]{1,0:T(2,128)(2,1)S(1)}, u32[]{:S(2)}, u32[]{:S(2)}) collective-permute-start(bf16[1,4096]{1,0:T(2,128)(2,1)S(1)} %attend.1.rest_2_), channel_id=1, source_target_pairs={{0,8},{4,12},{8,0},{12,4},{1,9},{5,13},{9,1},{13,5},{2,10},{6,14},... | collective-permute-start | bytes 24584 | tf_op jit(solution)/shard_map/ppermute | solution.py:35
  33.7 4.6 %collective-permute-start.9 = (bf16[1,4096]{1,0:T(2,128)(2,1)S(1)}, bf16[1,4096]{1,0:T(2,128)(2,1)S(1)}, u32[]{:S(2)}, u32[]{:S(2)}) collective-permute-start(bf16[1,4096]{1,0:T(2,128)(2,1)S(1)} %attend.1.rest_2_), channel_id=1, source_target_pairs={{0,4},{4,0},{8,12},{12,8},{1,5},{5,1},{9,13},{13,9},{2,6},{6,2},{1... | collective-permute-start | bytes 24584 | tf_op jit(solution)/shard_map/ppermute | solution.py:35
  40.6 3.8 %collective-permute-start.12 = (f32[2,2048]{1,0:T(2,128)S(1)}, f32[2,2048]{1,0:T(2,128)S(1)}, u32[]{:S(2)}, u32[]{:S(2)}) collective-permute-start(f32[2,2048]{1,0:T(2,128)S(1)} %get-tuple-element.43), channel_id=1, source_target_pairs={{0,2},{2,0},{1,3},{3,1},{4,6},{6,4},{5,7},{7,5},{8,10},{10,8},{9,1... | collective-permute-start | bytes 49160 | tf_op jit(solution)/shard_map/ppermute | solution.py:35

commit v9 on v7

--- a/solution.py
+++ b/solution.py
@@ -76,8 +76,8 @@
 
 
 def gather_kernel(pools, sel_ref, lat_ref, query_ref, keys_ref, *rest):
-    value_refs = rest[:pools]
-    raw, line, sems = rest[pools:]
+    value_refs = rest[:-3]
+    raw, line, sems = rest[-3:]
     load = pltpu.make_async_copy(query_ref.at[0], line, sems.at[pools * CAP])
     load.start()
     shard_blocks = lat_ref.shape[2] // BLOCK
@@ -104,7 +104,7 @@
     wanted = ((within >> 6) << 7) + (within & (LANE - 1)) + jnp.where(target >= half, LANE, 0)
     pick = (source == wanted).astype(jnp.float32).astype(jnp.bfloat16)
     load.wait()
-    queries = heads_to_rows(line[...].astype(jnp.float32), width).astype(jnp.bfloat16)
+    queries = heads_to_rows(line[...].astype(jnp.float32), value_refs[0].shape[1]).astype(jnp.bfloat16)
     for copy in copies.values():
         copy.wait()
     for k in range(pools - 1, -1, -1):
@@ -114,7 +114,7 @@
                 preferred_element_type=jnp.float32,
             ).astype(jnp.bfloat16)
             keys_ref[k * rows : (k + 1) * rows, j * half : (j + 1) * half] = packed[:, :half]
-            value_refs[k][:rows, j * half : (j + 1) * half] = packed[:, half:]
+            value_refs[j * pools + k][:rows, :] = packed[:, half:]
         value_refs[k][rows:, :] = queries
 
 
@@ -189,8 +189,6 @@
     out_refs = rest[pools + 1 :]
     groups = key_ref.shape[1] // HEAD_SIZE
     rows = CAP * BLOCK
-    width = dense_ref.shape[1]
-    kept = dense_ref.shape[0] // BLOCK
     for k in range(pools - 1, -1, -1):
         live = live_ref[k : k + 1, :] > 0
         query = rows_to_heads(pay_refs[k][rows:, :].astype(jnp.float32))
@@ -205,6 +203,12 @@
                 (((1,), (1,)), ((), ())), preferred_element_type=jnp.float32,
             ) * (HEAD_SIZE ** -0.5)
             out_refs[k][mine, :] = jnp.where(live, scores, MASKED)
+    compact(pools, place_ref, pay_refs, dense_ref)
+
+
+def compact(pools, place_ref, value_refs, out_ref):
+    kept = out_ref.shape[0] // BLOCK
+    width = out_ref.shape[1]
     spare = pools * CAP - kept
     for i in range(kept):
         chosen = jnp.zeros((BLOCK, width), jnp.float32)
@@ -212,14 +216,18 @@
             place = place_ref[:, slot * BLOCK : slot * BLOCK + LANE]
             place = jnp.concatenate([place] * (width // LANE), axis=1)
             k, c = slot // CAP, slot % CAP
-            block = pay_refs[k][c * BLOCK : (c + 1) * BLOCK, :].astype(jnp.float32)
+            block = value_refs[k][c * BLOCK : (c + 1) * BLOCK, :].astype(jnp.float32)
             chosen = jnp.where(place == i, block, chosen)
-        dense_ref[i * BLOCK : (i + 1) * BLOCK, :] = chosen.astype(jnp.bfloat16)
-
-
-def attend_kernel(pools, heads, map_ref, place_ref, *rest):
+        out_ref[i * BLOCK : (i + 1) * BLOCK, :] = chosen.astype(jnp.bfloat16)
+
+
+def compact_kernel(pools, place_ref, *rest):
+    compact(pools, place_ref, rest[:pools][::-1], rest[-1])
+
+
+def attend_kernel(pools, heads, chunks, map_ref, place_ref, *rest):
     score_refs = rest[:pools][::-1]
-    value_refs = rest[pools : pools + heads]
+    value_refs = rest[pools : pools + heads * chunks]
     out_ref = rest[-1]
     head = lax.axis_index("heads")
     width = value_refs[0].shape[1]
@@ -243,8 +251,8 @@
         dense.append(chosen)
     attention = jnp.concatenate(dense, axis=1).astype(jnp.bfloat16)
     mixed = [None] * groups
-    for j in range(heads):
-        owner = head ^ j
+    for j in range(heads * chunks):
+        owner = (head ^ (j // chunks)) * chunks + j % chunks
         context = jnp.dot(
             attention, value_refs[j][...], preferred_element_type=jnp.float32
         ).astype(jnp.bfloat16)
@@ -256,15 +264,15 @@
                 preferred_element_type=jnp.float32,
             )
             mixed[g] = part if j == 0 else mixed[g] + part
-    for g in range(groups):
-        for q in range(QUERY_PER_GROUP):
-            at = (g * QUERY_PER_GROUP + q) * HEAD_SIZE
-            out_ref[:, at : at + HEAD_SIZE] = mixed[g][q : q + 1, :].astype(jnp.bfloat16)
+    out_ref[...] = jnp.concatenate(mixed, axis=0).astype(jnp.bfloat16)
 
 
 def join_kernel(*refs):
-    rows = [ref[...].reshape(-1, ref.shape[-1]).astype(jnp.float32) for ref in refs[:-1]]
-    refs[-1][...] = jnp.concatenate(rows, axis=0).astype(jnp.bfloat16)
+    lines = []
+    for ref in refs[:-1]:
+        block = ref[...].astype(jnp.float32)
+        lines.append(jnp.concatenate([block[n : n + 1, :] for n in range(block.shape[0])], axis=1))
+    refs[-1][...] = jnp.concatenate(lines, axis=0).astype(jnp.bfloat16)
 
 
 def project_kernel(pools, heads, reps, weight_ref, *rest):
@@ -310,7 +318,7 @@
     def join(*blocks):
         return pl.pallas_call(
             join_kernel,
-            out_shape=shape((sum(block.size for block in blocks) // queries.shape[2], queries.shape[2]), bf16),
+            out_shape=shape((len(blocks), queries.shape[2]), bf16),
             in_specs=[VMEM] * len(blocks),
             out_specs=VMEM,
             compiler_params=params(4),
@@ -325,13 +333,15 @@
         taken = {step: swap(blocks[step], axis, size, step) for step in range(size - 1, 0, -1)}
         return [blocks[0]] + [taken[step] for step in range(1, size)]
 
-    query_rows = queries.shape[2] // width
+    chunks = max(1, width // (2 * LANE))
+    query_rows = queries.shape[2] // (width // chunks)
     packed = pl.pallas_call(
         functools.partial(gather_kernel, pools),
         out_shape=[shape((pools * rows, width), bf16)]
-        + [shape((rows + query_rows, width), bf16)] * pools,
+        + [shape((rows + query_rows, width // chunks), bf16)] * pools
+        + [shape((rows, width // chunks), bf16)] * (pools * (chunks - 1)),
         in_specs=[SMEM, HBM, HBM],
-        out_specs=[VMEM] * (pools + 1),
+        out_specs=[VMEM] * (pools * chunks + 1),
         scratch_shapes=[
             pltpu.VMEM((pools * rows, 2 * width), bf16),
             pltpu.VMEM((1, queries.shape[2]), bf16),
@@ -341,25 +351,27 @@
         name="gather",
     )(in_hbm(selected), in_hbm(latents), in_hbm(queries))
     keys, values = packed[0], packed[1:]
+    late = (chunks - 1) * pools + (1 if chunks > 1 else 1)
 
     cosine, sine, turn, live, place, key_maps, value_maps, held = pl.pallas_call(
         functools.partial(table_kernel, pools, shard_blocks),
         out_shape=[shape((pools * rows, HEAD_SIZE), f32)] * 2
         + [shape((2 * pools, HEAD_SIZE), f32), shape((pools, rows), i32), shape((1, pools * rows), i32)]
         + [shape(key_latent_maps.shape, bf16), shape(value_latent_maps.shape, bf16)]
-        + [shape(values[1].shape, bf16)],
+        + [shape(values[late].shape, bf16)],
         in_specs=[SMEM, SMEM, VMEM] + [ANY] * 3,
         out_specs=[VMEM] * 7 + [ANY],
+        input_output_aliases={5: 7},
         scratch_shapes=[pltpu.SemaphoreType.DMA((2,))],
-        input_output_aliases={5: 7},
         compiler_params=params(16),
         name="tables",
     )(
         in_hbm(selected), in_hbm(lengths), in_hbm(freq), in_hbm(key_latent_maps),
-        in_hbm(value_latent_maps), values[1],
+        in_hbm(value_latent_maps), values[late],
     )
     key_parts = exchange(keys, "heads", heads)
-    value_parts = scatter([values[0], held, *values[2:]], "pool", pools)
+    values = [*values[:late], held, *values[late + 1 :]]
+    value_parts = [scatter(values[c * pools : (c + 1) * pools], "pool", pools) for c in range(chunks)]
 
     turned = pl.pallas_call(
         functools.partial(rebuild_kernel, pools, heads),
@@ -371,19 +383,31 @@
     )(key_maps, cosine, sine, *key_parts)
     dense, *scores = pl.pallas_call(
         functools.partial(score_kernel, pools),
-        out_shape=[shape((sel_count * BLOCK, width), bf16)] + [shape((own_heads, rows), f32)] * pools,
+        out_shape=[shape((sel_count * BLOCK, width // chunks), bf16)]
+        + [shape((own_heads, rows), f32)] * pools,
         in_specs=[VMEM] * (4 + pools),
         out_specs=[VMEM] * (1 + pools),
         compiler_params=params(16),
         name="score",
-    )(turn, live, place, turned, *value_parts[::-1])
-    dense_parts = exchange(dense, "heads", heads)
+    )(turn, live, place, turned, *value_parts[0][::-1])
     score_parts = scatter(scores, "pool", pools)
+    dense = [dense]
+    for parts in value_parts[1:]:
+        dense.append(pl.pallas_call(
+            functools.partial(compact_kernel, pools),
+            out_shape=shape((sel_count * BLOCK, width // chunks), bf16),
+            in_specs=[VMEM] * (1 + pools) + [ANY] * (pools // 2),
+            out_specs=VMEM,
+            compiler_params=params(16),
+            name="compact",
+        )(place, *parts[::-1], *score_parts[pools // 2 :]))
+    dense = [exchange(block, "heads", heads) for block in dense]
+    dense_parts = [dense[c][j] for j in range(heads) for c in range(chunks)]
 
     mine = pl.pallas_call(
-        functools.partial(attend_kernel, pools, heads),
-        out_shape=shape((1, own_heads * HEAD_SIZE), bf16),
-        in_specs=[VMEM] * (2 + pools + heads),
+        functools.partial(attend_kernel, pools, heads, chunks),
+        out_shape=shape((own_heads, HEAD_SIZE), bf16),
+        in_specs=[VMEM] * (2 + pools + heads * chunks),
         out_specs=VMEM,
         compiler_params=params(16),
         name="attend",

time: 43.8 us -> 48.4 us (1.11)
  starting transfers between devices: 18.9 us -> 25.7 us
  waiting for transfers between devices: 14.8 us -> 12.3 us
    ppermute x15 -> x19, starting transfers between devices: 18.9 us -> 25.7 us  [swap(): return lax.ppermute(value, axes, [(i, i ^ step) for i in range(size)])]
    ppermute x15 -> x19, waiting for transfers between devices: 14.8 us -> 12.3 us  [swap(): return lax.ppermute(value, axes, [(i, i ^ step) for i in range(size)])]
    pallas_call x2 -> x3, Pallas kernels: 0.55 us -> 0.99 us  [the longest x1 0.8 us: per_device(): pl.pallas_call(functools.partial(attend_kernel, pools, heads, chunks), ou...]
  transfers between devices with their start and end apart: 15 -> 19, of which waited for: 9 -> 10; matrix products, arithmetic and copies ran while one was open for 0% -> 0% of each run, Pallas kernels for 9% -> 9%
where the time goes in v9:
time: 48.4 us; the launch traced here: 48.2 us
  starting transfers between devices  25.7 us (53%)
  waiting for transfers between devices  12.3 us (25%)
  Pallas kernels  10 us (21%)
    ppermute x19, starting transfers between devices, swap(): return lax.ppermute(value, axes, [(i, i ^ step) for i in range(size)])  25.7 us
    ppermute x19, waiting for transfers between devices, swap(): return lax.ppermute(value, axes, [(i, i ^ step) for i in range(size)])  12.3 us
    pallas_call x1, Pallas kernels, per_device(): pl.pallas_call(functools.partial(table_kernel, pools, shard_blocks), out_...  2.97 us
    pallas_call x1, Pallas kernels, per_device(): pl.pallas_call(functools.partial(gather_kernel, pools), out_shape=[shape(...  2.94 us
    pallas_call x1, Pallas kernels, per_device(): pl.pallas_call(functools.partial(project_kernel, pools, heads, reps), out...  1.2 us
  transfers between devices with their start and end apart: 19, of which 10 were waited for; matrix products, arithmetic and copies ran while one was open for 0% of the time, Pallas kernels for 9%

profile of v9, /device:TPU:0, one launch (start us, length us, event | category | flops | bytes accessed | tf_op | source)
XLA Modules:
  0.0 48.2 jit_solution(826786376935826565)
XLA Ops:
  0.0 2.9 %gather.1 = (bf16[1024,256]{1,0:T(8,128)(2,1)S(1)}, bf16[288,128]{1,0:T(8,128)(2,1)S(1)}, bf16[288,128]{1,0:T(8,128)(2,1)S(1)}, bf16[288,128]{1,0:T(8,128)(2,1)S...) custom-call(s32[1,4,4]{2,1,0:T(4,128)} %sel_ref.3, ...), custom_call_target="tpu_custom_call" | custom-call | tf_op jit(solution)/shard_map/gather/pallas_call | solution.py:338
  3.0 3.0 %collective-permute-start = (bf16[1024,256]{1,0:T(8,128)(2,1)S(1)}, bf16[1024,256]{1,0:T(8,128)(2,1)S(1)}, u32[]{:S(2)}, u32[]{:S(2)}) collective-permute-start(bf16[1024,256]{1,0:T(8,128)(2,1)S(1)} %get-tuple-element.39.rest_0_), channel_id=1, source_target_pairs={{0,2},{2,0},{1,3},{3,1},{4,6},{6,4},{5,7},{7,5},{8,10},{10,8},{9,1... | collective-permute-start | bytes 1572872 | tf_op jit(solution)/shard_map/ppermute | solution.py:35
  6.0 3.6 %collective-permute-start.1 = (bf16[288,128]{1,0:T(8,128)(2,1)S(1)}, bf16[288,128]{1,0:T(8,128)(2,1)S(1)}, u32[]{:S(2)}, u32[]{:S(2)}) collective-permute-start(bf16[288,128]{1,0:T(8,128)(2,1)S(1)} %get-tuple-element.40), channel_id=1, source_target_pairs={{0,12},{4,8},{8,4},{12,0},{1,13},{5,9},{9,5},{13,1},{2,14},{6,10},... | collective-permute-start | bytes 221192 | tf_op jit(solution)/shard_map/ppermute | solution.py:35
  9.6 0.8 %collective-permute-start.3 = (bf16[288,128]{1,0:T(8,128)(2,1)S(1)}, bf16[288,128]{1,0:T(8,128)(2,1)S(1)}, u32[]{:S(2)}, u32[]{:S(2)}) collective-permute-start(bf16[288,128]{1,0:T(8,128)(2,1)S(1)} %get-tuple-element.42), channel_id=1, source_target_pairs={{0,4},{4,0},{8,12},{12,8},{1,5},{5,1},{9,13},{13,9},{2,6},{6,2},{1... | collective-permute-start | bytes 221192 | tf_op jit(solution)/shard_map/ppermute | solution.py:35
  10.3 3.6 %collective-permute-start.7 = (bf16[256,128]{1,0:T(8,128)(2,1)S(1)}, bf16[256,128]{1,0:T(8,128)(2,1)S(1)}, u32[]{:S(2)}, u32[]{:S(2)}) collective-permute-start(bf16[256,128]{1,0:T(8,128)(2,1)S(1)} %get-tuple-element.49), channel_id=1, source_target_pairs={{0,12},{4,8},{8,4},{12,0},{1,13},{5,9},{9,5},{13,1},{2,14},{6,10},... | collective-permute-start | bytes 196616 | tf_op jit(solution)/shard_map/ppermute | solution.py:35
  13.9 3.0 %tables.1 = (f32[1024,128]{1,0:T(8,128)S(1)}, f32[1024,128]{1,0:T(8,128)S(1)}, f32[8,128]{1,0:T(8,128)S(1)}, s32[4,256]{1,0:T(4,128)S(1)}, s32[1,1024]{1,0:T(1,1...) custom-call(s32[1,4,4]{2,1,0:T(4,128)} %sel_ref.3, ...), custom_call_target="tpu_custom_call", output_to_operand_aliasing={{7}: (5, {})} | custom-call | tf_op jit(solution)/shard_map/tables/pallas_call | solution.py:356
  16.9 0.3 collective-permute-start.8
  17.3 0.6 %collective-permute-done.rest_1_ = bf16[1024,256]{1,0:T(8,128)(2,1)S(1)} collective-permute-done((bf16[1024,256]{1,0:T(8,128)(2,1)S(1)}, bf16[1024,256]{1,0:T(8,128)(2,1)S(1)}, u32[]{:S(2)}, u32[]{:S(2)}) %collective-permute-start) | collective-permute-done | bytes 524320 | tf_op jit(solution)/shard_map/ppermute | solution.py:35
  17.9 1.8 %collective-permute-start.9 = (bf16[256,128]{1,0:T(8,128)(2,1)S(1)}, bf16[256,128]{1,0:T(8,128)(2,1)S(1)}, u32[]{:S(2)}, u32[]{:S(2)}) collective-permute-start(bf16[256,128]{1,0:T(8,128)(2,1)S(1)} %get-tuple-element.51), channel_id=1, source_target_pairs={{0,4},{4,0},{8,12},{12,8},{1,5},{5,1},{9,13},{13,9},{2,6},{6,2},{1... | collective-permute-start | bytes 196616 | tf_op jit(solution)/shard_map/ppermute | solution.py:35
  19.7 0.9 %rebuild.1.key_ref = bf16[1024,512]{1,0:T(8,128)(2,1)S(1)} custom-call(bf16[512,512]{1,0:T(8,128)(2,1)S(1)} %get-tuple-element.36.map_ref, f32[1024,128]{1,0:T(8,128)S(1)} %get-tuple-element.37.cos_ref, f32[1024,128]{1,0:T(8,128)S(1)} %get-tuple-element.38.sin_ref, bf16[1024,256]{1,0:T(8,128)(2,1)S(1)} %get-tuple-element.39.rest_0_, ...), custom_call_target="tpu_custom_call" | custom-call | tf_op jit(solution)/shard_map/rebuild/pallas_call | solution.py:376
  20.6 0.4 score.1
  21.0 2.5 %collective-permute-start.4 = (f32[32,256]{1,0:T(8,128)S(1)}, f32[32,256]{1,0:T(8,128)S(1)}, u32[]{:S(2)}, u32[]{:S(2)}) collective-permute-start(f32[32,256]{1,0:T(8,128)S(1)} %get-tuple-element.44), channel_id=1, source_target_pairs={{0,12},{4,8},{8,4},{12,0},{1,13},{5,9},{9,5},{13,1},{2,14},{6,10},... | collective-permute-start | bytes 98312 | tf_op jit(solution)/shard_map/ppermute | solution.py:35
  23.8 1.5 %collective-permute-start.10 = (bf16[512,128]{1,0:T(8,128)(2,1)S(1)}, bf16[512,128]{1,0:T(8,128)(2,1)S(1)}, u32[]{:S(2)}, u32[]{:S(2)}) collective-permute-start(bf16[512,128]{1,0:T(8,128)(2,1)S(1)} %get-tuple-element.48.rest_4_), channel_id=1, source_target_pairs={{0,2},{2,0},{1,3},{3,1},{4,6},{6,4},{5,7},{7,5},{8,10},{10,8},{9,1... | collective-permute-start | bytes 393224 | tf_op jit(solution)/shard_map/ppermute | solution.py:35
  25.3 1.5 %collective-permute-done.4.rest_5_.rest_0_ = f32[32,256]{1,0:T(8,128)S(1)} collective-permute-done((f32[32,256]{1,0:T(8,128)S(1)}, f32[32,256]{1,0:T(8,128)S(1)}, u32[]{:S(2)}, u32[]{:S(2)}) %collective-permute-start.4) | collective-permute-done | bytes 32800 | tf_op jit(solution)/shard_map/ppermute | solution.py:35
  26.8 1.9 %collective-permute-done.5.rest_4_.rest_1_ = f32[32,256]{1,0:T(8,128)S(1)} collective-permute-done((f32[32,256]{1,0:T(8,128)S(1)}, f32[32,256]{1,0:T(8,128)S(1)}, u32[]{:S(2)}, u32[]{:S(2)}) %collective-permute-start.5) | collective-permute-done | bytes 32800 | tf_op jit(solution)/shard_map/ppermute | solution.py:35
  28.9 1.6 %collective-permute-start.11 = (bf16[512,128]{1,0:T(8,128)(2,1)S(1)}, bf16[512,128]{1,0:T(8,128)(2,1)S(1)}, u32[]{:S(2)}, u32[]{:S(2)}) collective-permute-start(bf16[512,128]{1,0:T(8,128)(2,1)S(1)} %compact.1.rest_5_), channel_id=1, source_target_pairs={{0,2},{2,0},{1,3},{3,1},{4,6},{6,4},{5,7},{7,5},{8,10},{10,8},{9,1... | collective-permute-start | bytes 393224 | tf_op jit(solution)/shard_map/ppermute | solution.py:35
  30.4 0.4 collective-permute-start.6
  30.9 3.5 %collective-permute-done.6.rest_2_ = f32[32,256]{1,0:T(8,128)S(1)} collective-permute-done((f32[32,256]{1,0:T(8,128)S(1)}, f32[32,256]{1,0:T(8,128)S(1)}, u32[]{:S(2)}, u32[]{:S(2)}) %collective-permute-start.6) | collective-permute-done | bytes 32800 | tf_op jit(solution)/shard_map/ppermute | solution.py:35
  34.4 0.8 %attend.1.refs_0_ = bf16[32,128]{1,0:T(8,128)(2,1)S(1)} custom-call(bf16[512,512]{1,0:T(8,128)(2,1)S(1)} %get-tuple-element.32.map_ref, s32[1,1024]{1,0:T(1,128)S(1)} %get-tuple-element.33.place_ref, f32[32,256]{1,0:T(8,128)S(1)} %collective-permute-done.4.rest_5_.rest_0_, f32[32,256]{1,0:T(8,128)S(1)} %collective-permute-done.5.rest_4_.rest_1_, ...), custom_call_target="tpu_custom_call" | custom-call | tf_op jit(solution)/shard_map/attend/pallas_call | solution.py:407
  35.2 1.2 %collective-permute-done.12.refs_1_ = bf16[32,128]{1,0:T(8,128)(2,1)S(1)} collective-permute-done((bf16[32,128]{1,0:T(8,128)(2,1)S(1)}, bf16[32,128]{1,0:T(8,128)(2,1)S(1)}, u32[]{:S(2)}, u32[]{:S(2)}) %collective-permute-start.12) | collective-permute-done | bytes 8224 | tf_op jit(solution)/shard_map/ppermute | solution.py:35
  36.4 1.3 %collective-permute-start.15 = (bf16[2,4096]{1,0:T(2,128)(2,1)S(1)}, bf16[2,4096]{1,0:T(2,128)(2,1)S(1)}, u32[]{:S(2)}, u32[]{:S(2)}) collective-permute-start(bf16[2,4096]{1,0:T(2,128)(2,1)S(1)} %join.1.rest_0_), channel_id=1, source_target_pairs={{0,12},{4,8},{8,4},{12,0},{1,13},{5,9},{9,5},{13,1},{2,14},{6,10},... | collective-permute-start | bytes 49160 | tf_op jit(solution)/shard_map/ppermute | solution.py:35
  37.7 0.6 %collective-permute-start.14 = (bf16[2,4096]{1,0:T(2,128)(2,1)S(1)}, bf16[2,4096]{1,0:T(2,128)(2,1)S(1)}, u32[]{:S(2)}, u32[]{:S(2)}) collective-permute-start(bf16[2,4096]{1,0:T(2,128)(2,1)S(1)} %join.1.rest_0_), channel_id=1, source_target_pairs={{0,8},{4,12},{8,0},{12,4},{1,9},{5,13},{9,1},{13,5},{2,10},{6,14},... | collective-permute-start | bytes 49160 | tf_op jit(solution)/shard_map/ppermute | solution.py:35
  38.3 2.5 %collective-permute-start.13 = (bf16[2,4096]{1,0:T(2,128)(2,1)S(1)}, bf16[2,4096]{1,0:T(2,128)(2,1)S(1)}, u32[]{:S(2)}, u32[]{:S(2)}) collective-permute-start(bf16[2,4096]{1,0:T(2,128)(2,1)S(1)} %join.1.rest_0_), channel_id=1, source_target_pairs={{0,4},{4,0},{8,12},{12,8},{1,5},{5,1},{9,13},{13,9},{2,6},{6,2},{1... | collective-permute-start | bytes 49160 | tf_op jit(solution)/shard_map/ppermute | solution.py:35
  40.8 1.1 %collective-permute-done.15.rest_3_ = bf16[2,4096]{1,0:T(2,128)(2,1)S(1)} collective-permute-done((bf16[2,4096]{1,0:T(2,128)(2,1)S(1)}, bf16[2,4096]{1,0:T(2,128)(2,1)S(1)}, u32[]{:S(2)}, u32[]{:S(2)}) %collective-permute-start.15) | collective-permute-done | bytes 16416 | tf_op jit(solution)/shard_map/ppermute | solution.py:35
  42.0 0.4 collective-permute-done.14.rest_2_
  42.3 0.2 collective-permute-done.13.rest_1_
  42.5 1.2 %project.1 = (f32[2,1024]{1,0:T(2,128)S(1)}, f32[2,1024]{1,0:T(2,128)S(1)}, f32[2,1024]{1,0:T(2,128)S(1)}, f32[2,1024]{1,0:T(2,128)S(1)}) custom-call(bf16[4096,1024]{1,0:T(8,128)(2,1)S(1)} %copy-done, bf16[2,4096]{1,0:T(2,128)(2,1)S(1)} %join.1.rest_0_, bf16[2,4096]{1,0:T(2,128)(2,1)S(1)} %collective-permute-done.13.rest_1_, ...), custom_call_target="tpu_custom_call" | custom-call | tf_op jit(solution)/shard_map/project/pallas_call | solution.py:420
  43.8 1.1 %collective-permute-start.17 = (f32[2,1024]{1,0:T(2,128)S(1)}, f32[2,1024]{1,0:T(2,128)S(1)}, u32[]{:S(2)}, u32[]{:S(2)}) collective-permute-start(f32[2,1024]{1,0:T(2,128)S(1)} %get-tuple-element.54), channel_id=1, source_target_pairs={{0,2},{1,3},{2,0},{3,1},{4,6},{5,7},{6,4},{7,5},{8,10},{9,11},{10,... | collective-permute-start | bytes 24584 | tf_op jit(solution)/shard_map/ppermute | solution.py:35
  44.9 0.7 %collective-permute-start.18 = (f32[2,1024]{1,0:T(2,128)S(1)}, f32[2,1024]{1,0:T(2,128)S(1)}, u32[]{:S(2)}, u32[]{:S(2)}) collective-permute-start(f32[2,1024]{1,0:T(2,128)S(1)} %get-tuple-element.55), channel_id=1, source_target_pairs={{0,1},{1,0},{2,3},{3,2},{4,5},{5,4},{6,7},{7,6},{8,9},{9,8},{10,11... | collective-permute-start | bytes 24584 | tf_op jit(solution)/shard_map/ppermute | solution.py:35
  45.7 1.2 %collective-permute-done.16.refs_0_ = f32[2,1024]{1,0:T(2,128)S(1)} collective-permute-done((f32[2,1024]{1,0:T(2,128)S(1)}, f32[2,1024]{1,0:T(2,128)S(1)}, u32[]{:S(2)}, u32[]{:S(2)}) %collective-permute-start.16) | collective-permute-done | bytes 8224 | tf_op jit(solution)/shard_map/ppermute | solution.py:35
  46.9 0.7 %collective-permute-done.17.refs_1_ = f32[2,1024]{1,0:T(2,128)S(1)} collective-permute-done((f32[2,1024]{1,0:T(2,128)S(1)}, f32[2,1024]{1,0:T(2,128)S(1)}, u32[]{:S(2)}, u32[]{:S(2)}) %collective-permute-start.17) | collective-permute-done | bytes 8224 | tf_op jit(solution)/shard_map/ppermute | solution.py:35
  47.6 0.6 %finish.1 = bf16[1,2,2048]{2,1,0:T(2,128)(2,1)} custom-call(f32[2,1024]{1,0:T(2,128)S(1)} %collective-permute-done.16.refs_0_, f32[2,1024]{1,0:T(2,128)S(1)} %collective-permute-done.17.refs_1_, f32[2,1024]{1,0:T(2,128)S(1)} %collective-permute-done.18.refs_2_, f32[2,1024]{1,0:T(2,128)S(1)} %get-tuple-element.56.refs_3_), custom_call_target="tpu_custom_call" | custom-call | tf_op jit(solution)/shard_map/finish/pallas_call | solution.py:429
  (17 shorter events, 0.5 us)
Async XLA Ops:
  0.0 42.5 %copy-start = (bf16[4096,1024]{1,0:T(8,128)(2,1)S(1)}, bf16[4096,1024]{1,0:T(8,128)(2,1)}, u32[]{:S(2)}) copy-start(bf16[4096,1024]{1,0:T(8,128)(2,1)} %weight_ref.1) | copy-start | bytes 25165828
  3.0 14.9 %collective-permute-start = (bf16[1024,256]{1,0:T(8,128)(2,1)S(1)}, bf16[1024,256]{1,0:T(8,128)(2,1)S(1)}, u32[]{:S(2)}, u32[]{:S(2)}) collective-permute-start(bf16[1024,256]{1,0:T(8,128)(2,1)S(1)} %get-tuple-element.39.rest_0_), channel_id=1, source_target_pairs={{0,2},{2,0},{1,3},{3,1},{4,6},{6,4},{5,7},{7,5},{8,10},{10,8},{9,1... | collective-permute-start | bytes 1572872 | tf_op jit(solution)/shard_map/ppermute | solution.py:35
  6.0 11.0 %collective-permute-start.1 = (bf16[288,128]{1,0:T(8,128)(2,1)S(1)}, bf16[288,128]{1,0:T(8,128)(2,1)S(1)}, u32[]{:S(2)}, u32[]{:S(2)}) collective-permute-start(bf16[288,128]{1,0:T(8,128)(2,1)S(1)} %get-tuple-element.40), channel_id=1, source_target_pairs={{0,12},{4,8},{8,4},{12,0},{1,13},{5,9},{9,5},{13,1},{2,14},{6,10},... | collective-permute-start | bytes 221192 | tf_op jit(solution)/shard_map/ppermute | solution.py:35
  9.6 11.0 %collective-permute-start.2 = (bf16[288,128]{1,0:T(8,128)(2,1)S(1)}, bf16[288,128]{1,0:T(8,128)(2,1)S(1)}, u32[]{:S(2)}, u32[]{:S(2)}) collective-permute-start(bf16[288,128]{1,0:T(8,128)(2,1)S(1)} %get-tuple-element.41), channel_id=1, source_target_pairs={{0,8},{4,12},{8,0},{12,4},{1,9},{5,13},{9,1},{13,5},{2,10},{6,14},... | collective-permute-start | bytes 221192 | tf_op jit(solution)/shard_map/ppermute | solution.py:35
  9.6 11.0 %collective-permute-start.3 = (bf16[288,128]{1,0:T(8,128)(2,1)S(1)}, bf16[288,128]{1,0:T(8,128)(2,1)S(1)}, u32[]{:S(2)}, u32[]{:S(2)}) collective-permute-start(bf16[288,128]{1,0:T(8,128)(2,1)S(1)} %get-tuple-element.42), channel_id=1, source_target_pairs={{0,4},{4,0},{8,12},{12,8},{1,5},{5,1},{9,13},{13,9},{2,6},{6,2},{1... | collective-permute-start | bytes 221192 | tf_op jit(solution)/shard_map/ppermute | solution.py:35
  10.3 13.4 %collective-permute-start.7 = (bf16[256,128]{1,0:T(8,128)(2,1)S(1)}, bf16[256,128]{1,0:T(8,128)(2,1)S(1)}, u32[]{:S(2)}, u32[]{:S(2)}) collective-permute-start(bf16[256,128]{1,0:T(8,128)(2,1)S(1)} %get-tuple-element.49), channel_id=1, source_target_pairs={{0,12},{4,8},{8,4},{12,0},{1,13},{5,9},{9,5},{13,1},{2,14},{6,10},... | collective-permute-start | bytes 196616 | tf_op jit(solution)/shard_map/ppermute | solution.py:35
  16.9 8.3 %collective-permute-start.8 = (bf16[256,128]{1,0:T(8,128)(2,1)S(1)}, bf16[256,128]{1,0:T(8,128)(2,1)S(1)}, u32[]{:S(2)}, u32[]{:S(2)}) collective-permute-start(bf16[256,128]{1,0:T(8,128)(2,1)S(1)} %get-tuple-element.50), channel_id=1, source_target_pairs={{0,8},{4,12},{8,0},{12,4},{1,9},{5,13},{9,1},{13,5},{2,10},{6,14},... | collective-permute-start | bytes 196616 | tf_op jit(solution)/shard_map/ppermute | solution.py:35
  17.9 7.4 %collective-permute-start.9 = (bf16[256,128]{1,0:T(8,128)(2,1)S(1)}, bf16[256,128]{1,0:T(8,128)(2,1)S(1)}, u32[]{:S(2)}, u32[]{:S(2)}) collective-permute-start(bf16[256,128]{1,0:T(8,128)(2,1)S(1)} %get-tuple-element.51), channel_id=1, source_target_pairs={{0,4},{4,0},{8,12},{12,8},{1,5},{5,1},{9,13},{13,9},{2,6},{6,2},{1... | collective-permute-start | bytes 196616 | tf_op jit(solution)/shard_map/ppermute | solution.py:35
  21.0 5.8 %collective-permute-start.4 = (f32[32,256]{1,0:T(8,128)S(1)}, f32[32,256]{1,0:T(8,128)S(1)}, u32[]{:S(2)}, u32[]{:S(2)}) collective-permute-start(f32[32,256]{1,0:T(8,128)S(1)} %get-tuple-element.44), channel_id=1, source_target_pairs={{0,12},{4,8},{8,4},{12,0},{1,13},{5,9},{9,5},{13,1},{2,14},{6,10},... | collective-permute-start | bytes 98312 | tf_op jit(solution)/shard_map/ppermute | solution.py:35
  23.6 5.2 %collective-permute-start.5 = (f32[32,256]{1,0:T(8,128)S(1)}, f32[32,256]{1,0:T(8,128)S(1)}, u32[]{:S(2)}, u32[]{:S(2)}) collective-permute-start(f32[32,256]{1,0:T(8,128)S(1)} %get-tuple-element.45), channel_id=1, source_target_pairs={{0,8},{4,12},{8,0},{12,4},{1,9},{5,13},{9,1},{13,5},{2,10},{6,14},... | collective-permute-start | bytes 98312 | tf_op jit(solution)/shard_map/ppermute | solution.py:35
  23.8 10.6 %collective-permute-start.10 = (bf16[512,128]{1,0:T(8,128)(2,1)S(1)}, bf16[512,128]{1,0:T(8,128)(2,1)S(1)}, u32[]{:S(2)}, u32[]{:S(2)}) collective-permute-start(bf16[512,128]{1,0:T(8,128)(2,1)S(1)} %get-tuple-element.48.rest_4_), channel_id=1, source_target_pairs={{0,2},{2,0},{1,3},{3,1},{4,6},{6,4},{5,7},{7,5},{8,10},{10,8},{9,1... | collective-permute-start | bytes 393224 | tf_op jit(solution)/shard_map/ppermute | solution.py:35
  28.9 5.5 %collective-permute-start.11 = (bf16[512,128]{1,0:T(8,128)(2,1)S(1)}, bf16[512,128]{1,0:T(8,128)(2,1)S(1)}, u32[]{:S(2)}, u32[]{:S(2)}) collective-permute-start(bf16[512,128]{1,0:T(8,128)(2,1)S(1)} %compact.1.rest_5_), channel_id=1, source_target_pairs={{0,2},{2,0},{1,3},{3,1},{4,6},{6,4},{5,7},{7,5},{8,10},{10,8},{9,1... | collective-permute-start | bytes 393224 | tf_op jit(solution)/shard_map/ppermute | solution.py:35
  30.4 3.9 %collective-permute-start.6 = (f32[32,256]{1,0:T(8,128)S(1)}, f32[32,256]{1,0:T(8,128)S(1)}, u32[]{:S(2)}, u32[]{:S(2)}) collective-permute-start(f32[32,256]{1,0:T(8,128)S(1)} %get-tuple-element.46), channel_id=1, source_target_pairs={{0,4},{4,0},{8,12},{12,8},{1,5},{5,1},{9,13},{13,9},{2,6},{6,2},{1... | collective-permute-start | bytes 98312 | tf_op jit(solution)/shard_map/ppermute | solution.py:35
  35.2 1.2 %collective-permute-start.12 = (bf16[32,128]{1,0:T(8,128)(2,1)S(1)}, bf16[32,128]{1,0:T(8,128)(2,1)S(1)}, u32[]{:S(2)}, u32[]{:S(2)}) collective-permute-start(bf16[32,128]{1,0:T(8,128)(2,1)S(1)} %attend.1.refs_0_), channel_id=1, source_target_pairs={{0,1},{1,0},{2,3},{3,2},{4,5},{5,4},{6,7},{7,6},{8,9},{9,8},{10,11... | collective-permute-start | bytes 24584 | tf_op jit(solution)/shard_map/ppermute | solution.py:35
  36.4 5.6 %collective-permute-start.15 = (bf16[2,4096]{1,0:T(2,128)(2,1)S(1)}, bf16[2,4096]{1,0:T(2,128)(2,1)S(1)}, u32[]{:S(2)}, u32[]{:S(2)}) collective-permute-start(bf16[2,4096]{1,0:T(2,128)(2,1)S(1)} %join.1.rest_0_), channel_id=1, source_target_pairs={{0,12},{4,8},{8,4},{12,0},{1,13},{5,9},{9,5},{13,1},{2,14},{6,10},... | collective-permute-start | bytes 49160 | tf_op jit(solution)/shard_map/ppermute | solution.py:35
  37.7 4.6 %collective-permute-start.14 = (bf16[2,4096]{1,0:T(2,128)(2,1)S(1)}, bf16[2,4096]{1,0:T(2,128)(2,1)S(1)}, u32[]{:S(2)}, u32[]{:S(2)}) collective-permute-start(bf16[2,4096]{1,0:T(2,128)(2,1)S(1)} %join.1.rest_0_), channel_id=1, source_target_pairs={{0,8},{4,12},{8,0},{12,4},{1,9},{5,13},{9,1},{13,5},{2,10},{6,14},... | collective-permute-start | bytes 49160 | tf_op jit(solution)/shard_map/ppermute | solution.py:35
  38.3 4.2 %collective-permute-start.13 = (bf16[2,4096]{1,0:T(2,128)(2,1)S(1)}, bf16[2,4096]{1,0:T(2,128)(2,1)S(1)}, u32[]{:S(2)}, u32[]{:S(2)}) collective-permute-start(bf16[2,4096]{1,0:T(2,128)(2,1)S(1)} %join.1.rest_0_), channel_id=1, source_target_pairs={{0,4},{4,0},{8,12},{12,8},{1,5},{5,1},{9,13},{13,9},{2,6},{6,2},{1... | collective-permute-start | bytes 49160 | tf_op jit(solution)/shard_map/ppermute | solution.py:35
  43.8 3.1 %collective-permute-start.16 = (f32[2,1024]{1,0:T(2,128)S(1)}, f32[2,1024]{1,0:T(2,128)S(1)}, u32[]{:S(2)}, u32[]{:S(2)}) collective-permute-start(f32[2,1024]{1,0:T(2,128)S(1)} %get-tuple-element.53), channel_id=1, source_target_pairs={{0,3},{1,2},{2,1},{3,0},{4,7},{5,6},{6,5},{7,4},{8,11},{9,10},{10,... | collective-permute-start | bytes 24584 | tf_op jit(solution)/shard_map/ppermute | solution.py:35
  43.8 3.7 %collective-permute-start.17 = (f32[2,1024]{1,0:T(2,128)S(1)}, f32[2,1024]{1,0:T(2,128)S(1)}, u32[]{:S(2)}, u32[]{:S(2)}) collective-permute-start(f32[2,1024]{1,0:T(2,128)S(1)} %get-tuple-element.54), channel_id=1, source_target_pairs={{0,2},{1,3},{2,0},{3,1},{4,6},{5,7},{6,4},{7,5},{8,10},{9,11},{10,... | collective-permute-start | bytes 24584 | tf_op jit(solution)/shard_map/ppermute | solution.py:35
  44.9 2.6 %collective-permute-start.18 = (f32[2,1024]{1,0:T(2,128)S(1)}, f32[2,1024]{1,0:T(2,128)S(1)}, u32[]{:S(2)}, u32[]{:S(2)}) collective-permute-start(f32[2,1024]{1,0:T(2,128)S(1)} %get-tuple-element.55), channel_id=1, source_target_pairs={{0,1},{1,0},{2,3},{3,2},{4,5},{5,4},{6,7},{7,6},{8,9},{9,8},{10,11... | collective-permute-start | bytes 24584 | tf_op jit(solution)/shard_map/ppermute | solution.py:35

commit v10 on v7

--- a/solution.py
+++ b/solution.py
@@ -185,8 +185,8 @@
 
 def score_kernel(pools, turn_ref, live_ref, place_ref, key_ref, *rest):
     pay_refs = rest[:pools][::-1]
-    dense_ref = rest[pools]
-    out_refs = rest[pools + 1 :]
+    dense_ref, out_ref = rest[pools:]
+    me = lax.axis_index("pool")
     groups = key_ref.shape[1] // HEAD_SIZE
     rows = CAP * BLOCK
     width = dense_ref.shape[1]
@@ -204,7 +204,7 @@
                 query[mine, :], key_ref[k * rows : (k + 1) * rows, g * HEAD_SIZE : (g + 1) * HEAD_SIZE],
                 (((1,), (1,)), ((), ())), preferred_element_type=jnp.float32,
             ) * (HEAD_SIZE ** -0.5)
-            out_refs[k][mine, :] = jnp.where(live, scores, MASKED)
+            out_ref[me ^ k, mine, :] = jnp.where(live, scores, MASKED)
     spare = pools * CAP - kept
     for i in range(kept):
         chosen = jnp.zeros((BLOCK, width), jnp.float32)
@@ -218,13 +218,14 @@
 
 
 def attend_kernel(pools, heads, map_ref, place_ref, *rest):
-    score_refs = rest[:pools][::-1]
-    value_refs = rest[pools : pools + heads]
+    score_ref = rest[0]
+    value_refs = rest[1 : 1 + heads]
+    me = lax.axis_index("pool")
     out_ref = rest[-1]
     head = lax.axis_index("heads")
     width = value_refs[0].shape[1]
     groups = map_ref.shape[1] // HEAD_SIZE
-    scores = [ref[...] for ref in score_refs]
+    scores = [score_ref[me ^ k] for k in range(pools)]
     top = functools.reduce(jnp.maximum, [jnp.max(s, axis=1, keepdims=True) for s in scores])
     weights = [jnp.exp(s - top) for s in scores]
     total = functools.reduce(jnp.add, [jnp.sum(w, axis=1, keepdims=True) for w in weights])
@@ -263,22 +264,22 @@
 
 
 def join_kernel(*refs):
-    rows = [ref[...].reshape(-1, ref.shape[-1]).astype(jnp.float32) for ref in refs[:-1]]
-    refs[-1][...] = jnp.concatenate(rows, axis=0).astype(jnp.bfloat16)
-
-
-def project_kernel(pools, heads, reps, weight_ref, *rest):
-    row_refs = rest[:pools]
-    out_refs = rest[pools:-1]
+    rows = [ref[...].astype(jnp.float32) for ref in refs[:-1]]
+    rows = jnp.concatenate(rows, axis=0).astype(jnp.bfloat16)
+    for i in range(refs[-1].shape[0]):
+        refs[-1][i] = rows
+
+
+def project_kernel(pools, heads, reps, weight_ref, row_ref, *rest):
+    out_refs = rest[:-1]
     acc = rest[-1]
-    left = jnp.concatenate([ref[...].astype(jnp.float32) for ref in row_refs], axis=0).astype(jnp.bfloat16)
+    left = jnp.concatenate([row_ref[i].astype(jnp.float32) for i in range(pools)], axis=0).astype(jnp.bfloat16)
     acc[...] = jnp.dot(left, weight_ref[...], preferred_element_type=jnp.float32)
-    pool = lax.axis_index("pool")
     head = lax.axis_index("heads")
     each = pools // heads
     for d in range(heads * reps):
         for u in range(each):
-            n = (pool ^ ((head ^ (d // reps)) * each + u)) * reps + d % reps
+            n = ((head ^ (d // reps)) * each + u) * reps + d % reps
             out_refs[d][u : u + 1, :] = acc[pl.ds(n, 1), :]
 
 
@@ -310,7 +311,7 @@
     def join(*blocks):
         return pl.pallas_call(
             join_kernel,
-            out_shape=shape((sum(block.size for block in blocks) // queries.shape[2], queries.shape[2]), bf16),
+            out_shape=shape((pools, len(blocks), queries.shape[2]), bf16),
             in_specs=[VMEM] * len(blocks),
             out_specs=VMEM,
             compiler_params=params(4),
@@ -369,39 +370,39 @@
         compiler_params=params(20),
         name="rebuild",
     )(key_maps, cosine, sine, *key_parts)
-    dense, *scores = pl.pallas_call(
+    dense, scores = pl.pallas_call(
         functools.partial(score_kernel, pools),
-        out_shape=[shape((sel_count * BLOCK, width), bf16)] + [shape((own_heads, rows), f32)] * pools,
+        out_shape=[shape((sel_count * BLOCK, width), bf16), shape((pools, own_heads, rows), f32)],
         in_specs=[VMEM] * (4 + pools),
-        out_specs=[VMEM] * (1 + pools),
+        out_specs=[VMEM] * 2,
         compiler_params=params(16),
         name="score",
     )(turn, live, place, turned, *value_parts[::-1])
     dense_parts = exchange(dense, "heads", heads)
-    score_parts = scatter(scores, "pool", pools)
+    score_parts = lax.all_to_all(scores, "pool", split_axis=0, concat_axis=0, tiled=True)
 
     mine = pl.pallas_call(
         functools.partial(attend_kernel, pools, heads),
         out_shape=shape((1, own_heads * HEAD_SIZE), bf16),
-        in_specs=[VMEM] * (2 + pools + heads),
+        in_specs=[VMEM] * (3 + heads),
         out_specs=VMEM,
         compiler_params=params(16),
         name="attend",
-    )(value_maps, place, *score_parts[::-1], *dense_parts)
+    )(value_maps, place, score_parts, *dense_parts)
     own_rows = join(*exchange(mine, "rep", reps))
-    row_parts = exchange(own_rows, "pool", pools)
+    all_rows = lax.all_to_all(own_rows, "pool", split_axis=0, concat_axis=0, tiled=True)
 
     own_columns = out_weight.shape[1]
     each = pools // heads
     parts = pl.pallas_call(
         functools.partial(project_kernel, pools, heads, reps),
         out_shape=[shape((each, own_columns), f32)] * (heads * reps),
-        in_specs=[VMEM] * (pools + 1),
+        in_specs=[VMEM] * 2,
         out_specs=[VMEM] * (heads * reps),
         scratch_shapes=[pltpu.VMEM((pools * reps, own_columns), f32)],
         compiler_params=params(24),
         name="project",
-    )(in_vmem(out_weight), *row_parts)
+    )(in_vmem(out_weight), all_rows)
     return pl.pallas_call(
         functools.partial(finish_kernel, heads, reps),
         out_shape=shape((1, each, reps * own_columns), bf16),

time: 43.8 us -> 47.7 us (1.089)
  blocking collectives: 0 us -> 17.7 us
  starting transfers between devices: 18.9 us -> 10 us
  waiting for transfers between devices: 14.8 us -> 9.84 us
    all_to_all x0 -> x2, blocking collectives: none -> 17.7 us  [the longest x1 9.5 us: per_device(): lax.all_to_all(scores, 'pool', split_axis=0, concat_axis=0, tiled=True)]
    ppermute x15 -> x9, starting transfers between devices: 18.9 us -> 10 us  [swap(): return lax.ppermute(value, axes, [(i, i ^ step) for i in range(size)])]
    ppermute x15 -> x9, waiting for transfers between devices: 14.8 us -> 9.84 us  [swap(): return lax.ppermute(value, axes, [(i, i ^ step) for i in range(size)])]
  transfers between devices with their start and end apart: 15 -> 9, of which waited for: 9 -> 5; matrix products, arithmetic and copies ran while one was open for 0% -> 0% of each run, Pallas kernels for 9% -> 8%
where the time goes in v10:
time: 47.7 us; the launch traced here: 47.4 us
  blocking collectives  17.7 us (37%)
  starting transfers between devices  10 us (21%)
  waiting for transfers between devices  9.84 us (21%)
  Pallas kernels  9.71 us (20%)
    ppermute x9, starting transfers between devices, swap(): return lax.ppermute(value, axes, [(i, i ^ step) for i in range(size)])  10 us
    ppermute x9, waiting for transfers between devices, swap(): return lax.ppermute(value, axes, [(i, i ^ step) for i in range(size)])  9.84 us
    all_to_all x1, blocking collectives, per_device(): lax.all_to_all(scores, 'pool', split_axis=0, concat_axis=0, tiled=True)  9.5 us
    all_to_all x1, blocking collectives, per_device(): lax.all_to_all(own_rows, 'pool', split_axis=0, concat_axis=0, tiled=True)  8.22 us
    pallas_call x1, Pallas kernels, per_device(): pl.pallas_call(functools.partial(table_kernel, pools, shard_blocks), out_...  2.97 us
    pallas_call x1, Pallas kernels, per_device(): pl.pallas_call(functools.partial(gather_kernel, pools), out_shape=[shape(...  2.94 us
    pallas_call x1, Pallas kernels, per_device(): pl.pallas_call(functools.partial(project_kernel, pools, heads, reps), out...  1.2 us
  transfers between devices with their start and end apart: 9, of which 5 were waited for; matrix products, arithmetic and copies ran while one was open for 0% of the time, Pallas kernels for 8%

profile of v10, /device:TPU:0, one launch (start us, length us, event | category | flops | bytes accessed | tf_op | source)
XLA Modules:
  0.0 47.4 jit_solution(12561954064867211591)
XLA Ops:
  0.0 0.0 copy-start
  0.0 2.9 %gather.1 = (bf16[1024,256]{1,0:T(8,128)(2,1)S(1)}, bf16[272,256]{1,0:T(8,128)(2,1)S(1)}, bf16[272,256]{1,0:T(8,128)(2,1)S(1)}, bf16[272,256]{1,0:T(8,128)(2,1)S(1)}, bf16[272,256]{1,0:T(8,128)(2,1)S(1)}) custom-call(s32[1,4,4]{2,1,0:T(4,128)} %sel_ref.3, bf16[1,4,1024,512]{3,2,1,0:T(8,128)(2,1)} %lat_ref.1, bf16[1,1,4096]{2,1,0:T(2,128)(2,1)} %query_ref.1), custom_call_target="tpu_custom_call" | custom-call | tf_op jit(solution)/shard_map/gather/pallas_call | solution.py:330
  3.0 3.0 %collective-permute-start = (bf16[1024,256]{1,0:T(8,128)(2,1)S(1)}, bf16[1024,256]{1,0:T(8,128)(2,1)S(1)}, u32[]{:S(2)}, u32[]{:S(2)}) collective-permute-start(bf16[1024,256]{1,0:T(8,128)(2,1)S(1)} %get-tuple-element.32.rest_0_), channel_id=1, source_target_pairs={{0,2},{2,0},{1,3},{3,1},{4,6},{6,4},{5,7},{7,5},{8,10},{10,8},{9,1... | collective-permute-start | bytes 1572872 | tf_op jit(solution)/shard_map/ppermute | solution.py:35
  6.0 3.6 %collective-permute-start.1 = (bf16[272,256]{1,0:T(8,128)(2,1)S(1)}, bf16[272,256]{1,0:T(8,128)(2,1)S(1)}, u32[]{:S(2)}, u32[]{:S(2)}) collective-permute-start(bf16[272,256]{1,0:T(8,128)(2,1)S(1)} %get-tuple-element.33), channel_id=1, source_target_pairs={{0,12},{4,8},{8,4},{12,0},{1,13},{5,9},{9,5},{13,1},{2,14},{6,10},... | collective-permute-start | bytes 417800 | tf_op jit(solution)/shard_map/ppermute | solution.py:35
  9.6 0.0 collective-permute-start.2
  9.6 3.0 %tables.1 = (f32[1024,128]{1,0:T(8,128)S(1)}, f32[1024,128]{1,0:T(8,128)S(1)}, f32[8,128]{1,0:T(8,128)S(1)}, s32[4,256]{1,0:T(4,128)S(1)}, s32[1,1024]{1,0:T(1,1...) custom-call(s32[1,4,4]{2,1,0:T(4,128)} %sel_ref.3, ...), custom_call_target="tpu_custom_call", output_to_operand_aliasing={{7}: (5, {})} | custom-call | tf_op jit(solution)/shard_map/tables/pallas_call | solution.py:346
  12.5 0.8 %collective-permute-start.3 = (bf16[272,256]{1,0:T(8,128)(2,1)S(1)}, bf16[272,256]{1,0:T(8,128)(2,1)S(1)}, u32[]{:S(2)}, u32[]{:S(2)}) collective-permute-start(bf16[272,256]{1,0:T(8,128)(2,1)S(1)} %get-tuple-element.35), channel_id=1, source_target_pairs={{0,4},{4,0},{8,12},{12,8},{1,5},{5,1},{9,13},{13,9},{2,6},{6,2},{1... | collective-permute-start | bytes 417800 | tf_op jit(solution)/shard_map/ppermute | solution.py:35
  13.4 4.5 %collective-permute-done.rest_1_ = bf16[1024,256]{1,0:T(8,128)(2,1)S(1)} collective-permute-done((bf16[1024,256]{1,0:T(8,128)(2,1)S(1)}, bf16[1024,256]{1,0:T(8,128)(2,1)S(1)}, u32[]{:S(2)}, u32[]{:S(2)}) %collective-permute-start) | collective-permute-done | bytes 524320 | tf_op jit(solution)/shard_map/ppermute | solution.py:35
  17.9 0.9 %rebuild.1.key_ref = bf16[1024,512]{1,0:T(8,128)(2,1)S(1)} custom-call(bf16[512,512]{1,0:T(8,128)(2,1)S(1)} %get-tuple-element.29.map_ref, f32[1024,128]{1,0:T(8,128)S(1)} %get-tuple-element.30.cos_ref, f32[1024,128]{1,0:T(8,128)S(1)} %get-tuple-element.31.sin_ref, bf16[1024,256]{1,0:T(8,128)(2,1)S(1)} %get-tuple-element.32.rest_0_, ...), custom_call_target="tpu_custom_call" | custom-call | tf_op jit(solution)/shard_map/rebuild/pallas_call | solution.py:365
  18.7 0.0 collective-permute-done.1.rest_0_
  18.8 2.3 %collective-permute-done.2.rest_1_ = bf16[272,256]{1,0:T(8,128)(2,1)S(1)} collective-permute-done((bf16[272,256]{1,0:T(8,128)(2,1)S(1)}, bf16[272,256]{1,0:T(8,128)(2,1)S(1)}, u32[]{:S(2)}, u32[]{:S(2)}) %collective-permute-start.2) | collective-permute-done | bytes 139296 | tf_op jit(solution)/shard_map/ppermute | solution.py:35
  21.1 0.0 collective-permute-done.3.rest_2_
  21.1 0.6 %score.1 = (bf16[512,256]{1,0:T(8,128)(2,1)S(1)}, f32[4,32,256]{2,1,0:T(8,128)S(1)}) custom-call(f32[8,128]{1,0:T(8,128)S(1)} %get-tuple-element.27.turn_ref, s32[4,256]{1,0:T(4,128)S(1)} %get-tuple-element.28.live_ref, s32[1,1024]{1,0:T(1,128)S(1)} %get-tuple-element.26.place_ref, bf16[1024,512]{1,0:T(8,128)(2,1)S(1)} %rebuild.1.key_ref, ...), custom_call_target="tpu_custom_call" | custom-call | tf_op jit(solution)/shard_map/score/pallas_call | solution.py:373
  21.6 0.6 %collective-permute-start.4 = (bf16[512,256]{1,0:T(8,128)(2,1)S(1)}, bf16[512,256]{1,0:T(8,128)(2,1)S(1)}, u32[]{:S(2)}, u32[]{:S(2)}) collective-permute-start(bf16[512,256]{1,0:T(8,128)(2,1)S(1)} %get-tuple-element.38.rest_1_), channel_id=1, source_target_pairs={{0,2},{2,0},{1,3},{3,1},{4,6},{6,4},{5,7},{7,5},{8,10},{10,8},{9,1... | collective-permute-start | bytes 786440 | tf_op jit(solution)/shard_map/ppermute | solution.py:35
  22.2 9.5 %all_to_all.10.rest_0_ = f32[4,32,256]{2,1,0:T(8,128)S(1)} all-to-all(f32[4,32,256]{2,1,0:T(8,128)S(1)} %get-tuple-element.37), channel_id=1, replica_groups=mesh['groups'=2,'pool'=4,'heads'=2,'rep'=2] {'pool'}, dimensions={0} | all-to-all | bytes 262144 | tf_op jit(solution)/shard_map/all_to_all | solution.py:382
  31.7 0.0 collective-permute-done.4.rest_2_
  31.7 0.5 %attend.1.refs_0_ = bf16[1,4096]{1,0:T(2,128)(2,1)S(1)} custom-call(bf16[512,512]{1,0:T(8,128)(2,1)S(1)} %get-tuple-element.25.map_ref, s32[1,1024]{1,0:T(1,128)S(1)} %get-tuple-element.26.place_ref, f32[4,32,256]{2,1,0:T(8,128)S(1)} %all_to_all.10.rest_0_, bf16[512,256]{1,0:T(8,128)(2,1)S(1)} %get-tuple-element.38.rest_1_, ...), custom_call_target="tpu_custom_call" | custom-call | tf_op jit(solution)/shard_map/attend/pallas_call | solution.py:384
  32.3 0.1 collective-permute-start.5
  32.4 1.2 %collective-permute-done.5.refs_1_ = bf16[1,4096]{1,0:T(2,128)(2,1)S(1)} collective-permute-done((bf16[1,4096]{1,0:T(2,128)(2,1)S(1)}, bf16[1,4096]{1,0:T(2,128)(2,1)S(1)}, u32[]{:S(2)}, u32[]{:S(2)}) %collective-permute-start.5) | collective-permute-done | bytes 8224 | tf_op jit(solution)/shard_map/ppermute | solution.py:35
  33.6 8.2 %all_to_all.11.row_ref = bf16[4,2,4096]{2,1,0:T(2,128)(2,1)S(1)} all-to-all(bf16[4,2,4096]{2,1,0:T(2,128)(2,1)S(1)} %join.1), channel_id=1, replica_groups=mesh['groups'=2,'pool'=4,'heads'=2,'rep'=2] {'pool'}, dimensions={0} | all-to-all | bytes 131072 | tf_op jit(solution)/shard_map/all_to_all | solution.py:393
  41.8 0.0 copy-done
  41.8 1.2 %project.1 = (f32[2,1024]{1,0:T(2,128)S(1)}, f32[2,1024]{1,0:T(2,128)S(1)}, f32[2,1024]{1,0:T(2,128)S(1)}, f32[2,1024]{1,0:T(2,128)S(1)}) custom-call(bf16[4096,1024]{1,0:T(8,128)(2,1)S(1)} %copy-done, bf16[4,2,4096]{2,1,0:T(2,128)(2,1)S(1)} %all_to_all.11.row_ref), custom_call_target="tpu_custom_call" | custom-call | tf_op jit(solution)/shard_map/project/pallas_call | solution.py:397
  43.0 0.1 collective-permute-start.6
  43.1 1.5 %collective-permute-start.7 = (f32[2,1024]{1,0:T(2,128)S(1)}, f32[2,1024]{1,0:T(2,128)S(1)}, u32[]{:S(2)}, u32[]{:S(2)}) collective-permute-start(f32[2,1024]{1,0:T(2,128)S(1)} %get-tuple-element.40), channel_id=1, source_target_pairs={{0,2},{1,3},{2,0},{3,1},{4,6},{5,7},{6,4},{7,5},{8,10},{9,11},{10,... | collective-permute-start | bytes 24584 | tf_op jit(solution)/shard_map/ppermute | solution.py:35
  44.6 0.3 collective-permute-start.8
  44.9 1.3 %collective-permute-done.6.refs_0_ = f32[2,1024]{1,0:T(2,128)S(1)} collective-permute-done((f32[2,1024]{1,0:T(2,128)S(1)}, f32[2,1024]{1,0:T(2,128)S(1)}, u32[]{:S(2)}, u32[]{:S(2)}) %collective-permute-start.6) | collective-permute-done | bytes 8224 | tf_op jit(solution)/shard_map/ppermute | solution.py:35
  46.2 0.6 %collective-permute-done.7.refs_1_ = f32[2,1024]{1,0:T(2,128)S(1)} collective-permute-done((f32[2,1024]{1,0:T(2,128)S(1)}, f32[2,1024]{1,0:T(2,128)S(1)}, u32[]{:S(2)}, u32[]{:S(2)}) %collective-permute-start.7) | collective-permute-done | bytes 8224 | tf_op jit(solution)/shard_map/ppermute | solution.py:35
  46.8 0.0 collective-permute-done.8.refs_2_
  46.8 0.6 %finish.1 = bf16[1,2,2048]{2,1,0:T(2,128)(2,1)} custom-call(f32[2,1024]{1,0:T(2,128)S(1)} %collective-permute-done.6.refs_0_, f32[2,1024]{1,0:T(2,128)S(1)} %collective-permute-done.7.refs_1_, f32[2,1024]{1,0:T(2,128)S(1)} %collective-permute-done.8.refs_2_, f32[2,1024]{1,0:T(2,128)S(1)} %get-tuple-element.42.refs_3_), custom_call_target="tpu_custom_call" | custom-call | tf_op jit(solution)/shard_map/finish/pallas_call | solution.py:406
  (1 shorter events, 0.0 us)
Async XLA Ops:
  0.0 41.8 %copy-start = (bf16[4096,1024]{1,0:T(8,128)(2,1)S(1)}, bf16[4096,1024]{1,0:T(8,128)(2,1)}, u32[]{:S(2)}) copy-start(bf16[4096,1024]{1,0:T(8,128)(2,1)} %weight_ref.1) | copy-start | bytes 25165828
  3.0 14.9 %collective-permute-start = (bf16[1024,256]{1,0:T(8,128)(2,1)S(1)}, bf16[1024,256]{1,0:T(8,128)(2,1)S(1)}, u32[]{:S(2)}, u32[]{:S(2)}) collective-permute-start(bf16[1024,256]{1,0:T(8,128)(2,1)S(1)} %get-tuple-element.32.rest_0_), channel_id=1, source_target_pairs={{0,2},{2,0},{1,3},{3,1},{4,6},{6,4},{5,7},{7,5},{8,10},{10,8},{9,1... | collective-permute-start | bytes 1572872 | tf_op jit(solution)/shard_map/ppermute | solution.py:35
  6.0 12.8 %collective-permute-start.1 = (bf16[272,256]{1,0:T(8,128)(2,1)S(1)}, bf16[272,256]{1,0:T(8,128)(2,1)S(1)}, u32[]{:S(2)}, u32[]{:S(2)}) collective-permute-start(bf16[272,256]{1,0:T(8,128)(2,1)S(1)} %get-tuple-element.33), channel_id=1, source_target_pairs={{0,12},{4,8},{8,4},{12,0},{1,13},{5,9},{9,5},{13,1},{2,14},{6,10},... | collective-permute-start | bytes 417800 | tf_op jit(solution)/shard_map/ppermute | solution.py:35
  9.6 11.5 %collective-permute-start.2 = (bf16[272,256]{1,0:T(8,128)(2,1)S(1)}, bf16[272,256]{1,0:T(8,128)(2,1)S(1)}, u32[]{:S(2)}, u32[]{:S(2)}) collective-permute-start(bf16[272,256]{1,0:T(8,128)(2,1)S(1)} %get-tuple-element.34), channel_id=1, source_target_pairs={{0,8},{4,12},{8,0},{12,4},{1,9},{5,13},{9,1},{13,5},{2,10},{6,14},... | collective-permute-start | bytes 417800 | tf_op jit(solution)/shard_map/ppermute | solution.py:35
  12.5 8.5 %collective-permute-start.3 = (bf16[272,256]{1,0:T(8,128)(2,1)S(1)}, bf16[272,256]{1,0:T(8,128)(2,1)S(1)}, u32[]{:S(2)}, u32[]{:S(2)}) collective-permute-start(bf16[272,256]{1,0:T(8,128)(2,1)S(1)} %get-tuple-element.35), channel_id=1, source_target_pairs={{0,4},{4,0},{8,12},{12,8},{1,5},{5,1},{9,13},{13,9},{2,6},{6,2},{1... | collective-permute-start | bytes 417800 | tf_op jit(solution)/shard_map/ppermute | solution.py:35
  21.6 10.1 %collective-permute-start.4 = (bf16[512,256]{1,0:T(8,128)(2,1)S(1)}, bf16[512,256]{1,0:T(8,128)(2,1)S(1)}, u32[]{:S(2)}, u32[]{:S(2)}) collective-permute-start(bf16[512,256]{1,0:T(8,128)(2,1)S(1)} %get-tuple-element.38.rest_1_), channel_id=1, source_target_pairs={{0,2},{2,0},{1,3},{3,1},{4,6},{6,4},{5,7},{7,5},{8,10},{10,8},{9,1... | collective-permute-start | bytes 786440 | tf_op jit(solution)/shard_map/ppermute | solution.py:35
  32.3 1.2 %collective-permute-start.5 = (bf16[1,4096]{1,0:T(2,128)(2,1)S(1)}, bf16[1,4096]{1,0:T(2,128)(2,1)S(1)}, u32[]{:S(2)}, u32[]{:S(2)}) collective-permute-start(bf16[1,4096]{1,0:T(2,128)(2,1)S(1)} %attend.1.refs_0_), channel_id=1, source_target_pairs={{0,1},{1,0},{2,3},{3,2},{4,5},{5,4},{6,7},{7,6},{8,9},{9,8},{10,11... | collective-permute-start | bytes 24584 | tf_op jit(solution)/shard_map/ppermute | solution.py:35
  43.0 3.2 %collective-permute-start.6 = (f32[2,1024]{1,0:T(2,128)S(1)}, f32[2,1024]{1,0:T(2,128)S(1)}, u32[]{:S(2)}, u32[]{:S(2)}) collective-permute-start(f32[2,1024]{1,0:T(2,128)S(1)} %get-tuple-element.39), channel_id=1, source_target_pairs={{0,3},{1,2},{2,1},{3,0},{4,7},{5,6},{6,5},{7,4},{8,11},{9,10},{10,... | collective-permute-start | bytes 24584 | tf_op jit(solution)/shard_map/ppermute | solution.py:35
  43.1 3.7 %collective-permute-start.7 = (f32[2,1024]{1,0:T(2,128)S(1)}, f32[2,1024]{1,0:T(2,128)S(1)}, u32[]{:S(2)}, u32[]{:S(2)}) collective-permute-start(f32[2,1024]{1,0:T(2,128)S(1)} %get-tuple-element.40), channel_id=1, source_target_pairs={{0,2},{1,3},{2,0},{3,1},{4,6},{5,7},{6,4},{7,5},{8,10},{9,11},{10,... | collective-permute-start | bytes 24584 | tf_op jit(solution)/shard_map/ppermute | solution.py:35
  44.6 2.2 %collective-permute-start.8 = (f32[2,1024]{1,0:T(2,128)S(1)}, f32[2,1024]{1,0:T(2,128)S(1)}, u32[]{:S(2)}, u32[]{:S(2)}) collective-permute-start(f32[2,1024]{1,0:T(2,128)S(1)} %get-tuple-element.41), channel_id=1, source_target_pairs={{0,1},{1,0},{2,3},{3,2},{4,5},{5,4},{6,7},{7,6},{8,9},{9,8},{10,11... | collective-permute-start | bytes 24584 | tf_op jit(solution)/shard_map/ppermute | solution.py:35

commit v11 on v7

--- a/solution.py
+++ b/solution.py
@@ -77,9 +77,7 @@
 
 def gather_kernel(pools, sel_ref, lat_ref, query_ref, keys_ref, *rest):
     value_refs = rest[:pools]
-    raw, line, sems = rest[pools:]
-    load = pltpu.make_async_copy(query_ref.at[0], line, sems.at[pools * CAP])
-    load.start()
+    raw, sems = rest[pools:]
     shard_blocks = lat_ref.shape[2] // BLOCK
     columns = lat_ref.shape[3]
     width = columns // 2
@@ -103,8 +101,7 @@
     within = target & (half - 1)
     wanted = ((within >> 6) << 7) + (within & (LANE - 1)) + jnp.where(target >= half, LANE, 0)
     pick = (source == wanted).astype(jnp.float32).astype(jnp.bfloat16)
-    load.wait()
-    queries = heads_to_rows(line[...].astype(jnp.float32), width).astype(jnp.bfloat16)
+    queries = heads_to_rows(query_ref[0].astype(jnp.float32), width).astype(jnp.bfloat16)
     for copy in copies.values():
         copy.wait()
     for k in range(pools - 1, -1, -1):
@@ -118,12 +115,14 @@
         value_refs[k][rows:, :] = queries
 
 
-def table_kernel(pools, shard_blocks, sel_ref, len_ref, freq_ref, key_map_ref, value_map_ref, held_ref, *rest):
+def table_kernel(pools, shard_blocks, sel_ref, len_ref, freq_ref, key_map_ref, value_map_ref, held_ref, weight_ref, *rest):
     cos_ref, sin_ref, turn_ref, live_ref, place_ref, key_out_ref, value_out_ref = rest[:7]
+    weight_out_ref = rest[8]
     sems = rest[-1]
     loads = [
         pltpu.make_async_copy(key_map_ref, key_out_ref, sems.at[0]),
         pltpu.make_async_copy(value_map_ref, value_out_ref, sems.at[1]),
+        pltpu.make_async_copy(weight_ref, weight_out_ref, sems.at[2]),
     ]
     for load in loads:
         load.start()
@@ -330,33 +329,32 @@
         functools.partial(gather_kernel, pools),
         out_shape=[shape((pools * rows, width), bf16)]
         + [shape((rows + query_rows, width), bf16)] * pools,
-        in_specs=[SMEM, HBM, HBM],
+        in_specs=[SMEM, HBM, VMEM],
         out_specs=[VMEM] * (pools + 1),
         scratch_shapes=[
             pltpu.VMEM((pools * rows, 2 * width), bf16),
-            pltpu.VMEM((1, queries.shape[2]), bf16),
-            pltpu.SemaphoreType.DMA((pools * CAP + 1,)),
+            pltpu.SemaphoreType.DMA((pools * CAP,)),
         ],
         compiler_params=params(16),
         name="gather",
     )(in_hbm(selected), in_hbm(latents), in_hbm(queries))
     keys, values = packed[0], packed[1:]
 
-    cosine, sine, turn, live, place, key_maps, value_maps, held = pl.pallas_call(
+    cosine, sine, turn, live, place, key_maps, value_maps, held, weight = pl.pallas_call(
         functools.partial(table_kernel, pools, shard_blocks),
         out_shape=[shape((pools * rows, HEAD_SIZE), f32)] * 2
         + [shape((2 * pools, HEAD_SIZE), f32), shape((pools, rows), i32), shape((1, pools * rows), i32)]
         + [shape(key_latent_maps.shape, bf16), shape(value_latent_maps.shape, bf16)]
-        + [shape(values[1].shape, bf16)],
-        in_specs=[SMEM, SMEM, VMEM] + [ANY] * 3,
-        out_specs=[VMEM] * 7 + [ANY],
-        scratch_shapes=[pltpu.SemaphoreType.DMA((2,))],
+        + [shape(values[1].shape, bf16), shape(out_weight.shape, bf16)],
+        in_specs=[SMEM, SMEM, VMEM] + [ANY] * 3 + [HBM],
+        out_specs=[VMEM] * 7 + [ANY, VMEM],
+        scratch_shapes=[pltpu.SemaphoreType.DMA((3,))],
         input_output_aliases={5: 7},
         compiler_params=params(16),
         name="tables",
     )(
         in_hbm(selected), in_hbm(lengths), in_hbm(freq), in_hbm(key_latent_maps),
-        in_hbm(value_latent_maps), values[1],
+        in_hbm(value_latent_maps), values[1], in_hbm(out_weight),
     )
     key_parts = exchange(keys, "heads", heads)
     value_parts = scatter([values[0], held, *values[2:]], "pool", pools)
@@ -401,7 +399,7 @@
         scratch_shapes=[pltpu.VMEM((pools * reps, own_columns), f32)],
         compiler_params=params(24),
         name="project",
-    )(in_vmem(out_weight), *row_parts)
+    )(weight, *row_parts)
     return pl.pallas_call(
         functools.partial(finish_kernel, heads, reps),
         out_shape=shape((1, each, reps * own_columns), bf16),

time: 43.8 us -> 44.8 us (1.023)
  Pallas kernels: 9.71 us -> 11.6 us
  waiting for transfers between devices: 14.8 us -> 14 us
    pallas_call x1, Pallas kernels: 2.97 us -> 5.22 us  [per_device(): pl.pallas_call(functools.partial(table_kernel, pools, shard_blocks), out_...]
    ppermute x15, waiting for transfers between devices: 14.8 us -> 14 us  [swap(): return lax.ppermute(value, axes, [(i, i ^ step) for i in range(size)])]
  transfers between devices with their start and end apart: 15 -> 15, of which waited for: 9 -> 11; matrix products, arithmetic and copies ran while one was open for 0% -> 0% of each run, Pallas kernels for 9% -> 14%
where the time goes in v11:
time: 44.8 us; the launch traced here: 44.5 us
  starting transfers between devices  18.9 us (42%)
  waiting for transfers between devices  14 us (31%)
  Pallas kernels  11.6 us (26%)
    ppermute x15, starting transfers between devices, swap(): return lax.ppermute(value, axes, [(i, i ^ step) for i in range(size)])  18.9 us
    ppermute x15, waiting for transfers between devices, swap(): return lax.ppermute(value, axes, [(i, i ^ step) for i in range(size)])  14 us
    pallas_call x1, Pallas kernels, per_device(): pl.pallas_call(functools.partial(table_kernel, pools, shard_blocks), out_...  5.22 us
    pallas_call x1, Pallas kernels, per_device(): pl.pallas_call(functools.partial(gather_kernel, pools), out_shape=[shape(...  2.54 us
    pallas_call x1, Pallas kernels, per_device(): pl.pallas_call(functools.partial(project_kernel, pools, heads, reps), out...  1.2 us
  transfers between devices with their start and end apart: 15, of which 11 were waited for; matrix products, arithmetic and copies ran while one was open for 0% of the time, Pallas kernels for 14%

profile of v11, /device:TPU:0, one launch (start us, length us, event | category | flops | bytes accessed | tf_op | source)
XLA Modules:
  0.0 44.5 jit_solution(7818433065105960728)
XLA Ops:
  0.0 2.5 %gather.1 = (bf16[1024,256]{1,0:T(8,128)(2,1)S(1)}, bf16[272,256]{1,0:T(8,128)(2,1)S(1)}, bf16[272,256]{1,0:T(8,128)(2,1)S(1)}, bf16[272,256]{1,0:T(8,128)(2,1)S(1)}, bf16[272,256]{1,0:T(8,128)(2,1)S(1)}) custom-call(s32[1,4,4]{2,1,0:T(4,128)} %sel_ref.3, bf16[1,4,1024,512]{3,2,1,0:T(8,128)(2,1)} %lat_ref.1, bf16[1,1,4096]{2,1,0:T(2,128)(2,1)} %query_ref.1), custom_call_target="tpu_custom_call" | custom-call | tf_op jit(solution)/shard_map/gather/pallas_call | solution.py:328
  2.5 3.0 %collective-permute-start = (bf16[1024,256]{1,0:T(8,128)(2,1)S(1)}, bf16[1024,256]{1,0:T(8,128)(2,1)S(1)}, u32[]{:S(2)}, u32[]{:S(2)}) collective-permute-start(bf16[1024,256]{1,0:T(8,128)(2,1)S(1)} %get-tuple-element.37.rest_0_), channel_id=1, source_target_pairs={{0,2},{2,0},{1,3},{3,1},{4,6},{6,4},{5,7},{7,5},{8,10},{10,8},{9,1... | collective-permute-start | bytes 1572872 | tf_op jit(solution)/shard_map/ppermute | solution.py:35
  5.6 3.6 %collective-permute-start.1 = (bf16[272,256]{1,0:T(8,128)(2,1)S(1)}, bf16[272,256]{1,0:T(8,128)(2,1)S(1)}, u32[]{:S(2)}, u32[]{:S(2)}) collective-permute-start(bf16[272,256]{1,0:T(8,128)(2,1)S(1)} %get-tuple-element.38), channel_id=1, source_target_pairs={{0,12},{4,8},{8,4},{12,0},{1,13},{5,9},{9,5},{13,1},{2,14},{6,10},... | collective-permute-start | bytes 417800 | tf_op jit(solution)/shard_map/ppermute | solution.py:35
  9.2 5.2 %tables.1 = (f32[1024,128]{1,0:T(8,128)S(1)}, f32[1024,128]{1,0:T(8,128)S(1)}, f32[8,128]{1,0:T(8,128)S(1)}, s32[4,256]{1,0:T(4,128)S(1)}, s32[1,1024]{1,0:T(1,1...) custom-call(s32[1,4,4]{2,1,0:T(4,128)} %sel_ref.3, ...), custom_call_target="tpu_custom_call", output_to_operand_aliasing={{7}: (5, {})} | custom-call | tf_op jit(solution)/shard_map/tables/pallas_call | solution.py:343
  14.4 0.9 %collective-permute-start.3 = (bf16[272,256]{1,0:T(8,128)(2,1)S(1)}, bf16[272,256]{1,0:T(8,128)(2,1)S(1)}, u32[]{:S(2)}, u32[]{:S(2)}) collective-permute-start(bf16[272,256]{1,0:T(8,128)(2,1)S(1)} %get-tuple-element.40), channel_id=1, source_target_pairs={{0,4},{4,0},{8,12},{12,8},{1,5},{5,1},{9,13},{13,9},{2,6},{6,2},{1... | collective-permute-start | bytes 417800 | tf_op jit(solution)/shard_map/ppermute | solution.py:35
  15.2 2.2 %collective-permute-done.rest_1_ = bf16[1024,256]{1,0:T(8,128)(2,1)S(1)} collective-permute-done((bf16[1024,256]{1,0:T(8,128)(2,1)S(1)}, bf16[1024,256]{1,0:T(8,128)(2,1)S(1)}, u32[]{:S(2)}, u32[]{:S(2)}) %collective-permute-start) | collective-permute-done | bytes 524320 | tf_op jit(solution)/shard_map/ppermute | solution.py:35
  17.5 0.9 %rebuild.1.key_ref = bf16[1024,512]{1,0:T(8,128)(2,1)S(1)} custom-call(bf16[512,512]{1,0:T(8,128)(2,1)S(1)} %get-tuple-element.34.map_ref, f32[1024,128]{1,0:T(8,128)S(1)} %get-tuple-element.35.cos_ref, f32[1024,128]{1,0:T(8,128)S(1)} %get-tuple-element.36.sin_ref, bf16[1024,256]{1,0:T(8,128)(2,1)S(1)} %get-tuple-element.37.rest_0_, ...), custom_call_target="tpu_custom_call" | custom-call | tf_op jit(solution)/shard_map/rebuild/pallas_call | solution.py:362
  18.3 2.4 %collective-permute-done.2.rest_1_ = bf16[272,256]{1,0:T(8,128)(2,1)S(1)} collective-permute-done((bf16[272,256]{1,0:T(8,128)(2,1)S(1)}, bf16[272,256]{1,0:T(8,128)(2,1)S(1)}, u32[]{:S(2)}, u32[]{:S(2)}) %collective-permute-start.2) | collective-permute-done | bytes 139296 | tf_op jit(solution)/shard_map/ppermute | solution.py:35
  20.8 1.5 %collective-permute-done.3.rest_2_ = bf16[272,256]{1,0:T(8,128)(2,1)S(1)} collective-permute-done((bf16[272,256]{1,0:T(8,128)(2,1)S(1)}, bf16[272,256]{1,0:T(8,128)(2,1)S(1)}, u32[]{:S(2)}, u32[]{:S(2)}) %collective-permute-start.3) | collective-permute-done | bytes 139296 | tf_op jit(solution)/shard_map/ppermute | solution.py:35
  22.3 0.6 %score.1 = (bf16[512,256]{1,0:T(8,128)(2,1)S(1)}, f32[32,256]{1,0:T(8,128)S(1)}, f32[32,256]{1,0:T(8,128)S(1)}, f32[32,256]{1,0:T(8,128)S(1)}, f32[32,256]{1,0:T(8,128)S(1)}) custom-call(f32[8,128]{1,0:T(8,128)S(1)} %get-tuple-element.32.turn_ref, s32[4,256]{1,0:T(4,128)S(1)} %get-tuple-element.33.live_ref, s32[1,1024]{1,0:T(1,128)S(1)} %get-tuple-element.31.place_ref, ...), custom_call_target="tpu_custom_call" | custom-call | tf_op jit(solution)/shard_map/score/pallas_call | solution.py:370
  22.9 0.6 %collective-permute-start.7 = (bf16[512,256]{1,0:T(8,128)(2,1)S(1)}, bf16[512,256]{1,0:T(8,128)(2,1)S(1)}, u32[]{:S(2)}, u32[]{:S(2)}) collective-permute-start(bf16[512,256]{1,0:T(8,128)(2,1)S(1)} %get-tuple-element.46.rest_4_), channel_id=1, source_target_pairs={{0,2},{2,0},{1,3},{3,1},{4,6},{6,4},{5,7},{7,5},{8,10},{10,8},{9,1... | collective-permute-start | bytes 786440 | tf_op jit(solution)/shard_map/ppermute | solution.py:35
  23.5 2.1 %collective-permute-start.4 = (f32[32,256]{1,0:T(8,128)S(1)}, f32[32,256]{1,0:T(8,128)S(1)}, u32[]{:S(2)}, u32[]{:S(2)}) collective-permute-start(f32[32,256]{1,0:T(8,128)S(1)} %get-tuple-element.42), channel_id=1, source_target_pairs={{0,12},{4,8},{8,4},{12,0},{1,13},{5,9},{9,5},{13,1},{2,14},{6,10},... | collective-permute-start | bytes 98312 | tf_op jit(solution)/shard_map/ppermute | solution.py:35
  25.6 0.0 collective-permute-start.5
  25.6 2.3 %collective-permute-start.6 = (f32[32,256]{1,0:T(8,128)S(1)}, f32[32,256]{1,0:T(8,128)S(1)}, u32[]{:S(2)}, u32[]{:S(2)}) collective-permute-start(f32[32,256]{1,0:T(8,128)S(1)} %get-tuple-element.44), channel_id=1, source_target_pairs={{0,4},{4,0},{8,12},{12,8},{1,5},{5,1},{9,13},{13,9},{2,6},{6,2},{1... | collective-permute-start | bytes 98312 | tf_op jit(solution)/shard_map/ppermute | solution.py:35
  27.9 1.5 %collective-permute-done.4.rest_0_ = f32[32,256]{1,0:T(8,128)S(1)} collective-permute-done((f32[32,256]{1,0:T(8,128)S(1)}, f32[32,256]{1,0:T(8,128)S(1)}, u32[]{:S(2)}, u32[]{:S(2)}) %collective-permute-start.4) | collective-permute-done | bytes 32800 | tf_op jit(solution)/shard_map/ppermute | solution.py:35
  29.4 1.0 %collective-permute-done.5.rest_1_ = f32[32,256]{1,0:T(8,128)S(1)} collective-permute-done((f32[32,256]{1,0:T(8,128)S(1)}, f32[32,256]{1,0:T(8,128)S(1)}, u32[]{:S(2)}, u32[]{:S(2)}) %collective-permute-start.5) | collective-permute-done | bytes 32800 | tf_op jit(solution)/shard_map/ppermute | solution.py:35
  30.4 0.5 %attend.1.refs_0_ = bf16[1,4096]{1,0:T(2,128)(2,1)S(1)} custom-call(bf16[512,512]{1,0:T(8,128)(2,1)S(1)} %get-tuple-element.30.map_ref, s32[1,1024]{1,0:T(1,128)S(1)} %get-tuple-element.31.place_ref, f32[32,256]{1,0:T(8,128)S(1)} %collective-permute-done.4.rest_0_, f32[32,256]{1,0:T(8,128)S(1)} %collective-permute-done.5.rest_1_, ...), custom_call_target="tpu_custom_call" | custom-call | tf_op jit(solution)/shard_map/attend/pallas_call | solution.py:381
  30.9 0.1 collective-permute-start.8
  31.0 1.2 %collective-permute-done.8.refs_1_ = bf16[1,4096]{1,0:T(2,128)(2,1)S(1)} collective-permute-done((bf16[1,4096]{1,0:T(2,128)(2,1)S(1)}, bf16[1,4096]{1,0:T(2,128)(2,1)S(1)}, u32[]{:S(2)}, u32[]{:S(2)}) %collective-permute-start.8) | collective-permute-done | bytes 8224 | tf_op jit(solution)/shard_map/ppermute | solution.py:35
  32.2 1.9 %collective-permute-start.11 = (bf16[2,4096]{1,0:T(2,128)(2,1)S(1)}, bf16[2,4096]{1,0:T(2,128)(2,1)S(1)}, u32[]{:S(2)}, u32[]{:S(2)}) collective-permute-start(bf16[2,4096]{1,0:T(2,128)(2,1)S(1)} %join.1.rest_0_), channel_id=1, source_target_pairs={{0,12},{4,8},{8,4},{12,0},{1,13},{5,9},{9,5},{13,1},{2,14},{6,10},... | collective-permute-start | bytes 49160 | tf_op jit(solution)/shard_map/ppermute | solution.py:35
  34.1 1.0 %collective-permute-start.10 = (bf16[2,4096]{1,0:T(2,128)(2,1)S(1)}, bf16[2,4096]{1,0:T(2,128)(2,1)S(1)}, u32[]{:S(2)}, u32[]{:S(2)}) collective-permute-start(bf16[2,4096]{1,0:T(2,128)(2,1)S(1)} %join.1.rest_0_), channel_id=1, source_target_pairs={{0,8},{4,12},{8,0},{12,4},{1,9},{5,13},{9,1},{13,5},{2,10},{6,14},... | collective-permute-start | bytes 49160 | tf_op jit(solution)/shard_map/ppermute | solution.py:35
  35.1 1.6 %collective-permute-start.9 = (bf16[2,4096]{1,0:T(2,128)(2,1)S(1)}, bf16[2,4096]{1,0:T(2,128)(2,1)S(1)}, u32[]{:S(2)}, u32[]{:S(2)}) collective-permute-start(bf16[2,4096]{1,0:T(2,128)(2,1)S(1)} %join.1.rest_0_), channel_id=1, source_target_pairs={{0,4},{4,0},{8,12},{12,8},{1,5},{5,1},{9,13},{13,9},{2,6},{6,2},{1... | collective-permute-start | bytes 49160 | tf_op jit(solution)/shard_map/ppermute | solution.py:35
  36.7 1.3 %collective-permute-done.11.rest_3_ = bf16[2,4096]{1,0:T(2,128)(2,1)S(1)} collective-permute-done((bf16[2,4096]{1,0:T(2,128)(2,1)S(1)}, bf16[2,4096]{1,0:T(2,128)(2,1)S(1)}, u32[]{:S(2)}, u32[]{:S(2)}) %collective-permute-start.11) | collective-permute-done | bytes 16416 | tf_op jit(solution)/shard_map/ppermute | solution.py:35
  38.0 0.8 %collective-permute-done.10.rest_2_ = bf16[2,4096]{1,0:T(2,128)(2,1)S(1)} collective-permute-done((bf16[2,4096]{1,0:T(2,128)(2,1)S(1)}, bf16[2,4096]{1,0:T(2,128)(2,1)S(1)}, u32[]{:S(2)}, u32[]{:S(2)}) %collective-permute-start.10) | collective-permute-done | bytes 16416 | tf_op jit(solution)/shard_map/ppermute | solution.py:35
  38.7 0.2 collective-permute-done.9.rest_1_
  38.9 1.2 %project.1 = (f32[2,1024]{1,0:T(2,128)S(1)}, f32[2,1024]{1,0:T(2,128)S(1)}, f32[2,1024]{1,0:T(2,128)S(1)}, f32[2,1024]{1,0:T(2,128)S(1)}) custom-call(bf16[4096,1024]{1,0:T(8,128)(2,1)S(1)} %get-tuple-element.29.weight_ref, bf16[2,4096]{1,0:T(2,128)(2,1)S(1)} %join.1.rest_0_, bf16[2,4096]{1,0:T(2,128)(2,1)S(1)} %collective-permute-done.9.rest_1_, ...), custom_call_target="tpu_custom_call" | custom-call | tf_op jit(solution)/shard_map/project/pallas_call | solution.py:394
  40.1 0.1 collective-permute-start.12
  40.2 1.6 %collective-permute-start.13 = (f32[2,1024]{1,0:T(2,128)S(1)}, f32[2,1024]{1,0:T(2,128)S(1)}, u32[]{:S(2)}, u32[]{:S(2)}) collective-permute-start(f32[2,1024]{1,0:T(2,128)S(1)} %get-tuple-element.48), channel_id=1, source_target_pairs={{0,2},{1,3},{2,0},{3,1},{4,6},{5,7},{6,4},{7,5},{8,10},{9,11},{10,... | collective-permute-start | bytes 24584 | tf_op jit(solution)/shard_map/ppermute | solution.py:35
  41.8 0.3 collective-permute-start.14
  42.1 1.3 %collective-permute-done.12.refs_0_ = f32[2,1024]{1,0:T(2,128)S(1)} collective-permute-done((f32[2,1024]{1,0:T(2,128)S(1)}, f32[2,1024]{1,0:T(2,128)S(1)}, u32[]{:S(2)}, u32[]{:S(2)}) %collective-permute-start.12) | collective-permute-done | bytes 8224 | tf_op jit(solution)/shard_map/ppermute | solution.py:35
  43.3 0.6 %collective-permute-done.13.refs_1_ = f32[2,1024]{1,0:T(2,128)S(1)} collective-permute-done((f32[2,1024]{1,0:T(2,128)S(1)}, f32[2,1024]{1,0:T(2,128)S(1)}, u32[]{:S(2)}, u32[]{:S(2)}) %collective-permute-start.13) | collective-permute-done | bytes 8224 | tf_op jit(solution)/shard_map/ppermute | solution.py:35
  43.9 0.6 %finish.1 = bf16[1,2,2048]{2,1,0:T(2,128)(2,1)} custom-call(f32[2,1024]{1,0:T(2,128)S(1)} %collective-permute-done.12.refs_0_, f32[2,1024]{1,0:T(2,128)S(1)} %collective-permute-done.13.refs_1_, f32[2,1024]{1,0:T(2,128)S(1)} %collective-permute-done.14.refs_2_, f32[2,1024]{1,0:T(2,128)S(1)} %get-tuple-element.50.refs_3_), custom_call_target="tpu_custom_call" | custom-call | tf_op jit(solution)/shard_map/finish/pallas_call | solution.py:403
  (6 shorter events, 0.0 us)
Async XLA Ops:
  2.5 14.9 %collective-permute-start = (bf16[1024,256]{1,0:T(8,128)(2,1)S(1)}, bf16[1024,256]{1,0:T(8,128)(2,1)S(1)}, u32[]{:S(2)}, u32[]{:S(2)}) collective-permute-start(bf16[1024,256]{1,0:T(8,128)(2,1)S(1)} %get-tuple-element.37.rest_0_), channel_id=1, source_target_pairs={{0,2},{2,0},{1,3},{3,1},{4,6},{6,4},{5,7},{7,5},{8,10},{10,8},{9,1... | collective-permute-start | bytes 1572872 | tf_op jit(solution)/shard_map/ppermute | solution.py:35
  5.6 12.8 %collective-permute-start.1 = (bf16[272,256]{1,0:T(8,128)(2,1)S(1)}, bf16[272,256]{1,0:T(8,128)(2,1)S(1)}, u32[]{:S(2)}, u32[]{:S(2)}) collective-permute-start(bf16[272,256]{1,0:T(8,128)(2,1)S(1)} %get-tuple-element.38), channel_id=1, source_target_pairs={{0,12},{4,8},{8,4},{12,0},{1,13},{5,9},{9,5},{13,1},{2,14},{6,10},... | collective-permute-start | bytes 417800 | tf_op jit(solution)/shard_map/ppermute | solution.py:35
  9.2 11.6 %collective-permute-start.2 = (bf16[272,256]{1,0:T(8,128)(2,1)S(1)}, bf16[272,256]{1,0:T(8,128)(2,1)S(1)}, u32[]{:S(2)}, u32[]{:S(2)}) collective-permute-start(bf16[272,256]{1,0:T(8,128)(2,1)S(1)} %get-tuple-element.39), channel_id=1, source_target_pairs={{0,8},{4,12},{8,0},{12,4},{1,9},{5,13},{9,1},{13,5},{2,10},{6,14},... | collective-permute-start | bytes 417800 | tf_op jit(solution)/shard_map/ppermute | solution.py:35
  14.4 7.9 %collective-permute-start.3 = (bf16[272,256]{1,0:T(8,128)(2,1)S(1)}, bf16[272,256]{1,0:T(8,128)(2,1)S(1)}, u32[]{:S(2)}, u32[]{:S(2)}) collective-permute-start(bf16[272,256]{1,0:T(8,128)(2,1)S(1)} %get-tuple-element.40), channel_id=1, source_target_pairs={{0,4},{4,0},{8,12},{12,8},{1,5},{5,1},{9,13},{13,9},{2,6},{6,2},{1... | collective-permute-start | bytes 417800 | tf_op jit(solution)/shard_map/ppermute | solution.py:35
  22.9 7.5 %collective-permute-start.7 = (bf16[512,256]{1,0:T(8,128)(2,1)S(1)}, bf16[512,256]{1,0:T(8,128)(2,1)S(1)}, u32[]{:S(2)}, u32[]{:S(2)}) collective-permute-start(bf16[512,256]{1,0:T(8,128)(2,1)S(1)} %get-tuple-element.46.rest_4_), channel_id=1, source_target_pairs={{0,2},{2,0},{1,3},{3,1},{4,6},{6,4},{5,7},{7,5},{8,10},{10,8},{9,1... | collective-permute-start | bytes 786440 | tf_op jit(solution)/shard_map/ppermute | solution.py:35
  23.5 5.9 %collective-permute-start.4 = (f32[32,256]{1,0:T(8,128)S(1)}, f32[32,256]{1,0:T(8,128)S(1)}, u32[]{:S(2)}, u32[]{:S(2)}) collective-permute-start(f32[32,256]{1,0:T(8,128)S(1)} %get-tuple-element.42), channel_id=1, source_target_pairs={{0,12},{4,8},{8,4},{12,0},{1,13},{5,9},{9,5},{13,1},{2,14},{6,10},... | collective-permute-start | bytes 98312 | tf_op jit(solution)/shard_map/ppermute | solution.py:35
  25.6 4.8 %collective-permute-start.5 = (f32[32,256]{1,0:T(8,128)S(1)}, f32[32,256]{1,0:T(8,128)S(1)}, u32[]{:S(2)}, u32[]{:S(2)}) collective-permute-start(f32[32,256]{1,0:T(8,128)S(1)} %get-tuple-element.43), channel_id=1, source_target_pairs={{0,8},{4,12},{8,0},{12,4},{1,9},{5,13},{9,1},{13,5},{2,10},{6,14},... | collective-permute-start | bytes 98312 | tf_op jit(solution)/shard_map/ppermute | solution.py:35
  25.6 4.8 %collective-permute-start.6 = (f32[32,256]{1,0:T(8,128)S(1)}, f32[32,256]{1,0:T(8,128)S(1)}, u32[]{:S(2)}, u32[]{:S(2)}) collective-permute-start(f32[32,256]{1,0:T(8,128)S(1)} %get-tuple-element.44), channel_id=1, source_target_pairs={{0,4},{4,0},{8,12},{12,8},{1,5},{5,1},{9,13},{13,9},{2,6},{6,2},{1... | collective-permute-start | bytes 98312 | tf_op jit(solution)/shard_map/ppermute | solution.py:35
  30.9 1.2 %collective-permute-start.8 = (bf16[1,4096]{1,0:T(2,128)(2,1)S(1)}, bf16[1,4096]{1,0:T(2,128)(2,1)S(1)}, u32[]{:S(2)}, u32[]{:S(2)}) collective-permute-start(bf16[1,4096]{1,0:T(2,128)(2,1)S(1)} %attend.1.refs_0_), channel_id=1, source_target_pairs={{0,1},{1,0},{2,3},{3,2},{4,5},{5,4},{6,7},{7,6},{8,9},{9,8},{10,11... | collective-permute-start | bytes 24584 | tf_op jit(solution)/shard_map/ppermute | solution.py:35
  32.2 5.7 %collective-permute-start.11 = (bf16[2,4096]{1,0:T(2,128)(2,1)S(1)}, bf16[2,4096]{1,0:T(2,128)(2,1)S(1)}, u32[]{:S(2)}, u32[]{:S(2)}) collective-permute-start(bf16[2,4096]{1,0:T(2,128)(2,1)S(1)} %join.1.rest_0_), channel_id=1, source_target_pairs={{0,12},{4,8},{8,4},{12,0},{1,13},{5,9},{9,5},{13,1},{2,14},{6,10},... | collective-permute-start | bytes 49160 | tf_op jit(solution)/shard_map/ppermute | solution.py:35
  34.1 4.6 %collective-permute-start.10 = (bf16[2,4096]{1,0:T(2,128)(2,1)S(1)}, bf16[2,4096]{1,0:T(2,128)(2,1)S(1)}, u32[]{:S(2)}, u32[]{:S(2)}) collective-permute-start(bf16[2,4096]{1,0:T(2,128)(2,1)S(1)} %join.1.rest_0_), channel_id=1, source_target_pairs={{0,8},{4,12},{8,0},{12,4},{1,9},{5,13},{9,1},{13,5},{2,10},{6,14},... | collective-permute-start | bytes 49160 | tf_op jit(solution)/shard_map/ppermute | solution.py:35
  35.1 3.8 %collective-permute-start.9 = (bf16[2,4096]{1,0:T(2,128)(2,1)S(1)}, bf16[2,4096]{1,0:T(2,128)(2,1)S(1)}, u32[]{:S(2)}, u32[]{:S(2)}) collective-permute-start(bf16[2,4096]{1,0:T(2,128)(2,1)S(1)} %join.1.rest_0_), channel_id=1, source_target_pairs={{0,4},{4,0},{8,12},{12,8},{1,5},{5,1},{9,13},{13,9},{2,6},{6,2},{1... | collective-permute-start | bytes 49160 | tf_op jit(solution)/shard_map/ppermute | solution.py:35
  40.1 3.2 %collective-permute-start.12 = (f32[2,1024]{1,0:T(2,128)S(1)}, f32[2,1024]{1,0:T(2,128)S(1)}, u32[]{:S(2)}, u32[]{:S(2)}) collective-permute-start(f32[2,1024]{1,0:T(2,128)S(1)} %get-tuple-element.47), channel_id=1, source_target_pairs={{0,3},{1,2},{2,1},{3,0},{4,7},{5,6},{6,5},{7,4},{8,11},{9,10},{10,... | collective-permute-start | bytes 24584 | tf_op jit(solution)/shard_map/ppermute | solution.py:35
  40.2 3.7 %collective-permute-start.13 = (f32[2,1024]{1,0:T(2,128)S(1)}, f32[2,1024]{1,0:T(2,128)S(1)}, u32[]{:S(2)}, u32[]{:S(2)}) collective-permute-start(f32[2,1024]{1,0:T(2,128)S(1)} %get-tuple-element.48), channel_id=1, source_target_pairs={{0,2},{1,3},{2,0},{3,1},{4,6},{5,7},{6,4},{7,5},{8,10},{9,11},{10,... | collective-permute-start | bytes 24584 | tf_op jit(solution)/shard_map/ppermute | solution.py:35
  41.8 2.2 %collective-permute-start.14 = (f32[2,1024]{1,0:T(2,128)S(1)}, f32[2,1024]{1,0:T(2,128)S(1)}, u32[]{:S(2)}, u32[]{:S(2)}) collective-permute-start(f32[2,1024]{1,0:T(2,128)S(1)} %get-tuple-element.49), channel_id=1, source_target_pairs={{0,1},{1,0},{2,3},{3,2},{4,5},{5,4},{6,7},{7,6},{8,9},{9,8},{10,11... | collective-permute-start | bytes 24584 | tf_op jit(solution)/shard_map/ppermute | solution.py:35

commit v12 on v7

--- a/solution.py
+++ b/solution.py
@@ -77,9 +77,7 @@
 
 def gather_kernel(pools, sel_ref, lat_ref, query_ref, keys_ref, *rest):
     value_refs = rest[:pools]
-    raw, line, sems = rest[pools:]
-    load = pltpu.make_async_copy(query_ref.at[0], line, sems.at[pools * CAP])
-    load.start()
+    raw, sems = rest[pools:]
     shard_blocks = lat_ref.shape[2] // BLOCK
     columns = lat_ref.shape[3]
     width = columns // 2
@@ -103,8 +101,7 @@
     within = target & (half - 1)
     wanted = ((within >> 6) << 7) + (within & (LANE - 1)) + jnp.where(target >= half, LANE, 0)
     pick = (source == wanted).astype(jnp.float32).astype(jnp.bfloat16)
-    load.wait()
-    queries = heads_to_rows(line[...].astype(jnp.float32), width).astype(jnp.bfloat16)
+    queries = heads_to_rows(query_ref[0].astype(jnp.float32), width).astype(jnp.bfloat16)
     for copy in copies.values():
         copy.wait()
     for k in range(pools - 1, -1, -1):
@@ -160,7 +157,15 @@
         load.wait()
 
 
-def rebuild_kernel(pools, heads, map_ref, cos_ref, sin_ref, *rest):
+def stage_kernel(weight_ref, after_ref, out_ref, sem):
+    del after_ref
+    load = pltpu.make_async_copy(weight_ref, out_ref, sem)
+    load.start()
+    load.wait()
+
+
+def rebuild_kernel(pools, heads, map_ref, cos_ref, sin_ref, after_ref, *rest):
+    del after_ref
     key_refs = rest[:heads]
     out_ref = rest[heads]
     head = lax.axis_index("heads")
@@ -330,12 +335,11 @@
         functools.partial(gather_kernel, pools),
         out_shape=[shape((pools * rows, width), bf16)]
         + [shape((rows + query_rows, width), bf16)] * pools,
-        in_specs=[SMEM, HBM, HBM],
+        in_specs=[SMEM, HBM, VMEM],
         out_specs=[VMEM] * (pools + 1),
         scratch_shapes=[
             pltpu.VMEM((pools * rows, 2 * width), bf16),
-            pltpu.VMEM((1, queries.shape[2]), bf16),
-            pltpu.SemaphoreType.DMA((pools * CAP + 1,)),
+            pltpu.SemaphoreType.DMA((pools * CAP,)),
         ],
         compiler_params=params(16),
         name="gather",
@@ -361,14 +365,23 @@
     key_parts = exchange(keys, "heads", heads)
     value_parts = scatter([values[0], held, *values[2:]], "pool", pools)
 
+    weight = pl.pallas_call(
+        stage_kernel,
+        out_shape=shape(out_weight.shape, bf16),
+        in_specs=[HBM, ANY],
+        out_specs=VMEM,
+        scratch_shapes=[pltpu.SemaphoreType.DMA],
+        compiler_params=params(4),
+        name="stage",
+    )(in_hbm(out_weight), place)
     turned = pl.pallas_call(
         functools.partial(rebuild_kernel, pools, heads),
         out_shape=shape((pools * rows, own_heads // QUERY_PER_GROUP * HEAD_SIZE), bf16),
-        in_specs=[VMEM] * (3 + heads),
+        in_specs=[VMEM] * 3 + [ANY] + [VMEM] * heads,
         out_specs=VMEM,
         compiler_params=params(20),
         name="rebuild",
-    )(key_maps, cosine, sine, *key_parts)
+    )(key_maps, cosine, sine, weight, *key_parts)
     dense, *scores = pl.pallas_call(
         functools.partial(score_kernel, pools),
         out_shape=[shape((sel_count * BLOCK, width), bf16)] + [shape((own_heads, rows), f32)] * pools,
@@ -401,7 +414,7 @@
         scratch_shapes=[pltpu.VMEM((pools * reps, own_columns), f32)],
         compiler_params=params(24),
         name="project",
-    )(in_vmem(out_weight), *row_parts)
+    )(weight, *row_parts)
     return pl.pallas_call(
         functools.partial(finish_kernel, heads, reps),
         out_shape=shape((1, each, reps * own_columns), bf16),

time: 43.8 us -> 43.4 us (level)
  waiting for transfers between devices: 14.8 us -> 11.5 us
  Pallas kernels: 9.71 us -> 12.7 us
    ppermute x15, waiting for transfers between devices: 14.8 us -> 11.5 us  [swap(): return lax.ppermute(value, axes, [(i, i ^ step) for i in range(size)])]
    pallas_call x0 -> x1, Pallas kernels: none -> 3.39 us  [per_device(): pl.pallas_call(stage_kernel, out_shape=shape(out_weight.shape, bf16), in_...]
  transfers between devices with their start and end apart: 15 -> 15, of which waited for: 9 -> 9; matrix products, arithmetic and copies ran while one was open for 0% -> 0% of each run, Pallas kernels for 9% -> 17%
where the time goes in v12:
time: 43.4 us; the launch traced here: 43.1 us
  starting transfers between devices  18.9 us (44%)
  Pallas kernels  12.7 us (29%)
  waiting for transfers between devices  11.5 us (26%)
    ppermute x15, starting transfers between devices, swap(): return lax.ppermute(value, axes, [(i, i ^ step) for i in range(size)])  18.9 us
    ppermute x15, waiting for transfers between devices, swap(): return lax.ppermute(value, axes, [(i, i ^ step) for i in range(size)])  11.5 us
    pallas_call x1, Pallas kernels, per_device(): pl.pallas_call(stage_kernel, out_shape=shape(out_weight.shape, bf16), in_...  3.39 us
    pallas_call x1, Pallas kernels, per_device(): pl.pallas_call(functools.partial(table_kernel, pools, shard_blocks), out_...  2.97 us
    pallas_call x1, Pallas kernels, per_device(): pl.pallas_call(functools.partial(gather_kernel, pools), out_shape=[shape(...  2.54 us
    pallas_call x1, Pallas kernels, per_device(): pl.pallas_call(functools.partial(project_kernel, pools, heads, reps), out...  1.21 us
  transfers between devices with their start and end apart: 15, of which 9 were waited for; matrix products, arithmetic and copies ran while one was open for 0% of the time, Pallas kernels for 17%

profile of v12, /device:TPU:0, one launch (start us, length us, event | category | flops | bytes accessed | tf_op | source)
XLA Modules:
  0.0 43.1 jit_solution(3888699096599297568)
XLA Ops:
  0.0 2.5 %gather.1 = (bf16[1024,256]{1,0:T(8,128)(2,1)S(1)}, bf16[272,256]{1,0:T(8,128)(2,1)S(1)}, bf16[272,256]{1,0:T(8,128)(2,1)S(1)}, bf16[272,256]{1,0:T(8,128)(2,1)S(1)}, bf16[272,256]{1,0:T(8,128)(2,1)S(1)}) custom-call(s32[1,4,4]{2,1,0:T(4,128)} %sel_ref.3, bf16[1,4,1024,512]{3,2,1,0:T(8,128)(2,1)} %lat_ref.1, bf16[1,1,4096]{2,1,0:T(2,128)(2,1)} %query_ref.1), custom_call_target="tpu_custom_call" | custom-call | tf_op jit(solution)/shard_map/gather/pallas_call | solution.py:334
  2.5 3.0 %collective-permute-start = (bf16[1024,256]{1,0:T(8,128)(2,1)S(1)}, bf16[1024,256]{1,0:T(8,128)(2,1)S(1)}, u32[]{:S(2)}, u32[]{:S(2)}) collective-permute-start(bf16[1024,256]{1,0:T(8,128)(2,1)S(1)} %get-tuple-element.35.rest_0_), channel_id=1, source_target_pairs={{0,2},{2,0},{1,3},{3,1},{4,6},{6,4},{5,7},{7,5},{8,10},{10,8},{9,1... | collective-permute-start | bytes 1572872 | tf_op jit(solution)/shard_map/ppermute | solution.py:35
  5.6 3.6 %collective-permute-start.1 = (bf16[272,256]{1,0:T(8,128)(2,1)S(1)}, bf16[272,256]{1,0:T(8,128)(2,1)S(1)}, u32[]{:S(2)}, u32[]{:S(2)}) collective-permute-start(bf16[272,256]{1,0:T(8,128)(2,1)S(1)} %get-tuple-element.36), channel_id=1, source_target_pairs={{0,12},{4,8},{8,4},{12,0},{1,13},{5,9},{9,5},{13,1},{2,14},{6,10},... | collective-permute-start | bytes 417800 | tf_op jit(solution)/shard_map/ppermute | solution.py:35
  9.2 0.0 collective-permute-start.2
  9.2 3.0 %tables.1 = (f32[1024,128]{1,0:T(8,128)S(1)}, f32[1024,128]{1,0:T(8,128)S(1)}, f32[8,128]{1,0:T(8,128)S(1)}, s32[4,256]{1,0:T(4,128)S(1)}, s32[1,1024]{1,0:T(1,1...) custom-call(s32[1,4,4]{2,1,0:T(4,128)} %sel_ref.3, ...), custom_call_target="tpu_custom_call", output_to_operand_aliasing={{7}: (5, {})} | custom-call | tf_op jit(solution)/shard_map/tables/pallas_call | solution.py:349
  12.1 0.9 %collective-permute-start.3 = (bf16[272,256]{1,0:T(8,128)(2,1)S(1)}, bf16[272,256]{1,0:T(8,128)(2,1)S(1)}, u32[]{:S(2)}, u32[]{:S(2)}) collective-permute-start(bf16[272,256]{1,0:T(8,128)(2,1)S(1)} %get-tuple-element.38), channel_id=1, source_target_pairs={{0,4},{4,0},{8,12},{12,8},{1,5},{5,1},{9,13},{13,9},{2,6},{6,2},{1... | collective-permute-start | bytes 417800 | tf_op jit(solution)/shard_map/ppermute | solution.py:35
  13.0 3.4 %stage.1.after_ref.weight_ref = bf16[4096,1024]{1,0:T(8,128)(2,1)S(1)} custom-call(bf16[4096,1024]{1,0:T(8,128)(2,1)} %weight_ref.1, s32[1,1024]{1,0:T(1,128)S(1)} %get-tuple-element.28.after_ref.place_ref), custom_call_target="tpu_custom_call" | custom-call | tf_op jit(solution)/shard_map/stage/pallas_call | solution.py:368
  16.4 1.1 %collective-permute-done.rest_1_ = bf16[1024,256]{1,0:T(8,128)(2,1)S(1)} collective-permute-done((bf16[1024,256]{1,0:T(8,128)(2,1)S(1)}, bf16[1024,256]{1,0:T(8,128)(2,1)S(1)}, u32[]{:S(2)}, u32[]{:S(2)}) %collective-permute-start) | collective-permute-done | bytes 524320 | tf_op jit(solution)/shard_map/ppermute | solution.py:35
  17.5 0.9 %rebuild.1.key_ref = bf16[1024,512]{1,0:T(8,128)(2,1)S(1)} custom-call(bf16[512,512]{1,0:T(8,128)(2,1)S(1)} %get-tuple-element.32.map_ref, f32[1024,128]{1,0:T(8,128)S(1)} %get-tuple-element.33.cos_ref, f32[1024,128]{1,0:T(8,128)S(1)} %get-tuple-element.34.sin_ref, bf16[4096,1024]{1,0:T(8,128)(2,1)S(1)} %stage.1.after_ref.weight_ref, ...), custom_call_target="tpu_custom_call" | custom-call | tf_op jit(solution)/shard_map/rebuild/pallas_call | solution.py:377
  18.3 0.0 collective-permute-done.1.rest_0_
  18.3 2.3 %collective-permute-done.2.rest_1_ = bf16[272,256]{1,0:T(8,128)(2,1)S(1)} collective-permute-done((bf16[272,256]{1,0:T(8,128)(2,1)S(1)}, bf16[272,256]{1,0:T(8,128)(2,1)S(1)}, u32[]{:S(2)}, u32[]{:S(2)}) %collective-permute-start.2) | collective-permute-done | bytes 139296 | tf_op jit(solution)/shard_map/ppermute | solution.py:35
  20.7 0.6 %score.1 = (bf16[512,256]{1,0:T(8,128)(2,1)S(1)}, f32[32,256]{1,0:T(8,128)S(1)}, f32[32,256]{1,0:T(8,128)S(1)}, f32[32,256]{1,0:T(8,128)S(1)}, f32[32,256]{1,0:T(8,128)S(1)}) custom-call(f32[8,128]{1,0:T(8,128)S(1)} %get-tuple-element.30.turn_ref, s32[4,256]{1,0:T(4,128)S(1)} %get-tuple-element.31.live_ref, ...), custom_call_target="tpu_custom_call" | custom-call | tf_op jit(solution)/shard_map/score/pallas_call | solution.py:385
  21.2 0.6 %collective-permute-start.7 = (bf16[512,256]{1,0:T(8,128)(2,1)S(1)}, bf16[512,256]{1,0:T(8,128)(2,1)S(1)}, u32[]{:S(2)}, u32[]{:S(2)}) collective-permute-start(bf16[512,256]{1,0:T(8,128)(2,1)S(1)} %get-tuple-element.44.rest_4_), channel_id=1, source_target_pairs={{0,2},{2,0},{1,3},{3,1},{4,6},{6,4},{5,7},{7,5},{8,10},{10,8},{9,1... | collective-permute-start | bytes 786440 | tf_op jit(solution)/shard_map/ppermute | solution.py:35
  21.8 2.5 %collective-permute-start.4 = (f32[32,256]{1,0:T(8,128)S(1)}, f32[32,256]{1,0:T(8,128)S(1)}, u32[]{:S(2)}, u32[]{:S(2)}) collective-permute-start(f32[32,256]{1,0:T(8,128)S(1)} %get-tuple-element.40), channel_id=1, source_target_pairs={{0,12},{4,8},{8,4},{12,0},{1,13},{5,9},{9,5},{13,1},{2,14},{6,10},... | collective-permute-start | bytes 98312 | tf_op jit(solution)/shard_map/ppermute | solution.py:35
  24.4 1.9 %collective-permute-start.6 = (f32[32,256]{1,0:T(8,128)S(1)}, f32[32,256]{1,0:T(8,128)S(1)}, u32[]{:S(2)}, u32[]{:S(2)}) collective-permute-start(f32[32,256]{1,0:T(8,128)S(1)} %get-tuple-element.42), channel_id=1, source_target_pairs={{0,4},{4,0},{8,12},{12,8},{1,5},{5,1},{9,13},{13,9},{2,6},{6,2},{1... | collective-permute-start | bytes 98312 | tf_op jit(solution)/shard_map/ppermute | solution.py:35
  26.2 1.4 %collective-permute-done.4.rest_0_ = f32[32,256]{1,0:T(8,128)S(1)} collective-permute-done((f32[32,256]{1,0:T(8,128)S(1)}, f32[32,256]{1,0:T(8,128)S(1)}, u32[]{:S(2)}, u32[]{:S(2)}) %collective-permute-start.4) | collective-permute-done | bytes 32800 | tf_op jit(solution)/shard_map/ppermute | solution.py:35
  27.7 1.5 %collective-permute-done.5.rest_1_ = f32[32,256]{1,0:T(8,128)S(1)} collective-permute-done((f32[32,256]{1,0:T(8,128)S(1)}, f32[32,256]{1,0:T(8,128)S(1)}, u32[]{:S(2)}, u32[]{:S(2)}) %collective-permute-start.5) | collective-permute-done | bytes 32800 | tf_op jit(solution)/shard_map/ppermute | solution.py:35
  29.2 0.5 %attend.1.refs_0_ = bf16[1,4096]{1,0:T(2,128)(2,1)S(1)} custom-call(bf16[512,512]{1,0:T(8,128)(2,1)S(1)} %get-tuple-element.29.map_ref, s32[1,1024]{1,0:T(1,128)S(1)} %get-tuple-element.28.after_ref.place_ref, f32[32,256]{1,0:T(8,128)S(1)} %collective-permute-done.4.rest_0_, f32[32,256]{1,0:T(8,128)S(1)} %collective-permute-done.5.rest_1_, ...), custom_call_target="tpu_custom_call" | custom-call | tf_op jit(solution)/shard_map/attend/pallas_call | solution.py:396
  29.7 0.1 collective-permute-start.8
  29.8 1.2 %collective-permute-done.8.refs_1_ = bf16[1,4096]{1,0:T(2,128)(2,1)S(1)} collective-permute-done((bf16[1,4096]{1,0:T(2,128)(2,1)S(1)}, bf16[1,4096]{1,0:T(2,128)(2,1)S(1)}, u32[]{:S(2)}, u32[]{:S(2)}) %collective-permute-start.8) | collective-permute-done | bytes 8224 | tf_op jit(solution)/shard_map/ppermute | solution.py:35
  31.0 1.9 %collective-permute-start.11 = (bf16[2,4096]{1,0:T(2,128)(2,1)S(1)}, bf16[2,4096]{1,0:T(2,128)(2,1)S(1)}, u32[]{:S(2)}, u32[]{:S(2)}) collective-permute-start(bf16[2,4096]{1,0:T(2,128)(2,1)S(1)} %join.1.rest_0_), channel_id=1, source_target_pairs={{0,12},{4,8},{8,4},{12,0},{1,13},{5,9},{9,5},{13,1},{2,14},{6,10},... | collective-permute-start | bytes 49160 | tf_op jit(solution)/shard_map/ppermute | solution.py:35
  32.9 0.6 %collective-permute-start.10 = (bf16[2,4096]{1,0:T(2,128)(2,1)S(1)}, bf16[2,4096]{1,0:T(2,128)(2,1)S(1)}, u32[]{:S(2)}, u32[]{:S(2)}) collective-permute-start(bf16[2,4096]{1,0:T(2,128)(2,1)S(1)} %join.1.rest_0_), channel_id=1, source_target_pairs={{0,8},{4,12},{8,0},{12,4},{1,9},{5,13},{9,1},{13,5},{2,10},{6,14},... | collective-permute-start | bytes 49160 | tf_op jit(solution)/shard_map/ppermute | solution.py:35
  33.5 2.0 %collective-permute-start.9 = (bf16[2,4096]{1,0:T(2,128)(2,1)S(1)}, bf16[2,4096]{1,0:T(2,128)(2,1)S(1)}, u32[]{:S(2)}, u32[]{:S(2)}) collective-permute-start(bf16[2,4096]{1,0:T(2,128)(2,1)S(1)} %join.1.rest_0_), channel_id=1, source_target_pairs={{0,4},{4,0},{8,12},{12,8},{1,5},{5,1},{9,13},{13,9},{2,6},{6,2},{1... | collective-permute-start | bytes 49160 | tf_op jit(solution)/shard_map/ppermute | solution.py:35
  35.4 1.3 %collective-permute-done.11.rest_3_ = bf16[2,4096]{1,0:T(2,128)(2,1)S(1)} collective-permute-done((bf16[2,4096]{1,0:T(2,128)(2,1)S(1)}, bf16[2,4096]{1,0:T(2,128)(2,1)S(1)}, u32[]{:S(2)}, u32[]{:S(2)}) %collective-permute-start.11) | collective-permute-done | bytes 16416 | tf_op jit(solution)/shard_map/ppermute | solution.py:35
  36.7 0.8 %collective-permute-done.10.rest_2_ = bf16[2,4096]{1,0:T(2,128)(2,1)S(1)} collective-permute-done((bf16[2,4096]{1,0:T(2,128)(2,1)S(1)}, bf16[2,4096]{1,0:T(2,128)(2,1)S(1)}, u32[]{:S(2)}, u32[]{:S(2)}) %collective-permute-start.10) | collective-permute-done | bytes 16416 | tf_op jit(solution)/shard_map/ppermute | solution.py:35
  37.5 1.2 %project.1 = (f32[2,1024]{1,0:T(2,128)S(1)}, f32[2,1024]{1,0:T(2,128)S(1)}, f32[2,1024]{1,0:T(2,128)S(1)}, f32[2,1024]{1,0:T(2,128)S(1)}) custom-call(bf16[4096,1024]{1,0:T(8,128)(2,1)S(1)} %stage.1.after_ref.weight_ref, bf16[2,4096]{1,0:T(2,128)(2,1)S(1)} %join.1.rest_0_, bf16[2,4096]{1,0:T(2,128)(2,1)S(1)} %collective-permute-done.9.rest_1_, ...), custom_call_target="tpu_custom_call" | custom-call | tf_op jit(solution)/shard_map/project/pallas_call | solution.py:409
  38.7 0.2 collective-permute-start.12
  38.9 1.4 %collective-permute-start.13 = (f32[2,1024]{1,0:T(2,128)S(1)}, f32[2,1024]{1,0:T(2,128)S(1)}, u32[]{:S(2)}, u32[]{:S(2)}) collective-permute-start(f32[2,1024]{1,0:T(2,128)S(1)} %get-tuple-element.46), channel_id=1, source_target_pairs={{0,2},{1,3},{2,0},{3,1},{4,6},{5,7},{6,4},{7,5},{8,10},{9,11},{10,... | collective-permute-start | bytes 24584 | tf_op jit(solution)/shard_map/ppermute | solution.py:35
  40.3 0.3 collective-permute-start.14
  40.6 1.3 %collective-permute-done.12.refs_0_ = f32[2,1024]{1,0:T(2,128)S(1)} collective-permute-done((f32[2,1024]{1,0:T(2,128)S(1)}, f32[2,1024]{1,0:T(2,128)S(1)}, u32[]{:S(2)}, u32[]{:S(2)}) %collective-permute-start.12) | collective-permute-done | bytes 8224 | tf_op jit(solution)/shard_map/ppermute | solution.py:35
  41.9 0.6 %collective-permute-done.13.refs_1_ = f32[2,1024]{1,0:T(2,128)S(1)} collective-permute-done((f32[2,1024]{1,0:T(2,128)S(1)}, f32[2,1024]{1,0:T(2,128)S(1)}, u32[]{:S(2)}, u32[]{:S(2)}) %collective-permute-start.13) | collective-permute-done | bytes 8224 | tf_op jit(solution)/shard_map/ppermute | solution.py:35
  42.5 0.6 %finish.1 = bf16[1,2,2048]{2,1,0:T(2,128)(2,1)} custom-call(f32[2,1024]{1,0:T(2,128)S(1)} %collective-permute-done.12.refs_0_, f32[2,1024]{1,0:T(2,128)S(1)} %collective-permute-done.13.refs_1_, f32[2,1024]{1,0:T(2,128)S(1)} %collective-permute-done.14.refs_2_, f32[2,1024]{1,0:T(2,128)S(1)} %get-tuple-element.48.refs_3_), custom_call_target="tpu_custom_call" | custom-call | tf_op jit(solution)/shard_map/finish/pallas_call | solution.py:418
  (7 shorter events, 0.0 us)
Async XLA Ops:
  2.5 14.9 %collective-permute-start = (bf16[1024,256]{1,0:T(8,128)(2,1)S(1)}, bf16[1024,256]{1,0:T(8,128)(2,1)S(1)}, u32[]{:S(2)}, u32[]{:S(2)}) collective-permute-start(bf16[1024,256]{1,0:T(8,128)(2,1)S(1)} %get-tuple-element.35.rest_0_), channel_id=1, source_target_pairs={{0,2},{2,0},{1,3},{3,1},{4,6},{6,4},{5,7},{7,5},{8,10},{10,8},{9,1... | collective-permute-start | bytes 1572872 | tf_op jit(solution)/shard_map/ppermute | solution.py:35
  5.6 12.8 %collective-permute-start.1 = (bf16[272,256]{1,0:T(8,128)(2,1)S(1)}, bf16[272,256]{1,0:T(8,128)(2,1)S(1)}, u32[]{:S(2)}, u32[]{:S(2)}) collective-permute-start(bf16[272,256]{1,0:T(8,128)(2,1)S(1)} %get-tuple-element.36), channel_id=1, source_target_pairs={{0,12},{4,8},{8,4},{12,0},{1,13},{5,9},{9,5},{13,1},{2,14},{6,10},... | collective-permute-start | bytes 417800 | tf_op jit(solution)/shard_map/ppermute | solution.py:35
  9.2 11.5 %collective-permute-start.2 = (bf16[272,256]{1,0:T(8,128)(2,1)S(1)}, bf16[272,256]{1,0:T(8,128)(2,1)S(1)}, u32[]{:S(2)}, u32[]{:S(2)}) collective-permute-start(bf16[272,256]{1,0:T(8,128)(2,1)S(1)} %get-tuple-element.37), channel_id=1, source_target_pairs={{0,8},{4,12},{8,0},{12,4},{1,9},{5,13},{9,1},{13,5},{2,10},{6,14},... | collective-permute-start | bytes 417800 | tf_op jit(solution)/shard_map/ppermute | solution.py:35
  12.1 8.5 %collective-permute-start.3 = (bf16[272,256]{1,0:T(8,128)(2,1)S(1)}, bf16[272,256]{1,0:T(8,128)(2,1)S(1)}, u32[]{:S(2)}, u32[]{:S(2)}) collective-permute-start(bf16[272,256]{1,0:T(8,128)(2,1)S(1)} %get-tuple-element.38), channel_id=1, source_target_pairs={{0,4},{4,0},{8,12},{12,8},{1,5},{5,1},{9,13},{13,9},{2,6},{6,2},{1... | collective-permute-start | bytes 417800 | tf_op jit(solution)/shard_map/ppermute | solution.py:35
  21.2 7.9 %collective-permute-start.7 = (bf16[512,256]{1,0:T(8,128)(2,1)S(1)}, bf16[512,256]{1,0:T(8,128)(2,1)S(1)}, u32[]{:S(2)}, u32[]{:S(2)}) collective-permute-start(bf16[512,256]{1,0:T(8,128)(2,1)S(1)} %get-tuple-element.44.rest_4_), channel_id=1, source_target_pairs={{0,2},{2,0},{1,3},{3,1},{4,6},{6,4},{5,7},{7,5},{8,10},{10,8},{9,1... | collective-permute-start | bytes 786440 | tf_op jit(solution)/shard_map/ppermute | solution.py:35
  21.8 5.8 %collective-permute-start.4 = (f32[32,256]{1,0:T(8,128)S(1)}, f32[32,256]{1,0:T(8,128)S(1)}, u32[]{:S(2)}, u32[]{:S(2)}) collective-permute-start(f32[32,256]{1,0:T(8,128)S(1)} %get-tuple-element.40), channel_id=1, source_target_pairs={{0,12},{4,8},{8,4},{12,0},{1,13},{5,9},{9,5},{13,1},{2,14},{6,10},... | collective-permute-start | bytes 98312 | tf_op jit(solution)/shard_map/ppermute | solution.py:35
  24.3 4.8 %collective-permute-start.5 = (f32[32,256]{1,0:T(8,128)S(1)}, f32[32,256]{1,0:T(8,128)S(1)}, u32[]{:S(2)}, u32[]{:S(2)}) collective-permute-start(f32[32,256]{1,0:T(8,128)S(1)} %get-tuple-element.41), channel_id=1, source_target_pairs={{0,8},{4,12},{8,0},{12,4},{1,9},{5,13},{9,1},{13,5},{2,10},{6,14},... | collective-permute-start | bytes 98312 | tf_op jit(solution)/shard_map/ppermute | solution.py:35
  24.4 4.8 %collective-permute-start.6 = (f32[32,256]{1,0:T(8,128)S(1)}, f32[32,256]{1,0:T(8,128)S(1)}, u32[]{:S(2)}, u32[]{:S(2)}) collective-permute-start(f32[32,256]{1,0:T(8,128)S(1)} %get-tuple-element.42), channel_id=1, source_target_pairs={{0,4},{4,0},{8,12},{12,8},{1,5},{5,1},{9,13},{13,9},{2,6},{6,2},{1... | collective-permute-start | bytes 98312 | tf_op jit(solution)/shard_map/ppermute | solution.py:35
  29.7 1.2 %collective-permute-start.8 = (bf16[1,4096]{1,0:T(2,128)(2,1)S(1)}, bf16[1,4096]{1,0:T(2,128)(2,1)S(1)}, u32[]{:S(2)}, u32[]{:S(2)}) collective-permute-start(bf16[1,4096]{1,0:T(2,128)(2,1)S(1)} %attend.1.refs_0_), channel_id=1, source_target_pairs={{0,1},{1,0},{2,3},{3,2},{4,5},{5,4},{6,7},{7,6},{8,9},{9,8},{10,11... | collective-permute-start | bytes 24584 | tf_op jit(solution)/shard_map/ppermute | solution.py:35
  31.0 5.7 %collective-permute-start.11 = (bf16[2,4096]{1,0:T(2,128)(2,1)S(1)}, bf16[2,4096]{1,0:T(2,128)(2,1)S(1)}, u32[]{:S(2)}, u32[]{:S(2)}) collective-permute-start(bf16[2,4096]{1,0:T(2,128)(2,1)S(1)} %join.1.rest_0_), channel_id=1, source_target_pairs={{0,12},{4,8},{8,4},{12,0},{1,13},{5,9},{9,5},{13,1},{2,14},{6,10},... | collective-permute-start | bytes 49160 | tf_op jit(solution)/shard_map/ppermute | solution.py:35
  32.9 4.6 %collective-permute-start.10 = (bf16[2,4096]{1,0:T(2,128)(2,1)S(1)}, bf16[2,4096]{1,0:T(2,128)(2,1)S(1)}, u32[]{:S(2)}, u32[]{:S(2)}) collective-permute-start(bf16[2,4096]{1,0:T(2,128)(2,1)S(1)} %join.1.rest_0_), channel_id=1, source_target_pairs={{0,8},{4,12},{8,0},{12,4},{1,9},{5,13},{9,1},{13,5},{2,10},{6,14},... | collective-permute-start | bytes 49160 | tf_op jit(solution)/shard_map/ppermute | solution.py:35
  33.5 4.0 %collective-permute-start.9 = (bf16[2,4096]{1,0:T(2,128)(2,1)S(1)}, bf16[2,4096]{1,0:T(2,128)(2,1)S(1)}, u32[]{:S(2)}, u32[]{:S(2)}) collective-permute-start(bf16[2,4096]{1,0:T(2,128)(2,1)S(1)} %join.1.rest_0_), channel_id=1, source_target_pairs={{0,4},{4,0},{8,12},{12,8},{1,5},{5,1},{9,13},{13,9},{2,6},{6,2},{1... | collective-permute-start | bytes 49160 | tf_op jit(solution)/shard_map/ppermute | solution.py:35
  38.7 3.2 %collective-permute-start.12 = (f32[2,1024]{1,0:T(2,128)S(1)}, f32[2,1024]{1,0:T(2,128)S(1)}, u32[]{:S(2)}, u32[]{:S(2)}) collective-permute-start(f32[2,1024]{1,0:T(2,128)S(1)} %get-tuple-element.45), channel_id=1, source_target_pairs={{0,3},{1,2},{2,1},{3,0},{4,7},{5,6},{6,5},{7,4},{8,11},{9,10},{10,... | collective-permute-start | bytes 24584 | tf_op jit(solution)/shard_map/ppermute | solution.py:35
  38.9 3.7 %collective-permute-start.13 = (f32[2,1024]{1,0:T(2,128)S(1)}, f32[2,1024]{1,0:T(2,128)S(1)}, u32[]{:S(2)}, u32[]{:S(2)}) collective-permute-start(f32[2,1024]{1,0:T(2,128)S(1)} %get-tuple-element.46), channel_id=1, source_target_pairs={{0,2},{1,3},{2,0},{3,1},{4,6},{5,7},{6,4},{7,5},{8,10},{9,11},{10,... | collective-permute-start | bytes 24584 | tf_op jit(solution)/shard_map/ppermute | solution.py:35
  40.3 2.2 %collective-permute-start.14 = (f32[2,1024]{1,0:T(2,128)S(1)}, f32[2,1024]{1,0:T(2,128)S(1)}, u32[]{:S(2)}, u32[]{:S(2)}) collective-permute-start(f32[2,1024]{1,0:T(2,128)S(1)} %get-tuple-element.47), channel_id=1, source_target_pairs={{0,1},{1,0},{2,3},{3,2},{4,5},{5,4},{6,7},{7,6},{8,9},{9,8},{10,11... | collective-permute-start | bytes 24584 | tf_op jit(solution)/shard_map/ppermute | solution.py:35

commit v13 on v12

--- a/solution.py
+++ b/solution.py
@@ -41,6 +41,11 @@
 
 def in_vmem(value):
     return pltpu.with_memory_space_constraint(value, pltpu.VMEM)
+
+
+def served(size):
+    middle = size // 2
+    return [middle] + [k for k in range(size - 1, -1, -1) if k != middle]
 
 
 def params(mib, **more):
@@ -223,7 +228,7 @@
 
 
 def attend_kernel(pools, heads, map_ref, place_ref, *rest):
-    score_refs = rest[:pools][::-1]
+    score_refs = [rest[served(pools).index(k)] for k in range(pools)]
     value_refs = rest[pools : pools + heads]
     out_ref = rest[-1]
     head = lax.axis_index("heads")
@@ -273,7 +278,7 @@
 
 
 def project_kernel(pools, heads, reps, weight_ref, *rest):
-    row_refs = rest[:pools]
+    row_refs = [rest[served(pools)[::-1].index(k)] for k in range(pools)]
     out_refs = rest[pools:-1]
     acc = rest[-1]
     left = jnp.concatenate([ref[...].astype(jnp.float32) for ref in row_refs], axis=0).astype(jnp.bfloat16)
@@ -400,7 +405,7 @@
         out_specs=VMEM,
         compiler_params=params(16),
         name="attend",
-    )(value_maps, place, *score_parts[::-1], *dense_parts)
+    )(value_maps, place, *[score_parts[k] for k in served(pools)], *dense_parts)
     own_rows = join(*exchange(mine, "rep", reps))
     row_parts = exchange(own_rows, "pool", pools)
 
@@ -414,7 +419,7 @@
         scratch_shapes=[pltpu.VMEM((pools * reps, own_columns), f32)],
         compiler_params=params(24),
         name="project",
-    )(weight, *row_parts)
+    )(weight, *[row_parts[k] for k in served(pools)[::-1]])
     return pl.pallas_call(
         functools.partial(finish_kernel, heads, reps),
         out_shape=shape((1, each, reps * own_columns), bf16),

time: 43.4 us -> 43.6 us (level)
  waiting for transfers between devices: 11.5 us -> 13.5 us
  starting transfers between devices: 18.9 us -> 17.1 us
    ppermute x15, waiting for transfers between devices: 11.5 us -> 13.5 us  [swap(): return lax.ppermute(value, axes, [(i, i ^ step) for i in range(size)])]
    ppermute x15, starting transfers between devices: 18.9 us -> 17.1 us  [swap(): return lax.ppermute(value, axes, [(i, i ^ step) for i in range(size)])]
where the time goes in v13:
time: 43.6 us; the launch traced here: 43.3 us
  starting transfers between devices  17.1 us (39%)
  waiting for transfers between devices  13.5 us (31%)
  Pallas kernels  12.7 us (29%)
    ppermute x15, starting transfers between devices, swap(): return lax.ppermute(value, axes, [(i, i ^ step) for i in range(size)])  17.1 us
    ppermute x15, waiting for transfers between devices, swap(): return lax.ppermute(value, axes, [(i, i ^ step) for i in range(size)])  13.5 us
    pallas_call x1, Pallas kernels, per_device(): pl.pallas_call(stage_kernel, out_shape=shape(out_weight.shape, bf16), in_...  3.39 us
    pallas_call x1, Pallas kernels, per_device(): pl.pallas_call(functools.partial(table_kernel, pools, shard_blocks), out_...  2.97 us
    pallas_call x1, Pallas kernels, per_device(): pl.pallas_call(functools.partial(gather_kernel, pools), out_shape=[shape(...  2.54 us
    pallas_call x1, Pallas kernels, per_device(): pl.pallas_call(functools.partial(project_kernel, pools, heads, reps), out...  1.21 us
  transfers between devices with their start and end apart: 15, of which 9 were waited for; matrix products, arithmetic and copies ran while one was open for 0% of the time, Pallas kernels for 17%

profile of v13, /device:TPU:0, one launch (start us, length us, event | category | flops | bytes accessed | tf_op | source)
XLA Modules:
  0.0 43.3 jit_solution(7884584772789949880)
XLA Ops:
  0.0 2.5 %gather.1 = (bf16[1024,256]{1,0:T(8,128)(2,1)S(1)}, bf16[272,256]{1,0:T(8,128)(2,1)S(1)}, bf16[272,256]{1,0:T(8,128)(2,1)S(1)}, bf16[272,256]{1,0:T(8,128)(2,1)S(1)}, bf16[272,256]{1,0:T(8,128)(2,1)S(1)}) custom-call(s32[1,4,4]{2,1,0:T(4,128)} %sel_ref.3, bf16[1,4,1024,512]{3,2,1,0:T(8,128)(2,1)} %lat_ref.1, bf16[1,1,4096]{2,1,0:T(2,128)(2,1)} %query_ref.1), custom_call_target="tpu_custom_call" | custom-call | tf_op jit(solution)/shard_map/gather/pallas_call | solution.py:339
  2.5 3.0 %collective-permute-start = (bf16[1024,256]{1,0:T(8,128)(2,1)S(1)}, bf16[1024,256]{1,0:T(8,128)(2,1)S(1)}, u32[]{:S(2)}, u32[]{:S(2)}) collective-permute-start(bf16[1024,256]{1,0:T(8,128)(2,1)S(1)} %get-tuple-element.35.rest_0_), channel_id=1, source_target_pairs={{0,2},{2,0},{1,3},{3,1},{4,6},{6,4},{5,7},{7,5},{8,10},{10,8},{9,1... | collective-permute-start | bytes 1572872 | tf_op jit(solution)/shard_map/ppermute | solution.py:35
  5.6 3.6 %collective-permute-start.1 = (bf16[272,256]{1,0:T(8,128)(2,1)S(1)}, bf16[272,256]{1,0:T(8,128)(2,1)S(1)}, u32[]{:S(2)}, u32[]{:S(2)}) collective-permute-start(bf16[272,256]{1,0:T(8,128)(2,1)S(1)} %get-tuple-element.36), channel_id=1, source_target_pairs={{0,12},{4,8},{8,4},{12,0},{1,13},{5,9},{9,5},{13,1},{2,14},{6,10},... | collective-permute-start | bytes 417800 | tf_op jit(solution)/shard_map/ppermute | solution.py:35
  9.2 3.0 %tables.1 = (f32[1024,128]{1,0:T(8,128)S(1)}, f32[1024,128]{1,0:T(8,128)S(1)}, f32[8,128]{1,0:T(8,128)S(1)}, s32[4,256]{1,0:T(4,128)S(1)}, s32[1,1024]{1,0:T(1,1...) custom-call(s32[1,4,4]{2,1,0:T(4,128)} %sel_ref.3, ...), custom_call_target="tpu_custom_call", output_to_operand_aliasing={{7}: (5, {})} | custom-call | tf_op jit(solution)/shard_map/tables/pallas_call | solution.py:354
  12.1 0.9 %collective-permute-start.3 = (bf16[272,256]{1,0:T(8,128)(2,1)S(1)}, bf16[272,256]{1,0:T(8,128)(2,1)S(1)}, u32[]{:S(2)}, u32[]{:S(2)}) collective-permute-start(bf16[272,256]{1,0:T(8,128)(2,1)S(1)} %get-tuple-element.38), channel_id=1, source_target_pairs={{0,4},{4,0},{8,12},{12,8},{1,5},{5,1},{9,13},{13,9},{2,6},{6,2},{1... | collective-permute-start | bytes 417800 | tf_op jit(solution)/shard_map/ppermute | solution.py:35
  13.0 3.4 %stage.1.after_ref.weight_ref = bf16[4096,1024]{1,0:T(8,128)(2,1)S(1)} custom-call(bf16[4096,1024]{1,0:T(8,128)(2,1)} %weight_ref.1, s32[1,1024]{1,0:T(1,128)S(1)} %get-tuple-element.28.after_ref.place_ref), custom_call_target="tpu_custom_call" | custom-call | tf_op jit(solution)/shard_map/stage/pallas_call | solution.py:373
  16.4 1.1 %collective-permute-done.rest_1_ = bf16[1024,256]{1,0:T(8,128)(2,1)S(1)} collective-permute-done((bf16[1024,256]{1,0:T(8,128)(2,1)S(1)}, bf16[1024,256]{1,0:T(8,128)(2,1)S(1)}, u32[]{:S(2)}, u32[]{:S(2)}) %collective-permute-start) | collective-permute-done | bytes 524320 | tf_op jit(solution)/shard_map/ppermute | solution.py:35
  17.5 0.9 %rebuild.1.key_ref = bf16[1024,512]{1,0:T(8,128)(2,1)S(1)} custom-call(bf16[512,512]{1,0:T(8,128)(2,1)S(1)} %get-tuple-element.32.map_ref, f32[1024,128]{1,0:T(8,128)S(1)} %get-tuple-element.33.cos_ref, f32[1024,128]{1,0:T(8,128)S(1)} %get-tuple-element.34.sin_ref, bf16[4096,1024]{1,0:T(8,128)(2,1)S(1)} %stage.1.after_ref.weight_ref, ...), custom_call_target="tpu_custom_call" | custom-call | tf_op jit(solution)/shard_map/rebuild/pallas_call | solution.py:382
  18.3 2.3 %collective-permute-done.2.rest_1_ = bf16[272,256]{1,0:T(8,128)(2,1)S(1)} collective-permute-done((bf16[272,256]{1,0:T(8,128)(2,1)S(1)}, bf16[272,256]{1,0:T(8,128)(2,1)S(1)}, u32[]{:S(2)}, u32[]{:S(2)}) %collective-permute-start.2) | collective-permute-done | bytes 139296 | tf_op jit(solution)/shard_map/ppermute | solution.py:35
  20.7 0.6 %score.1 = (bf16[512,256]{1,0:T(8,128)(2,1)S(1)}, f32[32,256]{1,0:T(8,128)S(1)}, f32[32,256]{1,0:T(8,128)S(1)}, f32[32,256]{1,0:T(8,128)S(1)}, f32[32,256]{1,0:T(8,128)S(1)}) custom-call(f32[8,128]{1,0:T(8,128)S(1)} %get-tuple-element.30.turn_ref, s32[4,256]{1,0:T(4,128)S(1)} %get-tuple-element.31.live_ref, ...), custom_call_target="tpu_custom_call" | custom-call | tf_op jit(solution)/shard_map/score/pallas_call | solution.py:390
  21.2 0.6 %collective-permute-start.7 = (bf16[512,256]{1,0:T(8,128)(2,1)S(1)}, bf16[512,256]{1,0:T(8,128)(2,1)S(1)}, u32[]{:S(2)}, u32[]{:S(2)}) collective-permute-start(bf16[512,256]{1,0:T(8,128)(2,1)S(1)} %get-tuple-element.44.rest_4_), channel_id=1, source_target_pairs={{0,2},{2,0},{1,3},{3,1},{4,6},{6,4},{5,7},{7,5},{8,10},{10,8},{9,1... | collective-permute-start | bytes 786440 | tf_op jit(solution)/shard_map/ppermute | solution.py:35
  21.8 1.5 %collective-permute-start.4 = (f32[32,256]{1,0:T(8,128)S(1)}, f32[32,256]{1,0:T(8,128)S(1)}, u32[]{:S(2)}, u32[]{:S(2)}) collective-permute-start(f32[32,256]{1,0:T(8,128)S(1)} %get-tuple-element.40), channel_id=1, source_target_pairs={{0,8},{4,12},{8,0},{12,4},{1,9},{5,13},{9,1},{13,5},{2,10},{6,14},... | collective-permute-start | bytes 98312 | tf_op jit(solution)/shard_map/ppermute | solution.py:35
  23.3 1.3 %collective-permute-start.5 = (f32[32,256]{1,0:T(8,128)S(1)}, f32[32,256]{1,0:T(8,128)S(1)}, u32[]{:S(2)}, u32[]{:S(2)}) collective-permute-start(f32[32,256]{1,0:T(8,128)S(1)} %get-tuple-element.41), channel_id=1, source_target_pairs={{0,12},{4,8},{8,4},{12,0},{1,13},{5,9},{9,5},{13,1},{2,14},{6,10},... | collective-permute-start | bytes 98312 | tf_op jit(solution)/shard_map/ppermute | solution.py:35
  24.7 0.6 %collective-permute-start.6 = (f32[32,256]{1,0:T(8,128)S(1)}, f32[32,256]{1,0:T(8,128)S(1)}, u32[]{:S(2)}, u32[]{:S(2)}) collective-permute-start(f32[32,256]{1,0:T(8,128)S(1)} %get-tuple-element.42), channel_id=1, source_target_pairs={{0,4},{4,0},{8,12},{12,8},{1,5},{5,1},{9,13},{13,9},{2,6},{6,2},{1... | collective-permute-start | bytes 98312 | tf_op jit(solution)/shard_map/ppermute | solution.py:35
  25.3 1.9 %collective-permute-done.4.rest_0_ = f32[32,256]{1,0:T(8,128)S(1)} collective-permute-done((f32[32,256]{1,0:T(8,128)S(1)}, f32[32,256]{1,0:T(8,128)S(1)}, u32[]{:S(2)}, u32[]{:S(2)}) %collective-permute-start.4) | collective-permute-done | bytes 32800 | tf_op jit(solution)/shard_map/ppermute | solution.py:35
  27.2 1.9 %collective-permute-done.5.rest_1_ = f32[32,256]{1,0:T(8,128)S(1)} collective-permute-done((f32[32,256]{1,0:T(8,128)S(1)}, f32[32,256]{1,0:T(8,128)S(1)}, u32[]{:S(2)}, u32[]{:S(2)}) %collective-permute-start.5) | collective-permute-done | bytes 32800 | tf_op jit(solution)/shard_map/ppermute | solution.py:35
  29.1 0.5 %attend.1.refs_0_ = bf16[1,4096]{1,0:T(2,128)(2,1)S(1)} custom-call(bf16[512,512]{1,0:T(8,128)(2,1)S(1)} %get-tuple-element.29.map_ref, s32[1,1024]{1,0:T(1,128)S(1)} %get-tuple-element.28.after_ref.place_ref, f32[32,256]{1,0:T(8,128)S(1)} %collective-permute-done.4.rest_0_, f32[32,256]{1,0:T(8,128)S(1)} %collective-permute-done.5.rest_1_, ...), custom_call_target="tpu_custom_call" | custom-call | tf_op jit(solution)/shard_map/attend/pallas_call | solution.py:401
  29.6 0.1 collective-permute-start.8
  29.7 1.2 %collective-permute-done.8.refs_1_ = bf16[1,4096]{1,0:T(2,128)(2,1)S(1)} collective-permute-done((bf16[1,4096]{1,0:T(2,128)(2,1)S(1)}, bf16[1,4096]{1,0:T(2,128)(2,1)S(1)}, u32[]{:S(2)}, u32[]{:S(2)}) %collective-permute-start.8) | collective-permute-done | bytes 8224 | tf_op jit(solution)/shard_map/ppermute | solution.py:35
  30.9 1.3 %collective-permute-start.11 = (bf16[2,4096]{1,0:T(2,128)(2,1)S(1)}, bf16[2,4096]{1,0:T(2,128)(2,1)S(1)}, u32[]{:S(2)}, u32[]{:S(2)}) collective-permute-start(bf16[2,4096]{1,0:T(2,128)(2,1)S(1)} %join.1.rest_0_), channel_id=1, source_target_pairs={{0,8},{4,12},{8,0},{12,4},{1,9},{5,13},{9,1},{13,5},{2,10},{6,14},... | collective-permute-start | bytes 49160 | tf_op jit(solution)/shard_map/ppermute | solution.py:35
  32.2 1.3 %collective-permute-start.10 = (bf16[2,4096]{1,0:T(2,128)(2,1)S(1)}, bf16[2,4096]{1,0:T(2,128)(2,1)S(1)}, u32[]{:S(2)}, u32[]{:S(2)}) collective-permute-start(bf16[2,4096]{1,0:T(2,128)(2,1)S(1)} %join.1.rest_0_), channel_id=1, source_target_pairs={{0,12},{4,8},{8,4},{12,0},{1,13},{5,9},{9,5},{13,1},{2,14},{6,10},... | collective-permute-start | bytes 49160 | tf_op jit(solution)/shard_map/ppermute | solution.py:35
  33.5 0.9 %collective-permute-start.9 = (bf16[2,4096]{1,0:T(2,128)(2,1)S(1)}, bf16[2,4096]{1,0:T(2,128)(2,1)S(1)}, u32[]{:S(2)}, u32[]{:S(2)}) collective-permute-start(bf16[2,4096]{1,0:T(2,128)(2,1)S(1)} %join.1.rest_0_), channel_id=1, source_target_pairs={{0,4},{4,0},{8,12},{12,8},{1,5},{5,1},{9,13},{13,9},{2,6},{6,2},{1... | collective-permute-start | bytes 49160 | tf_op jit(solution)/shard_map/ppermute | solution.py:35
  34.4 1.3 %collective-permute-done.11.rest_3_ = bf16[2,4096]{1,0:T(2,128)(2,1)S(1)} collective-permute-done((bf16[2,4096]{1,0:T(2,128)(2,1)S(1)}, bf16[2,4096]{1,0:T(2,128)(2,1)S(1)}, u32[]{:S(2)}, u32[]{:S(2)}) %collective-permute-start.11) | collective-permute-done | bytes 16416 | tf_op jit(solution)/shard_map/ppermute | solution.py:35
  35.7 2.0 %collective-permute-done.10.rest_2_ = bf16[2,4096]{1,0:T(2,128)(2,1)S(1)} collective-permute-done((bf16[2,4096]{1,0:T(2,128)(2,1)S(1)}, bf16[2,4096]{1,0:T(2,128)(2,1)S(1)}, u32[]{:S(2)}, u32[]{:S(2)}) %collective-permute-start.10) | collective-permute-done | bytes 16416 | tf_op jit(solution)/shard_map/ppermute | solution.py:35
  37.7 1.2 %project.1 = (f32[2,1024]{1,0:T(2,128)S(1)}, f32[2,1024]{1,0:T(2,128)S(1)}, f32[2,1024]{1,0:T(2,128)S(1)}, f32[2,1024]{1,0:T(2,128)S(1)}) custom-call(bf16[4096,1024]{1,0:T(8,128)(2,1)S(1)} %stage.1.after_ref.weight_ref, bf16[2,4096]{1,0:T(2,128)(2,1)S(1)} %join.1.rest_0_, bf16[2,4096]{1,0:T(2,128)(2,1)S(1)} %collective-permute-done.9.rest_1_, ...), custom_call_target="tpu_custom_call" | custom-call | tf_op jit(solution)/shard_map/project/pallas_call | solution.py:414
  38.9 0.1 collective-permute-start.12
  39.0 1.5 %collective-permute-start.13 = (f32[2,1024]{1,0:T(2,128)S(1)}, f32[2,1024]{1,0:T(2,128)S(1)}, u32[]{:S(2)}, u32[]{:S(2)}) collective-permute-start(f32[2,1024]{1,0:T(2,128)S(1)} %get-tuple-element.46), channel_id=1, source_target_pairs={{0,2},{1,3},{2,0},{3,1},{4,6},{5,7},{6,4},{7,5},{8,10},{9,11},{10,... | collective-permute-start | bytes 24584 | tf_op jit(solution)/shard_map/ppermute | solution.py:35
  40.5 0.3 collective-permute-start.14
  40.9 1.3 %collective-permute-done.12.refs_0_ = f32[2,1024]{1,0:T(2,128)S(1)} collective-permute-done((f32[2,1024]{1,0:T(2,128)S(1)}, f32[2,1024]{1,0:T(2,128)S(1)}, u32[]{:S(2)}, u32[]{:S(2)}) %collective-permute-start.12) | collective-permute-done | bytes 8224 | tf_op jit(solution)/shard_map/ppermute | solution.py:35
  42.1 0.6 %collective-permute-done.13.refs_1_ = f32[2,1024]{1,0:T(2,128)S(1)} collective-permute-done((f32[2,1024]{1,0:T(2,128)S(1)}, f32[2,1024]{1,0:T(2,128)S(1)}, u32[]{:S(2)}, u32[]{:S(2)}) %collective-permute-start.13) | collective-permute-done | bytes 8224 | tf_op jit(solution)/shard_map/ppermute | solution.py:35
  42.7 0.0 collective-permute-done.14.refs_2_
  42.7 0.6 %finish.1 = bf16[1,2,2048]{2,1,0:T(2,128)(2,1)} custom-call(f32[2,1024]{1,0:T(2,128)S(1)} %collective-permute-done.12.refs_0_, f32[2,1024]{1,0:T(2,128)S(1)} %collective-permute-done.13.refs_1_, f32[2,1024]{1,0:T(2,128)S(1)} %collective-permute-done.14.refs_2_, f32[2,1024]{1,0:T(2,128)S(1)} %get-tuple-element.48.refs_3_), custom_call_target="tpu_custom_call" | custom-call | tf_op jit(solution)/shard_map/finish/pallas_call | solution.py:423
  (7 shorter events, 0.0 us)
Async XLA Ops:
  2.5 14.9 %collective-permute-start = (bf16[1024,256]{1,0:T(8,128)(2,1)S(1)}, bf16[1024,256]{1,0:T(8,128)(2,1)S(1)}, u32[]{:S(2)}, u32[]{:S(2)}) collective-permute-start(bf16[1024,256]{1,0:T(8,128)(2,1)S(1)} %get-tuple-element.35.rest_0_), channel_id=1, source_target_pairs={{0,2},{2,0},{1,3},{3,1},{4,6},{6,4},{5,7},{7,5},{8,10},{10,8},{9,1... | collective-permute-start | bytes 1572872 | tf_op jit(solution)/shard_map/ppermute | solution.py:35
  5.6 12.8 %collective-permute-start.1 = (bf16[272,256]{1,0:T(8,128)(2,1)S(1)}, bf16[272,256]{1,0:T(8,128)(2,1)S(1)}, u32[]{:S(2)}, u32[]{:S(2)}) collective-permute-start(bf16[272,256]{1,0:T(8,128)(2,1)S(1)} %get-tuple-element.36), channel_id=1, source_target_pairs={{0,12},{4,8},{8,4},{12,0},{1,13},{5,9},{9,5},{13,1},{2,14},{6,10},... | collective-permute-start | bytes 417800 | tf_op jit(solution)/shard_map/ppermute | solution.py:35
  9.2 11.5 %collective-permute-start.2 = (bf16[272,256]{1,0:T(8,128)(2,1)S(1)}, bf16[272,256]{1,0:T(8,128)(2,1)S(1)}, u32[]{:S(2)}, u32[]{:S(2)}) collective-permute-start(bf16[272,256]{1,0:T(8,128)(2,1)S(1)} %get-tuple-element.37), channel_id=1, source_target_pairs={{0,8},{4,12},{8,0},{12,4},{1,9},{5,13},{9,1},{13,5},{2,10},{6,14},... | collective-permute-start | bytes 417800 | tf_op jit(solution)/shard_map/ppermute | solution.py:35
  12.1 8.5 %collective-permute-start.3 = (bf16[272,256]{1,0:T(8,128)(2,1)S(1)}, bf16[272,256]{1,0:T(8,128)(2,1)S(1)}, u32[]{:S(2)}, u32[]{:S(2)}) collective-permute-start(bf16[272,256]{1,0:T(8,128)(2,1)S(1)} %get-tuple-element.38), channel_id=1, source_target_pairs={{0,4},{4,0},{8,12},{12,8},{1,5},{5,1},{9,13},{13,9},{2,6},{6,2},{1... | collective-permute-start | bytes 417800 | tf_op jit(solution)/shard_map/ppermute | solution.py:35
  21.2 7.8 %collective-permute-start.7 = (bf16[512,256]{1,0:T(8,128)(2,1)S(1)}, bf16[512,256]{1,0:T(8,128)(2,1)S(1)}, u32[]{:S(2)}, u32[]{:S(2)}) collective-permute-start(bf16[512,256]{1,0:T(8,128)(2,1)S(1)} %get-tuple-element.44.rest_4_), channel_id=1, source_target_pairs={{0,2},{2,0},{1,3},{3,1},{4,6},{6,4},{5,7},{7,5},{8,10},{10,8},{9,1... | collective-permute-start | bytes 786440 | tf_op jit(solution)/shard_map/ppermute | solution.py:35
  21.8 5.4 %collective-permute-start.4 = (f32[32,256]{1,0:T(8,128)S(1)}, f32[32,256]{1,0:T(8,128)S(1)}, u32[]{:S(2)}, u32[]{:S(2)}) collective-permute-start(f32[32,256]{1,0:T(8,128)S(1)} %get-tuple-element.40), channel_id=1, source_target_pairs={{0,8},{4,12},{8,0},{12,4},{1,9},{5,13},{9,1},{13,5},{2,10},{6,14},... | collective-permute-start | bytes 98312 | tf_op jit(solution)/shard_map/ppermute | solution.py:35
  23.3 5.7 %collective-permute-start.5 = (f32[32,256]{1,0:T(8,128)S(1)}, f32[32,256]{1,0:T(8,128)S(1)}, u32[]{:S(2)}, u32[]{:S(2)}) collective-permute-start(f32[32,256]{1,0:T(8,128)S(1)} %get-tuple-element.41), channel_id=1, source_target_pairs={{0,12},{4,8},{8,4},{12,0},{1,13},{5,9},{9,5},{13,1},{2,14},{6,10},... | collective-permute-start | bytes 98312 | tf_op jit(solution)/shard_map/ppermute | solution.py:35
  24.7 4.4 %collective-permute-start.6 = (f32[32,256]{1,0:T(8,128)S(1)}, f32[32,256]{1,0:T(8,128)S(1)}, u32[]{:S(2)}, u32[]{:S(2)}) collective-permute-start(f32[32,256]{1,0:T(8,128)S(1)} %get-tuple-element.42), channel_id=1, source_target_pairs={{0,4},{4,0},{8,12},{12,8},{1,5},{5,1},{9,13},{13,9},{2,6},{6,2},{1... | collective-permute-start | bytes 98312 | tf_op jit(solution)/shard_map/ppermute | solution.py:35
  29.6 1.2 %collective-permute-start.8 = (bf16[1,4096]{1,0:T(2,128)(2,1)S(1)}, bf16[1,4096]{1,0:T(2,128)(2,1)S(1)}, u32[]{:S(2)}, u32[]{:S(2)}) collective-permute-start(bf16[1,4096]{1,0:T(2,128)(2,1)S(1)} %attend.1.refs_0_), channel_id=1, source_target_pairs={{0,1},{1,0},{2,3},{3,2},{4,5},{5,4},{6,7},{7,6},{8,9},{9,8},{10,11... | collective-permute-start | bytes 24584 | tf_op jit(solution)/shard_map/ppermute | solution.py:35
  30.9 4.8 %collective-permute-start.11 = (bf16[2,4096]{1,0:T(2,128)(2,1)S(1)}, bf16[2,4096]{1,0:T(2,128)(2,1)S(1)}, u32[]{:S(2)}, u32[]{:S(2)}) collective-permute-start(bf16[2,4096]{1,0:T(2,128)(2,1)S(1)} %join.1.rest_0_), channel_id=1, source_target_pairs={{0,8},{4,12},{8,0},{12,4},{1,9},{5,13},{9,1},{13,5},{2,10},{6,14},... | collective-permute-start | bytes 49160 | tf_op jit(solution)/shard_map/ppermute | solution.py:35
  32.2 5.5 %collective-permute-start.10 = (bf16[2,4096]{1,0:T(2,128)(2,1)S(1)}, bf16[2,4096]{1,0:T(2,128)(2,1)S(1)}, u32[]{:S(2)}, u32[]{:S(2)}) collective-permute-start(bf16[2,4096]{1,0:T(2,128)(2,1)S(1)} %join.1.rest_0_), channel_id=1, source_target_pairs={{0,12},{4,8},{8,4},{12,0},{1,13},{5,9},{9,5},{13,1},{2,14},{6,10},... | collective-permute-start | bytes 49160 | tf_op jit(solution)/shard_map/ppermute | solution.py:35
  33.5 4.2 %collective-permute-start.9 = (bf16[2,4096]{1,0:T(2,128)(2,1)S(1)}, bf16[2,4096]{1,0:T(2,128)(2,1)S(1)}, u32[]{:S(2)}, u32[]{:S(2)}) collective-permute-start(bf16[2,4096]{1,0:T(2,128)(2,1)S(1)} %join.1.rest_0_), channel_id=1, source_target_pairs={{0,4},{4,0},{8,12},{12,8},{1,5},{5,1},{9,13},{13,9},{2,6},{6,2},{1... | collective-permute-start | bytes 49160 | tf_op jit(solution)/shard_map/ppermute | solution.py:35
  38.9 3.2 %collective-permute-start.12 = (f32[2,1024]{1,0:T(2,128)S(1)}, f32[2,1024]{1,0:T(2,128)S(1)}, u32[]{:S(2)}, u32[]{:S(2)}) collective-permute-start(f32[2,1024]{1,0:T(2,128)S(1)} %get-tuple-element.45), channel_id=1, source_target_pairs={{0,3},{1,2},{2,1},{3,0},{4,7},{5,6},{6,5},{7,4},{8,11},{9,10},{10,... | collective-permute-start | bytes 24584 | tf_op jit(solution)/shard_map/ppermute | solution.py:35
  39.0 3.7 %collective-permute-start.13 = (f32[2,1024]{1,0:T(2,128)S(1)}, f32[2,1024]{1,0:T(2,128)S(1)}, u32[]{:S(2)}, u32[]{:S(2)}) collective-permute-start(f32[2,1024]{1,0:T(2,128)S(1)} %get-tuple-element.46), channel_id=1, source_target_pairs={{0,2},{1,3},{2,0},{3,1},{4,6},{5,7},{6,4},{7,5},{8,10},{9,11},{10,... | collective-permute-start | bytes 24584 | tf_op jit(solution)/shard_map/ppermute | solution.py:35
  40.5 2.2 %collective-permute-start.14 = (f32[2,1024]{1,0:T(2,128)S(1)}, f32[2,1024]{1,0:T(2,128)S(1)}, u32[]{:S(2)}, u32[]{:S(2)}) collective-permute-start(f32[2,1024]{1,0:T(2,128)S(1)} %get-tuple-element.47), channel_id=1, source_target_pairs={{0,1},{1,0},{2,3},{3,2},{4,5},{5,4},{6,7},{7,6},{8,9},{9,8},{10,11... | collective-permute-start | bytes 24584 | tf_op jit(solution)/shard_map/ppermute | solution.py:35

commit v14 on v12

--- a/solution.py
+++ b/solution.py
@@ -104,14 +104,14 @@
     queries = heads_to_rows(query_ref[0].astype(jnp.float32), width).astype(jnp.bfloat16)
     for copy in copies.values():
         copy.wait()
-    for k in range(pools - 1, -1, -1):
-        for j in range(columns // chunk):
-            packed = jnp.dot(
-                raw[k * rows : (k + 1) * rows, j * chunk : (j + 1) * chunk], pick,
-                preferred_element_type=jnp.float32,
-            ).astype(jnp.bfloat16)
-            keys_ref[k * rows : (k + 1) * rows, j * half : (j + 1) * half] = packed[:, :half]
-            value_refs[k][:rows, j * half : (j + 1) * half] = packed[:, half:]
+    for j in range(columns // chunk):
+        packed = jnp.dot(
+            raw[:, j * chunk : (j + 1) * chunk], pick, preferred_element_type=jnp.float32
+        ).astype(jnp.bfloat16)
+        keys_ref[:, j * half : (j + 1) * half] = packed[:, :half]
+        for k in range(pools):
+            value_refs[k][:rows, j * half : (j + 1) * half] = packed[k * rows : (k + 1) * rows, half:]
+    for k in range(pools):
         value_refs[k][rows:, :] = queries
 
 

time: 43.4 us -> 43.4 us (level)
  no operation moved by 1% of the time
where the time goes in v14:
time: 43.4 us; the launch traced here: 43.1 us
  starting transfers between devices  18.9 us (44%)
  Pallas kernels  12.7 us (29%)
  waiting for transfers between devices  11.5 us (26%)
    ppermute x15, starting transfers between devices, swap(): return lax.ppermute(value, axes, [(i, i ^ step) for i in range(size)])  18.9 us
    ppermute x15, waiting for transfers between devices, swap(): return lax.ppermute(value, axes, [(i, i ^ step) for i in range(size)])  11.5 us
    pallas_call x1, Pallas kernels, per_device(): pl.pallas_call(stage_kernel, out_shape=shape(out_weight.shape, bf16), in_...  3.39 us
    pallas_call x1, Pallas kernels, per_device(): pl.pallas_call(functools.partial(table_kernel, pools, shard_blocks), out_...  2.97 us
    pallas_call x1, Pallas kernels, per_device(): pl.pallas_call(functools.partial(gather_kernel, pools), out_shape=[shape(...  2.53 us
    pallas_call x1, Pallas kernels, per_device(): pl.pallas_call(functools.partial(project_kernel, pools, heads, reps), out...  1.21 us
  transfers between devices with their start and end apart: 15, of which 9 were waited for; matrix products, arithmetic and copies ran while one was open for 0% of the time, Pallas kernels for 17%

profile of v14, /device:TPU:0, one launch (start us, length us, event | category | flops | bytes accessed | tf_op | source)
XLA Modules:
  0.0 43.1 jit_solution(14030902106666866031)
XLA Ops:
  0.0 2.5 %gather.1 = (bf16[1024,256]{1,0:T(8,128)(2,1)S(1)}, bf16[272,256]{1,0:T(8,128)(2,1)S(1)}, bf16[272,256]{1,0:T(8,128)(2,1)S(1)}, bf16[272,256]{1,0:T(8,128)(2,1)S(1)}, bf16[272,256]{1,0:T(8,128)(2,1)S(1)}) custom-call(s32[1,4,4]{2,1,0:T(4,128)} %sel_ref.3, bf16[1,4,1024,512]{3,2,1,0:T(8,128)(2,1)} %lat_ref.1, bf16[1,1,4096]{2,1,0:T(2,128)(2,1)} %query_ref.1), custom_call_target="tpu_custom_call" | custom-call | tf_op jit(solution)/shard_map/gather/pallas_call | solution.py:334
  2.5 3.0 %collective-permute-start = (bf16[1024,256]{1,0:T(8,128)(2,1)S(1)}, bf16[1024,256]{1,0:T(8,128)(2,1)S(1)}, u32[]{:S(2)}, u32[]{:S(2)}) collective-permute-start(bf16[1024,256]{1,0:T(8,128)(2,1)S(1)} %get-tuple-element.35.rest_0_), channel_id=1, source_target_pairs={{0,2},{2,0},{1,3},{3,1},{4,6},{6,4},{5,7},{7,5},{8,10},{10,8},{9,1... | collective-permute-start | bytes 1572872 | tf_op jit(solution)/shard_map/ppermute | solution.py:35
  5.5 3.6 %collective-permute-start.1 = (bf16[272,256]{1,0:T(8,128)(2,1)S(1)}, bf16[272,256]{1,0:T(8,128)(2,1)S(1)}, u32[]{:S(2)}, u32[]{:S(2)}) collective-permute-start(bf16[272,256]{1,0:T(8,128)(2,1)S(1)} %get-tuple-element.36), channel_id=1, source_target_pairs={{0,12},{4,8},{8,4},{12,0},{1,13},{5,9},{9,5},{13,1},{2,14},{6,10},... | collective-permute-start | bytes 417800 | tf_op jit(solution)/shard_map/ppermute | solution.py:35
  9.1 0.0 collective-permute-start.2
  9.1 3.0 %tables.1 = (f32[1024,128]{1,0:T(8,128)S(1)}, f32[1024,128]{1,0:T(8,128)S(1)}, f32[8,128]{1,0:T(8,128)S(1)}, s32[4,256]{1,0:T(4,128)S(1)}, s32[1,1024]{1,0:T(1,1...) custom-call(s32[1,4,4]{2,1,0:T(4,128)} %sel_ref.3, ...), custom_call_target="tpu_custom_call", output_to_operand_aliasing={{7}: (5, {})} | custom-call | tf_op jit(solution)/shard_map/tables/pallas_call | solution.py:349
  12.1 0.8 %collective-permute-start.3 = (bf16[272,256]{1,0:T(8,128)(2,1)S(1)}, bf16[272,256]{1,0:T(8,128)(2,1)S(1)}, u32[]{:S(2)}, u32[]{:S(2)}) collective-permute-start(bf16[272,256]{1,0:T(8,128)(2,1)S(1)} %get-tuple-element.38), channel_id=1, source_target_pairs={{0,4},{4,0},{8,12},{12,8},{1,5},{5,1},{9,13},{13,9},{2,6},{6,2},{1... | collective-permute-start | bytes 417800 | tf_op jit(solution)/shard_map/ppermute | solution.py:35
  13.0 3.4 %stage.1.after_ref.weight_ref = bf16[4096,1024]{1,0:T(8,128)(2,1)S(1)} custom-call(bf16[4096,1024]{1,0:T(8,128)(2,1)} %weight_ref.1, s32[1,1024]{1,0:T(1,128)S(1)} %get-tuple-element.28.after_ref.place_ref), custom_call_target="tpu_custom_call" | custom-call | tf_op jit(solution)/shard_map/stage/pallas_call | solution.py:368
  16.4 1.1 %collective-permute-done.rest_1_ = bf16[1024,256]{1,0:T(8,128)(2,1)S(1)} collective-permute-done((bf16[1024,256]{1,0:T(8,128)(2,1)S(1)}, bf16[1024,256]{1,0:T(8,128)(2,1)S(1)}, u32[]{:S(2)}, u32[]{:S(2)}) %collective-permute-start) | collective-permute-done | bytes 524320 | tf_op jit(solution)/shard_map/ppermute | solution.py:35
  17.5 0.9 %rebuild.1.key_ref = bf16[1024,512]{1,0:T(8,128)(2,1)S(1)} custom-call(bf16[512,512]{1,0:T(8,128)(2,1)S(1)} %get-tuple-element.32.map_ref, f32[1024,128]{1,0:T(8,128)S(1)} %get-tuple-element.33.cos_ref, f32[1024,128]{1,0:T(8,128)S(1)} %get-tuple-element.34.sin_ref, bf16[4096,1024]{1,0:T(8,128)(2,1)S(1)} %stage.1.after_ref.weight_ref, ...), custom_call_target="tpu_custom_call" | custom-call | tf_op jit(solution)/shard_map/rebuild/pallas_call | solution.py:377
  18.3 0.0 collective-permute-done.1.rest_0_
  18.3 2.3 %collective-permute-done.2.rest_1_ = bf16[272,256]{1,0:T(8,128)(2,1)S(1)} collective-permute-done((bf16[272,256]{1,0:T(8,128)(2,1)S(1)}, bf16[272,256]{1,0:T(8,128)(2,1)S(1)}, u32[]{:S(2)}, u32[]{:S(2)}) %collective-permute-start.2) | collective-permute-done | bytes 139296 | tf_op jit(solution)/shard_map/ppermute | solution.py:35
  20.7 0.6 %score.1 = (bf16[512,256]{1,0:T(8,128)(2,1)S(1)}, f32[32,256]{1,0:T(8,128)S(1)}, f32[32,256]{1,0:T(8,128)S(1)}, f32[32,256]{1,0:T(8,128)S(1)}, f32[32,256]{1,0:T(8,128)S(1)}) custom-call(f32[8,128]{1,0:T(8,128)S(1)} %get-tuple-element.30.turn_ref, s32[4,256]{1,0:T(4,128)S(1)} %get-tuple-element.31.live_ref, ...), custom_call_target="tpu_custom_call" | custom-call | tf_op jit(solution)/shard_map/score/pallas_call | solution.py:385
  21.2 0.6 %collective-permute-start.7 = (bf16[512,256]{1,0:T(8,128)(2,1)S(1)}, bf16[512,256]{1,0:T(8,128)(2,1)S(1)}, u32[]{:S(2)}, u32[]{:S(2)}) collective-permute-start(bf16[512,256]{1,0:T(8,128)(2,1)S(1)} %get-tuple-element.44.rest_4_), channel_id=1, source_target_pairs={{0,2},{2,0},{1,3},{3,1},{4,6},{6,4},{5,7},{7,5},{8,10},{10,8},{9,1... | collective-permute-start | bytes 786440 | tf_op jit(solution)/shard_map/ppermute | solution.py:35
  21.8 2.5 %collective-permute-start.4 = (f32[32,256]{1,0:T(8,128)S(1)}, f32[32,256]{1,0:T(8,128)S(1)}, u32[]{:S(2)}, u32[]{:S(2)}) collective-permute-start(f32[32,256]{1,0:T(8,128)S(1)} %get-tuple-element.40), channel_id=1, source_target_pairs={{0,12},{4,8},{8,4},{12,0},{1,13},{5,9},{9,5},{13,1},{2,14},{6,10},... | collective-permute-start | bytes 98312 | tf_op jit(solution)/shard_map/ppermute | solution.py:35
  24.3 1.9 %collective-permute-start.6 = (f32[32,256]{1,0:T(8,128)S(1)}, f32[32,256]{1,0:T(8,128)S(1)}, u32[]{:S(2)}, u32[]{:S(2)}) collective-permute-start(f32[32,256]{1,0:T(8,128)S(1)} %get-tuple-element.42), channel_id=1, source_target_pairs={{0,4},{4,0},{8,12},{12,8},{1,5},{5,1},{9,13},{13,9},{2,6},{6,2},{1... | collective-permute-start | bytes 98312 | tf_op jit(solution)/shard_map/ppermute | solution.py:35
  26.2 1.4 %collective-permute-done.4.rest_0_ = f32[32,256]{1,0:T(8,128)S(1)} collective-permute-done((f32[32,256]{1,0:T(8,128)S(1)}, f32[32,256]{1,0:T(8,128)S(1)}, u32[]{:S(2)}, u32[]{:S(2)}) %collective-permute-start.4) | collective-permute-done | bytes 32800 | tf_op jit(solution)/shard_map/ppermute | solution.py:35
  27.7 1.5 %collective-permute-done.5.rest_1_ = f32[32,256]{1,0:T(8,128)S(1)} collective-permute-done((f32[32,256]{1,0:T(8,128)S(1)}, f32[32,256]{1,0:T(8,128)S(1)}, u32[]{:S(2)}, u32[]{:S(2)}) %collective-permute-start.5) | collective-permute-done | bytes 32800 | tf_op jit(solution)/shard_map/ppermute | solution.py:35
  29.2 0.5 %attend.1.refs_0_ = bf16[1,4096]{1,0:T(2,128)(2,1)S(1)} custom-call(bf16[512,512]{1,0:T(8,128)(2,1)S(1)} %get-tuple-element.29.map_ref, s32[1,1024]{1,0:T(1,128)S(1)} %get-tuple-element.28.after_ref.place_ref, f32[32,256]{1,0:T(8,128)S(1)} %collective-permute-done.4.rest_0_, f32[32,256]{1,0:T(8,128)S(1)} %collective-permute-done.5.rest_1_, ...), custom_call_target="tpu_custom_call" | custom-call | tf_op jit(solution)/shard_map/attend/pallas_call | solution.py:396
  29.7 0.1 collective-permute-start.8
  29.8 1.2 %collective-permute-done.8.refs_1_ = bf16[1,4096]{1,0:T(2,128)(2,1)S(1)} collective-permute-done((bf16[1,4096]{1,0:T(2,128)(2,1)S(1)}, bf16[1,4096]{1,0:T(2,128)(2,1)S(1)}, u32[]{:S(2)}, u32[]{:S(2)}) %collective-permute-start.8) | collective-permute-done | bytes 8224 | tf_op jit(solution)/shard_map/ppermute | solution.py:35
  31.0 1.9 %collective-permute-start.11 = (bf16[2,4096]{1,0:T(2,128)(2,1)S(1)}, bf16[2,4096]{1,0:T(2,128)(2,1)S(1)}, u32[]{:S(2)}, u32[]{:S(2)}) collective-permute-start(bf16[2,4096]{1,0:T(2,128)(2,1)S(1)} %join.1.rest_0_), channel_id=1, source_target_pairs={{0,12},{4,8},{8,4},{12,0},{1,13},{5,9},{9,5},{13,1},{2,14},{6,10},... | collective-permute-start | bytes 49160 | tf_op jit(solution)/shard_map/ppermute | solution.py:35
  32.8 0.6 %collective-permute-start.10 = (bf16[2,4096]{1,0:T(2,128)(2,1)S(1)}, bf16[2,4096]{1,0:T(2,128)(2,1)S(1)}, u32[]{:S(2)}, u32[]{:S(2)}) collective-permute-start(bf16[2,4096]{1,0:T(2,128)(2,1)S(1)} %join.1.rest_0_), channel_id=1, source_target_pairs={{0,8},{4,12},{8,0},{12,4},{1,9},{5,13},{9,1},{13,5},{2,10},{6,14},... | collective-permute-start | bytes 49160 | tf_op jit(solution)/shard_map/ppermute | solution.py:35
  33.5 1.9 %collective-permute-start.9 = (bf16[2,4096]{1,0:T(2,128)(2,1)S(1)}, bf16[2,4096]{1,0:T(2,128)(2,1)S(1)}, u32[]{:S(2)}, u32[]{:S(2)}) collective-permute-start(bf16[2,4096]{1,0:T(2,128)(2,1)S(1)} %join.1.rest_0_), channel_id=1, source_target_pairs={{0,4},{4,0},{8,12},{12,8},{1,5},{5,1},{9,13},{13,9},{2,6},{6,2},{1... | collective-permute-start | bytes 49160 | tf_op jit(solution)/shard_map/ppermute | solution.py:35
  35.4 1.3 %collective-permute-done.11.rest_3_ = bf16[2,4096]{1,0:T(2,128)(2,1)S(1)} collective-permute-done((bf16[2,4096]{1,0:T(2,128)(2,1)S(1)}, bf16[2,4096]{1,0:T(2,128)(2,1)S(1)}, u32[]{:S(2)}, u32[]{:S(2)}) %collective-permute-start.11) | collective-permute-done | bytes 16416 | tf_op jit(solution)/shard_map/ppermute | solution.py:35
  36.7 0.8 %collective-permute-done.10.rest_2_ = bf16[2,4096]{1,0:T(2,128)(2,1)S(1)} collective-permute-done((bf16[2,4096]{1,0:T(2,128)(2,1)S(1)}, bf16[2,4096]{1,0:T(2,128)(2,1)S(1)}, u32[]{:S(2)}, u32[]{:S(2)}) %collective-permute-start.10) | collective-permute-done | bytes 16416 | tf_op jit(solution)/shard_map/ppermute | solution.py:35
  37.5 1.2 %project.1 = (f32[2,1024]{1,0:T(2,128)S(1)}, f32[2,1024]{1,0:T(2,128)S(1)}, f32[2,1024]{1,0:T(2,128)S(1)}, f32[2,1024]{1,0:T(2,128)S(1)}) custom-call(bf16[4096,1024]{1,0:T(8,128)(2,1)S(1)} %stage.1.after_ref.weight_ref, bf16[2,4096]{1,0:T(2,128)(2,1)S(1)} %join.1.rest_0_, bf16[2,4096]{1,0:T(2,128)(2,1)S(1)} %collective-permute-done.9.rest_1_, ...), custom_call_target="tpu_custom_call" | custom-call | tf_op jit(solution)/shard_map/project/pallas_call | solution.py:409
  38.7 0.2 collective-permute-start.12
  38.8 1.4 %collective-permute-start.13 = (f32[2,1024]{1,0:T(2,128)S(1)}, f32[2,1024]{1,0:T(2,128)S(1)}, u32[]{:S(2)}, u32[]{:S(2)}) collective-permute-start(f32[2,1024]{1,0:T(2,128)S(1)} %get-tuple-element.46), channel_id=1, source_target_pairs={{0,2},{1,3},{2,0},{3,1},{4,6},{5,7},{6,4},{7,5},{8,10},{9,11},{10,... | collective-permute-start | bytes 24584 | tf_op jit(solution)/shard_map/ppermute | solution.py:35
  40.3 0.3 collective-permute-start.14
  40.6 1.3 %collective-permute-done.12.refs_0_ = f32[2,1024]{1,0:T(2,128)S(1)} collective-permute-done((f32[2,1024]{1,0:T(2,128)S(1)}, f32[2,1024]{1,0:T(2,128)S(1)}, u32[]{:S(2)}, u32[]{:S(2)}) %collective-permute-start.12) | collective-permute-done | bytes 8224 | tf_op jit(solution)/shard_map/ppermute | solution.py:35
  41.9 0.6 %collective-permute-done.13.refs_1_ = f32[2,1024]{1,0:T(2,128)S(1)} collective-permute-done((f32[2,1024]{1,0:T(2,128)S(1)}, f32[2,1024]{1,0:T(2,128)S(1)}, u32[]{:S(2)}, u32[]{:S(2)}) %collective-permute-start.13) | collective-permute-done | bytes 8224 | tf_op jit(solution)/shard_map/ppermute | solution.py:35
  42.5 0.6 %finish.1 = bf16[1,2,2048]{2,1,0:T(2,128)(2,1)} custom-call(f32[2,1024]{1,0:T(2,128)S(1)} %collective-permute-done.12.refs_0_, f32[2,1024]{1,0:T(2,128)S(1)} %collective-permute-done.13.refs_1_, f32[2,1024]{1,0:T(2,128)S(1)} %collective-permute-done.14.refs_2_, f32[2,1024]{1,0:T(2,128)S(1)} %get-tuple-element.48.refs_3_), custom_call_target="tpu_custom_call" | custom-call | tf_op jit(solution)/shard_map/finish/pallas_call | solution.py:418
  (7 shorter events, 0.0 us)
Async XLA Ops:
  2.5 14.9 %collective-permute-start = (bf16[1024,256]{1,0:T(8,128)(2,1)S(1)}, bf16[1024,256]{1,0:T(8,128)(2,1)S(1)}, u32[]{:S(2)}, u32[]{:S(2)}) collective-permute-start(bf16[1024,256]{1,0:T(8,128)(2,1)S(1)} %get-tuple-element.35.rest_0_), channel_id=1, source_target_pairs={{0,2},{2,0},{1,3},{3,1},{4,6},{6,4},{5,7},{7,5},{8,10},{10,8},{9,1... | collective-permute-start | bytes 1572872 | tf_op jit(solution)/shard_map/ppermute | solution.py:35
  5.5 12.8 %collective-permute-start.1 = (bf16[272,256]{1,0:T(8,128)(2,1)S(1)}, bf16[272,256]{1,0:T(8,128)(2,1)S(1)}, u32[]{:S(2)}, u32[]{:S(2)}) collective-permute-start(bf16[272,256]{1,0:T(8,128)(2,1)S(1)} %get-tuple-element.36), channel_id=1, source_target_pairs={{0,12},{4,8},{8,4},{12,0},{1,13},{5,9},{9,5},{13,1},{2,14},{6,10},... | collective-permute-start | bytes 417800 | tf_op jit(solution)/shard_map/ppermute | solution.py:35
  9.1 11.5 %collective-permute-start.2 = (bf16[272,256]{1,0:T(8,128)(2,1)S(1)}, bf16[272,256]{1,0:T(8,128)(2,1)S(1)}, u32[]{:S(2)}, u32[]{:S(2)}) collective-permute-start(bf16[272,256]{1,0:T(8,128)(2,1)S(1)} %get-tuple-element.37), channel_id=1, source_target_pairs={{0,8},{4,12},{8,0},{12,4},{1,9},{5,13},{9,1},{13,5},{2,10},{6,14},... | collective-permute-start | bytes 417800 | tf_op jit(solution)/shard_map/ppermute | solution.py:35
  12.1 8.5 %collective-permute-start.3 = (bf16[272,256]{1,0:T(8,128)(2,1)S(1)}, bf16[272,256]{1,0:T(8,128)(2,1)S(1)}, u32[]{:S(2)}, u32[]{:S(2)}) collective-permute-start(bf16[272,256]{1,0:T(8,128)(2,1)S(1)} %get-tuple-element.38), channel_id=1, source_target_pairs={{0,4},{4,0},{8,12},{12,8},{1,5},{5,1},{9,13},{13,9},{2,6},{6,2},{1... | collective-permute-start | bytes 417800 | tf_op jit(solution)/shard_map/ppermute | solution.py:35
  21.2 7.9 %collective-permute-start.7 = (bf16[512,256]{1,0:T(8,128)(2,1)S(1)}, bf16[512,256]{1,0:T(8,128)(2,1)S(1)}, u32[]{:S(2)}, u32[]{:S(2)}) collective-permute-start(bf16[512,256]{1,0:T(8,128)(2,1)S(1)} %get-tuple-element.44.rest_4_), channel_id=1, source_target_pairs={{0,2},{2,0},{1,3},{3,1},{4,6},{6,4},{5,7},{7,5},{8,10},{10,8},{9,1... | collective-permute-start | bytes 786440 | tf_op jit(solution)/shard_map/ppermute | solution.py:35
  21.8 5.8 %collective-permute-start.4 = (f32[32,256]{1,0:T(8,128)S(1)}, f32[32,256]{1,0:T(8,128)S(1)}, u32[]{:S(2)}, u32[]{:S(2)}) collective-permute-start(f32[32,256]{1,0:T(8,128)S(1)} %get-tuple-element.40), channel_id=1, source_target_pairs={{0,12},{4,8},{8,4},{12,0},{1,13},{5,9},{9,5},{13,1},{2,14},{6,10},... | collective-permute-start | bytes 98312 | tf_op jit(solution)/shard_map/ppermute | solution.py:35
  24.3 4.8 %collective-permute-start.5 = (f32[32,256]{1,0:T(8,128)S(1)}, f32[32,256]{1,0:T(8,128)S(1)}, u32[]{:S(2)}, u32[]{:S(2)}) collective-permute-start(f32[32,256]{1,0:T(8,128)S(1)} %get-tuple-element.41), channel_id=1, source_target_pairs={{0,8},{4,12},{8,0},{12,4},{1,9},{5,13},{9,1},{13,5},{2,10},{6,14},... | collective-permute-start | bytes 98312 | tf_op jit(solution)/shard_map/ppermute | solution.py:35
  24.3 4.8 %collective-permute-start.6 = (f32[32,256]{1,0:T(8,128)S(1)}, f32[32,256]{1,0:T(8,128)S(1)}, u32[]{:S(2)}, u32[]{:S(2)}) collective-permute-start(f32[32,256]{1,0:T(8,128)S(1)} %get-tuple-element.42), channel_id=1, source_target_pairs={{0,4},{4,0},{8,12},{12,8},{1,5},{5,1},{9,13},{13,9},{2,6},{6,2},{1... | collective-permute-start | bytes 98312 | tf_op jit(solution)/shard_map/ppermute | solution.py:35
  29.7 1.2 %collective-permute-start.8 = (bf16[1,4096]{1,0:T(2,128)(2,1)S(1)}, bf16[1,4096]{1,0:T(2,128)(2,1)S(1)}, u32[]{:S(2)}, u32[]{:S(2)}) collective-permute-start(bf16[1,4096]{1,0:T(2,128)(2,1)S(1)} %attend.1.refs_0_), channel_id=1, source_target_pairs={{0,1},{1,0},{2,3},{3,2},{4,5},{5,4},{6,7},{7,6},{8,9},{9,8},{10,11... | collective-permute-start | bytes 24584 | tf_op jit(solution)/shard_map/ppermute | solution.py:35
  31.0 5.7 %collective-permute-start.11 = (bf16[2,4096]{1,0:T(2,128)(2,1)S(1)}, bf16[2,4096]{1,0:T(2,128)(2,1)S(1)}, u32[]{:S(2)}, u32[]{:S(2)}) collective-permute-start(bf16[2,4096]{1,0:T(2,128)(2,1)S(1)} %join.1.rest_0_), channel_id=1, source_target_pairs={{0,12},{4,8},{8,4},{12,0},{1,13},{5,9},{9,5},{13,1},{2,14},{6,10},... | collective-permute-start | bytes 49160 | tf_op jit(solution)/shard_map/ppermute | solution.py:35
  32.8 4.6 %collective-permute-start.10 = (bf16[2,4096]{1,0:T(2,128)(2,1)S(1)}, bf16[2,4096]{1,0:T(2,128)(2,1)S(1)}, u32[]{:S(2)}, u32[]{:S(2)}) collective-permute-start(bf16[2,4096]{1,0:T(2,128)(2,1)S(1)} %join.1.rest_0_), channel_id=1, source_target_pairs={{0,8},{4,12},{8,0},{12,4},{1,9},{5,13},{9,1},{13,5},{2,10},{6,14},... | collective-permute-start | bytes 49160 | tf_op jit(solution)/shard_map/ppermute | solution.py:35
  33.5 4.0 %collective-permute-start.9 = (bf16[2,4096]{1,0:T(2,128)(2,1)S(1)}, bf16[2,4096]{1,0:T(2,128)(2,1)S(1)}, u32[]{:S(2)}, u32[]{:S(2)}) collective-permute-start(bf16[2,4096]{1,0:T(2,128)(2,1)S(1)} %join.1.rest_0_), channel_id=1, source_target_pairs={{0,4},{4,0},{8,12},{12,8},{1,5},{5,1},{9,13},{13,9},{2,6},{6,2},{1... | collective-permute-start | bytes 49160 | tf_op jit(solution)/shard_map/ppermute | solution.py:35
  38.7 3.2 %collective-permute-start.12 = (f32[2,1024]{1,0:T(2,128)S(1)}, f32[2,1024]{1,0:T(2,128)S(1)}, u32[]{:S(2)}, u32[]{:S(2)}) collective-permute-start(f32[2,1024]{1,0:T(2,128)S(1)} %get-tuple-element.45), channel_id=1, source_target_pairs={{0,3},{1,2},{2,1},{3,0},{4,7},{5,6},{6,5},{7,4},{8,11},{9,10},{10,... | collective-permute-start | bytes 24584 | tf_op jit(solution)/shard_map/ppermute | solution.py:35
  38.8 3.7 %collective-permute-start.13 = (f32[2,1024]{1,0:T(2,128)S(1)}, f32[2,1024]{1,0:T(2,128)S(1)}, u32[]{:S(2)}, u32[]{:S(2)}) collective-permute-start(f32[2,1024]{1,0:T(2,128)S(1)} %get-tuple-element.46), channel_id=1, source_target_pairs={{0,2},{1,3},{2,0},{3,1},{4,6},{5,7},{6,4},{7,5},{8,10},{9,11},{10,... | collective-permute-start | bytes 24584 | tf_op jit(solution)/shard_map/ppermute | solution.py:35
  40.3 2.2 %collective-permute-start.14 = (f32[2,1024]{1,0:T(2,128)S(1)}, f32[2,1024]{1,0:T(2,128)S(1)}, u32[]{:S(2)}, u32[]{:S(2)}) collective-permute-start(f32[2,1024]{1,0:T(2,128)S(1)} %get-tuple-element.47), channel_id=1, source_target_pairs={{0,1},{1,0},{2,3},{3,2},{4,5},{5,4},{6,7},{7,6},{8,9},{9,8},{10,11... | collective-permute-start | bytes 24584 | tf_op jit(solution)/shard_map/ppermute | solution.py:35

commit v15 on v14

--- a/solution.py
+++ b/solution.py
@@ -170,22 +170,19 @@
     out_ref = rest[heads]
     head = lax.axis_index("heads")
     width = key_refs[0].shape[1]
-    rows = CAP * BLOCK
     maps = []
     for j in range(heads):
         owner = head ^ j
         maps.append(map_ref[pl.ds(pl.multiple_of(owner * width, width), width), :])
-    for k in range(pools):
-        at = slice(k * rows, (k + 1) * rows)
-        rebuilt = jnp.dot(key_refs[0][at, :], maps[0], preferred_element_type=jnp.float32)
+    for g in range(0, map_ref.shape[1] // HEAD_SIZE, 2):
+        pair = slice(g * HEAD_SIZE, min((g + 2) * HEAD_SIZE, map_ref.shape[1]))
+        rebuilt = jnp.dot(key_refs[0][...], maps[0][:, pair], preferred_element_type=jnp.float32)
         for j in range(1, heads):
-            rebuilt += jnp.dot(key_refs[j][at, :], maps[j], preferred_element_type=jnp.float32)
-        cosine = cos_ref[at, :]
-        sine = sin_ref[at, :]
-        for g in range(map_ref.shape[1] // HEAD_SIZE):
-            lanes = slice(g * HEAD_SIZE, (g + 1) * HEAD_SIZE)
-            one = rebuilt[:, lanes]
-            out_ref[at, lanes] = (one * cosine + pltpu.roll(one, HEAD_SIZE // 2, 1) * sine).astype(jnp.bfloat16)
+            rebuilt += jnp.dot(key_refs[j][...], maps[j][:, pair], preferred_element_type=jnp.float32)
+        for at in range(0, pair.stop - pair.start, HEAD_SIZE):
+            one = rebuilt[:, at : at + HEAD_SIZE]
+            turned = one * cos_ref[...] + pltpu.roll(one, HEAD_SIZE // 2, 1) * sin_ref[...]
+            out_ref[:, pair.start + at : pair.start + at + HEAD_SIZE] = turned.astype(jnp.bfloat16)
 
 
 def score_kernel(pools, turn_ref, live_ref, place_ref, key_ref, *rest):

time: 43.4 us -> 43.5 us (level)
  no operation moved by 1% of the time
where the time goes in v15:
time: 43.5 us; the launch traced here: 43.3 us
  starting transfers between devices  18.9 us (43%)
  Pallas kernels  12.9 us (30%)
  waiting for transfers between devices  11.4 us (26%)
    ppermute x15, starting transfers between devices, swap(): return lax.ppermute(value, axes, [(i, i ^ step) for i in range(size)])  18.9 us
    ppermute x15, waiting for transfers between devices, swap(): return lax.ppermute(value, axes, [(i, i ^ step) for i in range(size)])  11.4 us
    pallas_call x1, Pallas kernels, per_device(): pl.pallas_call(stage_kernel, out_shape=shape(out_weight.shape, bf16), in_...  3.39 us
    pallas_call x1, Pallas kernels, per_device(): pl.pallas_call(functools.partial(table_kernel, pools, shard_blocks), out_...  2.97 us
    pallas_call x1, Pallas kernels, per_device(): pl.pallas_call(functools.partial(gather_kernel, pools), out_shape=[shape(...  2.53 us
    pallas_call x1, Pallas kernels, per_device(): pl.pallas_call(functools.partial(project_kernel, pools, heads, reps), out...  1.21 us
    pallas_call x1, Pallas kernels, per_device(): pl.pallas_call(functools.partial(rebuild_kernel, pools, heads), out_shape...  1.04 us
  transfers between devices with their start and end apart: 15, of which 9 were waited for; matrix products, arithmetic and copies ran while one was open for 0% of the time, Pallas kernels for 17%

profile of v15, /device:TPU:0, one launch (start us, length us, event | category | flops | bytes accessed | tf_op | source)
XLA Modules:
  0.0 43.3 jit_solution(15613300186741670363)
XLA Ops:
  0.0 2.5 %gather.1 = (bf16[1024,256]{1,0:T(8,128)(2,1)S(1)}, bf16[272,256]{1,0:T(8,128)(2,1)S(1)}, bf16[272,256]{1,0:T(8,128)(2,1)S(1)}, bf16[272,256]{1,0:T(8,128)(2,1)S(1)}, bf16[272,256]{1,0:T(8,128)(2,1)S(1)}) custom-call(s32[1,4,4]{2,1,0:T(4,128)} %sel_ref.3, bf16[1,4,1024,512]{3,2,1,0:T(8,128)(2,1)} %lat_ref.1, bf16[1,1,4096]{2,1,0:T(2,128)(2,1)} %query_ref.1), custom_call_target="tpu_custom_call" | custom-call | tf_op jit(solution)/shard_map/gather/pallas_call | solution.py:331
  2.5 3.0 %collective-permute-start = (bf16[1024,256]{1,0:T(8,128)(2,1)S(1)}, bf16[1024,256]{1,0:T(8,128)(2,1)S(1)}, u32[]{:S(2)}, u32[]{:S(2)}) collective-permute-start(bf16[1024,256]{1,0:T(8,128)(2,1)S(1)} %get-tuple-element.35.rest_0_), channel_id=1, source_target_pairs={{0,2},{2,0},{1,3},{3,1},{4,6},{6,4},{5,7},{7,5},{8,10},{10,8},{9,1... | collective-permute-start | bytes 1572872 | tf_op jit(solution)/shard_map/ppermute | solution.py:35
  5.5 3.6 %collective-permute-start.1 = (bf16[272,256]{1,0:T(8,128)(2,1)S(1)}, bf16[272,256]{1,0:T(8,128)(2,1)S(1)}, u32[]{:S(2)}, u32[]{:S(2)}) collective-permute-start(bf16[272,256]{1,0:T(8,128)(2,1)S(1)} %get-tuple-element.36), channel_id=1, source_target_pairs={{0,12},{4,8},{8,4},{12,0},{1,13},{5,9},{9,5},{13,1},{2,14},{6,10},... | collective-permute-start | bytes 417800 | tf_op jit(solution)/shard_map/ppermute | solution.py:35
  9.1 0.0 collective-permute-start.2
  9.1 3.0 %tables.1 = (f32[1024,128]{1,0:T(8,128)S(1)}, f32[1024,128]{1,0:T(8,128)S(1)}, f32[8,128]{1,0:T(8,128)S(1)}, s32[4,256]{1,0:T(4,128)S(1)}, s32[1,1024]{1,0:T(1,1...) custom-call(s32[1,4,4]{2,1,0:T(4,128)} %sel_ref.3, ...), custom_call_target="tpu_custom_call", output_to_operand_aliasing={{7}: (5, {})} | custom-call | tf_op jit(solution)/shard_map/tables/pallas_call | solution.py:346
  12.1 0.8 %collective-permute-start.3 = (bf16[272,256]{1,0:T(8,128)(2,1)S(1)}, bf16[272,256]{1,0:T(8,128)(2,1)S(1)}, u32[]{:S(2)}, u32[]{:S(2)}) collective-permute-start(bf16[272,256]{1,0:T(8,128)(2,1)S(1)} %get-tuple-element.38), channel_id=1, source_target_pairs={{0,4},{4,0},{8,12},{12,8},{1,5},{5,1},{9,13},{13,9},{2,6},{6,2},{1... | collective-permute-start | bytes 417800 | tf_op jit(solution)/shard_map/ppermute | solution.py:35
  13.0 3.4 %stage.1.after_ref.weight_ref = bf16[4096,1024]{1,0:T(8,128)(2,1)S(1)} custom-call(bf16[4096,1024]{1,0:T(8,128)(2,1)} %weight_ref.1, s32[1,1024]{1,0:T(1,128)S(1)} %get-tuple-element.28.after_ref.place_ref), custom_call_target="tpu_custom_call" | custom-call | tf_op jit(solution)/shard_map/stage/pallas_call | solution.py:365
  16.4 1.1 %collective-permute-done.rest_1_ = bf16[1024,256]{1,0:T(8,128)(2,1)S(1)} collective-permute-done((bf16[1024,256]{1,0:T(8,128)(2,1)S(1)}, bf16[1024,256]{1,0:T(8,128)(2,1)S(1)}, u32[]{:S(2)}, u32[]{:S(2)}) %collective-permute-start) | collective-permute-done | bytes 524320 | tf_op jit(solution)/shard_map/ppermute | solution.py:35
  17.5 1.0 %rebuild.1.key_ref = bf16[1024,512]{1,0:T(8,128)(2,1)S(1)} custom-call(bf16[512,512]{1,0:T(8,128)(2,1)S(1)} %get-tuple-element.32.map_ref, f32[1024,128]{1,0:T(8,128)S(1)} %get-tuple-element.33.cos_ref, f32[1024,128]{1,0:T(8,128)S(1)} %get-tuple-element.34.sin_ref, bf16[4096,1024]{1,0:T(8,128)(2,1)S(1)} %stage.1.after_ref.weight_ref, ...), custom_call_target="tpu_custom_call" | custom-call | tf_op jit(solution)/shard_map/rebuild/pallas_call | solution.py:374
  18.5 0.0 collective-permute-done.1.rest_0_
  18.5 2.1 %collective-permute-done.2.rest_1_ = bf16[272,256]{1,0:T(8,128)(2,1)S(1)} collective-permute-done((bf16[272,256]{1,0:T(8,128)(2,1)S(1)}, bf16[272,256]{1,0:T(8,128)(2,1)S(1)}, u32[]{:S(2)}, u32[]{:S(2)}) %collective-permute-start.2) | collective-permute-done | bytes 139296 | tf_op jit(solution)/shard_map/ppermute | solution.py:35
  20.7 0.6 %score.1 = (bf16[512,256]{1,0:T(8,128)(2,1)S(1)}, f32[32,256]{1,0:T(8,128)S(1)}, f32[32,256]{1,0:T(8,128)S(1)}, f32[32,256]{1,0:T(8,128)S(1)}, f32[32,256]{1,0:T(8,128)S(1)}) custom-call(f32[8,128]{1,0:T(8,128)S(1)} %get-tuple-element.30.turn_ref, s32[4,256]{1,0:T(4,128)S(1)} %get-tuple-element.31.live_ref, ...), custom_call_target="tpu_custom_call" | custom-call | tf_op jit(solution)/shard_map/score/pallas_call | solution.py:382
  21.2 0.6 %collective-permute-start.7 = (bf16[512,256]{1,0:T(8,128)(2,1)S(1)}, bf16[512,256]{1,0:T(8,128)(2,1)S(1)}, u32[]{:S(2)}, u32[]{:S(2)}) collective-permute-start(bf16[512,256]{1,0:T(8,128)(2,1)S(1)} %get-tuple-element.44.rest_4_), channel_id=1, source_target_pairs={{0,2},{2,0},{1,3},{3,1},{4,6},{6,4},{5,7},{7,5},{8,10},{10,8},{9,1... | collective-permute-start | bytes 786440 | tf_op jit(solution)/shard_map/ppermute | solution.py:35
  21.8 2.7 %collective-permute-start.4 = (f32[32,256]{1,0:T(8,128)S(1)}, f32[32,256]{1,0:T(8,128)S(1)}, u32[]{:S(2)}, u32[]{:S(2)}) collective-permute-start(f32[32,256]{1,0:T(8,128)S(1)} %get-tuple-element.40), channel_id=1, source_target_pairs={{0,12},{4,8},{8,4},{12,0},{1,13},{5,9},{9,5},{13,1},{2,14},{6,10},... | collective-permute-start | bytes 98312 | tf_op jit(solution)/shard_map/ppermute | solution.py:35
  24.5 1.7 %collective-permute-start.6 = (f32[32,256]{1,0:T(8,128)S(1)}, f32[32,256]{1,0:T(8,128)S(1)}, u32[]{:S(2)}, u32[]{:S(2)}) collective-permute-start(f32[32,256]{1,0:T(8,128)S(1)} %get-tuple-element.42), channel_id=1, source_target_pairs={{0,4},{4,0},{8,12},{12,8},{1,5},{5,1},{9,13},{13,9},{2,6},{6,2},{1... | collective-permute-start | bytes 98312 | tf_op jit(solution)/shard_map/ppermute | solution.py:35
  26.2 1.3 %collective-permute-done.4.rest_0_ = f32[32,256]{1,0:T(8,128)S(1)} collective-permute-done((f32[32,256]{1,0:T(8,128)S(1)}, f32[32,256]{1,0:T(8,128)S(1)}, u32[]{:S(2)}, u32[]{:S(2)}) %collective-permute-start.4) | collective-permute-done | bytes 32800 | tf_op jit(solution)/shard_map/ppermute | solution.py:35
  27.5 1.8 %collective-permute-done.5.rest_1_ = f32[32,256]{1,0:T(8,128)S(1)} collective-permute-done((f32[32,256]{1,0:T(8,128)S(1)}, f32[32,256]{1,0:T(8,128)S(1)}, u32[]{:S(2)}, u32[]{:S(2)}) %collective-permute-start.5) | collective-permute-done | bytes 32800 | tf_op jit(solution)/shard_map/ppermute | solution.py:35
  29.4 0.5 %attend.1.refs_0_ = bf16[1,4096]{1,0:T(2,128)(2,1)S(1)} custom-call(bf16[512,512]{1,0:T(8,128)(2,1)S(1)} %get-tuple-element.29.map_ref, s32[1,1024]{1,0:T(1,128)S(1)} %get-tuple-element.28.after_ref.place_ref, f32[32,256]{1,0:T(8,128)S(1)} %collective-permute-done.4.rest_0_, f32[32,256]{1,0:T(8,128)S(1)} %collective-permute-done.5.rest_1_, ...), custom_call_target="tpu_custom_call" | custom-call | tf_op jit(solution)/shard_map/attend/pallas_call | solution.py:393
  29.9 0.1 collective-permute-start.8
  30.0 1.2 %collective-permute-done.8.refs_1_ = bf16[1,4096]{1,0:T(2,128)(2,1)S(1)} collective-permute-done((bf16[1,4096]{1,0:T(2,128)(2,1)S(1)}, bf16[1,4096]{1,0:T(2,128)(2,1)S(1)}, u32[]{:S(2)}, u32[]{:S(2)}) %collective-permute-start.8) | collective-permute-done | bytes 8224 | tf_op jit(solution)/shard_map/ppermute | solution.py:35
  31.2 1.8 %collective-permute-start.11 = (bf16[2,4096]{1,0:T(2,128)(2,1)S(1)}, bf16[2,4096]{1,0:T(2,128)(2,1)S(1)}, u32[]{:S(2)}, u32[]{:S(2)}) collective-permute-start(bf16[2,4096]{1,0:T(2,128)(2,1)S(1)} %join.1.rest_0_), channel_id=1, source_target_pairs={{0,12},{4,8},{8,4},{12,0},{1,13},{5,9},{9,5},{13,1},{2,14},{6,10},... | collective-permute-start | bytes 49160 | tf_op jit(solution)/shard_map/ppermute | solution.py:35
  33.0 0.5 %collective-permute-start.10 = (bf16[2,4096]{1,0:T(2,128)(2,1)S(1)}, bf16[2,4096]{1,0:T(2,128)(2,1)S(1)}, u32[]{:S(2)}, u32[]{:S(2)}) collective-permute-start(bf16[2,4096]{1,0:T(2,128)(2,1)S(1)} %join.1.rest_0_), channel_id=1, source_target_pairs={{0,8},{4,12},{8,0},{12,4},{1,9},{5,13},{9,1},{13,5},{2,10},{6,14},... | collective-permute-start | bytes 49160 | tf_op jit(solution)/shard_map/ppermute | solution.py:35
  33.5 2.1 %collective-permute-start.9 = (bf16[2,4096]{1,0:T(2,128)(2,1)S(1)}, bf16[2,4096]{1,0:T(2,128)(2,1)S(1)}, u32[]{:S(2)}, u32[]{:S(2)}) collective-permute-start(bf16[2,4096]{1,0:T(2,128)(2,1)S(1)} %join.1.rest_0_), channel_id=1, source_target_pairs={{0,4},{4,0},{8,12},{12,8},{1,5},{5,1},{9,13},{13,9},{2,6},{6,2},{1... | collective-permute-start | bytes 49160 | tf_op jit(solution)/shard_map/ppermute | solution.py:35
  35.6 1.3 %collective-permute-done.11.rest_3_ = bf16[2,4096]{1,0:T(2,128)(2,1)S(1)} collective-permute-done((bf16[2,4096]{1,0:T(2,128)(2,1)S(1)}, bf16[2,4096]{1,0:T(2,128)(2,1)S(1)}, u32[]{:S(2)}, u32[]{:S(2)}) %collective-permute-start.11) | collective-permute-done | bytes 16416 | tf_op jit(solution)/shard_map/ppermute | solution.py:35
  36.9 0.7 %collective-permute-done.10.rest_2_ = bf16[2,4096]{1,0:T(2,128)(2,1)S(1)} collective-permute-done((bf16[2,4096]{1,0:T(2,128)(2,1)S(1)}, bf16[2,4096]{1,0:T(2,128)(2,1)S(1)}, u32[]{:S(2)}, u32[]{:S(2)}) %collective-permute-start.10) | collective-permute-done | bytes 16416 | tf_op jit(solution)/shard_map/ppermute | solution.py:35
  37.7 1.2 %project.1 = (f32[2,1024]{1,0:T(2,128)S(1)}, f32[2,1024]{1,0:T(2,128)S(1)}, f32[2,1024]{1,0:T(2,128)S(1)}, f32[2,1024]{1,0:T(2,128)S(1)}) custom-call(bf16[4096,1024]{1,0:T(8,128)(2,1)S(1)} %stage.1.after_ref.weight_ref, bf16[2,4096]{1,0:T(2,128)(2,1)S(1)} %join.1.rest_0_, bf16[2,4096]{1,0:T(2,128)(2,1)S(1)} %collective-permute-done.9.rest_1_, ...), custom_call_target="tpu_custom_call" | custom-call | tf_op jit(solution)/shard_map/project/pallas_call | solution.py:406
  38.9 0.1 collective-permute-start.12
  38.9 1.4 %collective-permute-start.13 = (f32[2,1024]{1,0:T(2,128)S(1)}, f32[2,1024]{1,0:T(2,128)S(1)}, u32[]{:S(2)}, u32[]{:S(2)}) collective-permute-start(f32[2,1024]{1,0:T(2,128)S(1)} %get-tuple-element.46), channel_id=1, source_target_pairs={{0,2},{1,3},{2,0},{3,1},{4,6},{5,7},{6,4},{7,5},{8,10},{9,11},{10,... | collective-permute-start | bytes 24584 | tf_op jit(solution)/shard_map/ppermute | solution.py:35
  40.3 0.5 %collective-permute-start.14 = (f32[2,1024]{1,0:T(2,128)S(1)}, f32[2,1024]{1,0:T(2,128)S(1)}, u32[]{:S(2)}, u32[]{:S(2)}) collective-permute-start(f32[2,1024]{1,0:T(2,128)S(1)} %get-tuple-element.47), channel_id=1, source_target_pairs={{0,1},{1,0},{2,3},{3,2},{4,5},{5,4},{6,7},{7,6},{8,9},{9,8},{10,11... | collective-permute-start | bytes 24584 | tf_op jit(solution)/shard_map/ppermute | solution.py:35
  40.8 1.2 %collective-permute-done.12.refs_0_ = f32[2,1024]{1,0:T(2,128)S(1)} collective-permute-done((f32[2,1024]{1,0:T(2,128)S(1)}, f32[2,1024]{1,0:T(2,128)S(1)}, u32[]{:S(2)}, u32[]{:S(2)}) %collective-permute-start.12) | collective-permute-done | bytes 8224 | tf_op jit(solution)/shard_map/ppermute | solution.py:35
  42.0 0.7 %collective-permute-done.13.refs_1_ = f32[2,1024]{1,0:T(2,128)S(1)} collective-permute-done((f32[2,1024]{1,0:T(2,128)S(1)}, f32[2,1024]{1,0:T(2,128)S(1)}, u32[]{:S(2)}, u32[]{:S(2)}) %collective-permute-start.13) | collective-permute-done | bytes 8224 | tf_op jit(solution)/shard_map/ppermute | solution.py:35
  42.7 0.6 %finish.1 = bf16[1,2,2048]{2,1,0:T(2,128)(2,1)} custom-call(f32[2,1024]{1,0:T(2,128)S(1)} %collective-permute-done.12.refs_0_, f32[2,1024]{1,0:T(2,128)S(1)} %collective-permute-done.13.refs_1_, f32[2,1024]{1,0:T(2,128)S(1)} %collective-permute-done.14.refs_2_, f32[2,1024]{1,0:T(2,128)S(1)} %get-tuple-element.48.refs_3_), custom_call_target="tpu_custom_call" | custom-call | tf_op jit(solution)/shard_map/finish/pallas_call | solution.py:415
  (7 shorter events, 0.0 us)
Async XLA Ops:
  2.5 14.9 %collective-permute-start = (bf16[1024,256]{1,0:T(8,128)(2,1)S(1)}, bf16[1024,256]{1,0:T(8,128)(2,1)S(1)}, u32[]{:S(2)}, u32[]{:S(2)}) collective-permute-start(bf16[1024,256]{1,0:T(8,128)(2,1)S(1)} %get-tuple-element.35.rest_0_), channel_id=1, source_target_pairs={{0,2},{2,0},{1,3},{3,1},{4,6},{6,4},{5,7},{7,5},{8,10},{10,8},{9,1... | collective-permute-start | bytes 1572872 | tf_op jit(solution)/shard_map/ppermute | solution.py:35
  5.5 13.0 %collective-permute-start.1 = (bf16[272,256]{1,0:T(8,128)(2,1)S(1)}, bf16[272,256]{1,0:T(8,128)(2,1)S(1)}, u32[]{:S(2)}, u32[]{:S(2)}) collective-permute-start(bf16[272,256]{1,0:T(8,128)(2,1)S(1)} %get-tuple-element.36), channel_id=1, source_target_pairs={{0,12},{4,8},{8,4},{12,0},{1,13},{5,9},{9,5},{13,1},{2,14},{6,10},... | collective-permute-start | bytes 417800 | tf_op jit(solution)/shard_map/ppermute | solution.py:35
  9.1 11.5 %collective-permute-start.2 = (bf16[272,256]{1,0:T(8,128)(2,1)S(1)}, bf16[272,256]{1,0:T(8,128)(2,1)S(1)}, u32[]{:S(2)}, u32[]{:S(2)}) collective-permute-start(bf16[272,256]{1,0:T(8,128)(2,1)S(1)} %get-tuple-element.37), channel_id=1, source_target_pairs={{0,8},{4,12},{8,0},{12,4},{1,9},{5,13},{9,1},{13,5},{2,10},{6,14},... | collective-permute-start | bytes 417800 | tf_op jit(solution)/shard_map/ppermute | solution.py:35
  12.1 8.5 %collective-permute-start.3 = (bf16[272,256]{1,0:T(8,128)(2,1)S(1)}, bf16[272,256]{1,0:T(8,128)(2,1)S(1)}, u32[]{:S(2)}, u32[]{:S(2)}) collective-permute-start(bf16[272,256]{1,0:T(8,128)(2,1)S(1)} %get-tuple-element.38), channel_id=1, source_target_pairs={{0,4},{4,0},{8,12},{12,8},{1,5},{5,1},{9,13},{13,9},{2,6},{6,2},{1... | collective-permute-start | bytes 417800 | tf_op jit(solution)/shard_map/ppermute | solution.py:35
  21.2 8.1 %collective-permute-start.7 = (bf16[512,256]{1,0:T(8,128)(2,1)S(1)}, bf16[512,256]{1,0:T(8,128)(2,1)S(1)}, u32[]{:S(2)}, u32[]{:S(2)}) collective-permute-start(bf16[512,256]{1,0:T(8,128)(2,1)S(1)} %get-tuple-element.44.rest_4_), channel_id=1, source_target_pairs={{0,2},{2,0},{1,3},{3,1},{4,6},{6,4},{5,7},{7,5},{8,10},{10,8},{9,1... | collective-permute-start | bytes 786440 | tf_op jit(solution)/shard_map/ppermute | solution.py:35
  21.8 5.7 %collective-permute-start.4 = (f32[32,256]{1,0:T(8,128)S(1)}, f32[32,256]{1,0:T(8,128)S(1)}, u32[]{:S(2)}, u32[]{:S(2)}) collective-permute-start(f32[32,256]{1,0:T(8,128)S(1)} %get-tuple-element.40), channel_id=1, source_target_pairs={{0,12},{4,8},{8,4},{12,0},{1,13},{5,9},{9,5},{13,1},{2,14},{6,10},... | collective-permute-start | bytes 98312 | tf_op jit(solution)/shard_map/ppermute | solution.py:35
  24.5 4.8 %collective-permute-start.5 = (f32[32,256]{1,0:T(8,128)S(1)}, f32[32,256]{1,0:T(8,128)S(1)}, u32[]{:S(2)}, u32[]{:S(2)}) collective-permute-start(f32[32,256]{1,0:T(8,128)S(1)} %get-tuple-element.41), channel_id=1, source_target_pairs={{0,8},{4,12},{8,0},{12,4},{1,9},{5,13},{9,1},{13,5},{2,10},{6,14},... | collective-permute-start | bytes 98312 | tf_op jit(solution)/shard_map/ppermute | solution.py:35
  24.5 4.8 %collective-permute-start.6 = (f32[32,256]{1,0:T(8,128)S(1)}, f32[32,256]{1,0:T(8,128)S(1)}, u32[]{:S(2)}, u32[]{:S(2)}) collective-permute-start(f32[32,256]{1,0:T(8,128)S(1)} %get-tuple-element.42), channel_id=1, source_target_pairs={{0,4},{4,0},{8,12},{12,8},{1,5},{5,1},{9,13},{13,9},{2,6},{6,2},{1... | collective-permute-start | bytes 98312 | tf_op jit(solution)/shard_map/ppermute | solution.py:35
  29.9 1.2 %collective-permute-start.8 = (bf16[1,4096]{1,0:T(2,128)(2,1)S(1)}, bf16[1,4096]{1,0:T(2,128)(2,1)S(1)}, u32[]{:S(2)}, u32[]{:S(2)}) collective-permute-start(bf16[1,4096]{1,0:T(2,128)(2,1)S(1)} %attend.1.refs_0_), channel_id=1, source_target_pairs={{0,1},{1,0},{2,3},{3,2},{4,5},{5,4},{6,7},{7,6},{8,9},{9,8},{10,11... | collective-permute-start | bytes 24584 | tf_op jit(solution)/shard_map/ppermute | solution.py:35
  31.2 5.7 %collective-permute-start.11 = (bf16[2,4096]{1,0:T(2,128)(2,1)S(1)}, bf16[2,4096]{1,0:T(2,128)(2,1)S(1)}, u32[]{:S(2)}, u32[]{:S(2)}) collective-permute-start(bf16[2,4096]{1,0:T(2,128)(2,1)S(1)} %join.1.rest_0_), channel_id=1, source_target_pairs={{0,12},{4,8},{8,4},{12,0},{1,13},{5,9},{9,5},{13,1},{2,14},{6,10},... | collective-permute-start | bytes 49160 | tf_op jit(solution)/shard_map/ppermute | solution.py:35
  33.0 4.6 %collective-permute-start.10 = (bf16[2,4096]{1,0:T(2,128)(2,1)S(1)}, bf16[2,4096]{1,0:T(2,128)(2,1)S(1)}, u32[]{:S(2)}, u32[]{:S(2)}) collective-permute-start(bf16[2,4096]{1,0:T(2,128)(2,1)S(1)} %join.1.rest_0_), channel_id=1, source_target_pairs={{0,8},{4,12},{8,0},{12,4},{1,9},{5,13},{9,1},{13,5},{2,10},{6,14},... | collective-permute-start | bytes 49160 | tf_op jit(solution)/shard_map/ppermute | solution.py:35
  33.5 4.2 %collective-permute-start.9 = (bf16[2,4096]{1,0:T(2,128)(2,1)S(1)}, bf16[2,4096]{1,0:T(2,128)(2,1)S(1)}, u32[]{:S(2)}, u32[]{:S(2)}) collective-permute-start(bf16[2,4096]{1,0:T(2,128)(2,1)S(1)} %join.1.rest_0_), channel_id=1, source_target_pairs={{0,4},{4,0},{8,12},{12,8},{1,5},{5,1},{9,13},{13,9},{2,6},{6,2},{1... | collective-permute-start | bytes 49160 | tf_op jit(solution)/shard_map/ppermute | solution.py:35
  38.9 3.1 %collective-permute-start.12 = (f32[2,1024]{1,0:T(2,128)S(1)}, f32[2,1024]{1,0:T(2,128)S(1)}, u32[]{:S(2)}, u32[]{:S(2)}) collective-permute-start(f32[2,1024]{1,0:T(2,128)S(1)} %get-tuple-element.45), channel_id=1, source_target_pairs={{0,3},{1,2},{2,1},{3,0},{4,7},{5,6},{6,5},{7,4},{8,11},{9,10},{10,... | collective-permute-start | bytes 24584 | tf_op jit(solution)/shard_map/ppermute | solution.py:35
  38.9 3.7 %collective-permute-start.13 = (f32[2,1024]{1,0:T(2,128)S(1)}, f32[2,1024]{1,0:T(2,128)S(1)}, u32[]{:S(2)}, u32[]{:S(2)}) collective-permute-start(f32[2,1024]{1,0:T(2,128)S(1)} %get-tuple-element.46), channel_id=1, source_target_pairs={{0,2},{1,3},{2,0},{3,1},{4,6},{5,7},{6,4},{7,5},{8,10},{9,11},{10,... | collective-permute-start | bytes 24584 | tf_op jit(solution)/shard_map/ppermute | solution.py:35
  40.3 2.4 %collective-permute-start.14 = (f32[2,1024]{1,0:T(2,128)S(1)}, f32[2,1024]{1,0:T(2,128)S(1)}, u32[]{:S(2)}, u32[]{:S(2)}) collective-permute-start(f32[2,1024]{1,0:T(2,128)S(1)} %get-tuple-element.47), channel_id=1, source_target_pairs={{0,1},{1,0},{2,3},{3,2},{4,5},{5,4},{6,7},{7,6},{8,9},{9,8},{10,11... | collective-permute-start | bytes 24584 | tf_op jit(solution)/shard_map/ppermute | solution.py:35

commit v16 on v14

--- a/solution.py
+++ b/solution.py
@@ -41,6 +41,11 @@
 
 def in_vmem(value):
     return pltpu.with_memory_space_constraint(value, pltpu.VMEM)
+
+
+def served(size):
+    middle = size // 2
+    return [middle] + [k for k in range(size - 1, -1, -1) if k != middle]
 
 
 def params(mib, **more):
@@ -223,7 +228,7 @@
 
 
 def attend_kernel(pools, heads, map_ref, place_ref, *rest):
-    score_refs = rest[:pools][::-1]
+    score_refs = [rest[served(pools).index(k)] for k in range(pools)]
     value_refs = rest[pools : pools + heads]
     out_ref = rest[-1]
     head = lax.axis_index("heads")
@@ -273,7 +278,7 @@
 
 
 def project_kernel(pools, heads, reps, weight_ref, *rest):
-    row_refs = rest[:pools]
+    row_refs = [rest[served(pools)[::-1].index(k)] for k in range(pools)]
     out_refs = rest[pools:-1]
     acc = rest[-1]
     left = jnp.concatenate([ref[...].astype(jnp.float32) for ref in row_refs], axis=0).astype(jnp.bfloat16)
@@ -400,7 +405,7 @@
         out_specs=VMEM,
         compiler_params=params(16),
         name="attend",
-    )(value_maps, place, *score_parts[::-1], *dense_parts)
+    )(value_maps, place, *[score_parts[k] for k in served(pools)], *dense_parts)
     own_rows = join(*exchange(mine, "rep", reps))
     row_parts = exchange(own_rows, "pool", pools)
 
@@ -414,7 +419,7 @@
         scratch_shapes=[pltpu.VMEM((pools * reps, own_columns), f32)],
         compiler_params=params(24),
         name="project",
-    )(weight, *row_parts)
+    )(weight, *[row_parts[k] for k in served(pools)[::-1]])
     return pl.pallas_call(
         functools.partial(finish_kernel, heads, reps),
         out_shape=shape((1, each, reps * own_columns), bf16),

time: 43.4 us -> 43.6 us (level)
  waiting for transfers between devices: 11.5 us -> 13.5 us
  starting transfers between devices: 18.9 us -> 17.1 us
    ppermute x15, waiting for transfers between devices: 11.5 us -> 13.5 us  [swap(): return lax.ppermute(value, axes, [(i, i ^ step) for i in range(size)])]
    ppermute x15, starting transfers between devices: 18.9 us -> 17.1 us  [swap(): return lax.ppermute(value, axes, [(i, i ^ step) for i in range(size)])]
where the time goes in v16:
time: 43.6 us; the launch traced here: 43.3 us
  starting transfers between devices  17.1 us (39%)
  waiting for transfers between devices  13.5 us (31%)
  Pallas kernels  12.7 us (29%)
    ppermute x15, starting transfers between devices, swap(): return lax.ppermute(value, axes, [(i, i ^ step) for i in range(size)])  17.1 us
    ppermute x15, waiting for transfers between devices, swap(): return lax.ppermute(value, axes, [(i, i ^ step) for i in range(size)])  13.5 us
    pallas_call x1, Pallas kernels, per_device(): pl.pallas_call(stage_kernel, out_shape=shape(out_weight.shape, bf16), in_...  3.39 us
    pallas_call x1, Pallas kernels, per_device(): pl.pallas_call(functools.partial(table_kernel, pools, shard_blocks), out_...  2.97 us
    pallas_call x1, Pallas kernels, per_device(): pl.pallas_call(functools.partial(gather_kernel, pools), out_shape=[shape(...  2.53 us
    pallas_call x1, Pallas kernels, per_device(): pl.pallas_call(functools.partial(project_kernel, pools, heads, reps), out...  1.21 us
  transfers between devices with their start and end apart: 15, of which 9 were waited for; matrix products, arithmetic and copies ran while one was open for 0% of the time, Pallas kernels for 17%

profile of v16, /device:TPU:0, one launch (start us, length us, event | category | flops | bytes accessed | tf_op | source)
XLA Modules:
  0.0 43.3 jit_solution(6640372518417693600)
XLA Ops:
  0.0 2.5 %gather.1 = (bf16[1024,256]{1,0:T(8,128)(2,1)S(1)}, bf16[272,256]{1,0:T(8,128)(2,1)S(1)}, bf16[272,256]{1,0:T(8,128)(2,1)S(1)}, bf16[272,256]{1,0:T(8,128)(2,1)S(1)}, bf16[272,256]{1,0:T(8,128)(2,1)S(1)}) custom-call(s32[1,4,4]{2,1,0:T(4,128)} %sel_ref.3, bf16[1,4,1024,512]{3,2,1,0:T(8,128)(2,1)} %lat_ref.1, bf16[1,1,4096]{2,1,0:T(2,128)(2,1)} %query_ref.1), custom_call_target="tpu_custom_call" | custom-call | tf_op jit(solution)/shard_map/gather/pallas_call | solution.py:339
  2.5 3.0 %collective-permute-start = (bf16[1024,256]{1,0:T(8,128)(2,1)S(1)}, bf16[1024,256]{1,0:T(8,128)(2,1)S(1)}, u32[]{:S(2)}, u32[]{:S(2)}) collective-permute-start(bf16[1024,256]{1,0:T(8,128)(2,1)S(1)} %get-tuple-element.35.rest_0_), channel_id=1, source_target_pairs={{0,2},{2,0},{1,3},{3,1},{4,6},{6,4},{5,7},{7,5},{8,10},{10,8},{9,1... | collective-permute-start | bytes 1572872 | tf_op jit(solution)/shard_map/ppermute | solution.py:35
  5.5 3.6 %collective-permute-start.1 = (bf16[272,256]{1,0:T(8,128)(2,1)S(1)}, bf16[272,256]{1,0:T(8,128)(2,1)S(1)}, u32[]{:S(2)}, u32[]{:S(2)}) collective-permute-start(bf16[272,256]{1,0:T(8,128)(2,1)S(1)} %get-tuple-element.36), channel_id=1, source_target_pairs={{0,12},{4,8},{8,4},{12,0},{1,13},{5,9},{9,5},{13,1},{2,14},{6,10},... | collective-permute-start | bytes 417800 | tf_op jit(solution)/shard_map/ppermute | solution.py:35
  9.2 0.0 collective-permute-start.2
  9.2 3.0 %tables.1 = (f32[1024,128]{1,0:T(8,128)S(1)}, f32[1024,128]{1,0:T(8,128)S(1)}, f32[8,128]{1,0:T(8,128)S(1)}, s32[4,256]{1,0:T(4,128)S(1)}, s32[1,1024]{1,0:T(1,1...) custom-call(s32[1,4,4]{2,1,0:T(4,128)} %sel_ref.3, ...), custom_call_target="tpu_custom_call", output_to_operand_aliasing={{7}: (5, {})} | custom-call | tf_op jit(solution)/shard_map/tables/pallas_call | solution.py:354
  12.1 0.8 %collective-permute-start.3 = (bf16[272,256]{1,0:T(8,128)(2,1)S(1)}, bf16[272,256]{1,0:T(8,128)(2,1)S(1)}, u32[]{:S(2)}, u32[]{:S(2)}) collective-permute-start(bf16[272,256]{1,0:T(8,128)(2,1)S(1)} %get-tuple-element.38), channel_id=1, source_target_pairs={{0,4},{4,0},{8,12},{12,8},{1,5},{5,1},{9,13},{13,9},{2,6},{6,2},{1... | collective-permute-start | bytes 417800 | tf_op jit(solution)/shard_map/ppermute | solution.py:35
  13.0 3.4 %stage.1.after_ref.weight_ref = bf16[4096,1024]{1,0:T(8,128)(2,1)S(1)} custom-call(bf16[4096,1024]{1,0:T(8,128)(2,1)} %weight_ref.1, s32[1,1024]{1,0:T(1,128)S(1)} %get-tuple-element.28.after_ref.place_ref), custom_call_target="tpu_custom_call" | custom-call | tf_op jit(solution)/shard_map/stage/pallas_call | solution.py:373
  16.4 1.1 %collective-permute-done.rest_1_ = bf16[1024,256]{1,0:T(8,128)(2,1)S(1)} collective-permute-done((bf16[1024,256]{1,0:T(8,128)(2,1)S(1)}, bf16[1024,256]{1,0:T(8,128)(2,1)S(1)}, u32[]{:S(2)}, u32[]{:S(2)}) %collective-permute-start) | collective-permute-done | bytes 524320 | tf_op jit(solution)/shard_map/ppermute | solution.py:35
  17.5 0.9 %rebuild.1.key_ref = bf16[1024,512]{1,0:T(8,128)(2,1)S(1)} custom-call(bf16[512,512]{1,0:T(8,128)(2,1)S(1)} %get-tuple-element.32.map_ref, f32[1024,128]{1,0:T(8,128)S(1)} %get-tuple-element.33.cos_ref, f32[1024,128]{1,0:T(8,128)S(1)} %get-tuple-element.34.sin_ref, bf16[4096,1024]{1,0:T(8,128)(2,1)S(1)} %stage.1.after_ref.weight_ref, ...), custom_call_target="tpu_custom_call" | custom-call | tf_op jit(solution)/shard_map/rebuild/pallas_call | solution.py:382
  18.3 2.3 %collective-permute-done.2.rest_1_ = bf16[272,256]{1,0:T(8,128)(2,1)S(1)} collective-permute-done((bf16[272,256]{1,0:T(8,128)(2,1)S(1)}, bf16[272,256]{1,0:T(8,128)(2,1)S(1)}, u32[]{:S(2)}, u32[]{:S(2)}) %collective-permute-start.2) | collective-permute-done | bytes 139296 | tf_op jit(solution)/shard_map/ppermute | solution.py:35
  20.7 0.6 %score.1 = (bf16[512,256]{1,0:T(8,128)(2,1)S(1)}, f32[32,256]{1,0:T(8,128)S(1)}, f32[32,256]{1,0:T(8,128)S(1)}, f32[32,256]{1,0:T(8,128)S(1)}, f32[32,256]{1,0:T(8,128)S(1)}) custom-call(f32[8,128]{1,0:T(8,128)S(1)} %get-tuple-element.30.turn_ref, s32[4,256]{1,0:T(4,128)S(1)} %get-tuple-element.31.live_ref, ...), custom_call_target="tpu_custom_call" | custom-call | tf_op jit(solution)/shard_map/score/pallas_call | solution.py:390
  21.2 0.6 %collective-permute-start.7 = (bf16[512,256]{1,0:T(8,128)(2,1)S(1)}, bf16[512,256]{1,0:T(8,128)(2,1)S(1)}, u32[]{:S(2)}, u32[]{:S(2)}) collective-permute-start(bf16[512,256]{1,0:T(8,128)(2,1)S(1)} %get-tuple-element.44.rest_4_), channel_id=1, source_target_pairs={{0,2},{2,0},{1,3},{3,1},{4,6},{6,4},{5,7},{7,5},{8,10},{10,8},{9,1... | collective-permute-start | bytes 786440 | tf_op jit(solution)/shard_map/ppermute | solution.py:35
  21.8 1.5 %collective-permute-start.4 = (f32[32,256]{1,0:T(8,128)S(1)}, f32[32,256]{1,0:T(8,128)S(1)}, u32[]{:S(2)}, u32[]{:S(2)}) collective-permute-start(f32[32,256]{1,0:T(8,128)S(1)} %get-tuple-element.40), channel_id=1, source_target_pairs={{0,8},{4,12},{8,0},{12,4},{1,9},{5,13},{9,1},{13,5},{2,10},{6,14},... | collective-permute-start | bytes 98312 | tf_op jit(solution)/shard_map/ppermute | solution.py:35
  23.3 1.3 %collective-permute-start.5 = (f32[32,256]{1,0:T(8,128)S(1)}, f32[32,256]{1,0:T(8,128)S(1)}, u32[]{:S(2)}, u32[]{:S(2)}) collective-permute-start(f32[32,256]{1,0:T(8,128)S(1)} %get-tuple-element.41), channel_id=1, source_target_pairs={{0,12},{4,8},{8,4},{12,0},{1,13},{5,9},{9,5},{13,1},{2,14},{6,10},... | collective-permute-start | bytes 98312 | tf_op jit(solution)/shard_map/ppermute | solution.py:35
  24.7 0.6 %collective-permute-start.6 = (f32[32,256]{1,0:T(8,128)S(1)}, f32[32,256]{1,0:T(8,128)S(1)}, u32[]{:S(2)}, u32[]{:S(2)}) collective-permute-start(f32[32,256]{1,0:T(8,128)S(1)} %get-tuple-element.42), channel_id=1, source_target_pairs={{0,4},{4,0},{8,12},{12,8},{1,5},{5,1},{9,13},{13,9},{2,6},{6,2},{1... | collective-permute-start | bytes 98312 | tf_op jit(solution)/shard_map/ppermute | solution.py:35
  25.3 1.9 %collective-permute-done.4.rest_0_ = f32[32,256]{1,0:T(8,128)S(1)} collective-permute-done((f32[32,256]{1,0:T(8,128)S(1)}, f32[32,256]{1,0:T(8,128)S(1)}, u32[]{:S(2)}, u32[]{:S(2)}) %collective-permute-start.4) | collective-permute-done | bytes 32800 | tf_op jit(solution)/shard_map/ppermute | solution.py:35
  27.2 1.9 %collective-permute-done.5.rest_1_ = f32[32,256]{1,0:T(8,128)S(1)} collective-permute-done((f32[32,256]{1,0:T(8,128)S(1)}, f32[32,256]{1,0:T(8,128)S(1)}, u32[]{:S(2)}, u32[]{:S(2)}) %collective-permute-start.5) | collective-permute-done | bytes 32800 | tf_op jit(solution)/shard_map/ppermute | solution.py:35
  29.1 0.5 %attend.1.refs_0_ = bf16[1,4096]{1,0:T(2,128)(2,1)S(1)} custom-call(bf16[512,512]{1,0:T(8,128)(2,1)S(1)} %get-tuple-element.29.map_ref, s32[1,1024]{1,0:T(1,128)S(1)} %get-tuple-element.28.after_ref.place_ref, f32[32,256]{1,0:T(8,128)S(1)} %collective-permute-done.4.rest_0_, f32[32,256]{1,0:T(8,128)S(1)} %collective-permute-done.5.rest_1_, ...), custom_call_target="tpu_custom_call" | custom-call | tf_op jit(solution)/shard_map/attend/pallas_call | solution.py:401
  29.6 0.1 collective-permute-start.8
  29.7 1.2 %collective-permute-done.8.refs_1_ = bf16[1,4096]{1,0:T(2,128)(2,1)S(1)} collective-permute-done((bf16[1,4096]{1,0:T(2,128)(2,1)S(1)}, bf16[1,4096]{1,0:T(2,128)(2,1)S(1)}, u32[]{:S(2)}, u32[]{:S(2)}) %collective-permute-start.8) | collective-permute-done | bytes 8224 | tf_op jit(solution)/shard_map/ppermute | solution.py:35
  30.9 1.3 %collective-permute-start.11 = (bf16[2,4096]{1,0:T(2,128)(2,1)S(1)}, bf16[2,4096]{1,0:T(2,128)(2,1)S(1)}, u32[]{:S(2)}, u32[]{:S(2)}) collective-permute-start(bf16[2,4096]{1,0:T(2,128)(2,1)S(1)} %join.1.rest_0_), channel_id=1, source_target_pairs={{0,8},{4,12},{8,0},{12,4},{1,9},{5,13},{9,1},{13,5},{2,10},{6,14},... | collective-permute-start | bytes 49160 | tf_op jit(solution)/shard_map/ppermute | solution.py:35
  32.2 1.3 %collective-permute-start.10 = (bf16[2,4096]{1,0:T(2,128)(2,1)S(1)}, bf16[2,4096]{1,0:T(2,128)(2,1)S(1)}, u32[]{:S(2)}, u32[]{:S(2)}) collective-permute-start(bf16[2,4096]{1,0:T(2,128)(2,1)S(1)} %join.1.rest_0_), channel_id=1, source_target_pairs={{0,12},{4,8},{8,4},{12,0},{1,13},{5,9},{9,5},{13,1},{2,14},{6,10},... | collective-permute-start | bytes 49160 | tf_op jit(solution)/shard_map/ppermute | solution.py:35
  33.5 0.9 %collective-permute-start.9 = (bf16[2,4096]{1,0:T(2,128)(2,1)S(1)}, bf16[2,4096]{1,0:T(2,128)(2,1)S(1)}, u32[]{:S(2)}, u32[]{:S(2)}) collective-permute-start(bf16[2,4096]{1,0:T(2,128)(2,1)S(1)} %join.1.rest_0_), channel_id=1, source_target_pairs={{0,4},{4,0},{8,12},{12,8},{1,5},{5,1},{9,13},{13,9},{2,6},{6,2},{1... | collective-permute-start | bytes 49160 | tf_op jit(solution)/shard_map/ppermute | solution.py:35
  34.4 1.3 %collective-permute-done.11.rest_3_ = bf16[2,4096]{1,0:T(2,128)(2,1)S(1)} collective-permute-done((bf16[2,4096]{1,0:T(2,128)(2,1)S(1)}, bf16[2,4096]{1,0:T(2,128)(2,1)S(1)}, u32[]{:S(2)}, u32[]{:S(2)}) %collective-permute-start.11) | collective-permute-done | bytes 16416 | tf_op jit(solution)/shard_map/ppermute | solution.py:35
  35.7 2.0 %collective-permute-done.10.rest_2_ = bf16[2,4096]{1,0:T(2,128)(2,1)S(1)} collective-permute-done((bf16[2,4096]{1,0:T(2,128)(2,1)S(1)}, bf16[2,4096]{1,0:T(2,128)(2,1)S(1)}, u32[]{:S(2)}, u32[]{:S(2)}) %collective-permute-start.10) | collective-permute-done | bytes 16416 | tf_op jit(solution)/shard_map/ppermute | solution.py:35
  37.7 1.2 %project.1 = (f32[2,1024]{1,0:T(2,128)S(1)}, f32[2,1024]{1,0:T(2,128)S(1)}, f32[2,1024]{1,0:T(2,128)S(1)}, f32[2,1024]{1,0:T(2,128)S(1)}) custom-call(bf16[4096,1024]{1,0:T(8,128)(2,1)S(1)} %stage.1.after_ref.weight_ref, bf16[2,4096]{1,0:T(2,128)(2,1)S(1)} %join.1.rest_0_, bf16[2,4096]{1,0:T(2,128)(2,1)S(1)} %collective-permute-done.9.rest_1_, ...), custom_call_target="tpu_custom_call" | custom-call | tf_op jit(solution)/shard_map/project/pallas_call | solution.py:414
  38.9 0.1 collective-permute-start.12
  39.0 1.5 %collective-permute-start.13 = (f32[2,1024]{1,0:T(2,128)S(1)}, f32[2,1024]{1,0:T(2,128)S(1)}, u32[]{:S(2)}, u32[]{:S(2)}) collective-permute-start(f32[2,1024]{1,0:T(2,128)S(1)} %get-tuple-element.46), channel_id=1, source_target_pairs={{0,2},{1,3},{2,0},{3,1},{4,6},{5,7},{6,4},{7,5},{8,10},{9,11},{10,... | collective-permute-start | bytes 24584 | tf_op jit(solution)/shard_map/ppermute | solution.py:35
  40.5 0.3 collective-permute-start.14
  40.8 1.3 %collective-permute-done.12.refs_0_ = f32[2,1024]{1,0:T(2,128)S(1)} collective-permute-done((f32[2,1024]{1,0:T(2,128)S(1)}, f32[2,1024]{1,0:T(2,128)S(1)}, u32[]{:S(2)}, u32[]{:S(2)}) %collective-permute-start.12) | collective-permute-done | bytes 8224 | tf_op jit(solution)/shard_map/ppermute | solution.py:35
  42.1 0.6 %collective-permute-done.13.refs_1_ = f32[2,1024]{1,0:T(2,128)S(1)} collective-permute-done((f32[2,1024]{1,0:T(2,128)S(1)}, f32[2,1024]{1,0:T(2,128)S(1)}, u32[]{:S(2)}, u32[]{:S(2)}) %collective-permute-start.13) | collective-permute-done | bytes 8224 | tf_op jit(solution)/shard_map/ppermute | solution.py:35
  42.7 0.6 %finish.1 = bf16[1,2,2048]{2,1,0:T(2,128)(2,1)} custom-call(f32[2,1024]{1,0:T(2,128)S(1)} %collective-permute-done.12.refs_0_, f32[2,1024]{1,0:T(2,128)S(1)} %collective-permute-done.13.refs_1_, f32[2,1024]{1,0:T(2,128)S(1)} %collective-permute-done.14.refs_2_, f32[2,1024]{1,0:T(2,128)S(1)} %get-tuple-element.48.refs_3_), custom_call_target="tpu_custom_call" | custom-call | tf_op jit(solution)/shard_map/finish/pallas_call | solution.py:423
  (7 shorter events, 0.0 us)
Async XLA Ops:
  2.5 14.9 %collective-permute-start = (bf16[1024,256]{1,0:T(8,128)(2,1)S(1)}, bf16[1024,256]{1,0:T(8,128)(2,1)S(1)}, u32[]{:S(2)}, u32[]{:S(2)}) collective-permute-start(bf16[1024,256]{1,0:T(8,128)(2,1)S(1)} %get-tuple-element.35.rest_0_), channel_id=1, source_target_pairs={{0,2},{2,0},{1,3},{3,1},{4,6},{6,4},{5,7},{7,5},{8,10},{10,8},{9,1... | collective-permute-start | bytes 1572872 | tf_op jit(solution)/shard_map/ppermute | solution.py:35
  5.5 12.8 %collective-permute-start.1 = (bf16[272,256]{1,0:T(8,128)(2,1)S(1)}, bf16[272,256]{1,0:T(8,128)(2,1)S(1)}, u32[]{:S(2)}, u32[]{:S(2)}) collective-permute-start(bf16[272,256]{1,0:T(8,128)(2,1)S(1)} %get-tuple-element.36), channel_id=1, source_target_pairs={{0,12},{4,8},{8,4},{12,0},{1,13},{5,9},{9,5},{13,1},{2,14},{6,10},... | collective-permute-start | bytes 417800 | tf_op jit(solution)/shard_map/ppermute | solution.py:35
  9.2 11.5 %collective-permute-start.2 = (bf16[272,256]{1,0:T(8,128)(2,1)S(1)}, bf16[272,256]{1,0:T(8,128)(2,1)S(1)}, u32[]{:S(2)}, u32[]{:S(2)}) collective-permute-start(bf16[272,256]{1,0:T(8,128)(2,1)S(1)} %get-tuple-element.37), channel_id=1, source_target_pairs={{0,8},{4,12},{8,0},{12,4},{1,9},{5,13},{9,1},{13,5},{2,10},{6,14},... | collective-permute-start | bytes 417800 | tf_op jit(solution)/shard_map/ppermute | solution.py:35
  12.1 8.5 %collective-permute-start.3 = (bf16[272,256]{1,0:T(8,128)(2,1)S(1)}, bf16[272,256]{1,0:T(8,128)(2,1)S(1)}, u32[]{:S(2)}, u32[]{:S(2)}) collective-permute-start(bf16[272,256]{1,0:T(8,128)(2,1)S(1)} %get-tuple-element.38), channel_id=1, source_target_pairs={{0,4},{4,0},{8,12},{12,8},{1,5},{5,1},{9,13},{13,9},{2,6},{6,2},{1... | collective-permute-start | bytes 417800 | tf_op jit(solution)/shard_map/ppermute | solution.py:35
  21.2 7.8 %collective-permute-start.7 = (bf16[512,256]{1,0:T(8,128)(2,1)S(1)}, bf16[512,256]{1,0:T(8,128)(2,1)S(1)}, u32[]{:S(2)}, u32[]{:S(2)}) collective-permute-start(bf16[512,256]{1,0:T(8,128)(2,1)S(1)} %get-tuple-element.44.rest_4_), channel_id=1, source_target_pairs={{0,2},{2,0},{1,3},{3,1},{4,6},{6,4},{5,7},{7,5},{8,10},{10,8},{9,1... | collective-permute-start | bytes 786440 | tf_op jit(solution)/shard_map/ppermute | solution.py:35
  21.8 5.4 %collective-permute-start.4 = (f32[32,256]{1,0:T(8,128)S(1)}, f32[32,256]{1,0:T(8,128)S(1)}, u32[]{:S(2)}, u32[]{:S(2)}) collective-permute-start(f32[32,256]{1,0:T(8,128)S(1)} %get-tuple-element.40), channel_id=1, source_target_pairs={{0,8},{4,12},{8,0},{12,4},{1,9},{5,13},{9,1},{13,5},{2,10},{6,14},... | collective-permute-start | bytes 98312 | tf_op jit(solution)/shard_map/ppermute | solution.py:35
  23.3 5.7 %collective-permute-start.5 = (f32[32,256]{1,0:T(8,128)S(1)}, f32[32,256]{1,0:T(8,128)S(1)}, u32[]{:S(2)}, u32[]{:S(2)}) collective-permute-start(f32[32,256]{1,0:T(8,128)S(1)} %get-tuple-element.41), channel_id=1, source_target_pairs={{0,12},{4,8},{8,4},{12,0},{1,13},{5,9},{9,5},{13,1},{2,14},{6,10},... | collective-permute-start | bytes 98312 | tf_op jit(solution)/shard_map/ppermute | solution.py:35
  24.7 4.4 %collective-permute-start.6 = (f32[32,256]{1,0:T(8,128)S(1)}, f32[32,256]{1,0:T(8,128)S(1)}, u32[]{:S(2)}, u32[]{:S(2)}) collective-permute-start(f32[32,256]{1,0:T(8,128)S(1)} %get-tuple-element.42), channel_id=1, source_target_pairs={{0,4},{4,0},{8,12},{12,8},{1,5},{5,1},{9,13},{13,9},{2,6},{6,2},{1... | collective-permute-start | bytes 98312 | tf_op jit(solution)/shard_map/ppermute | solution.py:35
  29.6 1.2 %collective-permute-start.8 = (bf16[1,4096]{1,0:T(2,128)(2,1)S(1)}, bf16[1,4096]{1,0:T(2,128)(2,1)S(1)}, u32[]{:S(2)}, u32[]{:S(2)}) collective-permute-start(bf16[1,4096]{1,0:T(2,128)(2,1)S(1)} %attend.1.refs_0_), channel_id=1, source_target_pairs={{0,1},{1,0},{2,3},{3,2},{4,5},{5,4},{6,7},{7,6},{8,9},{9,8},{10,11... | collective-permute-start | bytes 24584 | tf_op jit(solution)/shard_map/ppermute | solution.py:35
  30.9 4.8 %collective-permute-start.11 = (bf16[2,4096]{1,0:T(2,128)(2,1)S(1)}, bf16[2,4096]{1,0:T(2,128)(2,1)S(1)}, u32[]{:S(2)}, u32[]{:S(2)}) collective-permute-start(bf16[2,4096]{1,0:T(2,128)(2,1)S(1)} %join.1.rest_0_), channel_id=1, source_target_pairs={{0,8},{4,12},{8,0},{12,4},{1,9},{5,13},{9,1},{13,5},{2,10},{6,14},... | collective-permute-start | bytes 49160 | tf_op jit(solution)/shard_map/ppermute | solution.py:35
  32.2 5.5 %collective-permute-start.10 = (bf16[2,4096]{1,0:T(2,128)(2,1)S(1)}, bf16[2,4096]{1,0:T(2,128)(2,1)S(1)}, u32[]{:S(2)}, u32[]{:S(2)}) collective-permute-start(bf16[2,4096]{1,0:T(2,128)(2,1)S(1)} %join.1.rest_0_), channel_id=1, source_target_pairs={{0,12},{4,8},{8,4},{12,0},{1,13},{5,9},{9,5},{13,1},{2,14},{6,10},... | collective-permute-start | bytes 49160 | tf_op jit(solution)/shard_map/ppermute | solution.py:35
  33.5 4.2 %collective-permute-start.9 = (bf16[2,4096]{1,0:T(2,128)(2,1)S(1)}, bf16[2,4096]{1,0:T(2,128)(2,1)S(1)}, u32[]{:S(2)}, u32[]{:S(2)}) collective-permute-start(bf16[2,4096]{1,0:T(2,128)(2,1)S(1)} %join.1.rest_0_), channel_id=1, source_target_pairs={{0,4},{4,0},{8,12},{12,8},{1,5},{5,1},{9,13},{13,9},{2,6},{6,2},{1... | collective-permute-start | bytes 49160 | tf_op jit(solution)/shard_map/ppermute | solution.py:35
  38.9 3.2 %collective-permute-start.12 = (f32[2,1024]{1,0:T(2,128)S(1)}, f32[2,1024]{1,0:T(2,128)S(1)}, u32[]{:S(2)}, u32[]{:S(2)}) collective-permute-start(f32[2,1024]{1,0:T(2,128)S(1)} %get-tuple-element.45), channel_id=1, source_target_pairs={{0,3},{1,2},{2,1},{3,0},{4,7},{5,6},{6,5},{7,4},{8,11},{9,10},{10,... | collective-permute-start | bytes 24584 | tf_op jit(solution)/shard_map/ppermute | solution.py:35
  39.0 3.7 %collective-permute-start.13 = (f32[2,1024]{1,0:T(2,128)S(1)}, f32[2,1024]{1,0:T(2,128)S(1)}, u32[]{:S(2)}, u32[]{:S(2)}) collective-permute-start(f32[2,1024]{1,0:T(2,128)S(1)} %get-tuple-element.46), channel_id=1, source_target_pairs={{0,2},{1,3},{2,0},{3,1},{4,6},{5,7},{6,4},{7,5},{8,10},{9,11},{10,... | collective-permute-start | bytes 24584 | tf_op jit(solution)/shard_map/ppermute | solution.py:35
  40.5 2.2 %collective-permute-start.14 = (f32[2,1024]{1,0:T(2,128)S(1)}, f32[2,1024]{1,0:T(2,128)S(1)}, u32[]{:S(2)}, u32[]{:S(2)}) collective-permute-start(f32[2,1024]{1,0:T(2,128)S(1)} %get-tuple-element.47), channel_id=1, source_target_pairs={{0,1},{1,0},{2,3},{3,2},{4,5},{5,4},{6,7},{7,6},{8,9},{9,8},{10,11... | collective-permute-start | bytes 24584 | tf_op jit(solution)/shard_map/ppermute | solution.py:35
